TPU v7x, 32 devices: a whole 2x2x4 slice. The times are simulated.
32 devices in a mesh: row: 8 (over y, x, core), col: 4 (over z).
Axes of the slice: x: 2, y: 2, z: 4, core: 2. Of those that a mesh axis runs over, the one named last changes fastest.
Arguments:
- features: bfloat16 [4096, 256], P(('row', 'col')), may hold values from -6 to 6
- degree: int32 [4096], P(('row', 'col')), may hold values from 1 to 128, as said below
- weight: bfloat16 [256, 256], replicated, may hold values from -0.375 to 0.375
- bias_vector: float32 [256], replicated, may hold values from -3 to 3
- cotangent: bfloat16 [4096, 256], P(('row', 'col')), may hold values from -6 to 6
- block_pos: int32 [8, 4, 16], P('row', 'col'), may hold values from 0 to 31
- edge_pos: int32 [8, 4, 16, 512], P('row', 'col'), may hold values from 0 to 16383
- block_count: int32 [8, 4], P('row', 'col'), may hold values from 2 to 16, as said below
Outputs:
- output: bfloat16 [4096, 256], P(('row', 'col'))
- grad_x: bfloat16 [4096, 256], P(('row', 'col'))
- grad_w: float32 [256, 256], replicated
- grad_b: float32 [256], replicated
Inputs may be any that keep to these rules, and one draw needn't show every extreme that they name: `degree`: powers of two up to 64 times 1 or 2; some node has 128. `block_count`: slots from this number on are ignored; some device has 16 live slots.
All inputs are finite; a program needn't handle non-finite values.
Results may differ from a plain program's by a relative error of at most 0.008.
Values may be sent and summed in bfloat16 or wider, within the bound.
No kernel may reach another device: no remote copies, remote signals or barrier semaphores. Data moves between devices by JAX's collectives and lax.ppermute only.
A program may use at most 64 MiB of HBM per device.

v0:
```python
import jax
import jax.numpy as jnp
from jax import lax
from jax.sharding import PartitionSpec as P

BLOCK = 128


def pointwise(agg_rows, weight, bias_vector, cot_rows, inv_rows):
    preact = jnp.dot(agg_rows, weight, preferred_element_type=jnp.float32) + bias_vector
    sig = jax.nn.sigmoid(preact)
    grad_pre = (cot_rows.astype(jnp.float32) * sig * (1.0 + preact * (1.0 - sig))).astype(
        jnp.bfloat16
    )
    grad_hidden = (
        jnp.dot(grad_pre, weight.T, preferred_element_type=jnp.float32) * inv_rows[:, None]
    ).astype(jnp.bfloat16)
    return (preact, grad_pre, grad_hidden)


def per_device(features, degree, weight, bias_vector, cotangent, block_pos, edge_pos, block_count):
    owned = features.shape[0]
    width = features.shape[1]
    row_count = lax.axis_size("row")
    col_count = lax.axis_size("col")
    row_blocks = owned * col_count // BLOCK
    col_blocks = owned * row_count // BLOCK
    slots = block_pos.shape[2]
    positions = block_pos.reshape(slots)
    edge_list = edge_pos.reshape(slots, edge_pos.shape[3])
    live_count = block_count.reshape(())
    inv_root = lax.rsqrt(degree.astype(jnp.float32))
    scaled = (features.astype(jnp.float32) * inv_root[:, None]).astype(jnp.bfloat16)
    gathered = lax.all_gather(scaled, "row", axis=0, tiled=True)
    flat_index = (
        jnp.arange(slots, dtype=jnp.int32)[:, None] * (BLOCK * BLOCK) + edge_list
    ).reshape(-1)
    blocks = jnp.zeros((slots * BLOCK * BLOCK,), jnp.float32).at[flat_index].add(1.0)
    blocks = blocks.reshape(slots, BLOCK, BLOCK).astype(jnp.bfloat16)
    live_mask = (jnp.arange(slots, dtype=jnp.int32) < live_count).astype(jnp.float32)
    row_sel = positions // col_blocks
    col_sel = positions % col_blocks
    picked = gathered.reshape(col_blocks, BLOCK, width)[col_sel]
    products = jnp.einsum("bmk,bkf->bmf", blocks, picked, preferred_element_type=jnp.float32)
    partial_rows = (
        jnp.zeros((row_blocks, BLOCK, width), jnp.float32)
        .at[row_sel]
        .add(products * live_mask[:, None, None])
    )
    partial_rows = partial_rows.reshape(row_blocks * BLOCK, width)
    own_sum = lax.psum_scatter(partial_rows, "col", scatter_dimension=0, tiled=True)
    agg_own = (own_sum * inv_root[:, None]).astype(jnp.bfloat16)
    preact, grad_pre_own, grad_hidden_own = pointwise(
        agg_own, weight, bias_vector, cotangent, inv_root
    )
    output = jax.nn.silu(preact).astype(jnp.bfloat16)
    hidden_rows = lax.all_gather(grad_hidden_own, "col", axis=0, tiled=True)
    weight_term = jnp.dot(agg_own.T, grad_pre_own, preferred_element_type=jnp.float32)
    bias_term = jnp.sum(grad_pre_own.astype(jnp.float32), axis=0)
    weight_sum, bias_sum = lax.psum((weight_term, bias_term), ("row", "col"))
    norm_scale = 1.0 / jnp.sqrt(jnp.float32(owned * row_count * col_count))
    grad_w = weight_sum * norm_scale
    grad_b = bias_sum * norm_scale
    picked_back = hidden_rows.reshape(row_blocks, BLOCK, width)[row_sel]
    back_products = jnp.einsum(
        "bmk,bmf->bkf", blocks, picked_back, preferred_element_type=jnp.float32
    )
    partial_cols = (
        jnp.zeros((col_blocks, BLOCK, width), jnp.float32)
        .at[col_sel]
        .add(back_products * live_mask[:, None, None])
    )
    partial_cols = partial_cols.reshape(col_blocks * BLOCK, width)
    col_sum = lax.psum_scatter(partial_cols, "row", scatter_dimension=0, tiled=True)
    grad_x = (col_sum * inv_root[:, None]).astype(jnp.bfloat16)
    return (output, grad_x, grad_w, grad_b)


def solution(mesh):
    placed = (
        P(("row", "col"), None),
        P(("row", "col")),
        P(),
        P(),
        P(("row", "col"), None),
        P("row", "col", None),
        P("row", "col", None, None),
        P("row", "col"),
    )
    return jax.shard_map(
        per_device,
        mesh=mesh,
        in_specs=placed,
        out_specs=(P(("row", "col"), None), P(("row", "col"), None), P(), P()),
        check_vma=False,
    )
```

profile of v0, /device:TPU:0, one launch (start us, length us, event | category | flops | bytes accessed | tf_op | source)
XLA Modules:
  0.0 270.2 jit_solution(12731081170074368418)
XLA Ops:
  7.2 0.0 copy-start
  7.2 0.0 reduce-scatter.3.cloned.1.call-start
  7.9 0.7 convert_rsqrt_fusion
  8.6 0.7 fusion.4
  9.3 0.1 broadcast_bitcast_fusion
  9.4 0.8 copy.16
  10.2 0.9 multiply_convert_fusion.4
  11.1 11.3 %all_gather.6 = bf16[1024,256]{1,0:T(8,128)(2,1)S(1)} all-gather(bf16[128,256]{1,0:T(8,128)(2,1)S(1)} %multiply_convert_fusion.4), channel_id=1, replica_groups=mesh['row'=8,'col'=4] {'row'}, dimensions={0}, use_global_device_ids=true | all-gather | bytes 589824 | tf_op jit(solution)/shard_map/all_gather | solution.py:34
  22.5 43.5 %scatter_custom_fusion = f32[262144]{0:T(1024)S(1)} fusion(s32[8192]{0:T(1024)S(1)} %bitcast.54, f32[8192]{0:T(1024)S(1)} %broadcast.154, f32[]{:T(128)} %constant.19.clone.1), kind=kCustom, calls=%fused_computation.10 | custom fusion | flops 8192 | bytes 1048580 | tf_op jit(solution)/shard_map/scatter-add | solution.py:38
  66.0 0.1 convert_element_type.43
  66.0 0.0 copy-start.3
  66.0 1.6 gather_fusion
  67.6 1.6 convolution_multiply_fusion.1
  69.3 0.0 copy-done.3
  69.3 0.0 copy-start.5
  69.3 0.0 copy-start.6
  69.4 2.2 scatter_fusion
  71.6 0.0 copy-start.1
  71.6 0.8 copy-done.1
  72.3 0.0 reduce-scatter.3.cloned.1.call-update
  72.4 0.0 all-reduce.2.cloned.1.call-start
  72.4 0.0 copy-start.4
  72.4 22.0 %reduce-scatter.3.cloned.1.call-done = f32[128,256]{1,0:T(8,128)} async-done(((f32[512,256]{1,0:T(8,128)}), f32[128,256]{1,0:T(8,128)}) %reduce-scatter.3.cloned.1.call-update) | async-done | bytes 131088 | tf_op jit(solution)/shard_map/reduce_scatter | solution.py:51
  94.5 0.0 copy-done
  94.5 0.0 copy-done.5
  94.5 0.0 copy-done.6
  94.5 1.8 convert_reduce_fusion
  96.3 0.2 fusion
  96.5 1.9 fusion.5
  98.4 0.0 all-reduce.2.cloned.1.call-update
  98.4 0.0 reduce-scatter.5.cloned.1.call-start
  98.5 14.1 %all_gather.7 = bf16[512,256]{1,0:T(8,128)(2,1)S(1)} all-gather(bf16[128,256]{1,0:T(8,128)(2,1)S(1)} %fusion), channel_id=1, replica_groups=mesh['row'=8,'col'=4] {'col'}, dimensions={0}, use_global_device_ids=true | all-gather | bytes 327680 | tf_op jit(solution)/shard_map/all_gather | solution.py:57
  112.6 1.6 gather_fusion.1
  114.2 0.0 copy-done.4
  114.2 1.7 convolution_multiply_fusion
  115.9 0.1 broadcast_in_dim.11
  116.0 2.2 scatter_fusion.1
  118.2 0.0 copy-start.2
  118.2 1.0 copy-done.2
  119.2 0.0 reduce-scatter.5.cloned.1.call-update
  119.2 38.4 %psum.15 = f32[256]{0:T(256)S(1)} all-reduce(f32[256]{0:T(256)S(1)} %get-tuple-element.4), channel_id=1, replica_groups=mesh['row'=8,'col'=4] {'row','col'}, use_global_device_ids=true, to_apply=%region_7.8 | all-reduce | flops 256 | bytes 2048 | tf_op jit(solution)/shard_map/psum | solution.py:60
  157.7 0.6 broadcast_multiply_fusion.1
  158.2 65.6 %all-reduce.2.cloned.1.call-done = f32[256,256]{1,0:T(8,128)} async-done(((f32[256,256]{1,0:T(8,128)}), f32[256,256]{1,0:T(8,128)}) %all-reduce.2.cloned.1.call-update) | async-done | bytes 262160 | tf_op jit(solution)/shard_map/psum | solution.py:60
  223.8 1.7 broadcast_multiply_fusion
  225.5 36.6 %reduce-scatter.5.cloned.1.call-done = f32[128,256]{1,0:T(8,128)} async-done(((f32[1024,256]{1,0:T(8,128)}), f32[128,256]{1,0:T(8,128)}) %reduce-scatter.5.cloned.1.call-update) | async-done | bytes 131088 | tf_op jit(solution)/shard_map/reduce_scatter | solution.py:74
  262.1 1.6 multiply_convert_fusion
  (8 shorter events, 0.1 us)
Async XLA Ops:
  7.2 87.3 %copy-start = (bf16[256,256]{1,0:T(8,128)(2,1)S(1)}, bf16[256,256]{1,0:T(8,128)(2,1)}, u32[]{:S(2)}) copy-start(bf16[256,256]{1,0:T(8,128)(2,1)} %param.10) | copy-start | bytes 393220
  7.2 87.3 %reduce-scatter.3.cloned.1.call-start = ((), (), s32[]{:S(2)}) async-start(), calls=%async_computation.2 | async-start | bytes 655360 | tf_op jit(solution)/shard_map/reduce_scatter | solution.py:51
  66.0 3.3 %copy-start.3 = (bf16[262144]{0:T(1024)(128)(2,1)}, bf16[262144]{0:T(1024)(128)(2,1)S(1)}, u32[]{:S(2)}) copy-start(bf16[262144]{0:T(1024)(128)(2,1)S(1)} %convert_element_type.43) | copy-start | bytes 1572868
  69.3 25.1 %copy-start.5 = (bf16[128,256]{1,0:T(8,128)(2,1)S(1)}, bf16[128,256]{1,0:T(8,128)(2,1)}, u32[]{:S(2)}) copy-start(bf16[128,256]{1,0:T(8,128)(2,1)} %param.12) | copy-start | bytes 196612
  69.3 25.1 %copy-start.6 = (f32[256]{0:T(256)S(1)}, f32[256]{0:T(256)}, u32[]{:S(2)}) copy-start(f32[256]{0:T(256)} %param.11) | copy-start | bytes 3076
  71.6 0.8 copy-start.1
  72.4 151.4 %all-reduce.2.cloned.1.call-start = ((), (), s32[]{:S(2)}) async-start(), calls=%async_computation.4 | async-start | bytes 524288 | tf_op jit(solution)/shard_map/psum | solution.py:60
  72.4 41.8 %copy-start.4 = (bf16[262144]{0:T(1024)(128)(2,1)S(1)}, bf16[262144]{0:T(1024)(128)(2,1)}, u32[]{:S(2)}) copy-start(bf16[262144]{0:T(1024)(128)(2,1)} %copy-done.3) | copy-start | bytes 1572868
  98.4 163.7 %reduce-scatter.5.cloned.1.call-start = ((), (), s32[]{:S(2)}) async-start(), calls=%async_computation.3 | async-start | bytes 1179648 | tf_op jit(solution)/shard_map/reduce_scatter | solution.py:74
  118.2 1.0 copy-start.2
Sparse Core Ops, SparseCore 0:
  72.5 21.9 reduce-scatter.2
  100.6 123.1 all-reduce.1
  227.0 35.0 reduce-scatter.4
where the time goes:
time: 271 us; the launch traced here: 270 us
  waiting for transfers between devices  124 us (46%)
  blocking collectives  63.9 us (24%)
  other arithmetic  54.1 us (20%)
  between operations  14.6 us (5%)
  matrix products  7.25 us (3%)
  local copies, waits for them, and re-layouts  6.02 us (2%)
    psum x1, waiting for transfers between devices, per_device(): weight_sum, bias_sum = lax.psum((weight_term, bias_term), ('row', 'col'))  65.6 us
    scatter-add x1, other arithmetic, per_device(): jnp.zeros((slots * BLOCK * BLOCK,), jnp.float32).at[flat_index].add(1.0)  43.5 us
    psum x1, blocking collectives, per_device(): weight_sum, bias_sum = lax.psum((weight_term, bias_term), ('row', 'col'))  38.4 us
    reduce_scatter x1, waiting for transfers between devices, per_device(): lax.psum_scatter(partial_cols, 'row', scatter_dimension=0, tiled=True)  36.6 us
    reduce_scatter x1, waiting for transfers between devices, per_device(): lax.psum_scatter(partial_rows, 'col', scatter_dimension=0, tiled=True)  22 us
    all_gather x1, blocking collectives, per_device(): hidden_rows = lax.all_gather(grad_hidden_own, 'col', axis=0, tiled=True)  14.1 us
    all_gather x1, blocking collectives, per_device(): gathered = lax.all_gather(scaled, 'row', axis=0, tiled=True)  11.3 us
  transfers between devices with their start and end apart: 3, of which 3 were waited for; matrix products, arithmetic and copies ran while one was open for 3% of the time, Pallas kernels for 0%

commit v1 on v0

v1 whole, which is shorter than its diff:
```python
import functools

import jax
import jax.numpy as jnp
from jax import lax
from jax.experimental import pallas as pl
from jax.experimental.pallas import tpu as pltpu
from jax.sharding import PartitionSpec as P

BLOCK = 128
CORES = 2
EXTRA = 16
VMEM = pl.BlockSpec(memory_space=pltpu.VMEM)
SMEM = pl.BlockSpec(memory_space=pltpu.SMEM)
NT = (((1,), (1,)), ((), ()))
TN = (((0,), (0,)), ((), ()))
BF16 = jnp.bfloat16
F32 = jnp.float32


def is_power(n):
    return n & (n - 1) == 0


def target(n, i, k):
    return i ^ k if is_power(n) else (i + k) % n


def offset_to(n, me, other):
    return me ^ other if is_power(n) else lax.rem(other - me + n, n)


def offset_from(n, me, other):
    return me ^ other if is_power(n) else lax.rem(me - other + n, n)


def to_core(x, rows):
    return lax.ppermute(x, "row", [(i, i ^ 1) for i in range(rows)])


def to_chip(x, rows, k):
    chips = rows // CORES
    pairs = [
        (a * CORES + b, target(chips, a, k) * CORES + b)
        for a in range(chips)
        for b in range(CORES)
    ]
    return lax.ppermute(x, "row", pairs)


def to_col(x, cols, k):
    return lax.ppermute(x, "col", [(i, target(cols, i, k)) for i in range(cols)])


def spread_inv(degree_ref, width):
    inv = lax.rsqrt(degree_ref[...].astype(F32))
    owned = inv.shape[1]
    tall = jnp.broadcast_to(inv, (BLOCK, owned)).T
    return jnp.concatenate([tall] * (width // BLOCK), axis=1)


def scale_kernel(features_ref, degree_ref, out_ref):
    inv = spread_inv(degree_ref, features_ref.shape[1])
    out_ref[...] = (features_ref[...].astype(F32) * inv).astype(BF16)


def for_live(count_ref, slots, body):
    count = count_ref[0, 0]

    def step(i, carry):
        body(i)
        return carry

    lax.fori_loop(0, count, step, 0)


def build_kernel(count_ref, edge_ref, blocks_ref):
    slots, edges = edge_ref.shape[2], edge_ref.shape[3]
    node = lax.broadcasted_iota(jnp.int32, (BLOCK, edges), 0)

    def build(s):
        edge = edge_ref[0, 0, pl.ds(s, 1), :]
        row_hot = jnp.where(node == edge // BLOCK, 1.0, 0.0).astype(BF16)
        col_hot = jnp.where(node == edge % BLOCK, 1.0, 0.0).astype(BF16)
        counts = lax.dot_general(row_hot, col_hot, NT, preferred_element_type=F32)
        blocks_ref[s] = counts.astype(BF16)

    for_live(count_ref, slots, build)


def forward_kernel(rows, cols, pos_ref, count_ref, blocks_ref, *refs):
    near = refs[: 2 * (rows // CORES)]
    own_ref, *send = refs[len(near) : len(near) + cols]
    gathered, acc = refs[len(near) + cols :]
    chips = rows // CORES
    row, col = lax.axis_index("row"), lax.axis_index("col")
    for n, ref in enumerate(near):
        gathered[n] = ref[...]
    acc[...] = jnp.zeros_like(acc)

    def add(s):
        p = pos_ref[0, 0, s]
        u, v = p // rows, lax.rem(p, rows)
        k = offset_from(chips, row // CORES, v // CORES)
        src = (lax.rem(v, CORES) ^ lax.rem(row, CORES)) * chips + k
        dst = offset_to(cols, col, u)
        acc[dst] += jnp.dot(blocks_ref[s], gathered[src], preferred_element_type=F32)

    for_live(count_ref, blocks_ref.shape[0], add)
    own_ref[...] = acc[0]
    for k, ref in enumerate(send, 1):
        ref[...] = acc[k].astype(BF16)


def pack_bias(total, rows):
    head = total.astype(BF16)
    tail = (total - head.astype(F32)).astype(BF16)
    index = lax.broadcasted_iota(jnp.int32, (rows, total.shape[1]), 0)
    both = jnp.where(index == 0, head.astype(F32), jnp.where(index == 1, tail.astype(F32), 0.0))
    return both.astype(BF16)


def add_bias(packed):
    return jnp.sum(packed.astype(F32), axis=0, keepdims=True)


def pointwise_kernel(cols, weight_ref, bias_ref, cot_ref, degree_ref, *refs):
    own_ref, *parts = refs[:cols]
    out_ref, hidden_ref, keep_ref, bias_keep_ref, send_ref = refs[cols:]
    width = out_ref.shape[1]
    half = width // CORES
    core = lax.rem(lax.axis_index("row"), CORES)
    inv = spread_inv(degree_ref, width)
    total = own_ref[...]
    for ref in parts:
        total = total + ref[...].astype(F32)
    agg = (total * inv).astype(BF16)
    weight = weight_ref[...]
    preact = jnp.dot(agg, weight, preferred_element_type=F32) + bias_ref[...]
    sig = jax.nn.sigmoid(preact)
    out_ref[...] = (preact * sig).astype(BF16)
    grad_pre = (cot_ref[...].astype(F32) * sig * (1.0 + preact * (1.0 - sig))).astype(BF16)
    hidden = lax.dot_general(grad_pre, weight, NT, preferred_element_type=F32)
    hidden_ref[...] = (hidden * inv).astype(BF16)
    term = lax.dot_general(agg, grad_pre, TN, preferred_element_type=F32)
    low, high = term[:half], term[half:]
    first = core == 0
    keep_ref[...] = jnp.where(first, low, high)
    send_ref[:half] = jnp.where(first, high, low).astype(BF16)
    bias_sum = jnp.sum(grad_pre.astype(F32), axis=0, keepdims=True)
    bias_keep_ref[...] = bias_sum
    send_ref[half:] = pack_bias(bias_sum, EXTRA)


def pair_sum_kernel(keep_ref, bias_keep_ref, got_ref, out_ref):
    half = keep_ref.shape[0]
    out_ref[:half] = (keep_ref[...] + got_ref[:half].astype(F32)).astype(BF16)
    out_ref[half:] = pack_bias(bias_keep_ref[...] + add_bias(got_ref[half:]), EXTRA)


def add_kernel(half, a_ref, b_ref, out_ref):
    out_ref[:half] = (a_ref[:half].astype(F32) + b_ref[:half].astype(F32)).astype(BF16)
    out_ref[half:] = pack_bias(add_bias(a_ref[half:]) + add_bias(b_ref[half:]), EXTRA)


def backward_kernel(rows, cols, pos_ref, count_ref, blocks_ref, *refs):
    hidden_parts = refs[:cols]
    keep_ref, send_ref, hidden, acc = refs[cols:]
    chips = rows // CORES
    row, col = lax.axis_index("row"), lax.axis_index("col")
    for n, ref in enumerate(hidden_parts):
        hidden[n] = ref[...]
    acc[...] = jnp.zeros_like(acc)

    def add(s):
        p = pos_ref[0, 0, s]
        u, v = p // rows, lax.rem(p, rows)
        src = offset_from(cols, col, u)
        k = offset_to(chips, row // CORES, v // CORES)
        dst = (lax.rem(v, CORES) ^ lax.rem(row, CORES)) * chips + k
        acc[dst] += lax.dot_general(blocks_ref[s], hidden[src], TN, preferred_element_type=F32)

    for_live(count_ref, blocks_ref.shape[0], add)
    keep_ref[...] = acc[:chips]
    send_ref[...] = acc[chips:].astype(BF16)


def merge_kernel(keep_ref, got_ref, grads_ref, own_ref, *send):
    own_ref[...] = keep_ref[0] + got_ref[0].astype(F32)
    for k, ref in enumerate(send, 1):
        ref[:BLOCK] = (keep_ref[k] + got_ref[k].astype(F32)).astype(BF16)
        ref[BLOCK:] = grads_ref[...]


def finish_kernel(chips, norm, degree_ref, own_ref, grads_ref, *refs):
    parts = refs[: chips - 1]
    grad_x_ref, half_ref, grad_b_ref = refs[chips - 1 :]
    half = half_ref.shape[0]
    total = own_ref[...]
    grads = grads_ref[:half].astype(F32)
    bias = add_bias(grads_ref[half:])
    for ref in parts:
        total = total + ref[:BLOCK].astype(F32)
        grads = grads + ref[BLOCK : BLOCK + half].astype(F32)
        bias = bias + add_bias(ref[BLOCK + half :])
    grad_x_ref[...] = (total * spread_inv(degree_ref, total.shape[1])).astype(BF16)
    half_ref[...] = grads * norm
    grad_b_ref[...] = bias * norm


def join_kernel(mine_ref, got_ref, out_ref):
    half = mine_ref.shape[0]
    first = lax.rem(lax.axis_index("row"), CORES) == 0
    out_ref[:half] = jnp.where(first, mine_ref[...], got_ref[...])
    out_ref[half:] = jnp.where(first, got_ref[...], mine_ref[...])


def call(kernel, specs, outs, scratch=(), flops=1_000_000):
    shapes = [jax.ShapeDtypeStruct(shape, dtype) for shape, dtype in outs]
    single = len(shapes) == 1
    return pl.pallas_call(
        kernel,
        out_shape=shapes[0] if single else tuple(shapes),
        in_specs=specs,
        out_specs=VMEM if single else tuple(VMEM for _ in shapes),
        scratch_shapes=[pltpu.VMEM(shape, dtype) for shape, dtype in scratch],
        compiler_params=pltpu.CompilerParams(vmem_limit_bytes=40 * 1024 * 1024),
        cost_estimate=pl.CostEstimate(flops=flops, bytes_accessed=1_000_000, transcendentals=0),
    )


def per_device(features, degree, weight, bias_vector, cotangent, block_pos, edge_pos, block_count):
    owned, width = features.shape
    rows, cols = lax.axis_size("row"), lax.axis_size("col")
    chips = rows // CORES
    slots = block_pos.shape[2]
    half = width // CORES
    piece = (owned, width)
    grads_shape = (half + EXTRA, width)
    degree = degree.reshape(1, owned)
    bias_vector = bias_vector.reshape(1, width)

    scaled = call(scale_kernel, [VMEM, VMEM], [(piece, BF16)])(features, degree)
    near = [scaled] + [to_chip(scaled, rows, k) for k in range(1, chips)]
    blocks = call(
        build_kernel, [SMEM, VMEM], [((slots, BLOCK, BLOCK), BF16)], flops=2_000_000_000
    )(block_count, edge_pos)
    near = near + [to_core(x, rows) for x in near]

    own, *send = call(
        functools.partial(forward_kernel, rows, cols),
        [SMEM, SMEM, VMEM] + [VMEM] * len(near),
        [(piece, F32)] + [(piece, BF16)] * (cols - 1),
        [((rows,) + piece, BF16), ((cols,) + piece, F32)],
    )(block_pos, block_count, blocks, *near)
    parts = [to_col(x, cols, k) for k, x in enumerate(send, 1)]

    output, hidden, keep, bias_keep, half_send = call(
        functools.partial(pointwise_kernel, cols),
        [VMEM] * (4 + cols),
        [(piece, BF16), (piece, BF16), ((half, width), F32), ((1, width), F32), (grads_shape, BF16)],
    )(weight, bias_vector, cotangent, degree, own, *parts)
    hidden_parts = [hidden] + [to_col(hidden, cols, k) for k in range(1, cols)]

    grads = call(pair_sum_kernel, [VMEM] * 3, [(grads_shape, BF16)])(
        keep, bias_keep, to_core(half_send, rows)
    )
    step = 1
    while step < cols:
        grads = call(functools.partial(add_kernel, half), [VMEM] * 2, [(grads_shape, BF16)])(
            grads, to_col(grads, cols, step)
        )
        step *= 2

    col_keep, col_send = call(
        functools.partial(backward_kernel, rows, cols),
        [SMEM, SMEM, VMEM] + [VMEM] * cols,
        [((chips,) + piece, F32), ((chips,) + piece, BF16)],
        [((cols,) + piece, BF16), ((rows,) + piece, F32)],
    )(block_pos, block_count, blocks, *hidden_parts)
    own_x, *send_x = call(
        merge_kernel,
        [VMEM] * 3,
        [(piece, F32)] + [((owned + half + EXTRA, width), BF16)] * (chips - 1),
    )(col_keep, to_core(col_send, rows), grads)
    parts_x = [to_chip(x, rows, k) for k, x in enumerate(send_x, 1)]

    norm = float((owned * rows * cols) ** -0.5)
    grad_x, mine, grad_b = call(
        functools.partial(finish_kernel, chips, norm),
        [VMEM] * (2 + chips),
        [(piece, BF16), ((half, width), F32), ((1, width), F32)],
    )(degree, own_x, grads, *parts_x)
    grad_w = call(join_kernel, [VMEM] * 2, [((width, width), F32)])(mine, to_core(mine, rows))
    return (output, grad_x, grad_w, grad_b.reshape(width))


def solution(mesh):
    placed = (
        P(("row", "col"), None),
        P(("row", "col")),
        P(),
        P(),
        P(("row", "col"), None),
        P("row", "col", None),
        P("row", "col", None, None),
        P("row", "col"),
    )
    return jax.shard_map(
        per_device,
        mesh=mesh,
        in_specs=placed,
        out_specs=(P(("row", "col"), None), P(("row", "col"), None), P(), P()),
        check_vma=False,
    )
```

time: 271 us -> 62.2 us (0.23)
  waiting for transfers between devices: 124 us -> 29.5 us
  blocking collectives: 63.9 us -> 0 us
  other arithmetic: 54.1 us -> 0 us
  starting transfers between devices: 0.12 us -> 22.7 us
  between operations: 14.6 us -> 1.41 us
  matrix products: 7.25 us -> 0 us
  Pallas kernels: 0 us -> 5.66 us
  local copies, waits for them, and re-layouts: 6.02 us -> 2.18 us
    psum x1 -> x0, waiting for transfers between devices: 65.6 us -> none  [per_device(): weight_sum, bias_sum = lax.psum((weight_term, bias_term), ('row', 'col'))]
    reduce_scatter x2 -> x0, waiting for transfers between devices: 58.6 us -> none  [the longest x1 36.6 us: per_device(): lax.psum_scatter(partial_cols, 'row', scatter_dimension=0, tiled=True)]
    scatter-add x3 -> x0, other arithmetic: 47.9 us -> none  [the longest x1 43.5 us: per_device(): jnp.zeros((slots * BLOCK * BLOCK,), jnp.float32).at[flat_index].add(1.0)]
    psum x1 -> x0, blocking collectives: 38.4 us -> none  [per_device(): weight_sum, bias_sum = lax.psum((weight_term, bias_term), ('row', 'col'))]
    ppermute x0 -> x21, waiting for transfers between devices: none -> 29.5 us  [the longest x8 17.2 us: to_col(): lax.ppermute(x, 'col', [(i, target(cols, i, k)) for i in range(cols)])]
    all_gather x2 -> x0, blocking collectives: 25.4 us -> none  [the longest x1 14.1 us: per_device(): hidden_rows = lax.all_gather(grad_hidden_own, 'col', axis=0, tiled=True)]
    ppermute x0 -> x21, starting transfers between devices: none -> 22.7 us  [the longest x8 13.6 us: to_col(): lax.ppermute(x, 'col', [(i, target(cols, i, k)) for i in range(cols)])]
    dot_general x5 -> x0, matrix products: 7.25 us -> none  [the longest x1 1.9 us: per_device(): jnp.dot(agg_own.T, grad_pre_own, preferred_element_type=jnp.float32)]
  transfers between devices with their start and end apart: 3 -> 21, of which waited for: 3 -> 13; matrix products, arithmetic and copies ran while one was open for 3% -> 0% of each run, Pallas kernels for 0% -> 1%
where the time goes in v1:
time: 62.2 us; the launch traced here: 61.5 us
  waiting for transfers between devices  29.5 us (47%)
  starting transfers between devices  22.7 us (36%)
  Pallas kernels  5.66 us (9%)
  local copies, waits for them, and re-layouts  2.18 us (4%)
  between operations  1.41 us (2%)
    ppermute x8, waiting for transfers between devices, to_col(): lax.ppermute(x, 'col', [(i, target(cols, i, k)) for i in range(cols)])  17.2 us
    ppermute x8, starting transfers between devices, to_col(): lax.ppermute(x, 'col', [(i, target(cols, i, k)) for i in range(cols)])  13.6 us
    ppermute x6, waiting for transfers between devices, to_chip(): return lax.ppermute(x, 'row', pairs)  9.31 us
    ppermute x6, starting transfers between devices, to_chip(): return lax.ppermute(x, 'row', pairs)  8.1 us
    ppermute x7, waiting for transfers between devices, to_core(): return lax.ppermute(x, 'row', [(i, i ^ 1) for i in range(rows)])  3.07 us
    unnamed x14, local copies, waits for them, and re-layouts  2.18 us
    pallas_call x1, Pallas kernels, per_device(): call(functools.partial(backward_kernel, rows, cols), [SMEM, SMEM, VMEM] +...  1.28 us
  transfers between devices with their start and end apart: 21, of which 13 were waited for; matrix products, arithmetic and copies ran while one was open for 0% of the time, Pallas kernels for 1%

profile of v1, /device:TPU:0, one launch (start us, length us, event | category | flops | bytes accessed | tf_op | source)
XLA Modules:
  0.0 61.5 jit_solution(6047822665598035772)
XLA Ops:
  0.6 0.6 %copy-done.3 = s32[128]{0:T(128)S(1)} copy-done((s32[128]{0:T(128)S(1)}, s32[128]{0:T(128)}, u32[]{:S(2)}) %copy-start.3) | copy-done | bytes 536
  1.3 0.8 %copy-done.2 = bf16[128,256]{1,0:T(8,128)(2,1)S(1)} copy-done((bf16[128,256]{1,0:T(8,128)(2,1)S(1)}, bf16[128,256]{1,0:T(8,128)(2,1)}, u32[]{:S(2)}) %copy-start.2) | copy-done | bytes 65560
  2.1 0.1 shard_map.112.refs_0_
  2.2 3.0 %collective-permute-start = (bf16[128,256]{1,0:T(8,128)(2,1)S(1)}, bf16[128,256]{1,0:T(8,128)(2,1)S(1)}, u32[]{:S(2)}, u32[]{:S(2)}) collective-permute-start(bf16[128,256]{1,0:T(8,128)(2,1)S(1)} %shard_map.112.refs_0_), channel_id=1, source_target_pairs={{0,8},{4,12},{8,0},{12,4},{16,24},{20,28},{24,16},{28,20},{1,9},{5... | collective-permute-start | bytes 196616 | tf_op jit(solution)/shard_map/ppermute | solution.py:48
  5.2 1.5 %collective-permute-start.1 = (bf16[128,256]{1,0:T(8,128)(2,1)S(1)}, bf16[128,256]{1,0:T(8,128)(2,1)S(1)}, u32[]{:S(2)}, u32[]{:S(2)}) collective-permute-start(bf16[128,256]{1,0:T(8,128)(2,1)S(1)} %shard_map.112.refs_0_), channel_id=1, source_target_pairs={{0,16},{4,20},{8,24},{12,28},{16,0},{20,4},{24,8},{28,12},{1,17},{... | collective-permute-start | bytes 196616 | tf_op jit(solution)/shard_map/ppermute | solution.py:48
  6.8 0.0 collective-permute-start.2
  7.4 0.0 copy-start.4
  7.5 0.1 collective-permute-done.refs_1_
  7.6 0.4 collective-permute-start.4
  8.0 1.5 %collective-permute-done.1.refs_2_ = bf16[128,256]{1,0:T(8,128)(2,1)S(1)} collective-permute-done((bf16[128,256]{1,0:T(8,128)(2,1)S(1)}, bf16[128,256]{1,0:T(8,128)(2,1)S(1)}, u32[]{:S(2)}, u32[]{:S(2)}) %collective-permute-start.1) | collective-permute-done | bytes 65568 | tf_op jit(solution)/shard_map/ppermute | solution.py:48
  9.5 2.4 %collective-permute-done.2.refs_3_ = bf16[128,256]{1,0:T(8,128)(2,1)S(1)} collective-permute-done((bf16[128,256]{1,0:T(8,128)(2,1)S(1)}, bf16[128,256]{1,0:T(8,128)(2,1)S(1)}, u32[]{:S(2)}, u32[]{:S(2)}) %collective-permute-start.2) | collective-permute-done | bytes 65568 | tf_op jit(solution)/shard_map/ppermute | solution.py:48
  11.9 0.6 shard_map.111.blocks_ref
  12.5 0.0 copy-start
  12.6 0.0 copy-start.1
  12.6 0.0 collective-permute-done.3.refs_4_
  12.6 0.0 collective-permute-done.4.refs_5_
  12.6 0.6 collective-permute-done.6.refs_7_
  13.2 1.1 %shard_map.113 = (f32[128,256]{1,0:T(8,128)S(1)}, bf16[128,256]{1,0:T(8,128)(2,1)S(1)}, bf16[128,256]{1,0:T(8,128)(2,1)S(1)}, bf16[128,256]{1,0:T(8,128)(2,1)S(1)}) custom-call(s32[1,1,16]{2,1,0:T(1,128)S(1)} %copy-done.4, s32[1,1]{1,0:T(1,128)S(6)} %copy.12.count_ref, bf16[16,128,128]{2,1,0:T(8,128)(2,1)S(1)} %shard_map.111.blocks_ref, ...), custom_call_target="tpu_custom_call" | custom-call | flops 1000000 | bytes 1000000 | tf_op jit(solution)/shard_map/pallas_call | solution.py:250
  14.3 2.2 %collective-permute-start.7 = (bf16[128,256]{1,0:T(8,128)(2,1)S(1)}, bf16[128,256]{1,0:T(8,128)(2,1)S(1)}, u32[]{:S(2)}, u32[]{:S(2)}) collective-permute-start(bf16[128,256]{1,0:T(8,128)(2,1)S(1)} %get-tuple-element.23), channel_id=1, source_target_pairs={{0,1},{1,0},{2,3},{3,2},{4,5},{5,4},{6,7},{7,6},{8,9},{9,8},{10,11... | collective-permute-start | bytes 196616 | tf_op jit(solution)/shard_map/ppermute | solution.py:52
  16.5 2.4 %collective-permute-start.8 = (bf16[128,256]{1,0:T(8,128)(2,1)S(1)}, bf16[128,256]{1,0:T(8,128)(2,1)S(1)}, u32[]{:S(2)}, u32[]{:S(2)}) collective-permute-start(bf16[128,256]{1,0:T(8,128)(2,1)S(1)} %get-tuple-element.24), channel_id=1, source_target_pairs={{0,2},{1,3},{2,0},{3,1},{4,6},{5,7},{6,4},{7,5},{8,10},{9,11},{10,... | collective-permute-start | bytes 196616 | tf_op jit(solution)/shard_map/ppermute | solution.py:52
  18.9 0.1 collective-permute-start.9
  19.0 0.0 collective-permute-done.7.refs_1_
  19.0 4.8 %collective-permute-done.8.refs_2_ = bf16[128,256]{1,0:T(8,128)(2,1)S(1)} collective-permute-done((bf16[128,256]{1,0:T(8,128)(2,1)S(1)}, bf16[128,256]{1,0:T(8,128)(2,1)S(1)}, u32[]{:S(2)}, u32[]{:S(2)}) %collective-permute-start.8) | collective-permute-done | bytes 65568 | tf_op jit(solution)/shard_map/ppermute | solution.py:52
  23.7 1.9 %collective-permute-done.9.refs_3_ = bf16[128,256]{1,0:T(8,128)(2,1)S(1)} collective-permute-done((bf16[128,256]{1,0:T(8,128)(2,1)S(1)}, bf16[128,256]{1,0:T(8,128)(2,1)S(1)}, u32[]{:S(2)}, u32[]{:S(2)}) %collective-permute-start.9) | collective-permute-done | bytes 65568 | tf_op jit(solution)/shard_map/ppermute | solution.py:52
  25.6 0.7 %copy-done.5 = f32[256]{0:T(256)S(1)} copy-done((f32[256]{0:T(256)S(1)}, f32[256]{0:T(256)}, u32[]{:S(2)}) %copy-start.5) | copy-done | bytes 1048
  26.3 0.9 %shard_map.114 = (bf16[128,256]{1,0:T(8,128)(2,1)}, bf16[128,256]{1,0:T(8,128)(2,1)S(1)}, f32[128,256]{1,0:T(8,128)S(1)}, f32[1,256]{1,0:T(1,128)S(1)}, bf16[144,256]{1,0:T(8,128)(2,1)S(1)}) custom-call(bf16[256,256]{1,0:T(8,128)(2,1)S(1)} %copy-done, f32[1,256]{1,0:T(1,128)S(1)} %bitcast.6, bf16[128,256]{1,0:T(8,128)(2,1)S(1)} %copy-done.1, ...), custom_call_target="tpu_custom_call" | custom-call | flops 1000000 | bytes 1000000 | tf_op jit(solution)/shard_map/pallas_call | solution.py:258
  27.2 1.4 %collective-permute-start.10 = (bf16[128,256]{1,0:T(8,128)(2,1)S(1)}, bf16[128,256]{1,0:T(8,128)(2,1)S(1)}, u32[]{:S(2)}, u32[]{:S(2)}) collective-permute-start(bf16[128,256]{1,0:T(8,128)(2,1)S(1)} %get-tuple-element.27.refs_0_), channel_id=1, source_target_pairs={{0,1},{1,0},{2,3},{3,2},{4,5},{5,4},{6,7},{7,6},{8,9},{9,8},{10,11... | collective-permute-start | bytes 196616 | tf_op jit(solution)/shard_map/ppermute | solution.py:52
  28.6 1.1 %collective-permute-start.11 = (bf16[128,256]{1,0:T(8,128)(2,1)S(1)}, bf16[128,256]{1,0:T(8,128)(2,1)S(1)}, u32[]{:S(2)}, u32[]{:S(2)}) collective-permute-start(bf16[128,256]{1,0:T(8,128)(2,1)S(1)} %get-tuple-element.27.refs_0_), channel_id=1, source_target_pairs={{0,2},{1,3},{2,0},{3,1},{4,6},{5,7},{6,4},{7,5},{8,10},{9,11},{10,... | collective-permute-start | bytes 196616 | tf_op jit(solution)/shard_map/ppermute | solution.py:52
  29.8 1.8 %collective-permute-start.12 = (bf16[128,256]{1,0:T(8,128)(2,1)S(1)}, bf16[128,256]{1,0:T(8,128)(2,1)S(1)}, u32[]{:S(2)}, u32[]{:S(2)}) collective-permute-start(bf16[128,256]{1,0:T(8,128)(2,1)S(1)} %get-tuple-element.27.refs_0_), channel_id=1, source_target_pairs={{0,3},{1,2},{2,1},{3,0},{4,7},{5,6},{6,5},{7,4},{8,11},{9,10},{10,... | collective-permute-start | bytes 196616 | tf_op jit(solution)/shard_map/ppermute | solution.py:52
  31.6 0.0 collective-permute-done.10.refs_1_
  31.6 5.2 %collective-permute-done.11.refs_2_ = bf16[128,256]{1,0:T(8,128)(2,1)S(1)} collective-permute-done((bf16[128,256]{1,0:T(8,128)(2,1)S(1)}, bf16[128,256]{1,0:T(8,128)(2,1)S(1)}, u32[]{:S(2)}, u32[]{:S(2)}) %collective-permute-start.11) | collective-permute-done | bytes 65568 | tf_op jit(solution)/shard_map/ppermute | solution.py:52
  36.8 1.3 %shard_map.115 = (f32[4,128,256]{2,1,0:T(8,128)S(1)}, bf16[4,128,256]{2,1,0:T(8,128)(2,1)S(1)}) custom-call(s32[1,1,16]{2,1,0:T(1,128)S(1)} %copy-done.4, s32[1,1]{1,0:T(1,128)S(6)} %copy.12.count_ref, bf16[16,128,128]{2,1,0:T(8,128)(2,1)S(1)} %shard_map.111.blocks_ref, bf16[128,256]{1,0:T(8,128)(2,1)S(1)} %get-tuple-element.27.refs_0_, ...), custom_call_target="tpu_custom_call" | custom-call | flops 1000000 | bytes 1000000 | tf_op jit(solution)/shard_map/pallas_call | solution.py:275
  38.1 0.1 collective-permute-start.13
  38.1 0.5 collective-permute-start.14
  38.6 1.1 %collective-permute-done.14.got_ref = bf16[144,256]{1,0:T(8,128)(2,1)S(1)} collective-permute-done((bf16[144,256]{1,0:T(8,128)(2,1)S(1)}, bf16[144,256]{1,0:T(8,128)(2,1)S(1)}, u32[]{:S(2)}, u32[]{:S(2)}) %collective-permute-start.14) | collective-permute-done | bytes 73760 | tf_op jit(solution)/shard_map/ppermute | solution.py:38
  39.8 1.9 %collective-permute-start.15 = (bf16[144,256]{1,0:T(8,128)(2,1)S(1)}, bf16[144,256]{1,0:T(8,128)(2,1)S(1)}, u32[]{:S(2)}, u32[]{:S(2)}) collective-permute-start(bf16[144,256]{1,0:T(8,128)(2,1)S(1)} %shard_map.116.a_ref), channel_id=1, source_target_pairs={{0,1},{1,0},{2,3},{3,2},{4,5},{5,4},{6,7},{7,6},{8,9},{9,8},{10,11... | collective-permute-start | bytes 221192 | tf_op jit(solution)/shard_map/ppermute | solution.py:52
  41.7 2.6 %collective-permute-done.15.b_ref = bf16[144,256]{1,0:T(8,128)(2,1)S(1)} collective-permute-done((bf16[144,256]{1,0:T(8,128)(2,1)S(1)}, bf16[144,256]{1,0:T(8,128)(2,1)S(1)}, u32[]{:S(2)}, u32[]{:S(2)}) %collective-permute-start.15) | collective-permute-done | bytes 73760 | tf_op jit(solution)/shard_map/ppermute | solution.py:52
  44.3 2.6 %collective-permute-start.16 = (bf16[144,256]{1,0:T(8,128)(2,1)S(1)}, bf16[144,256]{1,0:T(8,128)(2,1)S(1)}, u32[]{:S(2)}, u32[]{:S(2)}) collective-permute-start(bf16[144,256]{1,0:T(8,128)(2,1)S(1)} %shard_map.117.a_ref), channel_id=1, source_target_pairs={{0,2},{1,3},{2,0},{3,1},{4,6},{5,7},{6,4},{7,5},{8,10},{9,11},{10,... | collective-permute-start | bytes 221192 | tf_op jit(solution)/shard_map/ppermute | solution.py:52
  47.0 2.7 %collective-permute-done.16.b_ref = bf16[144,256]{1,0:T(8,128)(2,1)S(1)} collective-permute-done((bf16[144,256]{1,0:T(8,128)(2,1)S(1)}, bf16[144,256]{1,0:T(8,128)(2,1)S(1)}, u32[]{:S(2)}, u32[]{:S(2)}) %collective-permute-start.16) | collective-permute-done | bytes 73760 | tf_op jit(solution)/shard_map/ppermute | solution.py:52
  49.8 0.1 shard_map.119
  49.8 0.8 %collective-permute-start.17 = (bf16[272,256]{1,0:T(8,128)(2,1)S(1)}, bf16[272,256]{1,0:T(8,128)(2,1)S(1)}, u32[]{:S(2)}, u32[]{:S(2)}) collective-permute-start(bf16[272,256]{1,0:T(8,128)(2,1)S(1)} %get-tuple-element.34), channel_id=1, source_target_pairs={{0,8},{4,12},{8,0},{12,4},{16,24},{20,28},{24,16},{28,20},{1,9},{5... | collective-permute-start | bytes 417800 | tf_op jit(solution)/shard_map/ppermute | solution.py:48
  50.6 1.7 %collective-permute-start.18 = (bf16[272,256]{1,0:T(8,128)(2,1)S(1)}, bf16[272,256]{1,0:T(8,128)(2,1)S(1)}, u32[]{:S(2)}, u32[]{:S(2)}) collective-permute-start(bf16[272,256]{1,0:T(8,128)(2,1)S(1)} %get-tuple-element.35), channel_id=1, source_target_pairs={{0,16},{4,20},{8,24},{12,28},{16,0},{20,4},{24,8},{28,12},{1,17},{... | collective-permute-start | bytes 417800 | tf_op jit(solution)/shard_map/ppermute | solution.py:48
  52.3 1.1 %collective-permute-start.19 = (bf16[272,256]{1,0:T(8,128)(2,1)S(1)}, bf16[272,256]{1,0:T(8,128)(2,1)S(1)}, u32[]{:S(2)}, u32[]{:S(2)}) collective-permute-start(bf16[272,256]{1,0:T(8,128)(2,1)S(1)} %get-tuple-element.36), channel_id=1, source_target_pairs={{0,24},{4,28},{8,16},{12,20},{16,8},{20,12},{24,0},{28,4},{1,25},{... | collective-permute-start | bytes 417800 | tf_op jit(solution)/shard_map/ppermute | solution.py:48
  53.4 2.7 %collective-permute-done.17.refs_0_ = bf16[272,256]{1,0:T(8,128)(2,1)S(1)} collective-permute-done((bf16[272,256]{1,0:T(8,128)(2,1)S(1)}, bf16[272,256]{1,0:T(8,128)(2,1)S(1)}, u32[]{:S(2)}, u32[]{:S(2)}) %collective-permute-start.17) | collective-permute-done | bytes 139296 | tf_op jit(solution)/shard_map/ppermute | solution.py:48
  56.1 2.5 %collective-permute-done.18.refs_1_ = bf16[272,256]{1,0:T(8,128)(2,1)S(1)} collective-permute-done((bf16[272,256]{1,0:T(8,128)(2,1)S(1)}, bf16[272,256]{1,0:T(8,128)(2,1)S(1)}, u32[]{:S(2)}, u32[]{:S(2)}) %collective-permute-start.18) | collective-permute-done | bytes 139296 | tf_op jit(solution)/shard_map/ppermute | solution.py:48
  58.7 0.7 %shard_map.120 = (bf16[128,256]{1,0:T(8,128)(2,1)}, f32[128,256]{1,0:T(8,128)S(1)}, f32[1,256]{1,0:T(1,128)}) custom-call(s32[1,128]{1,0:T(1,128)S(1)} %bitcast.5, f32[128,256]{1,0:T(8,128)S(1)} %get-tuple-element.33.own_ref, bf16[144,256]{1,0:T(8,128)(2,1)S(1)} %shard_map.118.grads_ref, bf16[272,256]{1,0:T(8,128)(2,1)S(1)} %collective-permute-done.17.refs_0_, ...), custom_call_target="tpu_custom_call" | custom-call | flops 1000000 | bytes 1000000 | tf_op jit(solution)/shard_map/pallas_call | solution.py:289
  59.4 1.3 %collective-permute-done.20.got_ref = f32[128,256]{1,0:T(8,128)S(1)} collective-permute-done((f32[128,256]{1,0:T(8,128)S(1)}, f32[128,256]{1,0:T(8,128)S(1)}, u32[]{:S(2)}, u32[]{:S(2)}) %collective-permute-start.20) | collective-permute-done | bytes 131104 | tf_op jit(solution)/shard_map/ppermute | solution.py:38
  60.8 0.7 %shard_map.121 = f32[256,256]{1,0:T(8,128)} custom-call(f32[128,256]{1,0:T(8,128)S(1)} %get-tuple-element.38.mine_ref, f32[128,256]{1,0:T(8,128)S(1)} %collective-permute-done.20.got_ref), custom_call_target="tpu_custom_call" | custom-call | flops 1000000 | bytes 1000000 | tf_op jit(solution)/shard_map/pallas_call | solution.py:294
  (19 shorter events, 0.1 us)
Async XLA Ops:
  0.6 0.7 %copy-start.3 = (s32[128]{0:T(128)S(1)}, s32[128]{0:T(128)}, u32[]{:S(2)}) copy-start(s32[128]{0:T(128)} %param.9) | copy-start | bytes 1540
  1.3 0.8 %copy-start.2 = (bf16[128,256]{1,0:T(8,128)(2,1)S(1)}, bf16[128,256]{1,0:T(8,128)(2,1)}, u32[]{:S(2)}) copy-start(bf16[128,256]{1,0:T(8,128)(2,1)} %features_ref.1) | copy-start | bytes 196612
  2.1 9.8 %copy-start.6 = (s32[1,1,16,512]{3,2,1,0:T(8,128)S(1)}, s32[1,1,16,512]{3,2,1,0:T(8,128)}, u32[]{:S(2)}) copy-start(s32[1,1,16,512]{3,2,1,0:T(8,128)} %edge_ref.1) | copy-start | bytes 98308
  2.2 5.4 %collective-permute-start = (bf16[128,256]{1,0:T(8,128)(2,1)S(1)}, bf16[128,256]{1,0:T(8,128)(2,1)S(1)}, u32[]{:S(2)}, u32[]{:S(2)}) collective-permute-start(bf16[128,256]{1,0:T(8,128)(2,1)S(1)} %shard_map.112.refs_0_), channel_id=1, source_target_pairs={{0,8},{4,12},{8,0},{12,4},{16,24},{20,28},{24,16},{28,20},{1,9},{5... | collective-permute-start | bytes 196616 | tf_op jit(solution)/shard_map/ppermute | solution.py:48
  5.2 4.3 %collective-permute-start.1 = (bf16[128,256]{1,0:T(8,128)(2,1)S(1)}, bf16[128,256]{1,0:T(8,128)(2,1)S(1)}, u32[]{:S(2)}, u32[]{:S(2)}) collective-permute-start(bf16[128,256]{1,0:T(8,128)(2,1)S(1)} %shard_map.112.refs_0_), channel_id=1, source_target_pairs={{0,16},{4,20},{8,24},{12,28},{16,0},{20,4},{24,8},{28,12},{1,17},{... | collective-permute-start | bytes 196616 | tf_op jit(solution)/shard_map/ppermute | solution.py:48
  6.8 5.2 %collective-permute-start.2 = (bf16[128,256]{1,0:T(8,128)(2,1)S(1)}, bf16[128,256]{1,0:T(8,128)(2,1)S(1)}, u32[]{:S(2)}, u32[]{:S(2)}) collective-permute-start(bf16[128,256]{1,0:T(8,128)(2,1)S(1)} %shard_map.112.refs_0_), channel_id=1, source_target_pairs={{0,24},{4,28},{8,16},{12,20},{16,8},{20,12},{24,0},{28,4},{1,25},{... | collective-permute-start | bytes 196616 | tf_op jit(solution)/shard_map/ppermute | solution.py:48
  6.8 5.8 %collective-permute-start.3 = (bf16[128,256]{1,0:T(8,128)(2,1)S(1)}, bf16[128,256]{1,0:T(8,128)(2,1)S(1)}, u32[]{:S(2)}, u32[]{:S(2)}) collective-permute-start(bf16[128,256]{1,0:T(8,128)(2,1)S(1)} %shard_map.112.refs_0_), channel_id=1, source_target_pairs={{0,4},{4,0},{8,12},{12,8},{16,20},{20,16},{24,28},{28,24},{1,5},{5... | collective-permute-start | bytes 196616 | tf_op jit(solution)/shard_map/ppermute | solution.py:38
  7.4 5.7 %copy-start.4 = (s32[1,1,16]{2,1,0:T(1,128)S(1)}, s32[1,1,16]{2,1,0:T(1,128)}, u32[]{:S(2)}) copy-start(s32[1,1,16]{2,1,0:T(1,128)} %pos_ref.3) | copy-start | bytes 196
  7.6 5.0 %collective-permute-start.4 = (bf16[128,256]{1,0:T(8,128)(2,1)S(1)}, bf16[128,256]{1,0:T(8,128)(2,1)S(1)}, u32[]{:S(2)}, u32[]{:S(2)}) collective-permute-start(bf16[128,256]{1,0:T(8,128)(2,1)S(1)} %collective-permute-done.refs_1_), channel_id=1, source_target_pairs={{0,4},{4,0},{8,12},{12,8},{16,20},{20,16},{24,28},{28,24},{1,5},{5... | collective-permute-start | bytes 196616 | tf_op jit(solution)/shard_map/ppermute | solution.py:38
  9.5 3.1 %collective-permute-start.5 = (bf16[128,256]{1,0:T(8,128)(2,1)S(1)}, bf16[128,256]{1,0:T(8,128)(2,1)S(1)}, u32[]{:S(2)}, u32[]{:S(2)}) collective-permute-start(bf16[128,256]{1,0:T(8,128)(2,1)S(1)} %collective-permute-done.1.refs_2_), channel_id=1, source_target_pairs={{0,4},{4,0},{8,12},{12,8},{16,20},{20,16},{24,28},{28,24},{1,5},{5... | collective-permute-start | bytes 196616 | tf_op jit(solution)/shard_map/ppermute | solution.py:38
  11.9 1.3 %collective-permute-start.6 = (bf16[128,256]{1,0:T(8,128)(2,1)S(1)}, bf16[128,256]{1,0:T(8,128)(2,1)S(1)}, u32[]{:S(2)}, u32[]{:S(2)}) collective-permute-start(bf16[128,256]{1,0:T(8,128)(2,1)S(1)} %collective-permute-done.2.refs_3_), channel_id=1, source_target_pairs={{0,4},{4,0},{8,12},{12,8},{16,20},{20,16},{24,28},{28,24},{1,5},{5... | collective-permute-start | bytes 196616 | tf_op jit(solution)/shard_map/ppermute | solution.py:38
  12.5 13.1 %copy-start = (bf16[256,256]{1,0:T(8,128)(2,1)S(1)}, bf16[256,256]{1,0:T(8,128)(2,1)}, u32[]{:S(2)}) copy-start(bf16[256,256]{1,0:T(8,128)(2,1)} %weight_ref.1) | copy-start | bytes 393220
  12.6 13.1 %copy-start.1 = (bf16[128,256]{1,0:T(8,128)(2,1)S(1)}, bf16[128,256]{1,0:T(8,128)(2,1)}, u32[]{:S(2)}) copy-start(bf16[128,256]{1,0:T(8,128)(2,1)} %cot_ref.1) | copy-start | bytes 196612
  14.3 4.6 %collective-permute-start.7 = (bf16[128,256]{1,0:T(8,128)(2,1)S(1)}, bf16[128,256]{1,0:T(8,128)(2,1)S(1)}, u32[]{:S(2)}, u32[]{:S(2)}) collective-permute-start(bf16[128,256]{1,0:T(8,128)(2,1)S(1)} %get-tuple-element.23), channel_id=1, source_target_pairs={{0,1},{1,0},{2,3},{3,2},{4,5},{5,4},{6,7},{7,6},{8,9},{9,8},{10,11... | collective-permute-start | bytes 196616 | tf_op jit(solution)/shard_map/ppermute | solution.py:52
  16.5 7.3 %collective-permute-start.8 = (bf16[128,256]{1,0:T(8,128)(2,1)S(1)}, bf16[128,256]{1,0:T(8,128)(2,1)S(1)}, u32[]{:S(2)}, u32[]{:S(2)}) collective-permute-start(bf16[128,256]{1,0:T(8,128)(2,1)S(1)} %get-tuple-element.24), channel_id=1, source_target_pairs={{0,2},{1,3},{2,0},{3,1},{4,6},{5,7},{6,4},{7,5},{8,10},{9,11},{10,... | collective-permute-start | bytes 196616 | tf_op jit(solution)/shard_map/ppermute | solution.py:52
  18.9 6.8 %collective-permute-start.9 = (bf16[128,256]{1,0:T(8,128)(2,1)S(1)}, bf16[128,256]{1,0:T(8,128)(2,1)S(1)}, u32[]{:S(2)}, u32[]{:S(2)}) collective-permute-start(bf16[128,256]{1,0:T(8,128)(2,1)S(1)} %get-tuple-element.25), channel_id=1, source_target_pairs={{0,3},{1,2},{2,1},{3,0},{4,7},{5,6},{6,5},{7,4},{8,11},{9,10},{10,... | collective-permute-start | bytes 196616 | tf_op jit(solution)/shard_map/ppermute | solution.py:52
  25.6 0.7 %copy-start.5 = (f32[256]{0:T(256)S(1)}, f32[256]{0:T(256)}, u32[]{:S(2)}) copy-start(f32[256]{0:T(256)} %param.11) | copy-start | bytes 3076
  27.2 4.4 %collective-permute-start.10 = (bf16[128,256]{1,0:T(8,128)(2,1)S(1)}, bf16[128,256]{1,0:T(8,128)(2,1)S(1)}, u32[]{:S(2)}, u32[]{:S(2)}) collective-permute-start(bf16[128,256]{1,0:T(8,128)(2,1)S(1)} %get-tuple-element.27.refs_0_), channel_id=1, source_target_pairs={{0,1},{1,0},{2,3},{3,2},{4,5},{5,4},{6,7},{7,6},{8,9},{9,8},{10,11... | collective-permute-start | bytes 196616 | tf_op jit(solution)/shard_map/ppermute | solution.py:52
  28.6 8.2 %collective-permute-start.11 = (bf16[128,256]{1,0:T(8,128)(2,1)S(1)}, bf16[128,256]{1,0:T(8,128)(2,1)S(1)}, u32[]{:S(2)}, u32[]{:S(2)}) collective-permute-start(bf16[128,256]{1,0:T(8,128)(2,1)S(1)} %get-tuple-element.27.refs_0_), channel_id=1, source_target_pairs={{0,2},{1,3},{2,0},{3,1},{4,6},{5,7},{6,4},{7,5},{8,10},{9,11},{10,... | collective-permute-start | bytes 196616 | tf_op jit(solution)/shard_map/ppermute | solution.py:52
  29.8 7.0 %collective-permute-start.12 = (bf16[128,256]{1,0:T(8,128)(2,1)S(1)}, bf16[128,256]{1,0:T(8,128)(2,1)S(1)}, u32[]{:S(2)}, u32[]{:S(2)}) collective-permute-start(bf16[128,256]{1,0:T(8,128)(2,1)S(1)} %get-tuple-element.27.refs_0_), channel_id=1, source_target_pairs={{0,3},{1,2},{2,1},{3,0},{4,7},{5,6},{6,5},{7,4},{8,11},{9,10},{10,... | collective-permute-start | bytes 196616 | tf_op jit(solution)/shard_map/ppermute | solution.py:52
  38.1 11.7 %collective-permute-start.13 = (bf16[4,128,256]{2,1,0:T(8,128)(2,1)S(1)}, bf16[4,128,256]{2,1,0:T(8,128)(2,1)S(1)}, u32[]{:S(2)}, u32[]{:S(2)}) collective-permute-start(bf16[4,128,256]{2,1,0:T(8,128)(2,1)S(1)} %get-tuple-element.29), channel_id=1, source_target_pairs={{0,4},{4,0},{8,12},{12,8},{16,20},{20,16},{24,28},{28,24},{1,5},{5... | collective-permute-start | bytes 786440 | tf_op jit(solution)/shard_map/ppermute | solution.py:38
  38.1 1.6 %collective-permute-start.14 = (bf16[144,256]{1,0:T(8,128)(2,1)S(1)}, bf16[144,256]{1,0:T(8,128)(2,1)S(1)}, u32[]{:S(2)}, u32[]{:S(2)}) collective-permute-start(bf16[144,256]{1,0:T(8,128)(2,1)S(1)} %get-tuple-element.32), channel_id=1, source_target_pairs={{0,4},{4,0},{8,12},{12,8},{16,20},{20,16},{24,28},{28,24},{1,5},{5... | collective-permute-start | bytes 221192 | tf_op jit(solution)/shard_map/ppermute | solution.py:38
  39.8 4.5 %collective-permute-start.15 = (bf16[144,256]{1,0:T(8,128)(2,1)S(1)}, bf16[144,256]{1,0:T(8,128)(2,1)S(1)}, u32[]{:S(2)}, u32[]{:S(2)}) collective-permute-start(bf16[144,256]{1,0:T(8,128)(2,1)S(1)} %shard_map.116.a_ref), channel_id=1, source_target_pairs={{0,1},{1,0},{2,3},{3,2},{4,5},{5,4},{6,7},{7,6},{8,9},{9,8},{10,11... | collective-permute-start | bytes 221192 | tf_op jit(solution)/shard_map/ppermute | solution.py:52
  44.3 5.4 %collective-permute-start.16 = (bf16[144,256]{1,0:T(8,128)(2,1)S(1)}, bf16[144,256]{1,0:T(8,128)(2,1)S(1)}, u32[]{:S(2)}, u32[]{:S(2)}) collective-permute-start(bf16[144,256]{1,0:T(8,128)(2,1)S(1)} %shard_map.117.a_ref), channel_id=1, source_target_pairs={{0,2},{1,3},{2,0},{3,1},{4,6},{5,7},{6,4},{7,5},{8,10},{9,11},{10,... | collective-permute-start | bytes 221192 | tf_op jit(solution)/shard_map/ppermute | solution.py:52
  49.8 6.3 %collective-permute-start.17 = (bf16[272,256]{1,0:T(8,128)(2,1)S(1)}, bf16[272,256]{1,0:T(8,128)(2,1)S(1)}, u32[]{:S(2)}, u32[]{:S(2)}) collective-permute-start(bf16[272,256]{1,0:T(8,128)(2,1)S(1)} %get-tuple-element.34), channel_id=1, source_target_pairs={{0,8},{4,12},{8,0},{12,4},{16,24},{20,28},{24,16},{28,20},{1,9},{5... | collective-permute-start | bytes 417800 | tf_op jit(solution)/shard_map/ppermute | solution.py:48
  50.6 8.1 %collective-permute-start.18 = (bf16[272,256]{1,0:T(8,128)(2,1)S(1)}, bf16[272,256]{1,0:T(8,128)(2,1)S(1)}, u32[]{:S(2)}, u32[]{:S(2)}) collective-permute-start(bf16[272,256]{1,0:T(8,128)(2,1)S(1)} %get-tuple-element.35), channel_id=1, source_target_pairs={{0,16},{4,20},{8,24},{12,28},{16,0},{20,4},{24,8},{28,12},{1,17},{... | collective-permute-start | bytes 417800 | tf_op jit(solution)/shard_map/ppermute | solution.py:48
  52.3 6.3 %collective-permute-start.19 = (bf16[272,256]{1,0:T(8,128)(2,1)S(1)}, bf16[272,256]{1,0:T(8,128)(2,1)S(1)}, u32[]{:S(2)}, u32[]{:S(2)}) collective-permute-start(bf16[272,256]{1,0:T(8,128)(2,1)S(1)} %get-tuple-element.36), channel_id=1, source_target_pairs={{0,24},{4,28},{8,16},{12,20},{16,8},{20,12},{24,0},{28,4},{1,25},{... | collective-permute-start | bytes 417800 | tf_op jit(solution)/shard_map/ppermute | solution.py:48
  59.4 1.3 %collective-permute-start.20 = (f32[128,256]{1,0:T(8,128)S(1)}, f32[128,256]{1,0:T(8,128)S(1)}, u32[]{:S(2)}, u32[]{:S(2)}) collective-permute-start(f32[128,256]{1,0:T(8,128)S(1)} %get-tuple-element.38.mine_ref), channel_id=1, source_target_pairs={{0,4},{4,0},{8,12},{12,8},{16,20},{20,16},{24,28},{28,24},{1,5},{5... | collective-permute-start | bytes 393224 | tf_op jit(solution)/shard_map/ppermute | solution.py:38

commit v2 on v1

--- a/solution.py
+++ b/solution.py
@@ -10,6 +10,7 @@
 BLOCK = 128
 CORES = 2
 EXTRA = 16
+LONG = 4_000_000_000
 VMEM = pl.BlockSpec(memory_space=pltpu.VMEM)
 SMEM = pl.BlockSpec(memory_space=pltpu.SMEM)
 NT = (((1,), (1,)), ((), ()))
@@ -59,8 +60,16 @@
     return jnp.concatenate([tall] * (width // BLOCK), axis=1)
 
 
-def scale_kernel(features_ref, degree_ref, out_ref):
+def scale_kernel(features_hbm, degree_hbm, out_ref, features_ref, degree_ref, sems):
+    copies = [
+        pltpu.make_async_copy(degree_hbm, degree_ref, sems.at[0]),
+        pltpu.make_async_copy(features_hbm, features_ref, sems.at[1]),
+    ]
+    for copy in copies:
+        copy.start()
+    copies[0].wait()
     inv = spread_inv(degree_ref, features_ref.shape[1])
+    copies[1].wait()
     out_ref[...] = (features_ref[...].astype(F32) * inv).astype(BF16)
 
 
@@ -74,7 +83,8 @@
     lax.fori_loop(0, count, step, 0)
 
 
-def build_kernel(count_ref, edge_ref, blocks_ref):
+def build_kernel(count_ref, edge_ref, bias_ref, blocks_ref, bias_out_ref):
+    bias_out_ref[...] = bias_ref[...]
     slots, edges = edge_ref.shape[2], edge_ref.shape[3]
     node = lax.broadcasted_iota(jnp.int32, (BLOCK, edges), 0)
 
@@ -152,15 +162,22 @@
     send_ref[half:] = pack_bias(bias_sum, EXTRA)
 
 
-def pair_sum_kernel(keep_ref, bias_keep_ref, got_ref, out_ref):
-    half = keep_ref.shape[0]
-    out_ref[:half] = (keep_ref[...] + got_ref[:half].astype(F32)).astype(BF16)
-    out_ref[half:] = pack_bias(bias_keep_ref[...] + add_bias(got_ref[half:]), EXTRA)
+def pair_sum_kernel(keep_ref, bias_keep_ref, got_ref, hidden_ref, out_ref):
+    owned, half = hidden_ref.shape[0], keep_ref.shape[0]
+    out_ref[:owned] = hidden_ref[...]
+    out_ref[owned : owned + half] = (keep_ref[...] + got_ref[:half].astype(F32)).astype(BF16)
+    out_ref[owned + half :] = pack_bias(bias_keep_ref[...] + add_bias(got_ref[half:]), EXTRA)
+
+
+def add_grads(half, a, b):
+    total = (a[:half].astype(F32) + b[:half].astype(F32)).astype(BF16)
+    return total, pack_bias(add_bias(a[half:]) + add_bias(b[half:]), EXTRA)
 
 
 def add_kernel(half, a_ref, b_ref, out_ref):
-    out_ref[:half] = (a_ref[:half].astype(F32) + b_ref[:half].astype(F32)).astype(BF16)
-    out_ref[half:] = pack_bias(add_bias(a_ref[half:]) + add_bias(b_ref[half:]), EXTRA)
+    rows = half + EXTRA
+    a, b = (ref[ref.shape[0] - rows :] for ref in (a_ref, b_ref))
+    out_ref[:half], out_ref[half:] = add_grads(half, a, b)
 
 
 def backward_kernel(rows, cols, pos_ref, count_ref, blocks_ref, *refs):
@@ -169,7 +186,7 @@
     chips = rows // CORES
     row, col = lax.axis_index("row"), lax.axis_index("col")
     for n, ref in enumerate(hidden_parts):
-        hidden[n] = ref[...]
+        hidden[n] = ref[:BLOCK]
     acc[...] = jnp.zeros_like(acc)
 
     def add(s):
@@ -185,27 +202,36 @@
     send_ref[...] = acc[chips:].astype(BF16)
 
 
-def merge_kernel(keep_ref, got_ref, grads_ref, own_ref, *send):
+def merge_kernel(keep_ref, got_ref, a_ref, b_ref, own_ref, grads_ref, *send):
     own_ref[...] = keep_ref[0] + got_ref[0].astype(F32)
+    half = grads_ref.shape[0] - EXTRA
+    total, bias = add_grads(half, a_ref[...], b_ref[...])
+    grads_ref[:half] = total
+    grads_ref[half:] = bias
     for k, ref in enumerate(send, 1):
         ref[:BLOCK] = (keep_ref[k] + got_ref[k].astype(F32)).astype(BF16)
-        ref[BLOCK:] = grads_ref[...]
-
-
-def finish_kernel(chips, norm, degree_ref, own_ref, grads_ref, *refs):
-    parts = refs[: chips - 1]
-    grad_x_ref, half_ref, grad_b_ref = refs[chips - 1 :]
+        ref[BLOCK : BLOCK + half] = total
+        ref[BLOCK + half :] = bias
+
+
+def finish_grads_kernel(norm, grads_ref, *refs):
+    *parts, half_ref, grad_b_ref = refs
     half = half_ref.shape[0]
-    total = own_ref[...]
     grads = grads_ref[:half].astype(F32)
     bias = add_bias(grads_ref[half:])
     for ref in parts:
-        total = total + ref[:BLOCK].astype(F32)
         grads = grads + ref[BLOCK : BLOCK + half].astype(F32)
         bias = bias + add_bias(ref[BLOCK + half :])
-    grad_x_ref[...] = (total * spread_inv(degree_ref, total.shape[1])).astype(BF16)
     half_ref[...] = grads * norm
     grad_b_ref[...] = bias * norm
+
+
+def finish_kernel(degree_ref, own_ref, *refs):
+    *parts, grad_x_ref = refs
+    total = own_ref[...]
+    for ref in parts:
+        total = total + ref[:BLOCK].astype(F32)
+    grad_x_ref[...] = (total * spread_inv(degree_ref, total.shape[1])).astype(BF16)
 
 
 def join_kernel(mine_ref, got_ref, out_ref):
@@ -223,7 +249,7 @@
         out_shape=shapes[0] if single else tuple(shapes),
         in_specs=specs,
         out_specs=VMEM if single else tuple(VMEM for _ in shapes),
-        scratch_shapes=[pltpu.VMEM(shape, dtype) for shape, dtype in scratch],
+        scratch_shapes=[pltpu.VMEM(*s) if isinstance(s, tuple) else s for s in scratch],
         compiler_params=pltpu.CompilerParams(vmem_limit_bytes=40 * 1024 * 1024),
         cost_estimate=pl.CostEstimate(flops=flops, bytes_accessed=1_000_000, transcendentals=0),
     )
@@ -240,11 +266,21 @@
     degree = degree.reshape(1, owned)
     bias_vector = bias_vector.reshape(1, width)
 
-    scaled = call(scale_kernel, [VMEM, VMEM], [(piece, BF16)])(features, degree)
+    scaled = call(
+        scale_kernel,
+        [pl.BlockSpec(memory_space=pltpu.HBM)] * 2,
+        [(piece, BF16)],
+        [(piece, BF16), ((1, owned), jnp.int32), pltpu.SemaphoreType.DMA((2,))],
+    )(features, degree)
     near = [scaled] + [to_chip(scaled, rows, k) for k in range(1, chips)]
-    blocks = call(
-        build_kernel, [SMEM, VMEM], [((slots, BLOCK, BLOCK), BF16)], flops=2_000_000_000
-    )(block_count, edge_pos)
+    blocks, bias_vector = call(
+        build_kernel,
+        [SMEM, VMEM, VMEM],
+        [((slots, BLOCK, BLOCK), BF16), ((1, width), F32)],
+        flops=LONG,
+    )(block_count, edge_pos, bias_vector)
+    blocks, *got = lax.optimization_barrier((blocks, *near[1:]))
+    near = [scaled, *got]
     near = near + [to_core(x, rows) for x in near]
 
     own, *send = call(
@@ -253,45 +289,54 @@
         [(piece, F32)] + [(piece, BF16)] * (cols - 1),
         [((rows,) + piece, BF16), ((cols,) + piece, F32)],
     )(block_pos, block_count, blocks, *near)
-    parts = [to_col(x, cols, k) for k, x in enumerate(send, 1)]
+    order = list(range(2, cols)) + [1]
+    parts = [to_col(send[k - 1], cols, k) for k in order]
 
     output, hidden, keep, bias_keep, half_send = call(
         functools.partial(pointwise_kernel, cols),
         [VMEM] * (4 + cols),
         [(piece, BF16), (piece, BF16), ((half, width), F32), ((1, width), F32), (grads_shape, BF16)],
     )(weight, bias_vector, cotangent, degree, own, *parts)
-    hidden_parts = [hidden] + [to_col(hidden, cols, k) for k in range(1, cols)]
-
-    grads = call(pair_sum_kernel, [VMEM] * 3, [(grads_shape, BF16)])(
-        keep, bias_keep, to_core(half_send, rows)
-    )
-    step = 1
+
+    half_got = to_core(half_send, rows)
+    far = [to_col(hidden, cols, k) for k in range(2, cols)]
+    message = call(
+        pair_sum_kernel, [VMEM] * 4, [((owned + half + EXTRA, width), BF16)], flops=LONG
+    )(keep, bias_keep, half_got, hidden)
+    next_to = to_col(message, cols, 1)
+    grads, other = message, next_to
+    add = call(functools.partial(add_kernel, half), [VMEM] * 2, [(grads_shape, BF16)])
+    step = 2
     while step < cols:
-        grads = call(functools.partial(add_kernel, half), [VMEM] * 2, [(grads_shape, BF16)])(
-            grads, to_col(grads, cols, step)
-        )
+        grads = add(grads, other)
+        other = to_col(grads, cols, step)
         step *= 2
 
+    grads, next_to = lax.optimization_barrier((grads, next_to))
     col_keep, col_send = call(
         functools.partial(backward_kernel, rows, cols),
         [SMEM, SMEM, VMEM] + [VMEM] * cols,
         [((chips,) + piece, F32), ((chips,) + piece, BF16)],
         [((cols,) + piece, BF16), ((rows,) + piece, F32)],
-    )(block_pos, block_count, blocks, *hidden_parts)
-    own_x, *send_x = call(
+        flops=LONG,
+    )(block_pos, block_count, blocks, hidden, next_to, *far)
+    own_x, grads, *send_x = call(
         merge_kernel,
-        [VMEM] * 3,
-        [(piece, F32)] + [((owned + half + EXTRA, width), BF16)] * (chips - 1),
-    )(col_keep, to_core(col_send, rows), grads)
+        [VMEM] * 4,
+        [(piece, F32), (grads_shape, BF16)]
+        + [((owned + half + EXTRA, width), BF16)] * (chips - 1),
+    )(col_keep, to_core(col_send, rows), grads, other)
     parts_x = [to_chip(x, rows, k) for k, x in enumerate(send_x, 1)]
 
     norm = float((owned * rows * cols) ** -0.5)
-    grad_x, mine, grad_b = call(
-        functools.partial(finish_kernel, chips, norm),
-        [VMEM] * (2 + chips),
-        [(piece, BF16), ((half, width), F32), ((1, width), F32)],
-    )(degree, own_x, grads, *parts_x)
-    grad_w = call(join_kernel, [VMEM] * 2, [((width, width), F32)])(mine, to_core(mine, rows))
+    mine, grad_b = call(
+        functools.partial(finish_grads_kernel, norm),
+        [VMEM] * chips,
+        [((half, width), F32), ((1, width), F32)],
+    )(grads, *parts_x)
+    theirs = to_core(mine, rows)
+    grad_x = call(finish_kernel, [VMEM] * (1 + chips), [(piece, BF16)])(degree, own_x, *parts_x)
+    grad_w = call(join_kernel, [VMEM] * 2, [((width, width), F32)])(mine, theirs)
     return (output, grad_x, grad_w, grad_b.reshape(width))
 
 

time: 62.2 us -> 58.6 us (0.942)
  starting transfers between devices: 22.7 us -> 17.9 us
  waiting for transfers between devices: 29.5 us -> 30.4 us
    ppermute x8 -> x7, starting transfers between devices: 13.6 us -> 9.05 us  [to_col(): lax.ppermute(x, 'col', [(i, target(cols, i, k)) for i in range(cols)])]
    ppermute x8 -> x7, waiting for transfers between devices: 17.2 us -> 19.2 us  [to_col(): lax.ppermute(x, 'col', [(i, target(cols, i, k)) for i in range(cols)])]
    ppermute x6, waiting for transfers between devices: 9.31 us -> 8.08 us  [to_chip(): return lax.ppermute(x, 'row', pairs)]
  transfers between devices with their start and end apart: 21 -> 20, of which waited for: 13 -> 18; matrix products, arithmetic and copies ran while one was open for 0% -> 0% of each run, Pallas kernels for 1% -> 2%
where the time goes in v2:
time: 58.6 us; the launch traced here: 57.6 us
  waiting for transfers between devices  30.4 us (52%)
  starting transfers between devices  17.9 us (31%)
  Pallas kernels  5.74 us (10%)
  local copies, waits for them, and re-layouts  2.17 us (4%)
  between operations  1.39 us (2%)
    ppermute x7, waiting for transfers between devices, to_col(): lax.ppermute(x, 'col', [(i, target(cols, i, k)) for i in range(cols)])  19.2 us
    ppermute x7, starting transfers between devices, to_col(): lax.ppermute(x, 'col', [(i, target(cols, i, k)) for i in range(cols)])  9.05 us
    ppermute x6, waiting for transfers between devices, to_chip(): return lax.ppermute(x, 'row', pairs)  8.08 us
    ppermute x6, starting transfers between devices, to_chip(): return lax.ppermute(x, 'row', pairs)  7.72 us
    ppermute x7, waiting for transfers between devices, to_core(): return lax.ppermute(x, 'row', [(i, i ^ 1) for i in range(rows)])  3.06 us
    unnamed x14, local copies, waits for them, and re-layouts  2.17 us
  transfers between devices with their start and end apart: 20, of which 18 were waited for; matrix products, arithmetic and copies ran while one was open for 0% of the time, Pallas kernels for 2%

profile of v2, /device:TPU:0, one launch (start us, length us, event | category | flops | bytes accessed | tf_op | source)
XLA Modules:
  0.0 57.6 jit_solution(5137114464625173849)
XLA Ops:
  0.6 0.6 %copy-done.3 = s32[128]{0:T(128)S(1)} copy-done((s32[128]{0:T(128)S(1)}, s32[128]{0:T(128)}, u32[]{:S(2)}) %copy-start.3) | copy-done | bytes 536
  1.3 0.8 %copy-done.2 = bf16[128,256]{1,0:T(8,128)(2,1)S(1)} copy-done((bf16[128,256]{1,0:T(8,128)(2,1)S(1)}, bf16[128,256]{1,0:T(8,128)(2,1)}, u32[]{:S(2)}) %copy-start.2) | copy-done | bytes 65560
  2.1 0.2 shard_map.112.refs_0_
  2.3 0.5 collective-permute-start.3
  2.9 3.5 %collective-permute-start.2 = (bf16[128,256]{1,0:T(8,128)(2,1)S(1)}, bf16[128,256]{1,0:T(8,128)(2,1)S(1)}, u32[]{:S(2)}, u32[]{:S(2)}) collective-permute-start(bf16[128,256]{1,0:T(8,128)(2,1)S(1)} %shard_map.112.refs_0_), channel_id=1, source_target_pairs={{0,24},{4,28},{8,16},{12,20},{16,8},{20,12},{24,0},{28,4},{1,25},{... | collective-permute-start | bytes 196616 | tf_op jit(solution)/shard_map/ppermute | solution.py:49
  6.4 0.5 collective-permute-start.1
  6.9 0.1 collective-permute-start
  7.7 0.0 copy-start.6
  7.7 0.7 %copy-done.6 = f32[256]{0:T(256)S(1)} copy-done((f32[256]{0:T(256)S(1)}, f32[256]{0:T(256)}, u32[]{:S(2)}) %copy-start.6) | copy-done | bytes 1048
  8.4 0.4 shard_map.111
  8.8 0.0 copy-start.4
  8.8 0.3 collective-permute-done.2.refs_3_
  9.1 1.6 %collective-permute-done.1.refs_2_ = bf16[128,256]{1,0:T(8,128)(2,1)S(1)} collective-permute-done((bf16[128,256]{1,0:T(8,128)(2,1)S(1)}, bf16[128,256]{1,0:T(8,128)(2,1)S(1)}, u32[]{:S(2)}, u32[]{:S(2)}) %collective-permute-start.1) | collective-permute-done | bytes 65568 | tf_op jit(solution)/shard_map/ppermute | solution.py:49
  10.7 0.5 collective-permute-done.refs_1_
  11.2 0.5 collective-permute-start.5
  11.7 0.1 collective-permute-start.6
  11.7 0.7 %collective-permute-done.4.refs_5_ = bf16[128,256]{1,0:T(8,128)(2,1)S(1)} collective-permute-done((bf16[128,256]{1,0:T(8,128)(2,1)S(1)}, bf16[128,256]{1,0:T(8,128)(2,1)S(1)}, u32[]{:S(2)}, u32[]{:S(2)}) %collective-permute-start.4) | collective-permute-done | bytes 65568 | tf_op jit(solution)/shard_map/ppermute | solution.py:39
  12.4 0.2 collective-permute-done.5.refs_6_
  12.6 0.4 collective-permute-done.6.refs_7_
  12.9 1.0 %shard_map.113 = (f32[128,256]{1,0:T(8,128)S(1)}, bf16[128,256]{1,0:T(8,128)(2,1)S(1)}, bf16[128,256]{1,0:T(8,128)(2,1)S(1)}, bf16[128,256]{1,0:T(8,128)(2,1)S(1)}) custom-call(s32[1,1,16]{2,1,0:T(1,128)S(1)} %copy-done.4, s32[1,1]{1,0:T(1,128)S(6)} %copy.12.count_ref, bf16[16,128,128]{2,1,0:T(8,128)(2,1)S(1)} %get-tuple-element.32.blocks_ref, ...), custom_call_target="tpu_custom_call" | custom-call | flops 1000000 | bytes 1000000 | tf_op jit(solution)/shard_map/pallas_call | solution.py:286
  13.9 2.8 %collective-permute-start.7 = (bf16[128,256]{1,0:T(8,128)(2,1)S(1)}, bf16[128,256]{1,0:T(8,128)(2,1)S(1)}, u32[]{:S(2)}, u32[]{:S(2)}) collective-permute-start(bf16[128,256]{1,0:T(8,128)(2,1)S(1)} %get-tuple-element.37), channel_id=1, source_target_pairs={{0,2},{1,3},{2,0},{3,1},{4,6},{5,7},{6,4},{7,5},{8,10},{9,11},{10,... | collective-permute-start | bytes 196616 | tf_op jit(solution)/shard_map/ppermute | solution.py:53
  16.7 2.0 %collective-permute-start.8 = (bf16[128,256]{1,0:T(8,128)(2,1)S(1)}, bf16[128,256]{1,0:T(8,128)(2,1)S(1)}, u32[]{:S(2)}, u32[]{:S(2)}) collective-permute-start(bf16[128,256]{1,0:T(8,128)(2,1)S(1)} %get-tuple-element.38), channel_id=1, source_target_pairs={{0,3},{1,2},{2,1},{3,0},{4,7},{5,6},{6,5},{7,4},{8,11},{9,10},{10,... | collective-permute-start | bytes 196616 | tf_op jit(solution)/shard_map/ppermute | solution.py:53
  18.7 0.1 collective-permute-start.9
  18.8 2.4 %collective-permute-done.7.refs_1_ = bf16[128,256]{1,0:T(8,128)(2,1)S(1)} collective-permute-done((bf16[128,256]{1,0:T(8,128)(2,1)S(1)}, bf16[128,256]{1,0:T(8,128)(2,1)S(1)}, u32[]{:S(2)}, u32[]{:S(2)}) %collective-permute-start.7) | collective-permute-done | bytes 65568 | tf_op jit(solution)/shard_map/ppermute | solution.py:53
  21.2 2.3 %collective-permute-done.8.refs_2_ = bf16[128,256]{1,0:T(8,128)(2,1)S(1)} collective-permute-done((bf16[128,256]{1,0:T(8,128)(2,1)S(1)}, bf16[128,256]{1,0:T(8,128)(2,1)S(1)}, u32[]{:S(2)}, u32[]{:S(2)}) %collective-permute-start.8) | collective-permute-done | bytes 65568 | tf_op jit(solution)/shard_map/ppermute | solution.py:53
  23.5 0.5 collective-permute-done.9.refs_3_
  24.0 0.9 %shard_map.114 = (bf16[128,256]{1,0:T(8,128)(2,1)}, bf16[128,256]{1,0:T(8,128)(2,1)S(1)}, f32[128,256]{1,0:T(8,128)S(1)}, f32[1,256]{1,0:T(1,128)S(1)}, bf16[144,256]{1,0:T(8,128)(2,1)S(1)}) custom-call(bf16[256,256]{1,0:T(8,128)(2,1)S(1)} %copy-done, f32[1,256]{1,0:T(1,128)S(1)} %get-tuple-element.30.bias_ref, bf16[128,256]{1,0:T(8,128)(2,1)S(1)} %copy-done.1, ...), custom_call_target="tpu_custom_call" | custom-call | flops 1000000 | bytes 1000000 | tf_op jit(solution)/shard_map/pallas_call | solution.py:295
  24.9 1.3 %collective-permute-done.10.got_ref = bf16[144,256]{1,0:T(8,128)(2,1)S(1)} collective-permute-done((bf16[144,256]{1,0:T(8,128)(2,1)S(1)}, bf16[144,256]{1,0:T(8,128)(2,1)S(1)}, u32[]{:S(2)}, u32[]{:S(2)}) %collective-permute-start.10) | collective-permute-done | bytes 73760 | tf_op jit(solution)/shard_map/ppermute | solution.py:39
  26.2 0.7 %collective-permute-start.11 = (bf16[272,256]{1,0:T(8,128)(2,1)S(1)}, bf16[272,256]{1,0:T(8,128)(2,1)S(1)}, u32[]{:S(2)}, u32[]{:S(2)}) collective-permute-start(bf16[272,256]{1,0:T(8,128)(2,1)S(1)} %shard_map.115.a_ref), channel_id=1, source_target_pairs={{0,1},{1,0},{2,3},{3,2},{4,5},{5,4},{6,7},{7,6},{8,9},{9,8},{10,11... | collective-permute-start | bytes 417800 | tf_op jit(solution)/shard_map/ppermute | solution.py:53
  26.9 3.2 %collective-permute-start.13 = (bf16[128,256]{1,0:T(8,128)(2,1)S(1)}, bf16[128,256]{1,0:T(8,128)(2,1)S(1)}, u32[]{:S(2)}, u32[]{:S(2)}) collective-permute-start(bf16[128,256]{1,0:T(8,128)(2,1)S(1)} %get-tuple-element.41.hidden_ref.refs_0_), channel_id=1, source_target_pairs={{0,3},{1,2},{2,1},{3,0},{4,7},{5,6},{6,5},{7,4},{8,11},{9,10},{10,... | collective-permute-start | bytes 196616 | tf_op jit(solution)/shard_map/ppermute | solution.py:53
  30.0 1.9 %collective-permute-done.11.b_ref.refs_1_ = bf16[272,256]{1,0:T(8,128)(2,1)S(1)} collective-permute-done((bf16[272,256]{1,0:T(8,128)(2,1)S(1)}, bf16[272,256]{1,0:T(8,128)(2,1)S(1)}, u32[]{:S(2)}, u32[]{:S(2)}) %collective-permute-start.11) | collective-permute-done | bytes 139296 | tf_op jit(solution)/shard_map/ppermute | solution.py:53
  32.0 3.9 %collective-permute-done.13.refs_3_ = bf16[128,256]{1,0:T(8,128)(2,1)S(1)} collective-permute-done((bf16[128,256]{1,0:T(8,128)(2,1)S(1)}, bf16[128,256]{1,0:T(8,128)(2,1)S(1)}, u32[]{:S(2)}, u32[]{:S(2)}) %collective-permute-start.13) | collective-permute-done | bytes 65568 | tf_op jit(solution)/shard_map/ppermute | solution.py:53
  36.0 1.3 %collective-permute-done.12.refs_2_ = bf16[128,256]{1,0:T(8,128)(2,1)S(1)} collective-permute-done((bf16[128,256]{1,0:T(8,128)(2,1)S(1)}, bf16[128,256]{1,0:T(8,128)(2,1)S(1)}, u32[]{:S(2)}, u32[]{:S(2)}) %collective-permute-start.12) | collective-permute-done | bytes 65568 | tf_op jit(solution)/shard_map/ppermute | solution.py:53
  37.3 1.1 %shard_map.117 = (f32[4,128,256]{2,1,0:T(8,128)S(1)}, bf16[4,128,256]{2,1,0:T(8,128)(2,1)S(1)}) custom-call(s32[1,1,16]{2,1,0:T(1,128)S(1)} %copy-done.4, s32[1,1]{1,0:T(1,128)S(6)} %copy.12.count_ref, bf16[16,128,128]{2,1,0:T(8,128)(2,1)S(1)} %get-tuple-element.32.blocks_ref, bf16[128,256]{1,0:T(8,128)(2,1)S(1)} %get-tuple-element.41.hidden_ref.refs_0_, ...), custom_call_target="tpu_custom_call" | custom-call | flops 4000000000 | bytes 1000000 | tf_op jit(solution)/shard_map/pallas_call | solution.py:316
  38.3 0.1 collective-permute-start.14
  38.4 0.3 collective-permute-start.15
  38.8 6.8 %collective-permute-done.15.b_ref = bf16[144,256]{1,0:T(8,128)(2,1)S(1)} collective-permute-done((bf16[144,256]{1,0:T(8,128)(2,1)S(1)}, bf16[144,256]{1,0:T(8,128)(2,1)S(1)}, u32[]{:S(2)}, u32[]{:S(2)}) %collective-permute-start.15) | collective-permute-done | bytes 73760 | tf_op jit(solution)/shard_map/ppermute | solution.py:53
  45.6 0.1 shard_map.118
  45.7 0.9 %collective-permute-start.16 = (bf16[272,256]{1,0:T(8,128)(2,1)S(1)}, bf16[272,256]{1,0:T(8,128)(2,1)S(1)}, u32[]{:S(2)}, u32[]{:S(2)}) collective-permute-start(bf16[272,256]{1,0:T(8,128)(2,1)S(1)} %get-tuple-element.50), channel_id=1, source_target_pairs={{0,8},{4,12},{8,0},{12,4},{16,24},{20,28},{24,16},{28,20},{1,9},{5... | collective-permute-start | bytes 417800 | tf_op jit(solution)/shard_map/ppermute | solution.py:49
  46.6 1.7 %collective-permute-start.17 = (bf16[272,256]{1,0:T(8,128)(2,1)S(1)}, bf16[272,256]{1,0:T(8,128)(2,1)S(1)}, u32[]{:S(2)}, u32[]{:S(2)}) collective-permute-start(bf16[272,256]{1,0:T(8,128)(2,1)S(1)} %get-tuple-element.51), channel_id=1, source_target_pairs={{0,16},{4,20},{8,24},{12,28},{16,0},{20,4},{24,8},{28,12},{1,17},{... | collective-permute-start | bytes 417800 | tf_op jit(solution)/shard_map/ppermute | solution.py:49
  48.3 0.9 %collective-permute-start.18 = (bf16[272,256]{1,0:T(8,128)(2,1)S(1)}, bf16[272,256]{1,0:T(8,128)(2,1)S(1)}, u32[]{:S(2)}, u32[]{:S(2)}) collective-permute-start(bf16[272,256]{1,0:T(8,128)(2,1)S(1)} %get-tuple-element.52), channel_id=1, source_target_pairs={{0,24},{4,28},{8,16},{12,20},{16,8},{20,12},{24,0},{28,4},{1,25},{... | collective-permute-start | bytes 417800 | tf_op jit(solution)/shard_map/ppermute | solution.py:49
  49.2 2.6 %collective-permute-done.16.refs_0_ = bf16[272,256]{1,0:T(8,128)(2,1)S(1)} collective-permute-done((bf16[272,256]{1,0:T(8,128)(2,1)S(1)}, bf16[272,256]{1,0:T(8,128)(2,1)S(1)}, u32[]{:S(2)}, u32[]{:S(2)}) %collective-permute-start.16) | collective-permute-done | bytes 139296 | tf_op jit(solution)/shard_map/ppermute | solution.py:49
  51.9 2.3 %collective-permute-done.17.refs_1_ = bf16[272,256]{1,0:T(8,128)(2,1)S(1)} collective-permute-done((bf16[272,256]{1,0:T(8,128)(2,1)S(1)}, bf16[272,256]{1,0:T(8,128)(2,1)S(1)}, u32[]{:S(2)}, u32[]{:S(2)}) %collective-permute-start.17) | collective-permute-done | bytes 139296 | tf_op jit(solution)/shard_map/ppermute | solution.py:49
  54.2 0.7 %collective-permute-done.18.refs_2_ = bf16[272,256]{1,0:T(8,128)(2,1)S(1)} collective-permute-done((bf16[272,256]{1,0:T(8,128)(2,1)S(1)}, bf16[272,256]{1,0:T(8,128)(2,1)S(1)}, u32[]{:S(2)}, u32[]{:S(2)}) %collective-permute-start.18) | collective-permute-done | bytes 139296 | tf_op jit(solution)/shard_map/ppermute | solution.py:49
  54.9 0.6 %shard_map.120 = (f32[128,256]{1,0:T(8,128)S(1)}, f32[1,256]{1,0:T(1,128)}) custom-call(bf16[144,256]{1,0:T(8,128)(2,1)S(1)} %get-tuple-element.53.grads_ref, bf16[272,256]{1,0:T(8,128)(2,1)S(1)} %collective-permute-done.16.refs_0_, bf16[272,256]{1,0:T(8,128)(2,1)S(1)} %collective-permute-done.17.refs_1_, bf16[272,256]{1,0:T(8,128)(2,1)S(1)} %collective-permute-done.18.refs_2_), custom_call_target="tpu_custom_call" | custom-call | flops 1000000 | bytes 1000000 | tf_op jit(solution)/shard_map/pallas_call | solution.py:332
  55.5 0.7 %shard_map.119 = bf16[128,256]{1,0:T(8,128)(2,1)} custom-call(s32[1,128]{1,0:T(1,128)S(1)} %bitcast.5, f32[128,256]{1,0:T(8,128)S(1)} %get-tuple-element.49.own_ref, bf16[272,256]{1,0:T(8,128)(2,1)S(1)} %collective-permute-done.16.refs_0_, bf16[272,256]{1,0:T(8,128)(2,1)S(1)} %collective-permute-done.17.refs_1_, ...), custom_call_target="tpu_custom_call" | custom-call | flops 1000000 | bytes 1000000 | tf_op jit(solution)/shard_map/pallas_call | solution.py:338
  56.3 0.6 %collective-permute-done.19.got_ref = f32[128,256]{1,0:T(8,128)S(1)} collective-permute-done((f32[128,256]{1,0:T(8,128)S(1)}, f32[128,256]{1,0:T(8,128)S(1)}, u32[]{:S(2)}, u32[]{:S(2)}) %collective-permute-start.19) | collective-permute-done | bytes 131104 | tf_op jit(solution)/shard_map/ppermute | solution.py:39
  56.9 0.7 %shard_map.121 = f32[256,256]{1,0:T(8,128)} custom-call(f32[128,256]{1,0:T(8,128)S(1)} %get-tuple-element.54.mine_ref, f32[128,256]{1,0:T(8,128)S(1)} %collective-permute-done.19.got_ref), custom_call_target="tpu_custom_call" | custom-call | flops 1000000 | bytes 1000000 | tf_op jit(solution)/shard_map/pallas_call | solution.py:339
  (17 shorter events, 0.1 us)
Async XLA Ops:
  0.6 0.7 %copy-start.3 = (s32[128]{0:T(128)S(1)}, s32[128]{0:T(128)}, u32[]{:S(2)}) copy-start(s32[128]{0:T(128)} %param.9) | copy-start | bytes 1540
  1.3 0.8 %copy-start.2 = (bf16[128,256]{1,0:T(8,128)(2,1)S(1)}, bf16[128,256]{1,0:T(8,128)(2,1)}, u32[]{:S(2)}) copy-start(bf16[128,256]{1,0:T(8,128)(2,1)} %features_hbm.1) | copy-start | bytes 196612
  2.1 5.6 %copy-start.5 = (s32[1,1,16,512]{3,2,1,0:T(8,128)S(1)}, s32[1,1,16,512]{3,2,1,0:T(8,128)}, u32[]{:S(2)}) copy-start(s32[1,1,16,512]{3,2,1,0:T(8,128)} %edge_ref.1) | copy-start | bytes 98308
  2.3 9.4 %collective-permute-start.3 = (bf16[128,256]{1,0:T(8,128)(2,1)S(1)}, bf16[128,256]{1,0:T(8,128)(2,1)S(1)}, u32[]{:S(2)}, u32[]{:S(2)}) collective-permute-start(bf16[128,256]{1,0:T(8,128)(2,1)S(1)} %shard_map.112.refs_0_), channel_id=1, source_target_pairs={{0,4},{4,0},{8,12},{12,8},{16,20},{20,16},{24,28},{28,24},{1,5},{5... | collective-permute-start | bytes 196616 | tf_op jit(solution)/shard_map/ppermute | solution.py:39
  2.9 6.2 %collective-permute-start.2 = (bf16[128,256]{1,0:T(8,128)(2,1)S(1)}, bf16[128,256]{1,0:T(8,128)(2,1)S(1)}, u32[]{:S(2)}, u32[]{:S(2)}) collective-permute-start(bf16[128,256]{1,0:T(8,128)(2,1)S(1)} %shard_map.112.refs_0_), channel_id=1, source_target_pairs={{0,24},{4,28},{8,16},{12,20},{16,8},{20,12},{24,0},{28,4},{1,25},{... | collective-permute-start | bytes 196616 | tf_op jit(solution)/shard_map/ppermute | solution.py:49
  6.4 4.3 %collective-permute-start.1 = (bf16[128,256]{1,0:T(8,128)(2,1)S(1)}, bf16[128,256]{1,0:T(8,128)(2,1)S(1)}, u32[]{:S(2)}, u32[]{:S(2)}) collective-permute-start(bf16[128,256]{1,0:T(8,128)(2,1)S(1)} %shard_map.112.refs_0_), channel_id=1, source_target_pairs={{0,16},{4,20},{8,24},{12,28},{16,0},{20,4},{24,8},{28,12},{1,17},{... | collective-permute-start | bytes 196616 | tf_op jit(solution)/shard_map/ppermute | solution.py:49
  6.9 4.3 %collective-permute-start = (bf16[128,256]{1,0:T(8,128)(2,1)S(1)}, bf16[128,256]{1,0:T(8,128)(2,1)S(1)}, u32[]{:S(2)}, u32[]{:S(2)}) collective-permute-start(bf16[128,256]{1,0:T(8,128)(2,1)S(1)} %shard_map.112.refs_0_), channel_id=1, source_target_pairs={{0,8},{4,12},{8,0},{12,4},{16,24},{20,28},{24,16},{28,20},{1,9},{5... | collective-permute-start | bytes 196616 | tf_op jit(solution)/shard_map/ppermute | solution.py:49
  7.7 0.7 %copy-start.6 = (f32[256]{0:T(256)S(1)}, f32[256]{0:T(256)}, u32[]{:S(2)}) copy-start(f32[256]{0:T(256)} %param.11) | copy-start | bytes 3076
  8.8 4.2 %copy-start.4 = (s32[1,1,16]{2,1,0:T(1,128)S(1)}, s32[1,1,16]{2,1,0:T(1,128)}, u32[]{:S(2)}) copy-start(s32[1,1,16]{2,1,0:T(1,128)} %pos_ref.3) | copy-start | bytes 196
  11.2 12.8 %copy-start = (bf16[256,256]{1,0:T(8,128)(2,1)S(1)}, bf16[256,256]{1,0:T(8,128)(2,1)}, u32[]{:S(2)}) copy-start(bf16[256,256]{1,0:T(8,128)(2,1)} %weight_ref.1) | copy-start | bytes 393220
  11.2 12.8 %copy-start.1 = (bf16[128,256]{1,0:T(8,128)(2,1)S(1)}, bf16[128,256]{1,0:T(8,128)(2,1)}, u32[]{:S(2)}) copy-start(bf16[128,256]{1,0:T(8,128)(2,1)} %cot_ref.1) | copy-start | bytes 196612
  11.2 1.3 %collective-permute-start.4 = (bf16[128,256]{1,0:T(8,128)(2,1)S(1)}, bf16[128,256]{1,0:T(8,128)(2,1)S(1)}, u32[]{:S(2)}, u32[]{:S(2)}) collective-permute-start(bf16[128,256]{1,0:T(8,128)(2,1)S(1)} %collective-permute-done.refs_1_), channel_id=1, source_target_pairs={{0,4},{4,0},{8,12},{12,8},{16,20},{20,16},{24,28},{28,24},{1,5},{5... | collective-permute-start | bytes 196616 | tf_op jit(solution)/shard_map/ppermute | solution.py:39
  11.2 1.4 %collective-permute-start.5 = (bf16[128,256]{1,0:T(8,128)(2,1)S(1)}, bf16[128,256]{1,0:T(8,128)(2,1)S(1)}, u32[]{:S(2)}, u32[]{:S(2)}) collective-permute-start(bf16[128,256]{1,0:T(8,128)(2,1)S(1)} %collective-permute-done.1.refs_2_), channel_id=1, source_target_pairs={{0,4},{4,0},{8,12},{12,8},{16,20},{20,16},{24,28},{28,24},{1,5},{5... | collective-permute-start | bytes 196616 | tf_op jit(solution)/shard_map/ppermute | solution.py:39
  11.7 1.3 %collective-permute-start.6 = (bf16[128,256]{1,0:T(8,128)(2,1)S(1)}, bf16[128,256]{1,0:T(8,128)(2,1)S(1)}, u32[]{:S(2)}, u32[]{:S(2)}) collective-permute-start(bf16[128,256]{1,0:T(8,128)(2,1)S(1)} %collective-permute-done.2.refs_3_), channel_id=1, source_target_pairs={{0,4},{4,0},{8,12},{12,8},{16,20},{20,16},{24,28},{28,24},{1,5},{5... | collective-permute-start | bytes 196616 | tf_op jit(solution)/shard_map/ppermute | solution.py:39
  13.9 7.3 %collective-permute-start.7 = (bf16[128,256]{1,0:T(8,128)(2,1)S(1)}, bf16[128,256]{1,0:T(8,128)(2,1)S(1)}, u32[]{:S(2)}, u32[]{:S(2)}) collective-permute-start(bf16[128,256]{1,0:T(8,128)(2,1)S(1)} %get-tuple-element.37), channel_id=1, source_target_pairs={{0,2},{1,3},{2,0},{3,1},{4,6},{5,7},{6,4},{7,5},{8,10},{9,11},{10,... | collective-permute-start | bytes 196616 | tf_op jit(solution)/shard_map/ppermute | solution.py:53
  16.7 6.8 %collective-permute-start.8 = (bf16[128,256]{1,0:T(8,128)(2,1)S(1)}, bf16[128,256]{1,0:T(8,128)(2,1)S(1)}, u32[]{:S(2)}, u32[]{:S(2)}) collective-permute-start(bf16[128,256]{1,0:T(8,128)(2,1)S(1)} %get-tuple-element.38), channel_id=1, source_target_pairs={{0,3},{1,2},{2,1},{3,0},{4,7},{5,6},{6,5},{7,4},{8,11},{9,10},{10,... | collective-permute-start | bytes 196616 | tf_op jit(solution)/shard_map/ppermute | solution.py:53
  18.7 5.3 %collective-permute-start.9 = (bf16[128,256]{1,0:T(8,128)(2,1)S(1)}, bf16[128,256]{1,0:T(8,128)(2,1)S(1)}, u32[]{:S(2)}, u32[]{:S(2)}) collective-permute-start(bf16[128,256]{1,0:T(8,128)(2,1)S(1)} %get-tuple-element.39), channel_id=1, source_target_pairs={{0,1},{1,0},{2,3},{3,2},{4,5},{5,4},{6,7},{7,6},{8,9},{9,8},{10,11... | collective-permute-start | bytes 196616 | tf_op jit(solution)/shard_map/ppermute | solution.py:53
  24.9 1.3 %collective-permute-start.10 = (bf16[144,256]{1,0:T(8,128)(2,1)S(1)}, bf16[144,256]{1,0:T(8,128)(2,1)S(1)}, u32[]{:S(2)}, u32[]{:S(2)}) collective-permute-start(bf16[144,256]{1,0:T(8,128)(2,1)S(1)} %get-tuple-element.44), channel_id=1, source_target_pairs={{0,4},{4,0},{8,12},{12,8},{16,20},{20,16},{24,28},{28,24},{1,5},{5... | collective-permute-start | bytes 221192 | tf_op jit(solution)/shard_map/ppermute | solution.py:39
  26.2 5.8 %collective-permute-start.11 = (bf16[272,256]{1,0:T(8,128)(2,1)S(1)}, bf16[272,256]{1,0:T(8,128)(2,1)S(1)}, u32[]{:S(2)}, u32[]{:S(2)}) collective-permute-start(bf16[272,256]{1,0:T(8,128)(2,1)S(1)} %shard_map.115.a_ref), channel_id=1, source_target_pairs={{0,1},{1,0},{2,3},{3,2},{4,5},{5,4},{6,7},{7,6},{8,9},{9,8},{10,11... | collective-permute-start | bytes 417800 | tf_op jit(solution)/shard_map/ppermute | solution.py:53
  26.9 9.1 %collective-permute-start.13 = (bf16[128,256]{1,0:T(8,128)(2,1)S(1)}, bf16[128,256]{1,0:T(8,128)(2,1)S(1)}, u32[]{:S(2)}, u32[]{:S(2)}) collective-permute-start(bf16[128,256]{1,0:T(8,128)(2,1)S(1)} %get-tuple-element.41.hidden_ref.refs_0_), channel_id=1, source_target_pairs={{0,3},{1,2},{2,1},{3,0},{4,7},{5,6},{6,5},{7,4},{8,11},{9,10},{10,... | collective-permute-start | bytes 196616 | tf_op jit(solution)/shard_map/ppermute | solution.py:53
  30.0 7.2 %collective-permute-start.12 = (bf16[128,256]{1,0:T(8,128)(2,1)S(1)}, bf16[128,256]{1,0:T(8,128)(2,1)S(1)}, u32[]{:S(2)}, u32[]{:S(2)}) collective-permute-start(bf16[128,256]{1,0:T(8,128)(2,1)S(1)} %get-tuple-element.41.hidden_ref.refs_0_), channel_id=1, source_target_pairs={{0,2},{1,3},{2,0},{3,1},{4,6},{5,7},{6,4},{7,5},{8,10},{9,11},{10,... | collective-permute-start | bytes 196616 | tf_op jit(solution)/shard_map/ppermute | solution.py:53
  38.3 7.2 %collective-permute-start.14 = (bf16[4,128,256]{2,1,0:T(8,128)(2,1)S(1)}, bf16[4,128,256]{2,1,0:T(8,128)(2,1)S(1)}, u32[]{:S(2)}, u32[]{:S(2)}) collective-permute-start(bf16[4,128,256]{2,1,0:T(8,128)(2,1)S(1)} %get-tuple-element.47), channel_id=1, source_target_pairs={{0,4},{4,0},{8,12},{12,8},{16,20},{20,16},{24,28},{28,24},{1,5},{5... | collective-permute-start | bytes 786440 | tf_op jit(solution)/shard_map/ppermute | solution.py:39
  38.4 7.2 %collective-permute-start.15 = (bf16[144,256]{1,0:T(8,128)(2,1)S(1)}, bf16[144,256]{1,0:T(8,128)(2,1)S(1)}, u32[]{:S(2)}, u32[]{:S(2)}) collective-permute-start(bf16[144,256]{1,0:T(8,128)(2,1)S(1)} %shard_map.116.a_ref), channel_id=1, source_target_pairs={{0,2},{1,3},{2,0},{3,1},{4,6},{5,7},{6,4},{7,5},{8,10},{9,11},{10,... | collective-permute-start | bytes 221192 | tf_op jit(solution)/shard_map/ppermute | solution.py:53
  45.7 6.2 %collective-permute-start.16 = (bf16[272,256]{1,0:T(8,128)(2,1)S(1)}, bf16[272,256]{1,0:T(8,128)(2,1)S(1)}, u32[]{:S(2)}, u32[]{:S(2)}) collective-permute-start(bf16[272,256]{1,0:T(8,128)(2,1)S(1)} %get-tuple-element.50), channel_id=1, source_target_pairs={{0,8},{4,12},{8,0},{12,4},{16,24},{20,28},{24,16},{28,20},{1,9},{5... | collective-permute-start | bytes 417800 | tf_op jit(solution)/shard_map/ppermute | solution.py:49
  46.6 7.6 %collective-permute-start.17 = (bf16[272,256]{1,0:T(8,128)(2,1)S(1)}, bf16[272,256]{1,0:T(8,128)(2,1)S(1)}, u32[]{:S(2)}, u32[]{:S(2)}) collective-permute-start(bf16[272,256]{1,0:T(8,128)(2,1)S(1)} %get-tuple-element.51), channel_id=1, source_target_pairs={{0,16},{4,20},{8,24},{12,28},{16,0},{20,4},{24,8},{28,12},{1,17},{... | collective-permute-start | bytes 417800 | tf_op jit(solution)/shard_map/ppermute | solution.py:49
  48.3 6.6 %collective-permute-start.18 = (bf16[272,256]{1,0:T(8,128)(2,1)S(1)}, bf16[272,256]{1,0:T(8,128)(2,1)S(1)}, u32[]{:S(2)}, u32[]{:S(2)}) collective-permute-start(bf16[272,256]{1,0:T(8,128)(2,1)S(1)} %get-tuple-element.52), channel_id=1, source_target_pairs={{0,24},{4,28},{8,16},{12,20},{16,8},{20,12},{24,0},{28,4},{1,25},{... | collective-permute-start | bytes 417800 | tf_op jit(solution)/shard_map/ppermute | solution.py:49
  55.5 1.3 %collective-permute-start.19 = (f32[128,256]{1,0:T(8,128)S(1)}, f32[128,256]{1,0:T(8,128)S(1)}, u32[]{:S(2)}, u32[]{:S(2)}) collective-permute-start(f32[128,256]{1,0:T(8,128)S(1)} %get-tuple-element.54.mine_ref), channel_id=1, source_target_pairs={{0,4},{4,0},{8,12},{12,8},{16,20},{20,16},{24,28},{28,24},{1,5},{5... | collective-permute-start | bytes 393224 | tf_op jit(solution)/shard_map/ppermute | solution.py:39

commit v3 on v2

--- a/solution.py
+++ b/solution.py
@@ -83,8 +83,7 @@
     lax.fori_loop(0, count, step, 0)
 
 
-def build_kernel(count_ref, edge_ref, bias_ref, blocks_ref, bias_out_ref):
-    bias_out_ref[...] = bias_ref[...]
+def build_kernel(count_ref, edge_ref, blocks_ref):
     slots, edges = edge_ref.shape[2], edge_ref.shape[3]
     node = lax.broadcasted_iota(jnp.int32, (BLOCK, edges), 0)
 
@@ -98,10 +97,10 @@
     for_live(count_ref, slots, build)
 
 
-def forward_kernel(rows, cols, pos_ref, count_ref, blocks_ref, *refs):
+def forward_kernel(rows, cols, pos_ref, count_ref, bias_ref, blocks_ref, *refs):
     near = refs[: 2 * (rows // CORES)]
-    own_ref, *send = refs[len(near) : len(near) + cols]
-    gathered, acc = refs[len(near) + cols :]
+    bias_out_ref, own_ref, *send, gathered, acc = refs[len(near) :]
+    bias_out_ref[...] = bias_ref[...]
     chips = rows // CORES
     row, col = lax.axis_index("row"), lax.axis_index("col")
     for n, ref in enumerate(near):
@@ -273,22 +272,19 @@
         [(piece, BF16), ((1, owned), jnp.int32), pltpu.SemaphoreType.DMA((2,))],
     )(features, degree)
     near = [scaled] + [to_chip(scaled, rows, k) for k in range(1, chips)]
-    blocks, bias_vector = call(
-        build_kernel,
-        [SMEM, VMEM, VMEM],
-        [((slots, BLOCK, BLOCK), BF16), ((1, width), F32)],
-        flops=LONG,
-    )(block_count, edge_pos, bias_vector)
+    blocks = call(build_kernel, [SMEM, VMEM], [((slots, BLOCK, BLOCK), BF16)], flops=LONG)(
+        block_count, edge_pos
+    )
     blocks, *got = lax.optimization_barrier((blocks, *near[1:]))
     near = [scaled, *got]
     near = near + [to_core(x, rows) for x in near]
 
-    own, *send = call(
+    bias_vector, own, *send = call(
         functools.partial(forward_kernel, rows, cols),
-        [SMEM, SMEM, VMEM] + [VMEM] * len(near),
-        [(piece, F32)] + [(piece, BF16)] * (cols - 1),
+        [SMEM, SMEM, VMEM, VMEM] + [VMEM] * len(near),
+        [((1, width), F32), (piece, F32)] + [(piece, BF16)] * (cols - 1),
         [((rows,) + piece, BF16), ((cols,) + piece, F32)],
-    )(block_pos, block_count, blocks, *near)
+    )(block_pos, block_count, bias_vector, blocks, *near)
     order = list(range(2, cols)) + [1]
     parts = [to_col(send[k - 1], cols, k) for k in order]
 
@@ -312,7 +308,6 @@
         other = to_col(grads, cols, step)
         step *= 2
 
-    grads, next_to = lax.optimization_barrier((grads, next_to))
     col_keep, col_send = call(
         functools.partial(backward_kernel, rows, cols),
         [SMEM, SMEM, VMEM] + [VMEM] * cols,
@@ -320,6 +315,7 @@
         [((cols,) + piece, BF16), ((rows,) + piece, F32)],
         flops=LONG,
     )(block_pos, block_count, blocks, hidden, next_to, *far)
+    col_send, other = lax.optimization_barrier((col_send, other))
     own_x, grads, *send_x = call(
         merge_kernel,
         [VMEM] * 4,

time: 58.6 us -> 56 us (0.956); the launches traced: 57.6 us -> 56.6 us
  waiting for transfers between devices: 30.4 us -> 21 us
  Pallas kernels: 5.74 us -> 13.6 us
  starting transfers between devices: 17.9 us -> 19 us
  local copies, waits for them, and re-layouts: 2.17 us -> 1.51 us
    ppermute x7, waiting for transfers between devices: 19.2 us -> 10.8 us  [to_col(): lax.ppermute(x, 'col', [(i, target(cols, i, k)) for i in range(cols)])]
    pallas_call x2, Pallas kernels: 1.36 us -> 6.42 us  [the longest x1 3.24 us: per_device(): call(build_kernel, [SMEM, VMEM], [((slots, BLOCK, BLOCK), BF16)], flops=L...]
    pallas_call x1, Pallas kernels: 1.08 us -> 3.88 us  [per_device(): call(functools.partial(backward_kernel, rows, cols), [SMEM, SMEM, VMEM] +...]
    ppermute x6, waiting for transfers between devices: 8.08 us -> 5.47 us  [to_chip(): return lax.ppermute(x, 'row', pairs)]
    ppermute x7, waiting for transfers between devices: 3.06 us -> 4.64 us  [to_core(): return lax.ppermute(x, 'row', [(i, i ^ 1) for i in range(rows)])]
    ppermute x7, starting transfers between devices: 9.05 us -> 10.2 us  [to_col(): lax.ppermute(x, 'col', [(i, target(cols, i, k)) for i in range(cols)])]
    unnamed x14, local copies, waits for them, and re-layouts: 2.17 us -> 1.51 us
  transfers between devices with their start and end apart: 20 -> 20, of which waited for: 18 -> 15; matrix products, arithmetic and copies ran while one was open for 0% -> 0% of each run, Pallas kernels for 2% -> 14%
where the time goes in v3:
time: 56 us; the launch traced here: 56.6 us
  waiting for transfers between devices  21 us (38%)
  starting transfers between devices  19 us (34%)
  Pallas kernels  13.6 us (24%)
  local copies, waits for them, and re-layouts  1.51 us (3%)
  between operations  1.42 us (3%)
    ppermute x7, waiting for transfers between devices, to_col(): lax.ppermute(x, 'col', [(i, target(cols, i, k)) for i in range(cols)])  10.8 us
    ppermute x7, starting transfers between devices, to_col(): lax.ppermute(x, 'col', [(i, target(cols, i, k)) for i in range(cols)])  10.2 us
    ppermute x6, starting transfers between devices, to_chip(): return lax.ppermute(x, 'row', pairs)  7.71 us
    ppermute x6, waiting for transfers between devices, to_chip(): return lax.ppermute(x, 'row', pairs)  5.47 us
    ppermute x7, waiting for transfers between devices, to_core(): return lax.ppermute(x, 'row', [(i, i ^ 1) for i in range(rows)])  4.64 us
    pallas_call x1, Pallas kernels, per_device(): call(functools.partial(backward_kernel, rows, cols), [SMEM, SMEM, VMEM] +...  3.88 us
    pallas_call x1, Pallas kernels, per_device(): call(build_kernel, [SMEM, VMEM], [((slots, BLOCK, BLOCK), BF16)], flops=L...  3.24 us
    pallas_call x1, Pallas kernels, per_device(): call(functools.partial(forward_kernel, rows, cols), [SMEM, SMEM, VMEM, VM...  3.18 us
  transfers between devices with their start and end apart: 20, of which 15 were waited for; matrix products, arithmetic and copies ran while one was open for 0% of the time, Pallas kernels for 14%

profile of v3, /device:TPU:0, one launch (start us, length us, event | category | flops | bytes accessed | tf_op | source)
XLA Modules:
  0.0 56.6 jit_solution(5941393217117609621)
XLA Ops:
  0.6 0.6 %copy-done.3 = s32[128]{0:T(128)S(1)} copy-done((s32[128]{0:T(128)S(1)}, s32[128]{0:T(128)}, u32[]{:S(2)}) %copy-start.3) | copy-done | bytes 536
  1.3 0.8 %copy-done.2 = bf16[128,256]{1,0:T(8,128)(2,1)S(1)} copy-done((bf16[128,256]{1,0:T(8,128)(2,1)S(1)}, bf16[128,256]{1,0:T(8,128)(2,1)}, u32[]{:S(2)}) %copy-start.2) | copy-done | bytes 65560
  2.1 0.2 shard_map.112.refs_0_
  2.3 0.5 collective-permute-start.3
  2.9 3.5 %collective-permute-start.2 = (bf16[128,256]{1,0:T(8,128)(2,1)S(1)}, bf16[128,256]{1,0:T(8,128)(2,1)S(1)}, u32[]{:S(2)}, u32[]{:S(2)}) collective-permute-start(bf16[128,256]{1,0:T(8,128)(2,1)S(1)} %shard_map.112.refs_0_), channel_id=1, source_target_pairs={{0,24},{4,28},{8,16},{12,20},{16,8},{20,12},{24,0},{28,4},{1,25},{... | collective-permute-start | bytes 196616 | tf_op jit(solution)/shard_map/ppermute | solution.py:49
  6.4 0.5 collective-permute-start.1
  6.9 0.1 collective-permute-start
  7.7 3.2 %shard_map.111.blocks_ref = bf16[16,128,128]{2,1,0:T(8,128)(2,1)S(1)} custom-call(s32[1,1]{1,0:T(1,128)S(6)} %copy.12.count_ref, s32[1,1,16,512]{3,2,1,0:T(8,128)S(1)} %copy-done.6), custom_call_target="tpu_custom_call" | custom-call | flops 4000000000 | bytes 1000000 | tf_op jit(solution)/shard_map/pallas_call | solution.py:275
  10.9 0.0 copy-start.4
  10.9 0.0 copy-start.5
  11.0 0.0 collective-permute-done.2.refs_3_
  11.0 0.0 collective-permute-done.1.refs_2_
  11.0 0.2 collective-permute-done.refs_1_
  11.2 0.5 collective-permute-start.5
  11.7 0.0 collective-permute-start.6
  11.7 0.7 %collective-permute-done.4.refs_5_ = bf16[128,256]{1,0:T(8,128)(2,1)S(1)} collective-permute-done((bf16[128,256]{1,0:T(8,128)(2,1)S(1)}, bf16[128,256]{1,0:T(8,128)(2,1)S(1)}, u32[]{:S(2)}, u32[]{:S(2)}) %collective-permute-start.4) | collective-permute-done | bytes 65568 | tf_op jit(solution)/shard_map/ppermute | solution.py:39
  12.4 0.2 collective-permute-done.5.refs_6_
  12.6 0.4 collective-permute-done.6.refs_7_
  12.9 3.2 %shard_map.113 = (f32[1,256]{1,0:T(1,128)S(1)}, f32[128,256]{1,0:T(8,128)S(1)}, bf16[128,256]{1,0:T(8,128)(2,1)S(1)}, bf16[128,256]{1,0:T(8,128)(2,1)S(1)}, bf16[128,256]{1,0:T(8,128)(2,1)S(1)}) custom-call(s32[1,1,16]{2,1,0:T(1,128)S(1)} %copy-done.5, s32[1,1]{1,0:T(1,128)S(6)} %copy.12.count_ref, f32[1,256]{1,0:T(1,128)S(1)} %bitcast.6, ...), custom_call_target="tpu_custom_call" | custom-call | flops 1000000 | bytes 1000000 | tf_op jit(solution)/shard_map/pallas_call | solution.py:282
  16.1 1.4 %collective-permute-start.7 = (bf16[128,256]{1,0:T(8,128)(2,1)S(1)}, bf16[128,256]{1,0:T(8,128)(2,1)S(1)}, u32[]{:S(2)}, u32[]{:S(2)}) collective-permute-start(bf16[128,256]{1,0:T(8,128)(2,1)S(1)} %get-tuple-element.35), channel_id=1, source_target_pairs={{0,2},{1,3},{2,0},{3,1},{4,6},{5,7},{6,4},{7,5},{8,10},{9,11},{10,... | collective-permute-start | bytes 196616 | tf_op jit(solution)/shard_map/ppermute | solution.py:53
  17.5 0.4 collective-permute-start.8
  17.9 1.8 %collective-permute-start.9 = (bf16[128,256]{1,0:T(8,128)(2,1)S(1)}, bf16[128,256]{1,0:T(8,128)(2,1)S(1)}, u32[]{:S(2)}, u32[]{:S(2)}) collective-permute-start(bf16[128,256]{1,0:T(8,128)(2,1)S(1)} %get-tuple-element.37), channel_id=1, source_target_pairs={{0,1},{1,0},{2,3},{3,2},{4,5},{5,4},{6,7},{7,6},{8,9},{9,8},{10,11... | collective-permute-start | bytes 196616 | tf_op jit(solution)/shard_map/ppermute | solution.py:53
  19.7 3.1 %collective-permute-done.7.refs_1_ = bf16[128,256]{1,0:T(8,128)(2,1)S(1)} collective-permute-done((bf16[128,256]{1,0:T(8,128)(2,1)S(1)}, bf16[128,256]{1,0:T(8,128)(2,1)S(1)}, u32[]{:S(2)}, u32[]{:S(2)}) %collective-permute-start.7) | collective-permute-done | bytes 65568 | tf_op jit(solution)/shard_map/ppermute | solution.py:53
  22.8 1.2 %collective-permute-done.8.refs_2_ = bf16[128,256]{1,0:T(8,128)(2,1)S(1)} collective-permute-done((bf16[128,256]{1,0:T(8,128)(2,1)S(1)}, bf16[128,256]{1,0:T(8,128)(2,1)S(1)}, u32[]{:S(2)}, u32[]{:S(2)}) %collective-permute-start.8) | collective-permute-done | bytes 65568 | tf_op jit(solution)/shard_map/ppermute | solution.py:53
  23.9 0.2 collective-permute-done.9.refs_3_
  24.1 0.9 %shard_map.114 = (bf16[128,256]{1,0:T(8,128)(2,1)}, bf16[128,256]{1,0:T(8,128)(2,1)S(1)}, f32[128,256]{1,0:T(8,128)S(1)}, f32[1,256]{1,0:T(1,128)S(1)}, bf16[144,256]{1,0:T(8,128)(2,1)S(1)}) custom-call(bf16[256,256]{1,0:T(8,128)(2,1)S(1)} %copy-done, f32[1,256]{1,0:T(1,128)S(1)} %get-tuple-element.33.bias_ref, bf16[128,256]{1,0:T(8,128)(2,1)S(1)} %copy-done.1, ...), custom_call_target="tpu_custom_call" | custom-call | flops 1000000 | bytes 1000000 | tf_op jit(solution)/shard_map/pallas_call | solution.py:291
  25.0 0.0 collective-permute-start.10
  25.0 1.3 %collective-permute-done.10.got_ref = bf16[144,256]{1,0:T(8,128)(2,1)S(1)} collective-permute-done((bf16[144,256]{1,0:T(8,128)(2,1)S(1)}, bf16[144,256]{1,0:T(8,128)(2,1)S(1)}, u32[]{:S(2)}, u32[]{:S(2)}) %collective-permute-start.10) | collective-permute-done | bytes 73760 | tf_op jit(solution)/shard_map/ppermute | solution.py:39
  26.3 0.7 %collective-permute-start.11 = (bf16[272,256]{1,0:T(8,128)(2,1)S(1)}, bf16[272,256]{1,0:T(8,128)(2,1)S(1)}, u32[]{:S(2)}, u32[]{:S(2)}) collective-permute-start(bf16[272,256]{1,0:T(8,128)(2,1)S(1)} %shard_map.115.a_ref), channel_id=1, source_target_pairs={{0,1},{1,0},{2,3},{3,2},{4,5},{5,4},{6,7},{7,6},{8,9},{9,8},{10,11... | collective-permute-start | bytes 417800 | tf_op jit(solution)/shard_map/ppermute | solution.py:53
  27.0 3.0 %collective-permute-start.13 = (bf16[128,256]{1,0:T(8,128)(2,1)S(1)}, bf16[128,256]{1,0:T(8,128)(2,1)S(1)}, u32[]{:S(2)}, u32[]{:S(2)}) collective-permute-start(bf16[128,256]{1,0:T(8,128)(2,1)S(1)} %get-tuple-element.39.hidden_ref.refs_0_), channel_id=1, source_target_pairs={{0,3},{1,2},{2,1},{3,0},{4,7},{5,6},{6,5},{7,4},{8,11},{9,10},{10,... | collective-permute-start | bytes 196616 | tf_op jit(solution)/shard_map/ppermute | solution.py:53
  30.0 2.1 %collective-permute-done.11.refs_1_.b_ref = bf16[272,256]{1,0:T(8,128)(2,1)S(1)} collective-permute-done((bf16[272,256]{1,0:T(8,128)(2,1)S(1)}, bf16[272,256]{1,0:T(8,128)(2,1)S(1)}, u32[]{:S(2)}, u32[]{:S(2)}) %collective-permute-start.11) | collective-permute-done | bytes 139296 | tf_op jit(solution)/shard_map/ppermute | solution.py:53
  32.2 3.0 %collective-permute-start.14 = (bf16[144,256]{1,0:T(8,128)(2,1)S(1)}, bf16[144,256]{1,0:T(8,128)(2,1)S(1)}, u32[]{:S(2)}, u32[]{:S(2)}) collective-permute-start(bf16[144,256]{1,0:T(8,128)(2,1)S(1)} %shard_map.117.a_ref), channel_id=1, source_target_pairs={{0,2},{1,3},{2,0},{3,1},{4,6},{5,7},{6,4},{7,5},{8,10},{9,11},{10,... | collective-permute-start | bytes 221192 | tf_op jit(solution)/shard_map/ppermute | solution.py:53
  35.2 0.8 %collective-permute-done.13.refs_3_ = bf16[128,256]{1,0:T(8,128)(2,1)S(1)} collective-permute-done((bf16[128,256]{1,0:T(8,128)(2,1)S(1)}, bf16[128,256]{1,0:T(8,128)(2,1)S(1)}, u32[]{:S(2)}, u32[]{:S(2)}) %collective-permute-start.13) | collective-permute-done | bytes 65568 | tf_op jit(solution)/shard_map/ppermute | solution.py:53
  36.0 3.5 %collective-permute-done.12.refs_2_ = bf16[128,256]{1,0:T(8,128)(2,1)S(1)} collective-permute-done((bf16[128,256]{1,0:T(8,128)(2,1)S(1)}, bf16[128,256]{1,0:T(8,128)(2,1)S(1)}, u32[]{:S(2)}, u32[]{:S(2)}) %collective-permute-start.12) | collective-permute-done | bytes 65568 | tf_op jit(solution)/shard_map/ppermute | solution.py:53
  39.5 3.9 %shard_map.116 = (f32[4,128,256]{2,1,0:T(8,128)S(1)}, bf16[4,128,256]{2,1,0:T(8,128)(2,1)S(1)}) custom-call(s32[1,1,16]{2,1,0:T(1,128)S(1)} %copy-done.5, s32[1,1]{1,0:T(1,128)S(6)} %copy.12.count_ref, bf16[16,128,128]{2,1,0:T(8,128)(2,1)S(1)} %shard_map.111.blocks_ref, bf16[128,256]{1,0:T(8,128)(2,1)S(1)} %get-tuple-element.39.hidden_ref.refs_0_, ...), custom_call_target="tpu_custom_call" | custom-call | flops 4000000000 | bytes 1000000 | tf_op jit(solution)/shard_map/pallas_call | solution.py:311
  43.4 0.1 collective-permute-start.15
  43.4 1.5 %collective-permute-done.15.got_ref = bf16[4,128,256]{2,1,0:T(8,128)(2,1)S(1)} collective-permute-done((bf16[4,128,256]{2,1,0:T(8,128)(2,1)S(1)}, bf16[4,128,256]{2,1,0:T(8,128)(2,1)S(1)}, u32[]{:S(2)}, u32[]{:S(2)}) %collective-permute-start.15) | collective-permute-done | bytes 262176 | tf_op jit(solution)/shard_map/ppermute | solution.py:39
  45.0 0.1 shard_map.118
  45.0 0.1 collective-permute-start.16
  45.1 0.5 collective-permute-start.17
  45.6 3.0 %collective-permute-start.18 = (bf16[272,256]{1,0:T(8,128)(2,1)S(1)}, bf16[272,256]{1,0:T(8,128)(2,1)S(1)}, u32[]{:S(2)}, u32[]{:S(2)}) collective-permute-start(bf16[272,256]{1,0:T(8,128)(2,1)S(1)} %get-tuple-element.50), channel_id=1, source_target_pairs={{0,24},{4,28},{8,16},{12,20},{16,8},{20,12},{24,0},{28,4},{1,25},{... | collective-permute-start | bytes 417800 | tf_op jit(solution)/shard_map/ppermute | solution.py:49
  48.6 3.0 %collective-permute-done.16.refs_0_ = bf16[272,256]{1,0:T(8,128)(2,1)S(1)} collective-permute-done((bf16[272,256]{1,0:T(8,128)(2,1)S(1)}, bf16[272,256]{1,0:T(8,128)(2,1)S(1)}, u32[]{:S(2)}, u32[]{:S(2)}) %collective-permute-start.16) | collective-permute-done | bytes 139296 | tf_op jit(solution)/shard_map/ppermute | solution.py:49
  51.6 2.3 %collective-permute-done.17.refs_1_ = bf16[272,256]{1,0:T(8,128)(2,1)S(1)} collective-permute-done((bf16[272,256]{1,0:T(8,128)(2,1)S(1)}, bf16[272,256]{1,0:T(8,128)(2,1)S(1)}, u32[]{:S(2)}, u32[]{:S(2)}) %collective-permute-start.17) | collective-permute-done | bytes 139296 | tf_op jit(solution)/shard_map/ppermute | solution.py:49
  53.9 0.0 collective-permute-done.18.refs_2_
  53.9 0.6 %shard_map.120 = (f32[128,256]{1,0:T(8,128)S(1)}, f32[1,256]{1,0:T(1,128)}) custom-call(bf16[144,256]{1,0:T(8,128)(2,1)S(1)} %get-tuple-element.51.grads_ref, bf16[272,256]{1,0:T(8,128)(2,1)S(1)} %collective-permute-done.16.refs_0_, bf16[272,256]{1,0:T(8,128)(2,1)S(1)} %collective-permute-done.17.refs_1_, bf16[272,256]{1,0:T(8,128)(2,1)S(1)} %collective-permute-done.18.refs_2_), custom_call_target="tpu_custom_call" | custom-call | flops 1000000 | bytes 1000000 | tf_op jit(solution)/shard_map/pallas_call | solution.py:328
  54.5 0.7 %shard_map.119 = bf16[128,256]{1,0:T(8,128)(2,1)} custom-call(s32[1,128]{1,0:T(1,128)S(1)} %bitcast.5, f32[128,256]{1,0:T(8,128)S(1)} %get-tuple-element.47.own_ref, bf16[272,256]{1,0:T(8,128)(2,1)S(1)} %collective-permute-done.16.refs_0_, bf16[272,256]{1,0:T(8,128)(2,1)S(1)} %collective-permute-done.17.refs_1_, ...), custom_call_target="tpu_custom_call" | custom-call | flops 1000000 | bytes 1000000 | tf_op jit(solution)/shard_map/pallas_call | solution.py:334
  55.2 0.6 %collective-permute-done.19.got_ref = f32[128,256]{1,0:T(8,128)S(1)} collective-permute-done((f32[128,256]{1,0:T(8,128)S(1)}, f32[128,256]{1,0:T(8,128)S(1)}, u32[]{:S(2)}, u32[]{:S(2)}) %collective-permute-start.19) | collective-permute-done | bytes 131104 | tf_op jit(solution)/shard_map/ppermute | solution.py:39
  55.8 0.7 %shard_map.121 = f32[256,256]{1,0:T(8,128)} custom-call(f32[128,256]{1,0:T(8,128)S(1)} %get-tuple-element.52.mine_ref, f32[128,256]{1,0:T(8,128)S(1)} %collective-permute-done.19.got_ref), custom_call_target="tpu_custom_call" | custom-call | flops 1000000 | bytes 1000000 | tf_op jit(solution)/shard_map/pallas_call | solution.py:335
  (17 shorter events, 0.1 us)
Async XLA Ops:
  0.6 0.7 %copy-start.3 = (s32[128]{0:T(128)S(1)}, s32[128]{0:T(128)}, u32[]{:S(2)}) copy-start(s32[128]{0:T(128)} %param.9) | copy-start | bytes 1540
  1.3 0.8 %copy-start.2 = (bf16[128,256]{1,0:T(8,128)(2,1)S(1)}, bf16[128,256]{1,0:T(8,128)(2,1)}, u32[]{:S(2)}) copy-start(bf16[128,256]{1,0:T(8,128)(2,1)} %features_hbm.1) | copy-start | bytes 196612
  2.1 5.6 %copy-start.6 = (s32[1,1,16,512]{3,2,1,0:T(8,128)S(1)}, s32[1,1,16,512]{3,2,1,0:T(8,128)}, u32[]{:S(2)}) copy-start(s32[1,1,16,512]{3,2,1,0:T(8,128)} %edge_ref.1) | copy-start | bytes 98308
  2.3 9.3 %collective-permute-start.3 = (bf16[128,256]{1,0:T(8,128)(2,1)S(1)}, bf16[128,256]{1,0:T(8,128)(2,1)S(1)}, u32[]{:S(2)}, u32[]{:S(2)}) collective-permute-start(bf16[128,256]{1,0:T(8,128)(2,1)S(1)} %shard_map.112.refs_0_), channel_id=1, source_target_pairs={{0,4},{4,0},{8,12},{12,8},{16,20},{20,16},{24,28},{28,24},{1,5},{5... | collective-permute-start | bytes 196616 | tf_op jit(solution)/shard_map/ppermute | solution.py:39
  2.9 8.1 %collective-permute-start.2 = (bf16[128,256]{1,0:T(8,128)(2,1)S(1)}, bf16[128,256]{1,0:T(8,128)(2,1)S(1)}, u32[]{:S(2)}, u32[]{:S(2)}) collective-permute-start(bf16[128,256]{1,0:T(8,128)(2,1)S(1)} %shard_map.112.refs_0_), channel_id=1, source_target_pairs={{0,24},{4,28},{8,16},{12,20},{16,8},{20,12},{24,0},{28,4},{1,25},{... | collective-permute-start | bytes 196616 | tf_op jit(solution)/shard_map/ppermute | solution.py:49
  6.4 4.6 %collective-permute-start.1 = (bf16[128,256]{1,0:T(8,128)(2,1)S(1)}, bf16[128,256]{1,0:T(8,128)(2,1)S(1)}, u32[]{:S(2)}, u32[]{:S(2)}) collective-permute-start(bf16[128,256]{1,0:T(8,128)(2,1)S(1)} %shard_map.112.refs_0_), channel_id=1, source_target_pairs={{0,16},{4,20},{8,24},{12,28},{16,0},{20,4},{24,8},{28,12},{1,17},{... | collective-permute-start | bytes 196616 | tf_op jit(solution)/shard_map/ppermute | solution.py:49
  6.9 4.3 %collective-permute-start = (bf16[128,256]{1,0:T(8,128)(2,1)S(1)}, bf16[128,256]{1,0:T(8,128)(2,1)S(1)}, u32[]{:S(2)}, u32[]{:S(2)}) collective-permute-start(bf16[128,256]{1,0:T(8,128)(2,1)S(1)} %shard_map.112.refs_0_), channel_id=1, source_target_pairs={{0,8},{4,12},{8,0},{12,4},{16,24},{20,28},{24,16},{28,20},{1,9},{5... | collective-permute-start | bytes 196616 | tf_op jit(solution)/shard_map/ppermute | solution.py:49
  10.9 2.0 %copy-start.4 = (f32[256]{0:T(256)S(1)}, f32[256]{0:T(256)}, u32[]{:S(2)}) copy-start(f32[256]{0:T(256)} %param.11) | copy-start | bytes 3076
  10.9 2.0 %copy-start.5 = (s32[1,1,16]{2,1,0:T(1,128)S(1)}, s32[1,1,16]{2,1,0:T(1,128)}, u32[]{:S(2)}) copy-start(s32[1,1,16]{2,1,0:T(1,128)} %pos_ref.3) | copy-start | bytes 196
  11.2 1.3 %collective-permute-start.4 = (bf16[128,256]{1,0:T(8,128)(2,1)S(1)}, bf16[128,256]{1,0:T(8,128)(2,1)S(1)}, u32[]{:S(2)}, u32[]{:S(2)}) collective-permute-start(bf16[128,256]{1,0:T(8,128)(2,1)S(1)} %collective-permute-done.refs_1_), channel_id=1, source_target_pairs={{0,4},{4,0},{8,12},{12,8},{16,20},{20,16},{24,28},{28,24},{1,5},{5... | collective-permute-start | bytes 196616 | tf_op jit(solution)/shard_map/ppermute | solution.py:39
  11.2 1.4 %collective-permute-start.5 = (bf16[128,256]{1,0:T(8,128)(2,1)S(1)}, bf16[128,256]{1,0:T(8,128)(2,1)S(1)}, u32[]{:S(2)}, u32[]{:S(2)}) collective-permute-start(bf16[128,256]{1,0:T(8,128)(2,1)S(1)} %collective-permute-done.1.refs_2_), channel_id=1, source_target_pairs={{0,4},{4,0},{8,12},{12,8},{16,20},{20,16},{24,28},{28,24},{1,5},{5... | collective-permute-start | bytes 196616 | tf_op jit(solution)/shard_map/ppermute | solution.py:39
  11.7 1.3 %collective-permute-start.6 = (bf16[128,256]{1,0:T(8,128)(2,1)S(1)}, bf16[128,256]{1,0:T(8,128)(2,1)S(1)}, u32[]{:S(2)}, u32[]{:S(2)}) collective-permute-start(bf16[128,256]{1,0:T(8,128)(2,1)S(1)} %collective-permute-done.2.refs_3_), channel_id=1, source_target_pairs={{0,4},{4,0},{8,12},{12,8},{16,20},{20,16},{24,28},{28,24},{1,5},{5... | collective-permute-start | bytes 196616 | tf_op jit(solution)/shard_map/ppermute | solution.py:39
  12.9 11.2 %copy-start = (bf16[256,256]{1,0:T(8,128)(2,1)S(1)}, bf16[256,256]{1,0:T(8,128)(2,1)}, u32[]{:S(2)}) copy-start(bf16[256,256]{1,0:T(8,128)(2,1)} %weight_ref.1) | copy-start | bytes 393220
  12.9 11.2 %copy-start.1 = (bf16[128,256]{1,0:T(8,128)(2,1)S(1)}, bf16[128,256]{1,0:T(8,128)(2,1)}, u32[]{:S(2)}) copy-start(bf16[128,256]{1,0:T(8,128)(2,1)} %cot_ref.1) | copy-start | bytes 196612
  16.1 6.6 %collective-permute-start.7 = (bf16[128,256]{1,0:T(8,128)(2,1)S(1)}, bf16[128,256]{1,0:T(8,128)(2,1)S(1)}, u32[]{:S(2)}, u32[]{:S(2)}) collective-permute-start(bf16[128,256]{1,0:T(8,128)(2,1)S(1)} %get-tuple-element.35), channel_id=1, source_target_pairs={{0,2},{1,3},{2,0},{3,1},{4,6},{5,7},{6,4},{7,5},{8,10},{9,11},{10,... | collective-permute-start | bytes 196616 | tf_op jit(solution)/shard_map/ppermute | solution.py:53
  17.5 6.4 %collective-permute-start.8 = (bf16[128,256]{1,0:T(8,128)(2,1)S(1)}, bf16[128,256]{1,0:T(8,128)(2,1)S(1)}, u32[]{:S(2)}, u32[]{:S(2)}) collective-permute-start(bf16[128,256]{1,0:T(8,128)(2,1)S(1)} %get-tuple-element.36), channel_id=1, source_target_pairs={{0,3},{1,2},{2,1},{3,0},{4,7},{5,6},{6,5},{7,4},{8,11},{9,10},{10,... | collective-permute-start | bytes 196616 | tf_op jit(solution)/shard_map/ppermute | solution.py:53
  17.9 6.2 %collective-permute-start.9 = (bf16[128,256]{1,0:T(8,128)(2,1)S(1)}, bf16[128,256]{1,0:T(8,128)(2,1)S(1)}, u32[]{:S(2)}, u32[]{:S(2)}) collective-permute-start(bf16[128,256]{1,0:T(8,128)(2,1)S(1)} %get-tuple-element.37), channel_id=1, source_target_pairs={{0,1},{1,0},{2,3},{3,2},{4,5},{5,4},{6,7},{7,6},{8,9},{9,8},{10,11... | collective-permute-start | bytes 196616 | tf_op jit(solution)/shard_map/ppermute | solution.py:53
  25.0 1.3 %collective-permute-start.10 = (bf16[144,256]{1,0:T(8,128)(2,1)S(1)}, bf16[144,256]{1,0:T(8,128)(2,1)S(1)}, u32[]{:S(2)}, u32[]{:S(2)}) collective-permute-start(bf16[144,256]{1,0:T(8,128)(2,1)S(1)} %get-tuple-element.42), channel_id=1, source_target_pairs={{0,4},{4,0},{8,12},{12,8},{16,20},{20,16},{24,28},{28,24},{1,5},{5... | collective-permute-start | bytes 221192 | tf_op jit(solution)/shard_map/ppermute | solution.py:39
  26.3 5.8 %collective-permute-start.11 = (bf16[272,256]{1,0:T(8,128)(2,1)S(1)}, bf16[272,256]{1,0:T(8,128)(2,1)S(1)}, u32[]{:S(2)}, u32[]{:S(2)}) collective-permute-start(bf16[272,256]{1,0:T(8,128)(2,1)S(1)} %shard_map.115.a_ref), channel_id=1, source_target_pairs={{0,1},{1,0},{2,3},{3,2},{4,5},{5,4},{6,7},{7,6},{8,9},{9,8},{10,11... | collective-permute-start | bytes 417800 | tf_op jit(solution)/shard_map/ppermute | solution.py:53
  27.0 9.0 %collective-permute-start.13 = (bf16[128,256]{1,0:T(8,128)(2,1)S(1)}, bf16[128,256]{1,0:T(8,128)(2,1)S(1)}, u32[]{:S(2)}, u32[]{:S(2)}) collective-permute-start(bf16[128,256]{1,0:T(8,128)(2,1)S(1)} %get-tuple-element.39.hidden_ref.refs_0_), channel_id=1, source_target_pairs={{0,3},{1,2},{2,1},{3,0},{4,7},{5,6},{6,5},{7,4},{8,11},{9,10},{10,... | collective-permute-start | bytes 196616 | tf_op jit(solution)/shard_map/ppermute | solution.py:53
  30.0 9.5 %collective-permute-start.12 = (bf16[128,256]{1,0:T(8,128)(2,1)S(1)}, bf16[128,256]{1,0:T(8,128)(2,1)S(1)}, u32[]{:S(2)}, u32[]{:S(2)}) collective-permute-start(bf16[128,256]{1,0:T(8,128)(2,1)S(1)} %get-tuple-element.39.hidden_ref.refs_0_), channel_id=1, source_target_pairs={{0,2},{1,3},{2,0},{3,1},{4,6},{5,7},{6,4},{7,5},{8,10},{9,11},{10,... | collective-permute-start | bytes 196616 | tf_op jit(solution)/shard_map/ppermute | solution.py:53
  32.2 11.2 %collective-permute-start.14 = (bf16[144,256]{1,0:T(8,128)(2,1)S(1)}, bf16[144,256]{1,0:T(8,128)(2,1)S(1)}, u32[]{:S(2)}, u32[]{:S(2)}) collective-permute-start(bf16[144,256]{1,0:T(8,128)(2,1)S(1)} %shard_map.117.a_ref), channel_id=1, source_target_pairs={{0,2},{1,3},{2,0},{3,1},{4,6},{5,7},{6,4},{7,5},{8,10},{9,11},{10,... | collective-permute-start | bytes 221192 | tf_op jit(solution)/shard_map/ppermute | solution.py:53
  43.4 1.6 %collective-permute-start.15 = (bf16[4,128,256]{2,1,0:T(8,128)(2,1)S(1)}, bf16[4,128,256]{2,1,0:T(8,128)(2,1)S(1)}, u32[]{:S(2)}, u32[]{:S(2)}) collective-permute-start(bf16[4,128,256]{2,1,0:T(8,128)(2,1)S(1)} %get-tuple-element.45), channel_id=1, source_target_pairs={{0,4},{4,0},{8,12},{12,8},{16,20},{20,16},{24,28},{28,24},{1,5},{5... | collective-permute-start | bytes 786440 | tf_op jit(solution)/shard_map/ppermute | solution.py:39
  45.0 6.6 %collective-permute-start.16 = (bf16[272,256]{1,0:T(8,128)(2,1)S(1)}, bf16[272,256]{1,0:T(8,128)(2,1)S(1)}, u32[]{:S(2)}, u32[]{:S(2)}) collective-permute-start(bf16[272,256]{1,0:T(8,128)(2,1)S(1)} %get-tuple-element.48), channel_id=1, source_target_pairs={{0,8},{4,12},{8,0},{12,4},{16,24},{20,28},{24,16},{28,20},{1,9},{5... | collective-permute-start | bytes 417800 | tf_op jit(solution)/shard_map/ppermute | solution.py:49
  45.1 8.8 %collective-permute-start.17 = (bf16[272,256]{1,0:T(8,128)(2,1)S(1)}, bf16[272,256]{1,0:T(8,128)(2,1)S(1)}, u32[]{:S(2)}, u32[]{:S(2)}) collective-permute-start(bf16[272,256]{1,0:T(8,128)(2,1)S(1)} %get-tuple-element.49), channel_id=1, source_target_pairs={{0,16},{4,20},{8,24},{12,28},{16,0},{20,4},{24,8},{28,12},{1,17},{... | collective-permute-start | bytes 417800 | tf_op jit(solution)/shard_map/ppermute | solution.py:49
  45.6 8.3 %collective-permute-start.18 = (bf16[272,256]{1,0:T(8,128)(2,1)S(1)}, bf16[272,256]{1,0:T(8,128)(2,1)S(1)}, u32[]{:S(2)}, u32[]{:S(2)}) collective-permute-start(bf16[272,256]{1,0:T(8,128)(2,1)S(1)} %get-tuple-element.50), channel_id=1, source_target_pairs={{0,24},{4,28},{8,16},{12,20},{16,8},{20,12},{24,0},{28,4},{1,25},{... | collective-permute-start | bytes 417800 | tf_op jit(solution)/shard_map/ppermute | solution.py:49
  54.5 1.3 %collective-permute-start.19 = (f32[128,256]{1,0:T(8,128)S(1)}, f32[128,256]{1,0:T(8,128)S(1)}, u32[]{:S(2)}, u32[]{:S(2)}) collective-permute-start(f32[128,256]{1,0:T(8,128)S(1)} %get-tuple-element.52.mine_ref), channel_id=1, source_target_pairs={{0,4},{4,0},{8,12},{12,8},{16,20},{20,16},{24,28},{28,24},{1,5},{5... | collective-permute-start | bytes 393224 | tf_op jit(solution)/shard_map/ppermute | solution.py:39

commit v4 on v3

--- a/solution.py
+++ b/solution.py
@@ -11,6 +11,7 @@
 CORES = 2
 EXTRA = 16
 LONG = 4_000_000_000
+GROUP = 4
 VMEM = pl.BlockSpec(memory_space=pltpu.VMEM)
 SMEM = pl.BlockSpec(memory_space=pltpu.SMEM)
 NT = (((1,), (1,)), ((), ()))
@@ -60,39 +61,37 @@
     return jnp.concatenate([tall] * (width // BLOCK), axis=1)
 
 
-def scale_kernel(features_hbm, degree_hbm, out_ref, features_ref, degree_ref, sems):
-    copies = [
-        pltpu.make_async_copy(degree_hbm, degree_ref, sems.at[0]),
-        pltpu.make_async_copy(features_hbm, features_ref, sems.at[1]),
-    ]
-    for copy in copies:
-        copy.start()
-    copies[0].wait()
+def scale_kernel(features_ref, degree_ref, out_ref, inv_ref):
     inv = spread_inv(degree_ref, features_ref.shape[1])
-    copies[1].wait()
+    inv_ref[...] = inv
     out_ref[...] = (features_ref[...].astype(F32) * inv).astype(BF16)
 
 
 def for_live(count_ref, slots, body):
     count = count_ref[0, 0]
+    group = GROUP if slots % GROUP == 0 else 1
 
     def step(i, carry):
-        body(i)
+        for j in range(group):
+            slot = i * group + j
+            body(slot, slot < count)
         return carry
 
-    lax.fori_loop(0, count, step, 0)
-
-
-def build_kernel(count_ref, edge_ref, blocks_ref):
+    lax.fori_loop(0, (count + group - 1) // group, step, 0)
+
+
+def build_kernel(count_ref, edge_ref, blocks_ref, turned_ref):
     slots, edges = edge_ref.shape[2], edge_ref.shape[3]
     node = lax.broadcasted_iota(jnp.int32, (BLOCK, edges), 0)
 
-    def build(s):
+    def build(s, live):
         edge = edge_ref[0, 0, pl.ds(s, 1), :]
         row_hot = jnp.where(node == edge // BLOCK, 1.0, 0.0).astype(BF16)
         col_hot = jnp.where(node == edge % BLOCK, 1.0, 0.0).astype(BF16)
         counts = lax.dot_general(row_hot, col_hot, NT, preferred_element_type=F32)
-        blocks_ref[s] = counts.astype(BF16)
+        block = jnp.where(live, counts, 0.0).astype(BF16)
+        blocks_ref[s] = block
+        turned_ref[s] = block.T
 
     for_live(count_ref, slots, build)
 
@@ -107,7 +106,7 @@
         gathered[n] = ref[...]
     acc[...] = jnp.zeros_like(acc)
 
-    def add(s):
+    def add(s, live):
         p = pos_ref[0, 0, s]
         u, v = p // rows, lax.rem(p, rows)
         k = offset_from(chips, row // CORES, v // CORES)
@@ -133,13 +132,13 @@
     return jnp.sum(packed.astype(F32), axis=0, keepdims=True)
 
 
-def pointwise_kernel(cols, weight_ref, bias_ref, cot_ref, degree_ref, *refs):
+def pointwise_kernel(cols, weight_ref, bias_ref, cot_ref, inv_ref, *refs):
     own_ref, *parts = refs[:cols]
     out_ref, hidden_ref, keep_ref, bias_keep_ref, send_ref = refs[cols:]
     width = out_ref.shape[1]
     half = width // CORES
     core = lax.rem(lax.axis_index("row"), CORES)
-    inv = spread_inv(degree_ref, width)
+    inv = inv_ref[...]
     total = own_ref[...]
     for ref in parts:
         total = total + ref[...].astype(F32)
@@ -179,7 +178,7 @@
     out_ref[:half], out_ref[half:] = add_grads(half, a, b)
 
 
-def backward_kernel(rows, cols, pos_ref, count_ref, blocks_ref, *refs):
+def backward_kernel(rows, cols, pos_ref, count_ref, turned_ref, *refs):
     hidden_parts = refs[:cols]
     keep_ref, send_ref, hidden, acc = refs[cols:]
     chips = rows // CORES
@@ -188,15 +187,15 @@
         hidden[n] = ref[:BLOCK]
     acc[...] = jnp.zeros_like(acc)
 
-    def add(s):
+    def add(s, live):
         p = pos_ref[0, 0, s]
         u, v = p // rows, lax.rem(p, rows)
         src = offset_from(cols, col, u)
         k = offset_to(chips, row // CORES, v // CORES)
         dst = (lax.rem(v, CORES) ^ lax.rem(row, CORES)) * chips + k
-        acc[dst] += lax.dot_general(blocks_ref[s], hidden[src], TN, preferred_element_type=F32)
-
-    for_live(count_ref, blocks_ref.shape[0], add)
+        acc[dst] += jnp.dot(turned_ref[s], hidden[src], preferred_element_type=F32)
+
+    for_live(count_ref, turned_ref.shape[0], add)
     keep_ref[...] = acc[:chips]
     send_ref[...] = acc[chips:].astype(BF16)
 
@@ -213,31 +212,31 @@
         ref[BLOCK + half :] = bias
 
 
-def finish_grads_kernel(norm, grads_ref, *refs):
-    *parts, half_ref, grad_b_ref = refs
+def sum_grads_kernel(grads_ref, *refs):
+    *parts, half_ref, bias_ref = refs
     half = half_ref.shape[0]
     grads = grads_ref[:half].astype(F32)
     bias = add_bias(grads_ref[half:])
     for ref in parts:
         grads = grads + ref[BLOCK : BLOCK + half].astype(F32)
         bias = bias + add_bias(ref[BLOCK + half :])
-    half_ref[...] = grads * norm
-    grad_b_ref[...] = bias * norm
-
-
-def finish_kernel(degree_ref, own_ref, *refs):
-    *parts, grad_x_ref = refs
+    half_ref[...] = grads
+    bias_ref[...] = bias
+
+
+def finish_kernel(norm, out_ref, inv_ref, own_ref, mine_ref, theirs_ref, bias_ref, *refs):
+    *parts, output_ref, grad_x_ref, grad_w_ref, grad_b_ref = refs
+    output_ref[...] = out_ref[...]
     total = own_ref[...]
     for ref in parts:
         total = total + ref[:BLOCK].astype(F32)
-    grad_x_ref[...] = (total * spread_inv(degree_ref, total.shape[1])).astype(BF16)
-
-
-def join_kernel(mine_ref, got_ref, out_ref):
+    grad_x_ref[...] = (total * inv_ref[...]).astype(BF16)
     half = mine_ref.shape[0]
     first = lax.rem(lax.axis_index("row"), CORES) == 0
-    out_ref[:half] = jnp.where(first, mine_ref[...], got_ref[...])
-    out_ref[half:] = jnp.where(first, got_ref[...], mine_ref[...])
+    mine, theirs = mine_ref[...] * norm, theirs_ref[...] * norm
+    grad_w_ref[:half] = jnp.where(first, mine, theirs)
+    grad_w_ref[half:] = jnp.where(first, theirs, mine)
+    grad_b_ref[...] = bias_ref[...] * norm
 
 
 def call(kernel, specs, outs, scratch=(), flops=1_000_000):
@@ -248,7 +247,7 @@
         out_shape=shapes[0] if single else tuple(shapes),
         in_specs=specs,
         out_specs=VMEM if single else tuple(VMEM for _ in shapes),
-        scratch_shapes=[pltpu.VMEM(*s) if isinstance(s, tuple) else s for s in scratch],
+        scratch_shapes=[pltpu.VMEM(*s) for s in scratch],
         compiler_params=pltpu.CompilerParams(vmem_limit_bytes=40 * 1024 * 1024),
         cost_estimate=pl.CostEstimate(flops=flops, bytes_accessed=1_000_000, transcendentals=0),
     )
@@ -265,16 +264,11 @@
     degree = degree.reshape(1, owned)
     bias_vector = bias_vector.reshape(1, width)
 
-    scaled = call(
-        scale_kernel,
-        [pl.BlockSpec(memory_space=pltpu.HBM)] * 2,
-        [(piece, BF16)],
-        [(piece, BF16), ((1, owned), jnp.int32), pltpu.SemaphoreType.DMA((2,))],
-    )(features, degree)
+    scaled, inv = call(scale_kernel, [VMEM, VMEM], [(piece, BF16), (piece, F32)])(features, degree)
     near = [scaled] + [to_chip(scaled, rows, k) for k in range(1, chips)]
-    blocks = call(build_kernel, [SMEM, VMEM], [((slots, BLOCK, BLOCK), BF16)], flops=LONG)(
-        block_count, edge_pos
-    )
+    blocks, turned = call(
+        build_kernel, [SMEM, VMEM], [((slots, BLOCK, BLOCK), BF16)] * 2, flops=LONG
+    )(block_count, edge_pos)
     blocks, *got = lax.optimization_barrier((blocks, *near[1:]))
     near = [scaled, *got]
     near = near + [to_core(x, rows) for x in near]
@@ -288,11 +282,11 @@
     order = list(range(2, cols)) + [1]
     parts = [to_col(send[k - 1], cols, k) for k in order]
 
-    output, hidden, keep, bias_keep, half_send = call(
+    out_piece, hidden, keep, bias_keep, half_send = call(
         functools.partial(pointwise_kernel, cols),
         [VMEM] * (4 + cols),
         [(piece, BF16), (piece, BF16), ((half, width), F32), ((1, width), F32), (grads_shape, BF16)],
-    )(weight, bias_vector, cotangent, degree, own, *parts)
+    )(weight, bias_vector, cotangent, inv, own, *parts)
 
     half_got = to_core(half_send, rows)
     far = [to_col(hidden, cols, k) for k in range(2, cols)]
@@ -314,7 +308,7 @@
         [((chips,) + piece, F32), ((chips,) + piece, BF16)],
         [((cols,) + piece, BF16), ((rows,) + piece, F32)],
         flops=LONG,
-    )(block_pos, block_count, blocks, hidden, next_to, *far)
+    )(block_pos, block_count, turned, hidden, next_to, *far)
     col_send, other = lax.optimization_barrier((col_send, other))
     own_x, grads, *send_x = call(
         merge_kernel,
@@ -324,15 +318,16 @@
     )(col_keep, to_core(col_send, rows), grads, other)
     parts_x = [to_chip(x, rows, k) for k, x in enumerate(send_x, 1)]
 
-    norm = float((owned * rows * cols) ** -0.5)
-    mine, grad_b = call(
-        functools.partial(finish_grads_kernel, norm),
-        [VMEM] * chips,
-        [((half, width), F32), ((1, width), F32)],
+    mine, bias_sum = call(
+        sum_grads_kernel, [VMEM] * chips, [((half, width), F32), ((1, width), F32)]
     )(grads, *parts_x)
     theirs = to_core(mine, rows)
-    grad_x = call(finish_kernel, [VMEM] * (1 + chips), [(piece, BF16)])(degree, own_x, *parts_x)
-    grad_w = call(join_kernel, [VMEM] * 2, [((width, width), F32)])(mine, theirs)
+    norm = float((owned * rows * cols) ** -0.5)
+    output, grad_x, grad_w, grad_b = call(
+        functools.partial(finish_kernel, norm),
+        [VMEM] * (5 + chips),
+        [(piece, BF16), (piece, BF16), ((width, width), F32), ((1, width), F32)],
+    )(out_piece, inv, own_x, mine, theirs, bias_sum, *parts_x)
     return (output, grad_x, grad_w, grad_b.reshape(width))
 
 

time: 56 us -> 53.6 us (0.957); the launches traced: 56.6 us -> 53.6 us
  Pallas kernels: 13.6 us -> 3.7 us
  waiting for transfers between devices: 21 us -> 25.7 us
  starting transfers between devices: 19 us -> 21.3 us
    pallas_call x5 -> x4, Pallas kernels: 5.5 us -> 1.34 us  [the longest x1 0.8 us: per_device(): call(functools.partial(finish_kernel, norm), [VMEM] * (5 + chips), [(piec...]
    ppermute x6, waiting for transfers between devices: 5.47 us -> 9.46 us  [to_chip(): return lax.ppermute(x, 'row', pairs)]
    pallas_call x1, Pallas kernels: 3.88 us -> 0.92 us  [per_device(): call(functools.partial(backward_kernel, rows, cols), [SMEM, SMEM, VMEM] +...]
    pallas_call x1, Pallas kernels: 3.18 us -> 0.88 us  [per_device(): call(functools.partial(forward_kernel, rows, cols), [SMEM, SMEM, VMEM, VM...]
    ppermute x7, starting transfers between devices: 10.2 us -> 12.3 us  [to_col(): lax.ppermute(x, 'col', [(i, target(cols, i, k)) for i in range(cols)])]
    ppermute x7, waiting for transfers between devices: 4.64 us -> 5.3 us  [to_core(): return lax.ppermute(x, 'row', [(i, i ^ 1) for i in range(rows)])]
  transfers between devices with their start and end apart: 20 -> 20, of which waited for: 15 -> 18; matrix products, arithmetic and copies ran while one was open for 0% -> 0% of each run, Pallas kernels for 14% -> 3%
where the time goes in v4:
time: 53.6 us
  waiting for transfers between devices  25.7 us (48%)
  starting transfers between devices  21.3 us (40%)
  Pallas kernels  3.7 us (7%)
  local copies, waits for them, and re-layouts  1.51 us (3%)
  between operations  1.4 us (3%)
    ppermute x7, starting transfers between devices, to_col(): lax.ppermute(x, 'col', [(i, target(cols, i, k)) for i in range(cols)])  12.3 us
    ppermute x7, waiting for transfers between devices, to_col(): lax.ppermute(x, 'col', [(i, target(cols, i, k)) for i in range(cols)])  10.9 us
    ppermute x6, waiting for transfers between devices, to_chip(): return lax.ppermute(x, 'row', pairs)  9.46 us
    ppermute x6, starting transfers between devices, to_chip(): return lax.ppermute(x, 'row', pairs)  7.72 us
    ppermute x7, waiting for transfers between devices, to_core(): return lax.ppermute(x, 'row', [(i, i ^ 1) for i in range(rows)])  5.3 us
    unnamed x14, local copies, waits for them, and re-layouts  1.51 us
    ppermute x7, starting transfers between devices, to_core(): return lax.ppermute(x, 'row', [(i, i ^ 1) for i in range(rows)])  1.3 us
  transfers between devices with their start and end apart: 20, of which 18 were waited for; matrix products, arithmetic and copies ran while one was open for 0% of the time, Pallas kernels for 3%

profile of v4, /device:TPU:0, one launch (start us, length us, event | category | flops | bytes accessed | tf_op | source)
XLA Modules:
  0.0 53.6 jit_solution(18373985718489254335)
XLA Ops:
  0.6 0.6 %copy-done.4 = s32[128]{0:T(128)S(1)} copy-done((s32[128]{0:T(128)S(1)}, s32[128]{0:T(128)}, u32[]{:S(2)}) %copy-start.4) | copy-done | bytes 536
  1.3 0.8 %copy-done.2 = bf16[128,256]{1,0:T(8,128)(2,1)S(1)} copy-done((bf16[128,256]{1,0:T(8,128)(2,1)S(1)}, bf16[128,256]{1,0:T(8,128)(2,1)}, u32[]{:S(2)}) %copy-start.2) | copy-done | bytes 65560
  2.1 0.1 shard_map.112
  2.2 0.5 collective-permute-start.3
  2.8 3.5 %collective-permute-start.2 = (bf16[128,256]{1,0:T(8,128)(2,1)S(1)}, bf16[128,256]{1,0:T(8,128)(2,1)S(1)}, u32[]{:S(2)}, u32[]{:S(2)}) collective-permute-start(bf16[128,256]{1,0:T(8,128)(2,1)S(1)} %get-tuple-element.38.refs_0_), channel_id=1, source_target_pairs={{0,24},{4,28},{8,16},{12,20},{16,8},{20,12},{24,0},{28,4},{1,25},{... | collective-permute-start | bytes 196616 | tf_op jit(solution)/shard_map/ppermute | solution.py:50
  6.3 0.5 collective-permute-start.1
  6.8 0.1 collective-permute-start
  7.6 0.4 shard_map.111
  8.0 1.0 %collective-permute-done.2.refs_3_ = bf16[128,256]{1,0:T(8,128)(2,1)S(1)} collective-permute-done((bf16[128,256]{1,0:T(8,128)(2,1)S(1)}, bf16[128,256]{1,0:T(8,128)(2,1)S(1)}, u32[]{:S(2)}, u32[]{:S(2)}) %collective-permute-start.2) | collective-permute-done | bytes 65568 | tf_op jit(solution)/shard_map/ppermute | solution.py:50
  9.0 1.6 %collective-permute-done.1.refs_2_ = bf16[128,256]{1,0:T(8,128)(2,1)S(1)} collective-permute-done((bf16[128,256]{1,0:T(8,128)(2,1)S(1)}, bf16[128,256]{1,0:T(8,128)(2,1)S(1)}, u32[]{:S(2)}, u32[]{:S(2)}) %collective-permute-start.1) | collective-permute-done | bytes 65568 | tf_op jit(solution)/shard_map/ppermute | solution.py:50
  10.5 0.5 collective-permute-done.refs_1_
  11.1 0.5 collective-permute-start.5
  11.6 0.1 collective-permute-start.6
  11.6 0.0 collective-permute-done.3.refs_4_
  11.6 0.7 %collective-permute-done.4.refs_5_ = bf16[128,256]{1,0:T(8,128)(2,1)S(1)} collective-permute-done((bf16[128,256]{1,0:T(8,128)(2,1)S(1)}, bf16[128,256]{1,0:T(8,128)(2,1)S(1)}, u32[]{:S(2)}, u32[]{:S(2)}) %collective-permute-start.4) | collective-permute-done | bytes 65568 | tf_op jit(solution)/shard_map/ppermute | solution.py:40
  12.3 0.2 collective-permute-done.5.refs_6_
  12.5 0.4 collective-permute-done.6.refs_7_
  12.8 0.9 %shard_map.113 = (f32[1,256]{1,0:T(1,128)S(1)}, f32[128,256]{1,0:T(8,128)S(1)}, bf16[128,256]{1,0:T(8,128)(2,1)S(1)}, bf16[128,256]{1,0:T(8,128)(2,1)S(1)}, bf16[128,256]{1,0:T(8,128)(2,1)S(1)}) custom-call(s32[1,1,16]{2,1,0:T(1,128)S(1)} %copy-done.5, s32[1,1]{1,0:T(1,128)S(6)} %copy.12.count_ref, f32[1,256]{1,0:T(1,128)S(1)} %bitcast.3, ...), custom_call_target="tpu_custom_call" | custom-call | flops 1000000 | bytes 1000000 | tf_op jit(solution)/shard_map/pallas_call | solution.py:276
  13.7 2.7 %collective-permute-start.7 = (bf16[128,256]{1,0:T(8,128)(2,1)S(1)}, bf16[128,256]{1,0:T(8,128)(2,1)S(1)}, u32[]{:S(2)}, u32[]{:S(2)}) collective-permute-start(bf16[128,256]{1,0:T(8,128)(2,1)S(1)} %get-tuple-element.46), channel_id=1, source_target_pairs={{0,2},{1,3},{2,0},{3,1},{4,6},{5,7},{6,4},{7,5},{8,10},{9,11},{10,... | collective-permute-start | bytes 196616 | tf_op jit(solution)/shard_map/ppermute | solution.py:54
  16.4 1.6 %collective-permute-start.8 = (bf16[128,256]{1,0:T(8,128)(2,1)S(1)}, bf16[128,256]{1,0:T(8,128)(2,1)S(1)}, u32[]{:S(2)}, u32[]{:S(2)}) collective-permute-start(bf16[128,256]{1,0:T(8,128)(2,1)S(1)} %get-tuple-element.47), channel_id=1, source_target_pairs={{0,3},{1,2},{2,1},{3,0},{4,7},{5,6},{6,5},{7,4},{8,11},{9,10},{10,... | collective-permute-start | bytes 196616 | tf_op jit(solution)/shard_map/ppermute | solution.py:54
  18.0 0.2 collective-permute-start.9
  18.2 2.4 %collective-permute-done.7.refs_1_ = bf16[128,256]{1,0:T(8,128)(2,1)S(1)} collective-permute-done((bf16[128,256]{1,0:T(8,128)(2,1)S(1)}, bf16[128,256]{1,0:T(8,128)(2,1)S(1)}, u32[]{:S(2)}, u32[]{:S(2)}) %collective-permute-start.7) | collective-permute-done | bytes 65568 | tf_op jit(solution)/shard_map/ppermute | solution.py:54
  20.6 2.4 %collective-permute-done.8.refs_2_ = bf16[128,256]{1,0:T(8,128)(2,1)S(1)} collective-permute-done((bf16[128,256]{1,0:T(8,128)(2,1)S(1)}, bf16[128,256]{1,0:T(8,128)(2,1)S(1)}, u32[]{:S(2)}, u32[]{:S(2)}) %collective-permute-start.8) | collective-permute-done | bytes 65568 | tf_op jit(solution)/shard_map/ppermute | solution.py:54
  23.0 0.2 collective-permute-done.9.refs_3_
  23.2 0.4 shard_map.114
  23.6 0.1 collective-permute-start.10
  23.7 1.3 %collective-permute-done.10.got_ref = bf16[144,256]{1,0:T(8,128)(2,1)S(1)} collective-permute-done((bf16[144,256]{1,0:T(8,128)(2,1)S(1)}, bf16[144,256]{1,0:T(8,128)(2,1)S(1)}, u32[]{:S(2)}, u32[]{:S(2)}) %collective-permute-start.10) | collective-permute-done | bytes 73760 | tf_op jit(solution)/shard_map/ppermute | solution.py:40
  25.0 0.9 %collective-permute-start.11 = (bf16[272,256]{1,0:T(8,128)(2,1)S(1)}, bf16[272,256]{1,0:T(8,128)(2,1)S(1)}, u32[]{:S(2)}, u32[]{:S(2)}) collective-permute-start(bf16[272,256]{1,0:T(8,128)(2,1)S(1)} %shard_map.115.a_ref), channel_id=1, source_target_pairs={{0,1},{1,0},{2,3},{3,2},{4,5},{5,4},{6,7},{7,6},{8,9},{9,8},{10,11... | collective-permute-start | bytes 417800 | tf_op jit(solution)/shard_map/ppermute | solution.py:54
  25.9 3.4 %collective-permute-start.13 = (bf16[128,256]{1,0:T(8,128)(2,1)S(1)}, bf16[128,256]{1,0:T(8,128)(2,1)S(1)}, u32[]{:S(2)}, u32[]{:S(2)}) collective-permute-start(bf16[128,256]{1,0:T(8,128)(2,1)S(1)} %get-tuple-element.51.hidden_ref.refs_0_), channel_id=1, source_target_pairs={{0,3},{1,2},{2,1},{3,0},{4,7},{5,6},{6,5},{7,4},{8,11},{9,10},{10,... | collective-permute-start | bytes 196616 | tf_op jit(solution)/shard_map/ppermute | solution.py:54
  29.2 0.0 collective-permute-start.12
  29.2 1.5 %collective-permute-done.11.refs_1_.b_ref = bf16[272,256]{1,0:T(8,128)(2,1)S(1)} collective-permute-done((bf16[272,256]{1,0:T(8,128)(2,1)S(1)}, bf16[272,256]{1,0:T(8,128)(2,1)S(1)}, u32[]{:S(2)}, u32[]{:S(2)}) %collective-permute-start.11) | collective-permute-done | bytes 139296 | tf_op jit(solution)/shard_map/ppermute | solution.py:54
  30.8 3.6 %collective-permute-start.14 = (bf16[144,256]{1,0:T(8,128)(2,1)S(1)}, bf16[144,256]{1,0:T(8,128)(2,1)S(1)}, u32[]{:S(2)}, u32[]{:S(2)}) collective-permute-start(bf16[144,256]{1,0:T(8,128)(2,1)S(1)} %shard_map.117.a_ref), channel_id=1, source_target_pairs={{0,2},{1,3},{2,0},{3,1},{4,6},{5,7},{6,4},{7,5},{8,10},{9,11},{10,... | collective-permute-start | bytes 221192 | tf_op jit(solution)/shard_map/ppermute | solution.py:54
  34.4 0.8 %collective-permute-done.13.refs_3_ = bf16[128,256]{1,0:T(8,128)(2,1)S(1)} collective-permute-done((bf16[128,256]{1,0:T(8,128)(2,1)S(1)}, bf16[128,256]{1,0:T(8,128)(2,1)S(1)}, u32[]{:S(2)}, u32[]{:S(2)}) %collective-permute-start.13) | collective-permute-done | bytes 65568 | tf_op jit(solution)/shard_map/ppermute | solution.py:54
  35.2 3.6 %collective-permute-done.12.refs_2_ = bf16[128,256]{1,0:T(8,128)(2,1)S(1)} collective-permute-done((bf16[128,256]{1,0:T(8,128)(2,1)S(1)}, bf16[128,256]{1,0:T(8,128)(2,1)S(1)}, u32[]{:S(2)}, u32[]{:S(2)}) %collective-permute-start.12) | collective-permute-done | bytes 65568 | tf_op jit(solution)/shard_map/ppermute | solution.py:54
  38.7 0.9 %shard_map.116 = (f32[4,128,256]{2,1,0:T(8,128)S(1)}, bf16[4,128,256]{2,1,0:T(8,128)(2,1)S(1)}) custom-call(s32[1,1,16]{2,1,0:T(1,128)S(1)} %copy-done.5, s32[1,1]{1,0:T(1,128)S(6)} %copy.12.count_ref, bf16[16,128,128]{2,1,0:T(8,128)(2,1)S(1)} %get-tuple-element.50.turned_ref, bf16[128,256]{1,0:T(8,128)(2,1)S(1)} %get-tuple-element.51.hidden_ref.refs_0_, ...), custom_call_target="tpu_custom_call" | custom-call | flops 4000000000 | bytes 1000000 | tf_op jit(solution)/shard_map/pallas_call | solution.py:305
  39.7 0.0 collective-permute-done.14.b_ref
  39.7 0.1 collective-permute-start.15
  39.8 1.5 %collective-permute-done.15.got_ref = bf16[4,128,256]{2,1,0:T(8,128)(2,1)S(1)} collective-permute-done((bf16[4,128,256]{2,1,0:T(8,128)(2,1)S(1)}, bf16[4,128,256]{2,1,0:T(8,128)(2,1)S(1)}, u32[]{:S(2)}, u32[]{:S(2)}) %collective-permute-start.15) | collective-permute-done | bytes 262176 | tf_op jit(solution)/shard_map/ppermute | solution.py:40
  41.3 0.1 shard_map.118
  41.4 1.4 %collective-permute-start.16 = (bf16[272,256]{1,0:T(8,128)(2,1)S(1)}, bf16[272,256]{1,0:T(8,128)(2,1)S(1)}, u32[]{:S(2)}, u32[]{:S(2)}) collective-permute-start(bf16[272,256]{1,0:T(8,128)(2,1)S(1)} %get-tuple-element.61), channel_id=1, source_target_pairs={{0,8},{4,12},{8,0},{12,4},{16,24},{20,28},{24,16},{28,20},{1,9},{5... | collective-permute-start | bytes 417800 | tf_op jit(solution)/shard_map/ppermute | solution.py:50
  42.7 0.8 %collective-permute-start.17 = (bf16[272,256]{1,0:T(8,128)(2,1)S(1)}, bf16[272,256]{1,0:T(8,128)(2,1)S(1)}, u32[]{:S(2)}, u32[]{:S(2)}) collective-permute-start(bf16[272,256]{1,0:T(8,128)(2,1)S(1)} %get-tuple-element.62), channel_id=1, source_target_pairs={{0,16},{4,20},{8,24},{12,28},{16,0},{20,4},{24,8},{28,12},{1,17},{... | collective-permute-start | bytes 417800 | tf_op jit(solution)/shard_map/ppermute | solution.py:50
  43.6 1.3 %collective-permute-start.18 = (bf16[272,256]{1,0:T(8,128)(2,1)S(1)}, bf16[272,256]{1,0:T(8,128)(2,1)S(1)}, u32[]{:S(2)}, u32[]{:S(2)}) collective-permute-start(bf16[272,256]{1,0:T(8,128)(2,1)S(1)} %get-tuple-element.63), channel_id=1, source_target_pairs={{0,24},{4,28},{8,16},{12,20},{16,8},{20,12},{24,0},{28,4},{1,25},{... | collective-permute-start | bytes 417800 | tf_op jit(solution)/shard_map/ppermute | solution.py:50
  44.9 2.9 %collective-permute-done.16.refs_0_ = bf16[272,256]{1,0:T(8,128)(2,1)S(1)} collective-permute-done((bf16[272,256]{1,0:T(8,128)(2,1)S(1)}, bf16[272,256]{1,0:T(8,128)(2,1)S(1)}, u32[]{:S(2)}, u32[]{:S(2)}) %collective-permute-start.16) | collective-permute-done | bytes 139296 | tf_op jit(solution)/shard_map/ppermute | solution.py:50
  47.9 1.7 %collective-permute-done.17.refs_1_ = bf16[272,256]{1,0:T(8,128)(2,1)S(1)} collective-permute-done((bf16[272,256]{1,0:T(8,128)(2,1)S(1)}, bf16[272,256]{1,0:T(8,128)(2,1)S(1)}, u32[]{:S(2)}, u32[]{:S(2)}) %collective-permute-start.17) | collective-permute-done | bytes 139296 | tf_op jit(solution)/shard_map/ppermute | solution.py:50
  49.6 1.8 %collective-permute-done.18.refs_2_ = bf16[272,256]{1,0:T(8,128)(2,1)S(1)} collective-permute-done((bf16[272,256]{1,0:T(8,128)(2,1)S(1)}, bf16[272,256]{1,0:T(8,128)(2,1)S(1)}, u32[]{:S(2)}, u32[]{:S(2)}) %collective-permute-start.18) | collective-permute-done | bytes 139296 | tf_op jit(solution)/shard_map/ppermute | solution.py:50
  51.4 0.1 collective-permute-start.19
  51.4 1.3 %collective-permute-done.19.theirs_ref = f32[128,256]{1,0:T(8,128)S(1)} collective-permute-done((f32[128,256]{1,0:T(8,128)S(1)}, f32[128,256]{1,0:T(8,128)S(1)}, u32[]{:S(2)}, u32[]{:S(2)}) %collective-permute-start.19) | collective-permute-done | bytes 131104 | tf_op jit(solution)/shard_map/ppermute | solution.py:40
  52.8 0.8 %shard_map.120 = (bf16[128,256]{1,0:T(8,128)(2,1)}, bf16[128,256]{1,0:T(8,128)(2,1)}, f32[256,256]{1,0:T(8,128)}, f32[1,256]{1,0:T(1,128)}) custom-call(bf16[128,256]{1,0:T(8,128)(2,1)S(1)} %get-tuple-element.49.out_ref, f32[128,256]{1,0:T(8,128)S(1)} %get-tuple-element.44.inv_ref, f32[128,256]{1,0:T(8,128)S(1)} %get-tuple-element.59.own_ref, ...), custom_call_target="tpu_custom_call" | custom-call | flops 1000000 | bytes 1000000 | tf_op jit(solution)/shard_map/pallas_call | solution.py:326
  (16 shorter events, 0.2 us)
Async XLA Ops:
  0.6 0.7 %copy-start.4 = (s32[128]{0:T(128)S(1)}, s32[128]{0:T(128)}, u32[]{:S(2)}) copy-start(s32[128]{0:T(128)} %param.9) | copy-start | bytes 1540
  1.3 0.8 %copy-start.2 = (bf16[128,256]{1,0:T(8,128)(2,1)S(1)}, bf16[128,256]{1,0:T(8,128)(2,1)}, u32[]{:S(2)}) copy-start(bf16[128,256]{1,0:T(8,128)(2,1)} %features_ref.1) | copy-start | bytes 196612
  2.1 5.5 %copy-start.6 = (s32[1,1,16,512]{3,2,1,0:T(8,128)S(1)}, s32[1,1,16,512]{3,2,1,0:T(8,128)}, u32[]{:S(2)}) copy-start(s32[1,1,16,512]{3,2,1,0:T(8,128)} %edge_ref.1) | copy-start | bytes 98308
  2.2 9.4 %collective-permute-start.3 = (bf16[128,256]{1,0:T(8,128)(2,1)S(1)}, bf16[128,256]{1,0:T(8,128)(2,1)S(1)}, u32[]{:S(2)}, u32[]{:S(2)}) collective-permute-start(bf16[128,256]{1,0:T(8,128)(2,1)S(1)} %get-tuple-element.38.refs_0_), channel_id=1, source_target_pairs={{0,4},{4,0},{8,12},{12,8},{16,20},{20,16},{24,28},{28,24},{1,5},{5... | collective-permute-start | bytes 196616 | tf_op jit(solution)/shard_map/ppermute | solution.py:40
  2.8 6.2 %collective-permute-start.2 = (bf16[128,256]{1,0:T(8,128)(2,1)S(1)}, bf16[128,256]{1,0:T(8,128)(2,1)S(1)}, u32[]{:S(2)}, u32[]{:S(2)}) collective-permute-start(bf16[128,256]{1,0:T(8,128)(2,1)S(1)} %get-tuple-element.38.refs_0_), channel_id=1, source_target_pairs={{0,24},{4,28},{8,16},{12,20},{16,8},{20,12},{24,0},{28,4},{1,25},{... | collective-permute-start | bytes 196616 | tf_op jit(solution)/shard_map/ppermute | solution.py:50
  6.3 4.3 %collective-permute-start.1 = (bf16[128,256]{1,0:T(8,128)(2,1)S(1)}, bf16[128,256]{1,0:T(8,128)(2,1)S(1)}, u32[]{:S(2)}, u32[]{:S(2)}) collective-permute-start(bf16[128,256]{1,0:T(8,128)(2,1)S(1)} %get-tuple-element.38.refs_0_), channel_id=1, source_target_pairs={{0,16},{4,20},{8,24},{12,28},{16,0},{20,4},{24,8},{28,12},{1,17},{... | collective-permute-start | bytes 196616 | tf_op jit(solution)/shard_map/ppermute | solution.py:50
  6.8 4.3 %collective-permute-start = (bf16[128,256]{1,0:T(8,128)(2,1)S(1)}, bf16[128,256]{1,0:T(8,128)(2,1)S(1)}, u32[]{:S(2)}, u32[]{:S(2)}) collective-permute-start(bf16[128,256]{1,0:T(8,128)(2,1)S(1)} %get-tuple-element.38.refs_0_), channel_id=1, source_target_pairs={{0,8},{4,12},{8,0},{12,4},{16,24},{20,28},{24,16},{28,20},{1,9},{5... | collective-permute-start | bytes 196616 | tf_op jit(solution)/shard_map/ppermute | solution.py:50
  11.1 1.8 %copy-start.3 = (f32[256]{0:T(256)S(1)}, f32[256]{0:T(256)}, u32[]{:S(2)}) copy-start(f32[256]{0:T(256)} %param.11) | copy-start | bytes 3076
  11.1 1.8 %copy-start.5 = (s32[1,1,16]{2,1,0:T(1,128)S(1)}, s32[1,1,16]{2,1,0:T(1,128)}, u32[]{:S(2)}) copy-start(s32[1,1,16]{2,1,0:T(1,128)} %pos_ref.3) | copy-start | bytes 196
  11.1 1.3 %collective-permute-start.4 = (bf16[128,256]{1,0:T(8,128)(2,1)S(1)}, bf16[128,256]{1,0:T(8,128)(2,1)S(1)}, u32[]{:S(2)}, u32[]{:S(2)}) collective-permute-start(bf16[128,256]{1,0:T(8,128)(2,1)S(1)} %collective-permute-done.refs_1_), channel_id=1, source_target_pairs={{0,4},{4,0},{8,12},{12,8},{16,20},{20,16},{24,28},{28,24},{1,5},{5... | collective-permute-start | bytes 196616 | tf_op jit(solution)/shard_map/ppermute | solution.py:40
  11.1 1.4 %collective-permute-start.5 = (bf16[128,256]{1,0:T(8,128)(2,1)S(1)}, bf16[128,256]{1,0:T(8,128)(2,1)S(1)}, u32[]{:S(2)}, u32[]{:S(2)}) collective-permute-start(bf16[128,256]{1,0:T(8,128)(2,1)S(1)} %collective-permute-done.1.refs_2_), channel_id=1, source_target_pairs={{0,4},{4,0},{8,12},{12,8},{16,20},{20,16},{24,28},{28,24},{1,5},{5... | collective-permute-start | bytes 196616 | tf_op jit(solution)/shard_map/ppermute | solution.py:40
  11.6 1.3 %collective-permute-start.6 = (bf16[128,256]{1,0:T(8,128)(2,1)S(1)}, bf16[128,256]{1,0:T(8,128)(2,1)S(1)}, u32[]{:S(2)}, u32[]{:S(2)}) collective-permute-start(bf16[128,256]{1,0:T(8,128)(2,1)S(1)} %collective-permute-done.2.refs_3_), channel_id=1, source_target_pairs={{0,4},{4,0},{8,12},{12,8},{16,20},{20,16},{24,28},{28,24},{1,5},{5... | collective-permute-start | bytes 196616 | tf_op jit(solution)/shard_map/ppermute | solution.py:40
  12.8 10.4 %copy-start = (bf16[256,256]{1,0:T(8,128)(2,1)S(1)}, bf16[256,256]{1,0:T(8,128)(2,1)}, u32[]{:S(2)}) copy-start(bf16[256,256]{1,0:T(8,128)(2,1)} %weight_ref.1) | copy-start | bytes 393220
  12.8 10.4 %copy-start.1 = (bf16[128,256]{1,0:T(8,128)(2,1)S(1)}, bf16[128,256]{1,0:T(8,128)(2,1)}, u32[]{:S(2)}) copy-start(bf16[128,256]{1,0:T(8,128)(2,1)} %cot_ref.1) | copy-start | bytes 196612
  13.7 6.9 %collective-permute-start.7 = (bf16[128,256]{1,0:T(8,128)(2,1)S(1)}, bf16[128,256]{1,0:T(8,128)(2,1)S(1)}, u32[]{:S(2)}, u32[]{:S(2)}) collective-permute-start(bf16[128,256]{1,0:T(8,128)(2,1)S(1)} %get-tuple-element.46), channel_id=1, source_target_pairs={{0,2},{1,3},{2,0},{3,1},{4,6},{5,7},{6,4},{7,5},{8,10},{9,11},{10,... | collective-permute-start | bytes 196616 | tf_op jit(solution)/shard_map/ppermute | solution.py:54
  16.4 6.6 %collective-permute-start.8 = (bf16[128,256]{1,0:T(8,128)(2,1)S(1)}, bf16[128,256]{1,0:T(8,128)(2,1)S(1)}, u32[]{:S(2)}, u32[]{:S(2)}) collective-permute-start(bf16[128,256]{1,0:T(8,128)(2,1)S(1)} %get-tuple-element.47), channel_id=1, source_target_pairs={{0,3},{1,2},{2,1},{3,0},{4,7},{5,6},{6,5},{7,4},{8,11},{9,10},{10,... | collective-permute-start | bytes 196616 | tf_op jit(solution)/shard_map/ppermute | solution.py:54
  18.0 5.2 %collective-permute-start.9 = (bf16[128,256]{1,0:T(8,128)(2,1)S(1)}, bf16[128,256]{1,0:T(8,128)(2,1)S(1)}, u32[]{:S(2)}, u32[]{:S(2)}) collective-permute-start(bf16[128,256]{1,0:T(8,128)(2,1)S(1)} %get-tuple-element.48), channel_id=1, source_target_pairs={{0,1},{1,0},{2,3},{3,2},{4,5},{5,4},{6,7},{7,6},{8,9},{9,8},{10,11... | collective-permute-start | bytes 196616 | tf_op jit(solution)/shard_map/ppermute | solution.py:54
  23.6 1.3 %collective-permute-start.10 = (bf16[144,256]{1,0:T(8,128)(2,1)S(1)}, bf16[144,256]{1,0:T(8,128)(2,1)S(1)}, u32[]{:S(2)}, u32[]{:S(2)}) collective-permute-start(bf16[144,256]{1,0:T(8,128)(2,1)S(1)} %get-tuple-element.54), channel_id=1, source_target_pairs={{0,4},{4,0},{8,12},{12,8},{16,20},{20,16},{24,28},{28,24},{1,5},{5... | collective-permute-start | bytes 221192 | tf_op jit(solution)/shard_map/ppermute | solution.py:40
  25.0 5.8 %collective-permute-start.11 = (bf16[272,256]{1,0:T(8,128)(2,1)S(1)}, bf16[272,256]{1,0:T(8,128)(2,1)S(1)}, u32[]{:S(2)}, u32[]{:S(2)}) collective-permute-start(bf16[272,256]{1,0:T(8,128)(2,1)S(1)} %shard_map.115.a_ref), channel_id=1, source_target_pairs={{0,1},{1,0},{2,3},{3,2},{4,5},{5,4},{6,7},{7,6},{8,9},{9,8},{10,11... | collective-permute-start | bytes 417800 | tf_op jit(solution)/shard_map/ppermute | solution.py:54
  25.9 9.3 %collective-permute-start.13 = (bf16[128,256]{1,0:T(8,128)(2,1)S(1)}, bf16[128,256]{1,0:T(8,128)(2,1)S(1)}, u32[]{:S(2)}, u32[]{:S(2)}) collective-permute-start(bf16[128,256]{1,0:T(8,128)(2,1)S(1)} %get-tuple-element.51.hidden_ref.refs_0_), channel_id=1, source_target_pairs={{0,3},{1,2},{2,1},{3,0},{4,7},{5,6},{6,5},{7,4},{8,11},{9,10},{10,... | collective-permute-start | bytes 196616 | tf_op jit(solution)/shard_map/ppermute | solution.py:54
  29.2 9.5 %collective-permute-start.12 = (bf16[128,256]{1,0:T(8,128)(2,1)S(1)}, bf16[128,256]{1,0:T(8,128)(2,1)S(1)}, u32[]{:S(2)}, u32[]{:S(2)}) collective-permute-start(bf16[128,256]{1,0:T(8,128)(2,1)S(1)} %get-tuple-element.51.hidden_ref.refs_0_), channel_id=1, source_target_pairs={{0,2},{1,3},{2,0},{3,1},{4,6},{5,7},{6,4},{7,5},{8,10},{9,11},{10,... | collective-permute-start | bytes 196616 | tf_op jit(solution)/shard_map/ppermute | solution.py:54
  30.8 8.9 %collective-permute-start.14 = (bf16[144,256]{1,0:T(8,128)(2,1)S(1)}, bf16[144,256]{1,0:T(8,128)(2,1)S(1)}, u32[]{:S(2)}, u32[]{:S(2)}) collective-permute-start(bf16[144,256]{1,0:T(8,128)(2,1)S(1)} %shard_map.117.a_ref), channel_id=1, source_target_pairs={{0,2},{1,3},{2,0},{3,1},{4,6},{5,7},{6,4},{7,5},{8,10},{9,11},{10,... | collective-permute-start | bytes 221192 | tf_op jit(solution)/shard_map/ppermute | solution.py:54
  39.7 1.6 %collective-permute-start.15 = (bf16[4,128,256]{2,1,0:T(8,128)(2,1)S(1)}, bf16[4,128,256]{2,1,0:T(8,128)(2,1)S(1)}, u32[]{:S(2)}, u32[]{:S(2)}) collective-permute-start(bf16[4,128,256]{2,1,0:T(8,128)(2,1)S(1)} %get-tuple-element.57), channel_id=1, source_target_pairs={{0,4},{4,0},{8,12},{12,8},{16,20},{20,16},{24,28},{28,24},{1,5},{5... | collective-permute-start | bytes 786440 | tf_op jit(solution)/shard_map/ppermute | solution.py:40
  41.4 6.5 %collective-permute-start.16 = (bf16[272,256]{1,0:T(8,128)(2,1)S(1)}, bf16[272,256]{1,0:T(8,128)(2,1)S(1)}, u32[]{:S(2)}, u32[]{:S(2)}) collective-permute-start(bf16[272,256]{1,0:T(8,128)(2,1)S(1)} %get-tuple-element.61), channel_id=1, source_target_pairs={{0,8},{4,12},{8,0},{12,4},{16,24},{20,28},{24,16},{28,20},{1,9},{5... | collective-permute-start | bytes 417800 | tf_op jit(solution)/shard_map/ppermute | solution.py:50
  42.7 6.8 %collective-permute-start.17 = (bf16[272,256]{1,0:T(8,128)(2,1)S(1)}, bf16[272,256]{1,0:T(8,128)(2,1)S(1)}, u32[]{:S(2)}, u32[]{:S(2)}) collective-permute-start(bf16[272,256]{1,0:T(8,128)(2,1)S(1)} %get-tuple-element.62), channel_id=1, source_target_pairs={{0,16},{4,20},{8,24},{12,28},{16,0},{20,4},{24,8},{28,12},{1,17},{... | collective-permute-start | bytes 417800 | tf_op jit(solution)/shard_map/ppermute | solution.py:50
  43.6 7.7 %collective-permute-start.18 = (bf16[272,256]{1,0:T(8,128)(2,1)S(1)}, bf16[272,256]{1,0:T(8,128)(2,1)S(1)}, u32[]{:S(2)}, u32[]{:S(2)}) collective-permute-start(bf16[272,256]{1,0:T(8,128)(2,1)S(1)} %get-tuple-element.63), channel_id=1, source_target_pairs={{0,24},{4,28},{8,16},{12,20},{16,8},{20,12},{24,0},{28,4},{1,25},{... | collective-permute-start | bytes 417800 | tf_op jit(solution)/shard_map/ppermute | solution.py:50
  51.4 1.4 %collective-permute-start.19 = (f32[128,256]{1,0:T(8,128)S(1)}, f32[128,256]{1,0:T(8,128)S(1)}, u32[]{:S(2)}, u32[]{:S(2)}) collective-permute-start(f32[128,256]{1,0:T(8,128)S(1)} %get-tuple-element.64.mine_ref), channel_id=1, source_target_pairs={{0,4},{4,0},{8,12},{12,8},{16,20},{20,16},{24,28},{28,24},{1,5},{5... | collective-permute-start | bytes 393224 | tf_op jit(solution)/shard_map/ppermute | solution.py:40

commit v5 on v4

--- a/solution.py
+++ b/solution.py
@@ -178,13 +178,20 @@
     out_ref[:half], out_ref[half:] = add_grads(half, a, b)
 
 
-def backward_kernel(rows, cols, pos_ref, count_ref, turned_ref, *refs):
-    hidden_parts = refs[:cols]
-    keep_ref, send_ref, hidden, acc = refs[cols:]
+def collect_kernel(*refs):
+    *parts, out_ref = refs
+    for n, ref in enumerate(parts):
+        out_ref[n] = ref[...]
+
+
+def backward_kernel(
+    rows, cols, pos_ref, count_ref, turned_ref, own_ref, next_ref, far_ref, keep_ref, send_ref, hidden, acc
+):
     chips = rows // CORES
     row, col = lax.axis_index("row"), lax.axis_index("col")
-    for n, ref in enumerate(hidden_parts):
-        hidden[n] = ref[:BLOCK]
+    hidden[0] = own_ref[...]
+    hidden[1] = next_ref[:BLOCK]
+    hidden[2:] = far_ref[...]
     acc[...] = jnp.zeros_like(acc)
 
     def add(s, live):
@@ -200,16 +207,11 @@
     send_ref[...] = acc[chips:].astype(BF16)
 
 
-def merge_kernel(keep_ref, got_ref, a_ref, b_ref, own_ref, grads_ref, *send):
+def merge_kernel(keep_ref, got_ref, grads_ref, own_ref, *send):
     own_ref[...] = keep_ref[0] + got_ref[0].astype(F32)
-    half = grads_ref.shape[0] - EXTRA
-    total, bias = add_grads(half, a_ref[...], b_ref[...])
-    grads_ref[:half] = total
-    grads_ref[half:] = bias
     for k, ref in enumerate(send, 1):
         ref[:BLOCK] = (keep_ref[k] + got_ref[k].astype(F32)).astype(BF16)
-        ref[BLOCK : BLOCK + half] = total
-        ref[BLOCK + half :] = bias
+        ref[BLOCK:] = grads_ref[...]
 
 
 def sum_grads_kernel(grads_ref, *refs):
@@ -294,8 +296,10 @@
         pair_sum_kernel, [VMEM] * 4, [((owned + half + EXTRA, width), BF16)], flops=LONG
     )(keep, bias_keep, half_got, hidden)
     next_to = to_col(message, cols, 1)
-    grads, other = message, next_to
-    add = call(functools.partial(add_kernel, half), [VMEM] * 2, [(grads_shape, BF16)])
+    far = call(collect_kernel, [VMEM] * len(far), [((cols - 2,) + piece, BF16)], flops=LONG)(*far)
+    far, other = lax.optimization_barrier((far, next_to))
+    next_to, grads = other, message
+    add = call(functools.partial(add_kernel, half), [VMEM] * 2, [(grads_shape, BF16)], flops=LONG)
     step = 2
     while step < cols:
         grads = add(grads, other)
@@ -304,19 +308,18 @@
 
     col_keep, col_send = call(
         functools.partial(backward_kernel, rows, cols),
-        [SMEM, SMEM, VMEM] + [VMEM] * cols,
+        [SMEM, SMEM] + [VMEM] * 4,
         [((chips,) + piece, F32), ((chips,) + piece, BF16)],
         [((cols,) + piece, BF16), ((rows,) + piece, F32)],
         flops=LONG,
-    )(block_pos, block_count, turned, hidden, next_to, *far)
-    col_send, other = lax.optimization_barrier((col_send, other))
-    own_x, grads, *send_x = call(
+    )(block_pos, block_count, turned, hidden, next_to, far)
+    grads = add(grads, other)
+    own_x, *send_x = call(
         merge_kernel,
-        [VMEM] * 4,
-        [(piece, F32), (grads_shape, BF16)]
-        + [((owned + half + EXTRA, width), BF16)] * (chips - 1),
-    )(col_keep, to_core(col_send, rows), grads, other)
-    parts_x = [to_chip(x, rows, k) for k, x in enumerate(send_x, 1)]
+        [VMEM] * 3,
+        [(piece, F32)] + [((owned + half + EXTRA, width), BF16)] * (chips - 1),
+    )(col_keep, to_core(col_send, rows), grads)
+    parts_x = [to_chip(send_x[k - 1], rows, k) for k in range(chips - 1, 0, -1)]
 
     mine, bias_sum = call(
         sum_grads_kernel, [VMEM] * chips, [((half, width), F32), ((1, width), F32)]

time: 53.6 us -> 52.6 us (0.981)
  starting transfers between devices: 21.3 us -> 18.4 us
  waiting for transfers between devices: 25.7 us -> 27 us
  Pallas kernels: 3.7 us -> 4.57 us
    ppermute x7, waiting for transfers between devices: 10.9 us -> 16.1 us  [to_col(): lax.ppermute(x, 'col', [(i, target(cols, i, k)) for i in range(cols)])]
    ppermute x7, starting transfers between devices: 12.3 us -> 9.34 us  [to_col(): lax.ppermute(x, 'col', [(i, target(cols, i, k)) for i in range(cols)])]
    ppermute x7, waiting for transfers between devices: 5.3 us -> 2.53 us  [to_core(): return lax.ppermute(x, 'row', [(i, i ^ 1) for i in range(rows)])]
    ppermute x6, waiting for transfers between devices: 9.46 us -> 8.31 us  [to_chip(): return lax.ppermute(x, 'row', pairs)]
    pallas_call x2 -> x3, Pallas kernels: 1.01 us -> 1.23 us  [the longest x1 1.16 us: per_device(): call(functools.partial(backward_kernel, rows, cols), [SMEM, SMEM] + [VMEM...]
  transfers between devices with their start and end apart: 20 -> 20, of which waited for: 18 -> 17; matrix products, arithmetic and copies ran while one was open for 0% -> 0% of each run, Pallas kernels for 3% -> 4%
where the time goes in v5:
time: 52.6 us; the launch traced here: 52.8 us
  waiting for transfers between devices  27 us (51%)
  starting transfers between devices  18.4 us (35%)
  Pallas kernels  4.57 us (9%)
  local copies, waits for them, and re-layouts  1.51 us (3%)
  between operations  1.41 us (3%)
    ppermute x7, waiting for transfers between devices, to_col(): lax.ppermute(x, 'col', [(i, target(cols, i, k)) for i in range(cols)])  16.1 us
    ppermute x7, starting transfers between devices, to_col(): lax.ppermute(x, 'col', [(i, target(cols, i, k)) for i in range(cols)])  9.34 us
    ppermute x6, waiting for transfers between devices, to_chip(): return lax.ppermute(x, 'row', pairs)  8.31 us
    ppermute x6, starting transfers between devices, to_chip(): return lax.ppermute(x, 'row', pairs)  7.72 us
    ppermute x7, waiting for transfers between devices, to_core(): return lax.ppermute(x, 'row', [(i, i ^ 1) for i in range(rows)])  2.53 us
    unnamed x14, local copies, waits for them, and re-layouts  1.51 us
    ppermute x7, starting transfers between devices, to_core(): return lax.ppermute(x, 'row', [(i, i ^ 1) for i in range(rows)])  1.3 us
    pallas_call x1, Pallas kernels, per_device(): call(functools.partial(backward_kernel, rows, cols), [SMEM, SMEM] + [VMEM...  1.16 us
  transfers between devices with their start and end apart: 20, of which 17 were waited for; matrix products, arithmetic and copies ran while one was open for 0% of the time, Pallas kernels for 4%

profile of v5, /device:TPU:0, one launch (start us, length us, event | category | flops | bytes accessed | tf_op | source)
XLA Modules:
  0.0 52.8 jit_solution(6548635541852628974)
XLA Ops:
  0.6 0.6 %copy-done.4 = s32[128]{0:T(128)S(1)} copy-done((s32[128]{0:T(128)S(1)}, s32[128]{0:T(128)}, u32[]{:S(2)}) %copy-start.4) | copy-done | bytes 536
  1.3 0.8 %copy-done.2 = bf16[128,256]{1,0:T(8,128)(2,1)S(1)} copy-done((bf16[128,256]{1,0:T(8,128)(2,1)S(1)}, bf16[128,256]{1,0:T(8,128)(2,1)}, u32[]{:S(2)}) %copy-start.2) | copy-done | bytes 65560
  2.1 0.1 shard_map.112
  2.2 0.5 collective-permute-start.3
  2.8 3.5 %collective-permute-start.2 = (bf16[128,256]{1,0:T(8,128)(2,1)S(1)}, bf16[128,256]{1,0:T(8,128)(2,1)S(1)}, u32[]{:S(2)}, u32[]{:S(2)}) collective-permute-start(bf16[128,256]{1,0:T(8,128)(2,1)S(1)} %get-tuple-element.37.refs_0_), channel_id=1, source_target_pairs={{0,24},{4,28},{8,16},{12,20},{16,8},{20,12},{24,0},{28,4},{1,25},{... | collective-permute-start | bytes 196616 | tf_op jit(solution)/shard_map/ppermute | solution.py:50
  6.3 0.5 collective-permute-start.1
  6.8 0.1 collective-permute-start
  7.6 0.8 %shard_map.111 = (bf16[16,128,128]{2,1,0:T(8,128)(2,1)S(1)}, bf16[16,128,128]{2,1,0:T(8,128)(2,1)S(1)}) custom-call(s32[1,1]{1,0:T(1,128)S(6)} %copy.12.count_ref, s32[1,1,16,512]{3,2,1,0:T(8,128)S(1)} %copy-done.6), custom_call_target="tpu_custom_call" | custom-call | flops 4000000000 | bytes 1000000 | tf_op jit(solution)/shard_map/pallas_call | solution.py:271
  8.4 0.6 %collective-permute-done.2.refs_3_ = bf16[128,256]{1,0:T(8,128)(2,1)S(1)} collective-permute-done((bf16[128,256]{1,0:T(8,128)(2,1)S(1)}, bf16[128,256]{1,0:T(8,128)(2,1)S(1)}, u32[]{:S(2)}, u32[]{:S(2)}) %collective-permute-start.2) | collective-permute-done | bytes 65568 | tf_op jit(solution)/shard_map/ppermute | solution.py:50
  9.0 1.6 %collective-permute-done.1.refs_2_ = bf16[128,256]{1,0:T(8,128)(2,1)S(1)} collective-permute-done((bf16[128,256]{1,0:T(8,128)(2,1)S(1)}, bf16[128,256]{1,0:T(8,128)(2,1)S(1)}, u32[]{:S(2)}, u32[]{:S(2)}) %collective-permute-start.1) | collective-permute-done | bytes 65568 | tf_op jit(solution)/shard_map/ppermute | solution.py:50
  10.5 0.5 collective-permute-done.refs_1_
  11.1 0.0 collective-permute-start.4
  11.1 0.5 collective-permute-start.5
  11.6 0.1 collective-permute-start.6
  11.6 0.0 collective-permute-done.3.refs_4_
  11.6 0.7 %collective-permute-done.4.refs_5_ = bf16[128,256]{1,0:T(8,128)(2,1)S(1)} collective-permute-done((bf16[128,256]{1,0:T(8,128)(2,1)S(1)}, bf16[128,256]{1,0:T(8,128)(2,1)S(1)}, u32[]{:S(2)}, u32[]{:S(2)}) %collective-permute-start.4) | collective-permute-done | bytes 65568 | tf_op jit(solution)/shard_map/ppermute | solution.py:40
  12.3 0.2 collective-permute-done.5.refs_6_
  12.5 0.4 collective-permute-done.6.refs_7_
  12.8 1.1 %shard_map.113 = (f32[1,256]{1,0:T(1,128)S(1)}, f32[128,256]{1,0:T(8,128)S(1)}, bf16[128,256]{1,0:T(8,128)(2,1)S(1)}, bf16[128,256]{1,0:T(8,128)(2,1)S(1)}, bf16[128,256]{1,0:T(8,128)(2,1)S(1)}) custom-call(s32[1,1,16]{2,1,0:T(1,128)S(1)} %copy-done.5, s32[1,1]{1,0:T(1,128)S(6)} %copy.12.count_ref, f32[1,256]{1,0:T(1,128)S(1)} %bitcast.3, ...), custom_call_target="tpu_custom_call" | custom-call | flops 1000000 | bytes 1000000 | tf_op jit(solution)/shard_map/pallas_call | solution.py:278
  14.0 2.7 %collective-permute-start.7 = (bf16[128,256]{1,0:T(8,128)(2,1)S(1)}, bf16[128,256]{1,0:T(8,128)(2,1)S(1)}, u32[]{:S(2)}, u32[]{:S(2)}) collective-permute-start(bf16[128,256]{1,0:T(8,128)(2,1)S(1)} %get-tuple-element.45), channel_id=1, source_target_pairs={{0,2},{1,3},{2,0},{3,1},{4,6},{5,7},{6,4},{7,5},{8,10},{9,11},{10,... | collective-permute-start | bytes 196616 | tf_op jit(solution)/shard_map/ppermute | solution.py:54
  16.6 1.4 %collective-permute-start.8 = (bf16[128,256]{1,0:T(8,128)(2,1)S(1)}, bf16[128,256]{1,0:T(8,128)(2,1)S(1)}, u32[]{:S(2)}, u32[]{:S(2)}) collective-permute-start(bf16[128,256]{1,0:T(8,128)(2,1)S(1)} %get-tuple-element.46), channel_id=1, source_target_pairs={{0,3},{1,2},{2,1},{3,0},{4,7},{5,6},{6,5},{7,4},{8,11},{9,10},{10,... | collective-permute-start | bytes 196616 | tf_op jit(solution)/shard_map/ppermute | solution.py:54
  18.0 0.0 collective-permute-start.9
  18.0 3.7 %collective-permute-done.7.refs_1_ = bf16[128,256]{1,0:T(8,128)(2,1)S(1)} collective-permute-done((bf16[128,256]{1,0:T(8,128)(2,1)S(1)}, bf16[128,256]{1,0:T(8,128)(2,1)S(1)}, u32[]{:S(2)}, u32[]{:S(2)}) %collective-permute-start.7) | collective-permute-done | bytes 65568 | tf_op jit(solution)/shard_map/ppermute | solution.py:54
  21.7 1.2 %collective-permute-done.8.refs_2_ = bf16[128,256]{1,0:T(8,128)(2,1)S(1)} collective-permute-done((bf16[128,256]{1,0:T(8,128)(2,1)S(1)}, bf16[128,256]{1,0:T(8,128)(2,1)S(1)}, u32[]{:S(2)}, u32[]{:S(2)}) %collective-permute-start.8) | collective-permute-done | bytes 65568 | tf_op jit(solution)/shard_map/ppermute | solution.py:54
  22.9 0.5 collective-permute-done.9.refs_3_
  23.4 0.4 shard_map.114
  23.8 0.1 collective-permute-start.12
  23.9 2.9 %collective-permute-start.11 = (bf16[128,256]{1,0:T(8,128)(2,1)S(1)}, bf16[128,256]{1,0:T(8,128)(2,1)S(1)}, u32[]{:S(2)}, u32[]{:S(2)}) collective-permute-start(bf16[128,256]{1,0:T(8,128)(2,1)S(1)} %get-tuple-element.50.hidden_ref.own_ref), channel_id=1, source_target_pairs={{0,3},{1,2},{2,1},{3,0},{4,7},{5,6},{6,5},{7,4},{8,11},{9,10},{10,... | collective-permute-start | bytes 196616 | tf_op jit(solution)/shard_map/ppermute | solution.py:54
  26.7 0.0 collective-permute-start.10
  26.8 1.6 %collective-permute-start.13 = (bf16[272,256]{1,0:T(8,128)(2,1)S(1)}, bf16[272,256]{1,0:T(8,128)(2,1)S(1)}, u32[]{:S(2)}, u32[]{:S(2)}) collective-permute-start(bf16[272,256]{1,0:T(8,128)(2,1)S(1)} %shard_map.116.a_ref), channel_id=1, source_target_pairs={{0,1},{1,0},{2,3},{3,2},{4,5},{5,4},{6,7},{7,6},{8,9},{9,8},{10,11... | collective-permute-start | bytes 417800 | tf_op jit(solution)/shard_map/ppermute | solution.py:54
  28.4 2.2 %collective-permute-done.11.refs_1_ = bf16[128,256]{1,0:T(8,128)(2,1)S(1)} collective-permute-done((bf16[128,256]{1,0:T(8,128)(2,1)S(1)}, bf16[128,256]{1,0:T(8,128)(2,1)S(1)}, u32[]{:S(2)}, u32[]{:S(2)}) %collective-permute-start.11) | collective-permute-done | bytes 65568 | tf_op jit(solution)/shard_map/ppermute | solution.py:54
  30.6 2.6 %collective-permute-done.10.refs_0_ = bf16[128,256]{1,0:T(8,128)(2,1)S(1)} collective-permute-done((bf16[128,256]{1,0:T(8,128)(2,1)S(1)}, bf16[128,256]{1,0:T(8,128)(2,1)S(1)}, u32[]{:S(2)}, u32[]{:S(2)}) %collective-permute-start.10) | collective-permute-done | bytes 65568 | tf_op jit(solution)/shard_map/ppermute | solution.py:54
  33.3 1.4 %collective-permute-done.13.next_ref.b_ref = bf16[272,256]{1,0:T(8,128)(2,1)S(1)} collective-permute-done((bf16[272,256]{1,0:T(8,128)(2,1)S(1)}, bf16[272,256]{1,0:T(8,128)(2,1)S(1)}, u32[]{:S(2)}, u32[]{:S(2)}) %collective-permute-start.13) | collective-permute-done | bytes 139296 | tf_op jit(solution)/shard_map/ppermute | solution.py:54
  34.7 0.8 %collective-permute-start.15 = (bf16[144,256]{1,0:T(8,128)(2,1)S(1)}, bf16[144,256]{1,0:T(8,128)(2,1)S(1)}, u32[]{:S(2)}, u32[]{:S(2)}) collective-permute-start(bf16[144,256]{1,0:T(8,128)(2,1)S(1)} %shard_map.118.a_ref), channel_id=1, source_target_pairs={{0,2},{1,3},{2,0},{3,1},{4,6},{5,7},{6,4},{7,5},{8,10},{9,11},{10,... | collective-permute-start | bytes 221192 | tf_op jit(solution)/shard_map/ppermute | solution.py:54
  35.5 1.2 %shard_map.117 = (f32[4,128,256]{2,1,0:T(8,128)S(1)}, bf16[4,128,256]{2,1,0:T(8,128)(2,1)S(1)}) custom-call(s32[1,1,16]{2,1,0:T(1,128)S(1)} %copy-done.5, s32[1,1]{1,0:T(1,128)S(6)} %copy.12.count_ref, bf16[16,128,128]{2,1,0:T(8,128)(2,1)S(1)} %get-tuple-element.49.turned_ref, bf16[128,256]{1,0:T(8,128)(2,1)S(1)} %get-tuple-element.50.hidden_ref.own_ref, ...), custom_call_target="tpu_custom_call" | custom-call | flops 4000000000 | bytes 1000000 | tf_op jit(solution)/shard_map/pallas_call | solution.py:309
  36.7 0.1 collective-permute-start.14
  36.7 4.5 %collective-permute-done.15.b_ref = bf16[144,256]{1,0:T(8,128)(2,1)S(1)} collective-permute-done((bf16[144,256]{1,0:T(8,128)(2,1)S(1)}, bf16[144,256]{1,0:T(8,128)(2,1)S(1)}, u32[]{:S(2)}, u32[]{:S(2)}) %collective-permute-start.15) | collective-permute-done | bytes 73760 | tf_op jit(solution)/shard_map/ppermute | solution.py:54
  41.3 0.0 collective-permute-done.14.got_ref
  41.3 0.1 shard_map.120
  41.4 1.2 %collective-permute-start.16 = (bf16[272,256]{1,0:T(8,128)(2,1)S(1)}, bf16[272,256]{1,0:T(8,128)(2,1)S(1)}, u32[]{:S(2)}, u32[]{:S(2)}) collective-permute-start(bf16[272,256]{1,0:T(8,128)(2,1)S(1)} %get-tuple-element.59), channel_id=1, source_target_pairs={{0,24},{4,28},{8,16},{12,20},{16,8},{20,12},{24,0},{28,4},{1,25},{... | collective-permute-start | bytes 417800 | tf_op jit(solution)/shard_map/ppermute | solution.py:50
  42.6 1.3 %collective-permute-start.17 = (bf16[272,256]{1,0:T(8,128)(2,1)S(1)}, bf16[272,256]{1,0:T(8,128)(2,1)S(1)}, u32[]{:S(2)}, u32[]{:S(2)}) collective-permute-start(bf16[272,256]{1,0:T(8,128)(2,1)S(1)} %get-tuple-element.60), channel_id=1, source_target_pairs={{0,16},{4,20},{8,24},{12,28},{16,0},{20,4},{24,8},{28,12},{1,17},{... | collective-permute-start | bytes 417800 | tf_op jit(solution)/shard_map/ppermute | solution.py:50
  43.9 1.0 %collective-permute-start.18 = (bf16[272,256]{1,0:T(8,128)(2,1)S(1)}, bf16[272,256]{1,0:T(8,128)(2,1)S(1)}, u32[]{:S(2)}, u32[]{:S(2)}) collective-permute-start(bf16[272,256]{1,0:T(8,128)(2,1)S(1)} %get-tuple-element.61), channel_id=1, source_target_pairs={{0,8},{4,12},{8,0},{12,4},{16,24},{20,28},{24,16},{28,20},{1,9},{5... | collective-permute-start | bytes 417800 | tf_op jit(solution)/shard_map/ppermute | solution.py:50
  44.9 4.0 %collective-permute-done.16.refs_0_ = bf16[272,256]{1,0:T(8,128)(2,1)S(1)} collective-permute-done((bf16[272,256]{1,0:T(8,128)(2,1)S(1)}, bf16[272,256]{1,0:T(8,128)(2,1)S(1)}, u32[]{:S(2)}, u32[]{:S(2)}) %collective-permute-start.16) | collective-permute-done | bytes 139296 | tf_op jit(solution)/shard_map/ppermute | solution.py:50
  48.9 1.1 %collective-permute-done.17.refs_1_ = bf16[272,256]{1,0:T(8,128)(2,1)S(1)} collective-permute-done((bf16[272,256]{1,0:T(8,128)(2,1)S(1)}, bf16[272,256]{1,0:T(8,128)(2,1)S(1)}, u32[]{:S(2)}, u32[]{:S(2)}) %collective-permute-start.17) | collective-permute-done | bytes 139296 | tf_op jit(solution)/shard_map/ppermute | solution.py:50
  50.0 0.5 collective-permute-done.18.refs_2_
  50.6 0.1 collective-permute-start.19
  50.7 1.3 %collective-permute-done.19.theirs_ref = f32[128,256]{1,0:T(8,128)S(1)} collective-permute-done((f32[128,256]{1,0:T(8,128)S(1)}, f32[128,256]{1,0:T(8,128)S(1)}, u32[]{:S(2)}, u32[]{:S(2)}) %collective-permute-start.19) | collective-permute-done | bytes 131104 | tf_op jit(solution)/shard_map/ppermute | solution.py:40
  52.0 0.8 %shard_map.122 = (bf16[128,256]{1,0:T(8,128)(2,1)}, bf16[128,256]{1,0:T(8,128)(2,1)}, f32[256,256]{1,0:T(8,128)}, f32[1,256]{1,0:T(1,128)}) custom-call(bf16[128,256]{1,0:T(8,128)(2,1)S(1)} %get-tuple-element.48.out_ref, f32[128,256]{1,0:T(8,128)S(1)} %get-tuple-element.43.inv_ref, f32[128,256]{1,0:T(8,128)S(1)} %get-tuple-element.58.own_ref, ...), custom_call_target="tpu_custom_call" | custom-call | flops 1000000 | bytes 1000000 | tf_op jit(solution)/shard_map/pallas_call | solution.py:329
  (18 shorter events, 0.2 us)
Async XLA Ops:
  0.6 0.7 %copy-start.4 = (s32[128]{0:T(128)S(1)}, s32[128]{0:T(128)}, u32[]{:S(2)}) copy-start(s32[128]{0:T(128)} %param.9) | copy-start | bytes 1540
  1.3 0.8 %copy-start.2 = (bf16[128,256]{1,0:T(8,128)(2,1)S(1)}, bf16[128,256]{1,0:T(8,128)(2,1)}, u32[]{:S(2)}) copy-start(bf16[128,256]{1,0:T(8,128)(2,1)} %features_ref.1) | copy-start | bytes 196612
  2.1 5.5 %copy-start.6 = (s32[1,1,16,512]{3,2,1,0:T(8,128)S(1)}, s32[1,1,16,512]{3,2,1,0:T(8,128)}, u32[]{:S(2)}) copy-start(s32[1,1,16,512]{3,2,1,0:T(8,128)} %edge_ref.1) | copy-start | bytes 98308
  2.2 9.4 %collective-permute-start.3 = (bf16[128,256]{1,0:T(8,128)(2,1)S(1)}, bf16[128,256]{1,0:T(8,128)(2,1)S(1)}, u32[]{:S(2)}, u32[]{:S(2)}) collective-permute-start(bf16[128,256]{1,0:T(8,128)(2,1)S(1)} %get-tuple-element.37.refs_0_), channel_id=1, source_target_pairs={{0,4},{4,0},{8,12},{12,8},{16,20},{20,16},{24,28},{28,24},{1,5},{5... | collective-permute-start | bytes 196616 | tf_op jit(solution)/shard_map/ppermute | solution.py:40
  2.8 6.2 %collective-permute-start.2 = (bf16[128,256]{1,0:T(8,128)(2,1)S(1)}, bf16[128,256]{1,0:T(8,128)(2,1)S(1)}, u32[]{:S(2)}, u32[]{:S(2)}) collective-permute-start(bf16[128,256]{1,0:T(8,128)(2,1)S(1)} %get-tuple-element.37.refs_0_), channel_id=1, source_target_pairs={{0,24},{4,28},{8,16},{12,20},{16,8},{20,12},{24,0},{28,4},{1,25},{... | collective-permute-start | bytes 196616 | tf_op jit(solution)/shard_map/ppermute | solution.py:50
  6.3 4.3 %collective-permute-start.1 = (bf16[128,256]{1,0:T(8,128)(2,1)S(1)}, bf16[128,256]{1,0:T(8,128)(2,1)S(1)}, u32[]{:S(2)}, u32[]{:S(2)}) collective-permute-start(bf16[128,256]{1,0:T(8,128)(2,1)S(1)} %get-tuple-element.37.refs_0_), channel_id=1, source_target_pairs={{0,16},{4,20},{8,24},{12,28},{16,0},{20,4},{24,8},{28,12},{1,17},{... | collective-permute-start | bytes 196616 | tf_op jit(solution)/shard_map/ppermute | solution.py:50
  6.8 4.3 %collective-permute-start = (bf16[128,256]{1,0:T(8,128)(2,1)S(1)}, bf16[128,256]{1,0:T(8,128)(2,1)S(1)}, u32[]{:S(2)}, u32[]{:S(2)}) collective-permute-start(bf16[128,256]{1,0:T(8,128)(2,1)S(1)} %get-tuple-element.37.refs_0_), channel_id=1, source_target_pairs={{0,8},{4,12},{8,0},{12,4},{16,24},{20,28},{24,16},{28,20},{1,9},{5... | collective-permute-start | bytes 196616 | tf_op jit(solution)/shard_map/ppermute | solution.py:50
  11.1 1.8 %copy-start.3 = (f32[256]{0:T(256)S(1)}, f32[256]{0:T(256)}, u32[]{:S(2)}) copy-start(f32[256]{0:T(256)} %param.11) | copy-start | bytes 3076
  11.1 1.8 %copy-start.5 = (s32[1,1,16]{2,1,0:T(1,128)S(1)}, s32[1,1,16]{2,1,0:T(1,128)}, u32[]{:S(2)}) copy-start(s32[1,1,16]{2,1,0:T(1,128)} %pos_ref.3) | copy-start | bytes 196
  11.1 1.3 %collective-permute-start.4 = (bf16[128,256]{1,0:T(8,128)(2,1)S(1)}, bf16[128,256]{1,0:T(8,128)(2,1)S(1)}, u32[]{:S(2)}, u32[]{:S(2)}) collective-permute-start(bf16[128,256]{1,0:T(8,128)(2,1)S(1)} %collective-permute-done.refs_1_), channel_id=1, source_target_pairs={{0,4},{4,0},{8,12},{12,8},{16,20},{20,16},{24,28},{28,24},{1,5},{5... | collective-permute-start | bytes 196616 | tf_op jit(solution)/shard_map/ppermute | solution.py:40
  11.1 1.4 %collective-permute-start.5 = (bf16[128,256]{1,0:T(8,128)(2,1)S(1)}, bf16[128,256]{1,0:T(8,128)(2,1)S(1)}, u32[]{:S(2)}, u32[]{:S(2)}) collective-permute-start(bf16[128,256]{1,0:T(8,128)(2,1)S(1)} %collective-permute-done.1.refs_2_), channel_id=1, source_target_pairs={{0,4},{4,0},{8,12},{12,8},{16,20},{20,16},{24,28},{28,24},{1,5},{5... | collective-permute-start | bytes 196616 | tf_op jit(solution)/shard_map/ppermute | solution.py:40
  11.6 1.3 %collective-permute-start.6 = (bf16[128,256]{1,0:T(8,128)(2,1)S(1)}, bf16[128,256]{1,0:T(8,128)(2,1)S(1)}, u32[]{:S(2)}, u32[]{:S(2)}) collective-permute-start(bf16[128,256]{1,0:T(8,128)(2,1)S(1)} %collective-permute-done.2.refs_3_), channel_id=1, source_target_pairs={{0,4},{4,0},{8,12},{12,8},{16,20},{20,16},{24,28},{28,24},{1,5},{5... | collective-permute-start | bytes 196616 | tf_op jit(solution)/shard_map/ppermute | solution.py:40
  12.8 10.6 %copy-start = (bf16[256,256]{1,0:T(8,128)(2,1)S(1)}, bf16[256,256]{1,0:T(8,128)(2,1)}, u32[]{:S(2)}) copy-start(bf16[256,256]{1,0:T(8,128)(2,1)} %weight_ref.1) | copy-start | bytes 393220
  12.8 10.6 %copy-start.1 = (bf16[128,256]{1,0:T(8,128)(2,1)S(1)}, bf16[128,256]{1,0:T(8,128)(2,1)}, u32[]{:S(2)}) copy-start(bf16[128,256]{1,0:T(8,128)(2,1)} %cot_ref.1) | copy-start | bytes 196612
  14.0 7.7 %collective-permute-start.7 = (bf16[128,256]{1,0:T(8,128)(2,1)S(1)}, bf16[128,256]{1,0:T(8,128)(2,1)S(1)}, u32[]{:S(2)}, u32[]{:S(2)}) collective-permute-start(bf16[128,256]{1,0:T(8,128)(2,1)S(1)} %get-tuple-element.45), channel_id=1, source_target_pairs={{0,2},{1,3},{2,0},{3,1},{4,6},{5,7},{6,4},{7,5},{8,10},{9,11},{10,... | collective-permute-start | bytes 196616 | tf_op jit(solution)/shard_map/ppermute | solution.py:54
  16.6 6.3 %collective-permute-start.8 = (bf16[128,256]{1,0:T(8,128)(2,1)S(1)}, bf16[128,256]{1,0:T(8,128)(2,1)S(1)}, u32[]{:S(2)}, u32[]{:S(2)}) collective-permute-start(bf16[128,256]{1,0:T(8,128)(2,1)S(1)} %get-tuple-element.46), channel_id=1, source_target_pairs={{0,3},{1,2},{2,1},{3,0},{4,7},{5,6},{6,5},{7,4},{8,11},{9,10},{10,... | collective-permute-start | bytes 196616 | tf_op jit(solution)/shard_map/ppermute | solution.py:54
  18.0 5.4 %collective-permute-start.9 = (bf16[128,256]{1,0:T(8,128)(2,1)S(1)}, bf16[128,256]{1,0:T(8,128)(2,1)S(1)}, u32[]{:S(2)}, u32[]{:S(2)}) collective-permute-start(bf16[128,256]{1,0:T(8,128)(2,1)S(1)} %get-tuple-element.47), channel_id=1, source_target_pairs={{0,1},{1,0},{2,3},{3,2},{4,5},{5,4},{6,7},{7,6},{8,9},{9,8},{10,11... | collective-permute-start | bytes 196616 | tf_op jit(solution)/shard_map/ppermute | solution.py:54
  23.8 3.0 %collective-permute-start.12 = (bf16[144,256]{1,0:T(8,128)(2,1)S(1)}, bf16[144,256]{1,0:T(8,128)(2,1)S(1)}, u32[]{:S(2)}, u32[]{:S(2)}) collective-permute-start(bf16[144,256]{1,0:T(8,128)(2,1)S(1)} %get-tuple-element.53), channel_id=1, source_target_pairs={{0,4},{4,0},{8,12},{12,8},{16,20},{20,16},{24,28},{28,24},{1,5},{5... | collective-permute-start | bytes 221192 | tf_op jit(solution)/shard_map/ppermute | solution.py:40
  23.9 6.8 %collective-permute-start.11 = (bf16[128,256]{1,0:T(8,128)(2,1)S(1)}, bf16[128,256]{1,0:T(8,128)(2,1)S(1)}, u32[]{:S(2)}, u32[]{:S(2)}) collective-permute-start(bf16[128,256]{1,0:T(8,128)(2,1)S(1)} %get-tuple-element.50.hidden_ref.own_ref), channel_id=1, source_target_pairs={{0,3},{1,2},{2,1},{3,0},{4,7},{5,6},{6,5},{7,4},{8,11},{9,10},{10,... | collective-permute-start | bytes 196616 | tf_op jit(solution)/shard_map/ppermute | solution.py:54
  26.7 6.5 %collective-permute-start.10 = (bf16[128,256]{1,0:T(8,128)(2,1)S(1)}, bf16[128,256]{1,0:T(8,128)(2,1)S(1)}, u32[]{:S(2)}, u32[]{:S(2)}) collective-permute-start(bf16[128,256]{1,0:T(8,128)(2,1)S(1)} %get-tuple-element.50.hidden_ref.own_ref), channel_id=1, source_target_pairs={{0,2},{1,3},{2,0},{3,1},{4,6},{5,7},{6,4},{7,5},{8,10},{9,11},{10,... | collective-permute-start | bytes 196616 | tf_op jit(solution)/shard_map/ppermute | solution.py:54
  26.8 7.9 %collective-permute-start.13 = (bf16[272,256]{1,0:T(8,128)(2,1)S(1)}, bf16[272,256]{1,0:T(8,128)(2,1)S(1)}, u32[]{:S(2)}, u32[]{:S(2)}) collective-permute-start(bf16[272,256]{1,0:T(8,128)(2,1)S(1)} %shard_map.116.a_ref), channel_id=1, source_target_pairs={{0,1},{1,0},{2,3},{3,2},{4,5},{5,4},{6,7},{7,6},{8,9},{9,8},{10,11... | collective-permute-start | bytes 417800 | tf_op jit(solution)/shard_map/ppermute | solution.py:54
  34.7 6.6 %collective-permute-start.15 = (bf16[144,256]{1,0:T(8,128)(2,1)S(1)}, bf16[144,256]{1,0:T(8,128)(2,1)S(1)}, u32[]{:S(2)}, u32[]{:S(2)}) collective-permute-start(bf16[144,256]{1,0:T(8,128)(2,1)S(1)} %shard_map.118.a_ref), channel_id=1, source_target_pairs={{0,2},{1,3},{2,0},{3,1},{4,6},{5,7},{6,4},{7,5},{8,10},{9,11},{10,... | collective-permute-start | bytes 221192 | tf_op jit(solution)/shard_map/ppermute | solution.py:54
  36.7 4.6 %collective-permute-start.14 = (bf16[4,128,256]{2,1,0:T(8,128)(2,1)S(1)}, bf16[4,128,256]{2,1,0:T(8,128)(2,1)S(1)}, u32[]{:S(2)}, u32[]{:S(2)}) collective-permute-start(bf16[4,128,256]{2,1,0:T(8,128)(2,1)S(1)} %get-tuple-element.57), channel_id=1, source_target_pairs={{0,4},{4,0},{8,12},{12,8},{16,20},{20,16},{24,28},{28,24},{1,5},{5... | collective-permute-start | bytes 786440 | tf_op jit(solution)/shard_map/ppermute | solution.py:40
  41.4 7.5 %collective-permute-start.16 = (bf16[272,256]{1,0:T(8,128)(2,1)S(1)}, bf16[272,256]{1,0:T(8,128)(2,1)S(1)}, u32[]{:S(2)}, u32[]{:S(2)}) collective-permute-start(bf16[272,256]{1,0:T(8,128)(2,1)S(1)} %get-tuple-element.59), channel_id=1, source_target_pairs={{0,24},{4,28},{8,16},{12,20},{16,8},{20,12},{24,0},{28,4},{1,25},{... | collective-permute-start | bytes 417800 | tf_op jit(solution)/shard_map/ppermute | solution.py:50
  42.6 7.5 %collective-permute-start.17 = (bf16[272,256]{1,0:T(8,128)(2,1)S(1)}, bf16[272,256]{1,0:T(8,128)(2,1)S(1)}, u32[]{:S(2)}, u32[]{:S(2)}) collective-permute-start(bf16[272,256]{1,0:T(8,128)(2,1)S(1)} %get-tuple-element.60), channel_id=1, source_target_pairs={{0,16},{4,20},{8,24},{12,28},{16,0},{20,4},{24,8},{28,12},{1,17},{... | collective-permute-start | bytes 417800 | tf_op jit(solution)/shard_map/ppermute | solution.py:50
  43.9 6.7 %collective-permute-start.18 = (bf16[272,256]{1,0:T(8,128)(2,1)S(1)}, bf16[272,256]{1,0:T(8,128)(2,1)S(1)}, u32[]{:S(2)}, u32[]{:S(2)}) collective-permute-start(bf16[272,256]{1,0:T(8,128)(2,1)S(1)} %get-tuple-element.61), channel_id=1, source_target_pairs={{0,8},{4,12},{8,0},{12,4},{16,24},{20,28},{24,16},{28,20},{1,9},{5... | collective-permute-start | bytes 417800 | tf_op jit(solution)/shard_map/ppermute | solution.py:50
  50.6 1.4 %collective-permute-start.19 = (f32[128,256]{1,0:T(8,128)S(1)}, f32[128,256]{1,0:T(8,128)S(1)}, u32[]{:S(2)}, u32[]{:S(2)}) collective-permute-start(f32[128,256]{1,0:T(8,128)S(1)} %get-tuple-element.62.mine_ref), channel_id=1, source_target_pairs={{0,4},{4,0},{8,12},{12,8},{16,20},{20,16},{24,28},{28,24},{1,5},{5... | collective-permute-start | bytes 393224 | tf_op jit(solution)/shard_map/ppermute | solution.py:40

commit v6 on v5

--- a/solution.py
+++ b/solution.py
@@ -80,7 +80,8 @@
     lax.fori_loop(0, (count + group - 1) // group, step, 0)
 
 
-def build_kernel(count_ref, edge_ref, blocks_ref, turned_ref):
+def build_kernel(count_ref, edge_ref, bias_ref, blocks_ref, turned_ref, bias_out_ref):
+    bias_out_ref[...] = bias_ref[...]
     slots, edges = edge_ref.shape[2], edge_ref.shape[3]
     node = lax.broadcasted_iota(jnp.int32, (BLOCK, edges), 0)
 
@@ -96,15 +97,16 @@
     for_live(count_ref, slots, build)
 
 
-def forward_kernel(rows, cols, pos_ref, count_ref, bias_ref, blocks_ref, *refs):
-    near = refs[: 2 * (rows // CORES)]
-    bias_out_ref, own_ref, *send, gathered, acc = refs[len(near) :]
-    bias_out_ref[...] = bias_ref[...]
+def forward_kernel(rows, cols, pos_hold_ref, count_ref, blocks_ref, near_ref, next_ref, *refs):
+    own_ref, *send, gathered, acc, pos_ref, sem = refs
+    fetch = pltpu.make_async_copy(pos_hold_ref, pos_ref, sem)
+    fetch.start()
     chips = rows // CORES
     row, col = lax.axis_index("row"), lax.axis_index("col")
-    for n, ref in enumerate(near):
-        gathered[n] = ref[...]
+    gathered[:chips] = near_ref[...]
+    gathered[chips:] = next_ref[...]
     acc[...] = jnp.zeros_like(acc)
+    fetch.wait()
 
     def add(s, live):
         p = pos_ref[0, 0, s]
@@ -184,15 +186,17 @@
         out_ref[n] = ref[...]
 
 
-def backward_kernel(
-    rows, cols, pos_ref, count_ref, turned_ref, own_ref, next_ref, far_ref, keep_ref, send_ref, hidden, acc
-):
+def backward_kernel(rows, cols, pos_hold_ref, count_ref, turned_ref, *refs):
+    own_ref, next_ref, far_ref, keep_ref, send_ref, hidden, acc, pos_ref, sem = refs
+    fetch = pltpu.make_async_copy(pos_hold_ref, pos_ref, sem)
+    fetch.start()
     chips = rows // CORES
     row, col = lax.axis_index("row"), lax.axis_index("col")
     hidden[0] = own_ref[...]
     hidden[1] = next_ref[:BLOCK]
     hidden[2:] = far_ref[...]
     acc[...] = jnp.zeros_like(acc)
+    fetch.wait()
 
     def add(s, live):
         p = pos_ref[0, 0, s]
@@ -249,7 +253,7 @@
         out_shape=shapes[0] if single else tuple(shapes),
         in_specs=specs,
         out_specs=VMEM if single else tuple(VMEM for _ in shapes),
-        scratch_shapes=[pltpu.VMEM(*s) for s in scratch],
+        scratch_shapes=scratch,
         compiler_params=pltpu.CompilerParams(vmem_limit_bytes=40 * 1024 * 1024),
         cost_estimate=pl.CostEstimate(flops=flops, bytes_accessed=1_000_000, transcendentals=0),
     )
@@ -267,20 +271,23 @@
     bias_vector = bias_vector.reshape(1, width)
 
     scaled, inv = call(scale_kernel, [VMEM, VMEM], [(piece, BF16), (piece, F32)])(features, degree)
-    near = [scaled] + [to_chip(scaled, rows, k) for k in range(1, chips)]
-    blocks, turned = call(
-        build_kernel, [SMEM, VMEM], [((slots, BLOCK, BLOCK), BF16)] * 2, flops=LONG
-    )(block_count, edge_pos)
-    blocks, *got = lax.optimization_barrier((blocks, *near[1:]))
-    near = [scaled, *got]
-    near = near + [to_core(x, rows) for x in near]
-
-    bias_vector, own, *send = call(
+    near = [to_chip(scaled, rows, k) for k in range(1, chips)]
+    blocks, turned, bias_vector = call(
+        build_kernel,
+        [SMEM, VMEM, VMEM],
+        [((slots, BLOCK, BLOCK), BF16)] * 2 + [((1, width), F32)],
+        flops=LONG,
+    )(block_count, edge_pos, bias_vector)
+    blocks, *near = lax.optimization_barrier((blocks, *near))
+    near = call(collect_kernel, [VMEM] * chips, [((chips,) + piece, BF16)])(scaled, *near)
+
+    fetched = [pltpu.SMEM(block_pos.shape, jnp.int32), pltpu.SemaphoreType.DMA]
+    own, *send = call(
         functools.partial(forward_kernel, rows, cols),
-        [SMEM, SMEM, VMEM, VMEM] + [VMEM] * len(near),
-        [((1, width), F32), (piece, F32)] + [(piece, BF16)] * (cols - 1),
-        [((rows,) + piece, BF16), ((cols,) + piece, F32)],
-    )(block_pos, block_count, bias_vector, blocks, *near)
+        [VMEM, SMEM, VMEM, VMEM, VMEM],
+        [(piece, F32)] + [(piece, BF16)] * (cols - 1),
+        [pltpu.VMEM((rows,) + piece, BF16), pltpu.VMEM((cols,) + piece, F32), *fetched],
+    )(block_pos, block_count, blocks, near, to_core(near, rows))
     order = list(range(2, cols)) + [1]
     parts = [to_col(send[k - 1], cols, k) for k in order]
 
@@ -308,9 +315,9 @@
 
     col_keep, col_send = call(
         functools.partial(backward_kernel, rows, cols),
-        [SMEM, SMEM] + [VMEM] * 4,
+        [VMEM, SMEM] + [VMEM] * 4,
         [((chips,) + piece, F32), ((chips,) + piece, BF16)],
-        [((cols,) + piece, BF16), ((rows,) + piece, F32)],
+        [pltpu.VMEM((cols,) + piece, BF16), pltpu.VMEM((rows,) + piece, F32), *fetched],
         flops=LONG,
     )(block_pos, block_count, turned, hidden, next_to, far)
     grads = add(grads, other)

time: 52.6 us -> 51.8 us (0.985)
  waiting for transfers between devices: 27 us -> 25.3 us
  local copies, waits for them, and re-layouts: 1.51 us -> 2.17 us
    ppermute x6, waiting for transfers between devices: 8.31 us -> 6.7 us  [to_chip(): return lax.ppermute(x, 'row', pairs)]
    ppermute x7 -> x4, starting transfers between devices: 1.3 us -> 0.28 us  [to_core(): return lax.ppermute(x, 'row', [(i, i ^ 1) for i in range(rows)])]
    unnamed x14, local copies, waits for them, and re-layouts: 1.51 us -> 2.17 us
    ppermute x7 -> x4, waiting for transfers between devices: 2.53 us -> 2.86 us  [to_core(): return lax.ppermute(x, 'row', [(i, i ^ 1) for i in range(rows)])]
    pallas_call x3 -> x4, Pallas kernels: 3.05 us -> 2.94 us  [the longest x1 1.09 us: per_device(): call(functools.partial(backward_kernel, rows, cols), [VMEM, SMEM] + [VMEM...]
  transfers between devices with their start and end apart: 20 -> 17, of which waited for: 17 -> 13; matrix products, arithmetic and copies ran while one was open for 0% -> 0% of each run, Pallas kernels for 4% -> 4%
where the time goes in v6:
time: 51.8 us; the launch traced here: 51.5 us
  waiting for transfers between devices  25.3 us (49%)
  starting transfers between devices  18.1 us (35%)
  Pallas kernels  4.47 us (9%)
  local copies, waits for them, and re-layouts  2.17 us (4%)
  between operations  1.44 us (3%)
    ppermute x7, waiting for transfers between devices, to_col(): lax.ppermute(x, 'col', [(i, target(cols, i, k)) for i in range(cols)])  15.7 us
    ppermute x7, starting transfers between devices, to_col(): lax.ppermute(x, 'col', [(i, target(cols, i, k)) for i in range(cols)])  9.66 us
    ppermute x6, starting transfers between devices, to_chip(): return lax.ppermute(x, 'row', pairs)  8.16 us
    ppermute x6, waiting for transfers between devices, to_chip(): return lax.ppermute(x, 'row', pairs)  6.7 us
    ppermute x4, waiting for transfers between devices, to_core(): return lax.ppermute(x, 'row', [(i, i ^ 1) for i in range(rows)])  2.86 us
    unnamed x14, local copies, waits for them, and re-layouts  2.17 us
    pallas_call x1, Pallas kernels, per_device(): call(functools.partial(backward_kernel, rows, cols), [VMEM, SMEM] + [VMEM...  1.09 us
    pallas_call x1, Pallas kernels, per_device(): call(functools.partial(forward_kernel, rows, cols), [VMEM, SMEM, VMEM, VM...  1.06 us
  transfers between devices with their start and end apart: 17, of which 13 were waited for; matrix products, arithmetic and copies ran while one was open for 0% of the time, Pallas kernels for 4%

profile of v6, /device:TPU:0, one launch (start us, length us, event | category | flops | bytes accessed | tf_op | source)
XLA Modules:
  0.0 51.5 jit_solution(4932280125364537881)
XLA Ops:
  0.6 0.6 %copy-done.4 = s32[128]{0:T(128)S(1)} copy-done((s32[128]{0:T(128)S(1)}, s32[128]{0:T(128)}, u32[]{:S(2)}) %copy-start.4) | copy-done | bytes 536
  1.3 0.8 %copy-done.2 = bf16[128,256]{1,0:T(8,128)(2,1)S(1)} copy-done((bf16[128,256]{1,0:T(8,128)(2,1)S(1)}, bf16[128,256]{1,0:T(8,128)(2,1)}, u32[]{:S(2)}) %copy-start.2) | copy-done | bytes 65560
  2.1 0.1 shard_map.112
  2.2 4.0 %collective-permute-start.2 = (bf16[128,256]{1,0:T(8,128)(2,1)S(1)}, bf16[128,256]{1,0:T(8,128)(2,1)S(1)}, u32[]{:S(2)}, u32[]{:S(2)}) collective-permute-start(bf16[128,256]{1,0:T(8,128)(2,1)S(1)} %get-tuple-element.39.refs_0_), channel_id=1, source_target_pairs={{0,24},{4,28},{8,16},{12,20},{16,8},{20,12},{24,0},{28,4},{1,25},{... | collective-permute-start | bytes 196616 | tf_op jit(solution)/shard_map/ppermute | solution.py:50
  6.2 0.5 collective-permute-start.1
  6.7 0.1 collective-permute-start
  7.5 0.0 copy-start.6
  7.5 0.0 copy-done.5
  7.5 0.7 %copy-done.6 = f32[256]{0:T(256)S(1)} copy-done((f32[256]{0:T(256)S(1)}, f32[256]{0:T(256)}, u32[]{:S(2)}) %copy-start.6) | copy-done | bytes 1048
  8.2 0.8 %shard_map.111 = (bf16[16,128,128]{2,1,0:T(8,128)(2,1)S(1)}, bf16[16,128,128]{2,1,0:T(8,128)(2,1)S(1)}, f32[1,256]{1,0:T(1,128)S(1)}) custom-call(s32[1,1]{1,0:T(1,128)S(6)} %copy.12.count_ref, s32[1,1,16,512]{3,2,1,0:T(8,128)S(1)} %copy-done.5, f32[1,256]{1,0:T(1,128)S(1)} %bitcast.4), custom_call_target="tpu_custom_call" | custom-call | flops 4000000000 | bytes 1000000 | tf_op jit(solution)/shard_map/pallas_call | solution.py:275
  9.0 0.0 collective-permute-done.2.refs_3_
  9.0 1.5 %collective-permute-done.1.refs_2_ = bf16[128,256]{1,0:T(8,128)(2,1)S(1)} collective-permute-done((bf16[128,256]{1,0:T(8,128)(2,1)S(1)}, bf16[128,256]{1,0:T(8,128)(2,1)S(1)}, u32[]{:S(2)}, u32[]{:S(2)}) %collective-permute-start.1) | collective-permute-done | bytes 65568 | tf_op jit(solution)/shard_map/ppermute | solution.py:50
  10.5 0.5 collective-permute-done.refs_1_
  11.0 0.0 copy-start
  11.0 0.0 copy-start.1
  11.0 0.1 collective-permute-start.3
  11.1 1.5 %collective-permute-done.3.next_ref = bf16[4,128,256]{2,1,0:T(8,128)(2,1)S(1)} collective-permute-done((bf16[4,128,256]{2,1,0:T(8,128)(2,1)S(1)}, bf16[4,128,256]{2,1,0:T(8,128)(2,1)S(1)}, u32[]{:S(2)}, u32[]{:S(2)}) %collective-permute-start.3) | collective-permute-done | bytes 262176 | tf_op jit(solution)/shard_map/ppermute | solution.py:40
  12.6 1.1 %shard_map.114 = (f32[128,256]{1,0:T(8,128)S(1)}, bf16[128,256]{1,0:T(8,128)(2,1)S(1)}, bf16[128,256]{1,0:T(8,128)(2,1)S(1)}, bf16[128,256]{1,0:T(8,128)(2,1)S(1)}) custom-call(s32[1,1,16]{2,1,0:T(1,128)S(1)} %copy-done.3, s32[1,1]{1,0:T(1,128)S(6)} %copy.12.count_ref, bf16[16,128,128]{2,1,0:T(8,128)(2,1)S(1)} %get-tuple-element.40.blocks_ref, ...), custom_call_target="tpu_custom_call" | custom-call | flops 1000000 | bytes 1000000 | tf_op jit(solution)/shard_map/pallas_call | solution.py:285
  13.7 2.4 %collective-permute-start.4 = (bf16[128,256]{1,0:T(8,128)(2,1)S(1)}, bf16[128,256]{1,0:T(8,128)(2,1)S(1)}, u32[]{:S(2)}, u32[]{:S(2)}) collective-permute-start(bf16[128,256]{1,0:T(8,128)(2,1)S(1)} %get-tuple-element.45), channel_id=1, source_target_pairs={{0,2},{1,3},{2,0},{3,1},{4,6},{5,7},{6,4},{7,5},{8,10},{9,11},{10,... | collective-permute-start | bytes 196616 | tf_op jit(solution)/shard_map/ppermute | solution.py:54
  16.1 1.6 %collective-permute-start.5 = (bf16[128,256]{1,0:T(8,128)(2,1)S(1)}, bf16[128,256]{1,0:T(8,128)(2,1)S(1)}, u32[]{:S(2)}, u32[]{:S(2)}) collective-permute-start(bf16[128,256]{1,0:T(8,128)(2,1)S(1)} %get-tuple-element.46), channel_id=1, source_target_pairs={{0,3},{1,2},{2,1},{3,0},{4,7},{5,6},{6,5},{7,4},{8,11},{9,10},{10,... | collective-permute-start | bytes 196616 | tf_op jit(solution)/shard_map/ppermute | solution.py:54
  17.7 0.2 collective-permute-start.6
  17.9 3.5 %collective-permute-done.4.refs_1_ = bf16[128,256]{1,0:T(8,128)(2,1)S(1)} collective-permute-done((bf16[128,256]{1,0:T(8,128)(2,1)S(1)}, bf16[128,256]{1,0:T(8,128)(2,1)S(1)}, u32[]{:S(2)}, u32[]{:S(2)}) %collective-permute-start.4) | collective-permute-done | bytes 65568 | tf_op jit(solution)/shard_map/ppermute | solution.py:54
  21.4 1.1 %collective-permute-done.5.refs_2_ = bf16[128,256]{1,0:T(8,128)(2,1)S(1)} collective-permute-done((bf16[128,256]{1,0:T(8,128)(2,1)S(1)}, bf16[128,256]{1,0:T(8,128)(2,1)S(1)}, u32[]{:S(2)}, u32[]{:S(2)}) %collective-permute-start.5) | collective-permute-done | bytes 65568 | tf_op jit(solution)/shard_map/ppermute | solution.py:54
  22.5 0.6 %collective-permute-done.6.refs_3_ = bf16[128,256]{1,0:T(8,128)(2,1)S(1)} collective-permute-done((bf16[128,256]{1,0:T(8,128)(2,1)S(1)}, bf16[128,256]{1,0:T(8,128)(2,1)S(1)}, u32[]{:S(2)}, u32[]{:S(2)}) %collective-permute-start.6) | collective-permute-done | bytes 65568 | tf_op jit(solution)/shard_map/ppermute | solution.py:54
  23.1 0.4 shard_map.115
  23.5 0.1 collective-permute-start.9
  23.6 3.1 %collective-permute-start.8 = (bf16[128,256]{1,0:T(8,128)(2,1)S(1)}, bf16[128,256]{1,0:T(8,128)(2,1)S(1)}, u32[]{:S(2)}, u32[]{:S(2)}) collective-permute-start(bf16[128,256]{1,0:T(8,128)(2,1)S(1)} %get-tuple-element.50.hidden_ref.refs_0_), channel_id=1, source_target_pairs={{0,3},{1,2},{2,1},{3,0},{4,7},{5,6},{6,5},{7,4},{8,11},{9,10},{10,... | collective-permute-start | bytes 196616 | tf_op jit(solution)/shard_map/ppermute | solution.py:54
  26.6 0.0 collective-permute-start.7
  26.6 0.0 collective-permute-done.9.got_ref
  26.7 1.4 %collective-permute-start.10 = (bf16[272,256]{1,0:T(8,128)(2,1)S(1)}, bf16[272,256]{1,0:T(8,128)(2,1)S(1)}, u32[]{:S(2)}, u32[]{:S(2)}) collective-permute-start(bf16[272,256]{1,0:T(8,128)(2,1)S(1)} %shard_map.117.a_ref), channel_id=1, source_target_pairs={{0,1},{1,0},{2,3},{3,2},{4,5},{5,4},{6,7},{7,6},{8,9},{9,8},{10,11... | collective-permute-start | bytes 417800 | tf_op jit(solution)/shard_map/ppermute | solution.py:54
  28.1 2.2 %collective-permute-done.8.refs_1_ = bf16[128,256]{1,0:T(8,128)(2,1)S(1)} collective-permute-done((bf16[128,256]{1,0:T(8,128)(2,1)S(1)}, bf16[128,256]{1,0:T(8,128)(2,1)S(1)}, u32[]{:S(2)}, u32[]{:S(2)}) %collective-permute-start.8) | collective-permute-done | bytes 65568 | tf_op jit(solution)/shard_map/ppermute | solution.py:54
  30.3 2.7 %collective-permute-done.7.refs_0_ = bf16[128,256]{1,0:T(8,128)(2,1)S(1)} collective-permute-done((bf16[128,256]{1,0:T(8,128)(2,1)S(1)}, bf16[128,256]{1,0:T(8,128)(2,1)S(1)}, u32[]{:S(2)}, u32[]{:S(2)}) %collective-permute-start.7) | collective-permute-done | bytes 65568 | tf_op jit(solution)/shard_map/ppermute | solution.py:54
  33.0 1.4 %collective-permute-done.10.refs_1_.b_ref = bf16[272,256]{1,0:T(8,128)(2,1)S(1)} collective-permute-done((bf16[272,256]{1,0:T(8,128)(2,1)S(1)}, bf16[272,256]{1,0:T(8,128)(2,1)S(1)}, u32[]{:S(2)}, u32[]{:S(2)}) %collective-permute-start.10) | collective-permute-done | bytes 139296 | tf_op jit(solution)/shard_map/ppermute | solution.py:54
  34.4 0.9 %collective-permute-start.12 = (bf16[144,256]{1,0:T(8,128)(2,1)S(1)}, bf16[144,256]{1,0:T(8,128)(2,1)S(1)}, u32[]{:S(2)}, u32[]{:S(2)}) collective-permute-start(bf16[144,256]{1,0:T(8,128)(2,1)S(1)} %shard_map.119.a_ref), channel_id=1, source_target_pairs={{0,2},{1,3},{2,0},{3,1},{4,6},{5,7},{6,4},{7,5},{8,10},{9,11},{10,... | collective-permute-start | bytes 221192 | tf_op jit(solution)/shard_map/ppermute | solution.py:54
  35.3 1.1 %shard_map.118 = (f32[4,128,256]{2,1,0:T(8,128)S(1)}, bf16[4,128,256]{2,1,0:T(8,128)(2,1)S(1)}) custom-call(s32[1,1,16]{2,1,0:T(1,128)S(1)} %copy-done.3, s32[1,1]{1,0:T(1,128)S(6)} %copy.12.count_ref, bf16[16,128,128]{2,1,0:T(8,128)(2,1)S(1)} %get-tuple-element.49.turned_ref, bf16[128,256]{1,0:T(8,128)(2,1)S(1)} %get-tuple-element.50.hidden_ref.refs_0_, ...), custom_call_target="tpu_custom_call" | custom-call | flops 4000000000 | bytes 1000000 | tf_op jit(solution)/shard_map/pallas_call | solution.py:316
  36.4 0.1 collective-permute-start.11
  36.5 4.4 %collective-permute-done.12.b_ref = bf16[144,256]{1,0:T(8,128)(2,1)S(1)} collective-permute-done((bf16[144,256]{1,0:T(8,128)(2,1)S(1)}, bf16[144,256]{1,0:T(8,128)(2,1)S(1)}, u32[]{:S(2)}, u32[]{:S(2)}) %collective-permute-start.12) | collective-permute-done | bytes 73760 | tf_op jit(solution)/shard_map/ppermute | solution.py:54
  40.9 0.0 collective-permute-done.11.got_ref
  40.9 0.1 shard_map.121
  41.0 1.6 %collective-permute-start.13 = (bf16[272,256]{1,0:T(8,128)(2,1)S(1)}, bf16[272,256]{1,0:T(8,128)(2,1)S(1)}, u32[]{:S(2)}, u32[]{:S(2)}) collective-permute-start(bf16[272,256]{1,0:T(8,128)(2,1)S(1)} %get-tuple-element.59), channel_id=1, source_target_pairs={{0,24},{4,28},{8,16},{12,20},{16,8},{20,12},{24,0},{28,4},{1,25},{... | collective-permute-start | bytes 417800 | tf_op jit(solution)/shard_map/ppermute | solution.py:50
  42.6 0.7 %collective-permute-start.14 = (bf16[272,256]{1,0:T(8,128)(2,1)S(1)}, bf16[272,256]{1,0:T(8,128)(2,1)S(1)}, u32[]{:S(2)}, u32[]{:S(2)}) collective-permute-start(bf16[272,256]{1,0:T(8,128)(2,1)S(1)} %get-tuple-element.60), channel_id=1, source_target_pairs={{0,16},{4,20},{8,24},{12,28},{16,0},{20,4},{24,8},{28,12},{1,17},{... | collective-permute-start | bytes 417800 | tf_op jit(solution)/shard_map/ppermute | solution.py:50
  43.2 1.3 %collective-permute-start.15 = (bf16[272,256]{1,0:T(8,128)(2,1)S(1)}, bf16[272,256]{1,0:T(8,128)(2,1)S(1)}, u32[]{:S(2)}, u32[]{:S(2)}) collective-permute-start(bf16[272,256]{1,0:T(8,128)(2,1)S(1)} %get-tuple-element.61), channel_id=1, source_target_pairs={{0,8},{4,12},{8,0},{12,4},{16,24},{20,28},{24,16},{28,20},{1,9},{5... | collective-permute-start | bytes 417800 | tf_op jit(solution)/shard_map/ppermute | solution.py:50
  44.5 3.3 %collective-permute-done.13.refs_0_ = bf16[272,256]{1,0:T(8,128)(2,1)S(1)} collective-permute-done((bf16[272,256]{1,0:T(8,128)(2,1)S(1)}, bf16[272,256]{1,0:T(8,128)(2,1)S(1)}, u32[]{:S(2)}, u32[]{:S(2)}) %collective-permute-start.13) | collective-permute-done | bytes 139296 | tf_op jit(solution)/shard_map/ppermute | solution.py:50
  47.8 1.4 %collective-permute-done.14.refs_1_ = bf16[272,256]{1,0:T(8,128)(2,1)S(1)} collective-permute-done((bf16[272,256]{1,0:T(8,128)(2,1)S(1)}, bf16[272,256]{1,0:T(8,128)(2,1)S(1)}, u32[]{:S(2)}, u32[]{:S(2)}) %collective-permute-start.14) | collective-permute-done | bytes 139296 | tf_op jit(solution)/shard_map/ppermute | solution.py:50
  49.2 0.0 collective-permute-done.15.refs_2_
  49.3 0.1 collective-permute-start.16
  49.4 1.3 %collective-permute-done.16.theirs_ref = f32[128,256]{1,0:T(8,128)S(1)} collective-permute-done((f32[128,256]{1,0:T(8,128)S(1)}, f32[128,256]{1,0:T(8,128)S(1)}, u32[]{:S(2)}, u32[]{:S(2)}) %collective-permute-start.16) | collective-permute-done | bytes 131104 | tf_op jit(solution)/shard_map/ppermute | solution.py:40
  50.7 0.8 %shard_map.123 = (bf16[128,256]{1,0:T(8,128)(2,1)}, bf16[128,256]{1,0:T(8,128)(2,1)}, f32[256,256]{1,0:T(8,128)}, f32[1,256]{1,0:T(1,128)}) custom-call(bf16[128,256]{1,0:T(8,128)(2,1)S(1)} %get-tuple-element.48.out_ref, f32[128,256]{1,0:T(8,128)S(1)} %get-tuple-element.37.inv_ref, f32[128,256]{1,0:T(8,128)S(1)} %get-tuple-element.58.own_ref, ...), custom_call_target="tpu_custom_call" | custom-call | flops 1000000 | bytes 1000000 | tf_op jit(solution)/shard_map/pallas_call | solution.py:336
  (13 shorter events, 0.2 us)
Async XLA Ops:
  0.6 0.7 %copy-start.4 = (s32[128]{0:T(128)S(1)}, s32[128]{0:T(128)}, u32[]{:S(2)}) copy-start(s32[128]{0:T(128)} %param.9) | copy-start | bytes 1540
  1.3 0.8 %copy-start.2 = (bf16[128,256]{1,0:T(8,128)(2,1)S(1)}, bf16[128,256]{1,0:T(8,128)(2,1)}, u32[]{:S(2)}) copy-start(bf16[128,256]{1,0:T(8,128)(2,1)} %features_ref.1) | copy-start | bytes 196612
  2.1 5.4 %copy-start.5 = (s32[1,1,16,512]{3,2,1,0:T(8,128)S(1)}, s32[1,1,16,512]{3,2,1,0:T(8,128)}, u32[]{:S(2)}) copy-start(s32[1,1,16,512]{3,2,1,0:T(8,128)} %edge_ref.1) | copy-start | bytes 98308
  2.2 6.7 %collective-permute-start.2 = (bf16[128,256]{1,0:T(8,128)(2,1)S(1)}, bf16[128,256]{1,0:T(8,128)(2,1)S(1)}, u32[]{:S(2)}, u32[]{:S(2)}) collective-permute-start(bf16[128,256]{1,0:T(8,128)(2,1)S(1)} %get-tuple-element.39.refs_0_), channel_id=1, source_target_pairs={{0,24},{4,28},{8,16},{12,20},{16,8},{20,12},{24,0},{28,4},{1,25},{... | collective-permute-start | bytes 196616 | tf_op jit(solution)/shard_map/ppermute | solution.py:50
  6.2 4.3 %collective-permute-start.1 = (bf16[128,256]{1,0:T(8,128)(2,1)S(1)}, bf16[128,256]{1,0:T(8,128)(2,1)S(1)}, u32[]{:S(2)}, u32[]{:S(2)}) collective-permute-start(bf16[128,256]{1,0:T(8,128)(2,1)S(1)} %get-tuple-element.39.refs_0_), channel_id=1, source_target_pairs={{0,16},{4,20},{8,24},{12,28},{16,0},{20,4},{24,8},{28,12},{1,17},{... | collective-permute-start | bytes 196616 | tf_op jit(solution)/shard_map/ppermute | solution.py:50
  6.7 4.3 %collective-permute-start = (bf16[128,256]{1,0:T(8,128)(2,1)S(1)}, bf16[128,256]{1,0:T(8,128)(2,1)S(1)}, u32[]{:S(2)}, u32[]{:S(2)}) collective-permute-start(bf16[128,256]{1,0:T(8,128)(2,1)S(1)} %get-tuple-element.39.refs_0_), channel_id=1, source_target_pairs={{0,8},{4,12},{8,0},{12,4},{16,24},{20,28},{24,16},{28,20},{1,9},{5... | collective-permute-start | bytes 196616 | tf_op jit(solution)/shard_map/ppermute | solution.py:50
  7.5 0.7 %copy-start.6 = (f32[256]{0:T(256)S(1)}, f32[256]{0:T(256)}, u32[]{:S(2)}) copy-start(f32[256]{0:T(256)} %param.11) | copy-start | bytes 3076
  11.0 1.7 %copy-start.3 = (s32[1,1,16]{2,1,0:T(1,128)S(1)}, s32[1,1,16]{2,1,0:T(1,128)}, u32[]{:S(2)}) copy-start(s32[1,1,16]{2,1,0:T(1,128)} %pos_hold_ref.3) | copy-start | bytes 196
  11.0 12.1 %copy-start = (bf16[256,256]{1,0:T(8,128)(2,1)S(1)}, bf16[256,256]{1,0:T(8,128)(2,1)}, u32[]{:S(2)}) copy-start(bf16[256,256]{1,0:T(8,128)(2,1)} %weight_ref.1) | copy-start | bytes 393220
  11.0 12.1 %copy-start.1 = (bf16[128,256]{1,0:T(8,128)(2,1)S(1)}, bf16[128,256]{1,0:T(8,128)(2,1)}, u32[]{:S(2)}) copy-start(bf16[128,256]{1,0:T(8,128)(2,1)} %cot_ref.1) | copy-start | bytes 196612
  11.0 1.6 %collective-permute-start.3 = (bf16[4,128,256]{2,1,0:T(8,128)(2,1)S(1)}, bf16[4,128,256]{2,1,0:T(8,128)(2,1)S(1)}, u32[]{:S(2)}, u32[]{:S(2)}) collective-permute-start(bf16[4,128,256]{2,1,0:T(8,128)(2,1)S(1)} %shard_map.113.near_ref), channel_id=1, source_target_pairs={{0,4},{4,0},{8,12},{12,8},{16,20},{20,16},{24,28},{28,24},{1,5},{5... | collective-permute-start | bytes 786440 | tf_op jit(solution)/shard_map/ppermute | solution.py:40
  13.7 7.7 %collective-permute-start.4 = (bf16[128,256]{1,0:T(8,128)(2,1)S(1)}, bf16[128,256]{1,0:T(8,128)(2,1)S(1)}, u32[]{:S(2)}, u32[]{:S(2)}) collective-permute-start(bf16[128,256]{1,0:T(8,128)(2,1)S(1)} %get-tuple-element.45), channel_id=1, source_target_pairs={{0,2},{1,3},{2,0},{3,1},{4,6},{5,7},{6,4},{7,5},{8,10},{9,11},{10,... | collective-permute-start | bytes 196616 | tf_op jit(solution)/shard_map/ppermute | solution.py:54
  16.1 6.4 %collective-permute-start.5 = (bf16[128,256]{1,0:T(8,128)(2,1)S(1)}, bf16[128,256]{1,0:T(8,128)(2,1)S(1)}, u32[]{:S(2)}, u32[]{:S(2)}) collective-permute-start(bf16[128,256]{1,0:T(8,128)(2,1)S(1)} %get-tuple-element.46), channel_id=1, source_target_pairs={{0,3},{1,2},{2,1},{3,0},{4,7},{5,6},{6,5},{7,4},{8,11},{9,10},{10,... | collective-permute-start | bytes 196616 | tf_op jit(solution)/shard_map/ppermute | solution.py:54
  17.7 5.4 %collective-permute-start.6 = (bf16[128,256]{1,0:T(8,128)(2,1)S(1)}, bf16[128,256]{1,0:T(8,128)(2,1)S(1)}, u32[]{:S(2)}, u32[]{:S(2)}) collective-permute-start(bf16[128,256]{1,0:T(8,128)(2,1)S(1)} %get-tuple-element.47), channel_id=1, source_target_pairs={{0,1},{1,0},{2,3},{3,2},{4,5},{5,4},{6,7},{7,6},{8,9},{9,8},{10,11... | collective-permute-start | bytes 196616 | tf_op jit(solution)/shard_map/ppermute | solution.py:54
  23.5 3.2 %collective-permute-start.9 = (bf16[144,256]{1,0:T(8,128)(2,1)S(1)}, bf16[144,256]{1,0:T(8,128)(2,1)S(1)}, u32[]{:S(2)}, u32[]{:S(2)}) collective-permute-start(bf16[144,256]{1,0:T(8,128)(2,1)S(1)} %get-tuple-element.53), channel_id=1, source_target_pairs={{0,4},{4,0},{8,12},{12,8},{16,20},{20,16},{24,28},{28,24},{1,5},{5... | collective-permute-start | bytes 221192 | tf_op jit(solution)/shard_map/ppermute | solution.py:40
  23.6 6.7 %collective-permute-start.8 = (bf16[128,256]{1,0:T(8,128)(2,1)S(1)}, bf16[128,256]{1,0:T(8,128)(2,1)S(1)}, u32[]{:S(2)}, u32[]{:S(2)}) collective-permute-start(bf16[128,256]{1,0:T(8,128)(2,1)S(1)} %get-tuple-element.50.hidden_ref.refs_0_), channel_id=1, source_target_pairs={{0,3},{1,2},{2,1},{3,0},{4,7},{5,6},{6,5},{7,4},{8,11},{9,10},{10,... | collective-permute-start | bytes 196616 | tf_op jit(solution)/shard_map/ppermute | solution.py:54
  26.6 6.3 %collective-permute-start.7 = (bf16[128,256]{1,0:T(8,128)(2,1)S(1)}, bf16[128,256]{1,0:T(8,128)(2,1)S(1)}, u32[]{:S(2)}, u32[]{:S(2)}) collective-permute-start(bf16[128,256]{1,0:T(8,128)(2,1)S(1)} %get-tuple-element.50.hidden_ref.refs_0_), channel_id=1, source_target_pairs={{0,2},{1,3},{2,0},{3,1},{4,6},{5,7},{6,4},{7,5},{8,10},{9,11},{10,... | collective-permute-start | bytes 196616 | tf_op jit(solution)/shard_map/ppermute | solution.py:54
  26.7 7.7 %collective-permute-start.10 = (bf16[272,256]{1,0:T(8,128)(2,1)S(1)}, bf16[272,256]{1,0:T(8,128)(2,1)S(1)}, u32[]{:S(2)}, u32[]{:S(2)}) collective-permute-start(bf16[272,256]{1,0:T(8,128)(2,1)S(1)} %shard_map.117.a_ref), channel_id=1, source_target_pairs={{0,1},{1,0},{2,3},{3,2},{4,5},{5,4},{6,7},{7,6},{8,9},{9,8},{10,11... | collective-permute-start | bytes 417800 | tf_op jit(solution)/shard_map/ppermute | solution.py:54
  34.4 6.5 %collective-permute-start.12 = (bf16[144,256]{1,0:T(8,128)(2,1)S(1)}, bf16[144,256]{1,0:T(8,128)(2,1)S(1)}, u32[]{:S(2)}, u32[]{:S(2)}) collective-permute-start(bf16[144,256]{1,0:T(8,128)(2,1)S(1)} %shard_map.119.a_ref), channel_id=1, source_target_pairs={{0,2},{1,3},{2,0},{3,1},{4,6},{5,7},{6,4},{7,5},{8,10},{9,11},{10,... | collective-permute-start | bytes 221192 | tf_op jit(solution)/shard_map/ppermute | solution.py:54
  36.4 4.5 %collective-permute-start.11 = (bf16[4,128,256]{2,1,0:T(8,128)(2,1)S(1)}, bf16[4,128,256]{2,1,0:T(8,128)(2,1)S(1)}, u32[]{:S(2)}, u32[]{:S(2)}) collective-permute-start(bf16[4,128,256]{2,1,0:T(8,128)(2,1)S(1)} %get-tuple-element.57), channel_id=1, source_target_pairs={{0,4},{4,0},{8,12},{12,8},{16,20},{20,16},{24,28},{28,24},{1,5},{5... | collective-permute-start | bytes 786440 | tf_op jit(solution)/shard_map/ppermute | solution.py:40
  41.0 6.9 %collective-permute-start.13 = (bf16[272,256]{1,0:T(8,128)(2,1)S(1)}, bf16[272,256]{1,0:T(8,128)(2,1)S(1)}, u32[]{:S(2)}, u32[]{:S(2)}) collective-permute-start(bf16[272,256]{1,0:T(8,128)(2,1)S(1)} %get-tuple-element.59), channel_id=1, source_target_pairs={{0,24},{4,28},{8,16},{12,20},{16,8},{20,12},{24,0},{28,4},{1,25},{... | collective-permute-start | bytes 417800 | tf_op jit(solution)/shard_map/ppermute | solution.py:50
  42.6 6.6 %collective-permute-start.14 = (bf16[272,256]{1,0:T(8,128)(2,1)S(1)}, bf16[272,256]{1,0:T(8,128)(2,1)S(1)}, u32[]{:S(2)}, u32[]{:S(2)}) collective-permute-start(bf16[272,256]{1,0:T(8,128)(2,1)S(1)} %get-tuple-element.60), channel_id=1, source_target_pairs={{0,16},{4,20},{8,24},{12,28},{16,0},{20,4},{24,8},{28,12},{1,17},{... | collective-permute-start | bytes 417800 | tf_op jit(solution)/shard_map/ppermute | solution.py:50
  43.2 6.0 %collective-permute-start.15 = (bf16[272,256]{1,0:T(8,128)(2,1)S(1)}, bf16[272,256]{1,0:T(8,128)(2,1)S(1)}, u32[]{:S(2)}, u32[]{:S(2)}) collective-permute-start(bf16[272,256]{1,0:T(8,128)(2,1)S(1)} %get-tuple-element.61), channel_id=1, source_target_pairs={{0,8},{4,12},{8,0},{12,4},{16,24},{20,28},{24,16},{28,20},{1,9},{5... | collective-permute-start | bytes 417800 | tf_op jit(solution)/shard_map/ppermute | solution.py:50
  49.3 1.4 %collective-permute-start.16 = (f32[128,256]{1,0:T(8,128)S(1)}, f32[128,256]{1,0:T(8,128)S(1)}, u32[]{:S(2)}, u32[]{:S(2)}) collective-permute-start(f32[128,256]{1,0:T(8,128)S(1)} %get-tuple-element.62.mine_ref), channel_id=1, source_target_pairs={{0,4},{4,0},{8,12},{12,8},{16,20},{20,16},{24,28},{28,24},{1,5},{5... | collective-permute-start | bytes 393224 | tf_op jit(solution)/shard_map/ppermute | solution.py:40

commit v7 on v6

--- a/solution.py
+++ b/solution.py
@@ -136,48 +136,20 @@
 
 def pointwise_kernel(cols, weight_ref, bias_ref, cot_ref, inv_ref, *refs):
     own_ref, *parts = refs[:cols]
-    out_ref, hidden_ref, keep_ref, bias_keep_ref, send_ref = refs[cols:]
-    width = out_ref.shape[1]
-    half = width // CORES
-    core = lax.rem(lax.axis_index("row"), CORES)
+    out_ref, message_ref = refs[cols:]
+    owned = out_ref.shape[0]
     inv = inv_ref[...]
     total = own_ref[...]
     for ref in parts:
         total = total + ref[...].astype(F32)
     agg = (total * inv).astype(BF16)
-    weight = weight_ref[...]
-    preact = jnp.dot(agg, weight, preferred_element_type=F32) + bias_ref[...]
+    preact = jnp.dot(agg, weight_ref[...], preferred_element_type=F32) + bias_ref[...]
     sig = jax.nn.sigmoid(preact)
     out_ref[...] = (preact * sig).astype(BF16)
-    grad_pre = (cot_ref[...].astype(F32) * sig * (1.0 + preact * (1.0 - sig))).astype(BF16)
-    hidden = lax.dot_general(grad_pre, weight, NT, preferred_element_type=F32)
-    hidden_ref[...] = (hidden * inv).astype(BF16)
-    term = lax.dot_general(agg, grad_pre, TN, preferred_element_type=F32)
-    low, high = term[:half], term[half:]
-    first = core == 0
-    keep_ref[...] = jnp.where(first, low, high)
-    send_ref[:half] = jnp.where(first, high, low).astype(BF16)
-    bias_sum = jnp.sum(grad_pre.astype(F32), axis=0, keepdims=True)
-    bias_keep_ref[...] = bias_sum
-    send_ref[half:] = pack_bias(bias_sum, EXTRA)
-
-
-def pair_sum_kernel(keep_ref, bias_keep_ref, got_ref, hidden_ref, out_ref):
-    owned, half = hidden_ref.shape[0], keep_ref.shape[0]
-    out_ref[:owned] = hidden_ref[...]
-    out_ref[owned : owned + half] = (keep_ref[...] + got_ref[:half].astype(F32)).astype(BF16)
-    out_ref[owned + half :] = pack_bias(bias_keep_ref[...] + add_bias(got_ref[half:]), EXTRA)
-
-
-def add_grads(half, a, b):
-    total = (a[:half].astype(F32) + b[:half].astype(F32)).astype(BF16)
-    return total, pack_bias(add_bias(a[half:]) + add_bias(b[half:]), EXTRA)
-
-
-def add_kernel(half, a_ref, b_ref, out_ref):
-    rows = half + EXTRA
-    a, b = (ref[ref.shape[0] - rows :] for ref in (a_ref, b_ref))
-    out_ref[:half], out_ref[half:] = add_grads(half, a, b)
+    grad_pre = (cot_ref[...].astype(F32) * sig * (1.0 + preact * (1.0 - sig))).astype(BF16).astype(F32)
+    message_ref[:owned] = (grad_pre * inv).astype(BF16)
+    message_ref[owned : 2 * owned] = total.astype(BF16)
+    message_ref[2 * owned :] = pack_bias(jnp.sum(grad_pre, axis=0, keepdims=True), EXTRA)
 
 
 def collect_kernel(*refs):
@@ -186,36 +158,70 @@
         out_ref[n] = ref[...]
 
 
-def backward_kernel(rows, cols, pos_hold_ref, count_ref, turned_ref, *refs):
-    own_ref, next_ref, far_ref, keep_ref, send_ref, hidden, acc, pos_ref, sem = refs
+def backward_kernel(rows, cols, pos_hold_ref, count_ref, turned_ref, weight_ref, *refs):
+    messages = refs[:cols]
+    keep_ref, grads_keep_ref, bias_keep_ref, send_ref = refs[cols : cols + 4]
+    rooted, sums, biases, hidden, acc, pos_ref, sem = refs[cols + 4 :]
     fetch = pltpu.make_async_copy(pos_hold_ref, pos_ref, sem)
     fetch.start()
     chips = rows // CORES
     row, col = lax.axis_index("row"), lax.axis_index("col")
-    hidden[0] = own_ref[...]
-    hidden[1] = next_ref[:BLOCK]
-    hidden[2:] = far_ref[...]
+    owned, width = rooted.shape[1:]
+    for k, ref in enumerate(messages):
+        owner = col ^ k if is_power(cols) else lax.rem(col - k + cols, cols)
+        rooted[owner] = ref[:owned]
+        sums[owner] = ref[owned : 2 * owned]
+        biases[owner] = ref[2 * owned :]
     acc[...] = jnp.zeros_like(acc)
+    for n in range(cols):
+        hidden[n] = lax.dot_general(
+            rooted[n], weight_ref[...], NT, preferred_element_type=F32
+        ).astype(BF16)
     fetch.wait()
 
     def add(s, live):
         p = pos_ref[0, 0, s]
         u, v = p // rows, lax.rem(p, rows)
-        src = offset_from(cols, col, u)
         k = offset_to(chips, row // CORES, v // CORES)
         dst = (lax.rem(v, CORES) ^ lax.rem(row, CORES)) * chips + k
-        acc[dst] += jnp.dot(turned_ref[s], hidden[src], preferred_element_type=F32)
+        acc[dst] += jnp.dot(turned_ref[s], hidden[u], preferred_element_type=F32)
 
     for_live(count_ref, turned_ref.shape[0], add)
     keep_ref[...] = acc[:chips]
-    send_ref[...] = acc[chips:].astype(BF16)
-
-
-def merge_kernel(keep_ref, got_ref, grads_ref, own_ref, *send):
-    own_ref[...] = keep_ref[0] + got_ref[0].astype(F32)
+    for k in range(chips):
+        send_ref[k * owned : (k + 1) * owned] = acc[chips + k].astype(BF16)
+
+    term = lax.dot_general(
+        sums[...].reshape(cols * owned, width),
+        rooted[...].reshape(cols * owned, width),
+        TN,
+        preferred_element_type=F32,
+    )
+    half = width // CORES
+    low, high = term[:half], term[half:]
+    first = lax.rem(row, CORES) == 0
+    grads_keep_ref[...] = jnp.where(first, low, high)
+    base = chips * owned
+    send_ref[base : base + half] = jnp.where(first, high, low).astype(BF16)
+    bias = jnp.sum(biases[...].astype(F32), axis=(0, 1)).reshape(1, width)
+    bias_keep_ref[...] = bias
+    send_ref[base + half :] = pack_bias(bias, EXTRA)
+
+
+def merge_kernel(keep_ref, grads_keep_ref, bias_keep_ref, got_ref, own_ref, grads_ref, *send):
+    chips, owned = keep_ref.shape[:2]
+    half = grads_keep_ref.shape[0]
+    base = chips * owned
+    grads = (grads_keep_ref[...] + got_ref[base : base + half].astype(F32)).astype(BF16)
+    bias = pack_bias(bias_keep_ref[...] + add_bias(got_ref[base + half :]), EXTRA)
+    grads_ref[:half] = grads
+    grads_ref[half:] = bias
+    own_ref[...] = keep_ref[0] + got_ref[:owned].astype(F32)
     for k, ref in enumerate(send, 1):
-        ref[:BLOCK] = (keep_ref[k] + got_ref[k].astype(F32)).astype(BF16)
-        ref[BLOCK:] = grads_ref[...]
+        part = got_ref[k * owned : (k + 1) * owned].astype(F32)
+        ref[:owned] = (keep_ref[k] + part).astype(BF16)
+        ref[owned : owned + half] = grads
+        ref[owned + half :] = bias
 
 
 def sum_grads_kernel(grads_ref, *refs):
@@ -291,41 +297,37 @@
     order = list(range(2, cols)) + [1]
     parts = [to_col(send[k - 1], cols, k) for k in order]
 
-    out_piece, hidden, keep, bias_keep, half_send = call(
+    out_piece, message = call(
         functools.partial(pointwise_kernel, cols),
         [VMEM] * (4 + cols),
-        [(piece, BF16), (piece, BF16), ((half, width), F32), ((1, width), F32), (grads_shape, BF16)],
+        [(piece, BF16), ((2 * owned + EXTRA, width), BF16)],
     )(weight, bias_vector, cotangent, inv, own, *parts)
-
-    half_got = to_core(half_send, rows)
-    far = [to_col(hidden, cols, k) for k in range(2, cols)]
-    message = call(
-        pair_sum_kernel, [VMEM] * 4, [((owned + half + EXTRA, width), BF16)], flops=LONG
-    )(keep, bias_keep, half_got, hidden)
-    next_to = to_col(message, cols, 1)
-    far = call(collect_kernel, [VMEM] * len(far), [((cols - 2,) + piece, BF16)], flops=LONG)(*far)
-    far, other = lax.optimization_barrier((far, next_to))
-    next_to, grads = other, message
-    add = call(functools.partial(add_kernel, half), [VMEM] * 2, [(grads_shape, BF16)], flops=LONG)
-    step = 2
-    while step < cols:
-        grads = add(grads, other)
-        other = to_col(grads, cols, step)
-        step *= 2
-
-    col_keep, col_send = call(
+    messages = {k: to_col(message, cols, k) for k in order}
+
+    col_keep, grads_keep, bias_keep, col_send = call(
         functools.partial(backward_kernel, rows, cols),
-        [VMEM, SMEM] + [VMEM] * 4,
-        [((chips,) + piece, F32), ((chips,) + piece, BF16)],
-        [pltpu.VMEM((cols,) + piece, BF16), pltpu.VMEM((rows,) + piece, F32), *fetched],
-        flops=LONG,
-    )(block_pos, block_count, turned, hidden, next_to, far)
-    grads = add(grads, other)
-    own_x, *send_x = call(
+        [VMEM, SMEM, VMEM, VMEM] + [VMEM] * cols,
+        [
+            ((chips,) + piece, F32),
+            ((half, width), F32),
+            ((1, width), F32),
+            ((chips * owned + half + EXTRA, width), BF16),
+        ],
+        [
+            pltpu.VMEM((cols,) + piece, BF16),
+            pltpu.VMEM((cols,) + piece, BF16),
+            pltpu.VMEM((cols, EXTRA, width), BF16),
+            pltpu.VMEM((cols,) + piece, BF16),
+            pltpu.VMEM((rows,) + piece, F32),
+            *fetched,
+        ],
+    )(block_pos, block_count, turned, weight, message, *(messages[k] for k in range(1, cols)))
+    own_x, grads, *send_x = call(
         merge_kernel,
-        [VMEM] * 3,
-        [(piece, F32)] + [((owned + half + EXTRA, width), BF16)] * (chips - 1),
-    )(col_keep, to_core(col_send, rows), grads)
+        [VMEM] * 4,
+        [(piece, F32), (grads_shape, BF16)]
+        + [((owned + half + EXTRA, width), BF16)] * (chips - 1),
+    )(col_keep, grads_keep, bias_keep, to_core(col_send, rows))
     parts_x = [to_chip(send_x[k - 1], rows, k) for k in range(chips - 1, 0, -1)]
 
     mine, bias_sum = call(

time: 51.8 us -> 53.9 us (1.041)
  waiting for transfers between devices: 25.3 us -> 28.6 us
  starting transfers between devices: 18.1 us -> 16.8 us
    ppermute x4 -> x3, waiting for transfers between devices: 2.86 us -> 4.48 us  [to_core(): return lax.ppermute(x, 'row', [(i, i ^ 1) for i in range(rows)])]
    ppermute x6, waiting for transfers between devices: 6.7 us -> 8.12 us  [to_chip(): return lax.ppermute(x, 'row', pairs)]
    ppermute x7 -> x6, starting transfers between devices: 9.66 us -> 8.46 us  [to_col(): lax.ppermute(x, 'col', [(i, target(cols, i, k)) for i in range(cols)])]
    pallas_call x6 -> x2, Pallas kernels: 1.28 us -> 1.52 us  [the longest x1 1.44 us: per_device(): call(functools.partial(backward_kernel, rows, cols), [VMEM, SMEM, VMEM, V...]
    ppermute x7 -> x6, waiting for transfers between devices: 15.7 us -> 16 us  [to_col(): lax.ppermute(x, 'col', [(i, target(cols, i, k)) for i in range(cols)])]
  transfers between devices with their start and end apart: 17 -> 15, of which waited for: 13 -> 12; matrix products, arithmetic and copies ran while one was open for 0% -> 0% of each run, Pallas kernels for 4% -> 1%
where the time goes in v7:
time: 53.9 us; the launch traced here: 53.6 us
  waiting for transfers between devices  28.6 us (53%)
  starting transfers between devices  16.8 us (31%)
  Pallas kernels  4.56 us (8%)
  local copies, waits for them, and re-layouts  2.17 us (4%)
  between operations  1.41 us (3%)
    ppermute x6, waiting for transfers between devices, to_col(): lax.ppermute(x, 'col', [(i, target(cols, i, k)) for i in range(cols)])  16 us
    ppermute x6, starting transfers between devices, to_col(): lax.ppermute(x, 'col', [(i, target(cols, i, k)) for i in range(cols)])  8.46 us
    ppermute x6, starting transfers between devices, to_chip(): return lax.ppermute(x, 'row', pairs)  8.16 us
    ppermute x6, waiting for transfers between devices, to_chip(): return lax.ppermute(x, 'row', pairs)  8.12 us
    ppermute x3, waiting for transfers between devices, to_core(): return lax.ppermute(x, 'row', [(i, i ^ 1) for i in range(rows)])  4.48 us
    unnamed x14, local copies, waits for them, and re-layouts  2.17 us
    pallas_call x1, Pallas kernels, per_device(): call(functools.partial(backward_kernel, rows, cols), [VMEM, SMEM, VMEM, V...  1.44 us
  transfers between devices with their start and end apart: 15, of which 12 were waited for; matrix products, arithmetic and copies ran while one was open for 0% of the time, Pallas kernels for 1%

profile of v7, /device:TPU:0, one launch (start us, length us, event | category | flops | bytes accessed | tf_op | source)
XLA Modules:
  0.0 53.6 jit_solution(1679899394686181966)
XLA Ops:
  0.6 0.0 copy-start.4
  0.6 0.6 %copy-done.4 = s32[128]{0:T(128)S(1)} copy-done((s32[128]{0:T(128)S(1)}, s32[128]{0:T(128)}, u32[]{:S(2)}) %copy-start.4) | copy-done | bytes 536
  1.3 0.8 %copy-done.2 = bf16[128,256]{1,0:T(8,128)(2,1)S(1)} copy-done((bf16[128,256]{1,0:T(8,128)(2,1)S(1)}, bf16[128,256]{1,0:T(8,128)(2,1)}, u32[]{:S(2)}) %copy-start.2) | copy-done | bytes 65560
  2.1 0.1 shard_map.112
  2.2 4.0 %collective-permute-start.2 = (bf16[128,256]{1,0:T(8,128)(2,1)S(1)}, bf16[128,256]{1,0:T(8,128)(2,1)S(1)}, u32[]{:S(2)}, u32[]{:S(2)}) collective-permute-start(bf16[128,256]{1,0:T(8,128)(2,1)S(1)} %get-tuple-element.37.refs_0_), channel_id=1, source_target_pairs={{0,24},{4,28},{8,16},{12,20},{16,8},{20,12},{24,0},{28,4},{1,25},{... | collective-permute-start | bytes 196616 | tf_op jit(solution)/shard_map/ppermute | solution.py:50
  6.2 0.5 collective-permute-start.1
  6.7 0.1 collective-permute-start
  7.5 0.0 copy-start.6
  7.5 0.0 copy-done.5
  7.5 0.7 %copy-done.6 = f32[256]{0:T(256)S(1)} copy-done((f32[256]{0:T(256)S(1)}, f32[256]{0:T(256)}, u32[]{:S(2)}) %copy-start.6) | copy-done | bytes 1048
  8.2 0.8 %shard_map.111 = (bf16[16,128,128]{2,1,0:T(8,128)(2,1)S(1)}, bf16[16,128,128]{2,1,0:T(8,128)(2,1)S(1)}, f32[1,256]{1,0:T(1,128)S(1)}) custom-call(s32[1,1]{1,0:T(1,128)S(6)} %copy.12.count_ref, s32[1,1,16,512]{3,2,1,0:T(8,128)S(1)} %copy-done.5, f32[1,256]{1,0:T(1,128)S(1)} %bitcast.4), custom_call_target="tpu_custom_call" | custom-call | flops 4000000000 | bytes 1000000 | tf_op jit(solution)/shard_map/pallas_call | solution.py:281
  9.0 0.0 collective-permute-done.2.refs_3_
  9.0 1.5 %collective-permute-done.1.refs_2_ = bf16[128,256]{1,0:T(8,128)(2,1)S(1)} collective-permute-done((bf16[128,256]{1,0:T(8,128)(2,1)S(1)}, bf16[128,256]{1,0:T(8,128)(2,1)S(1)}, u32[]{:S(2)}, u32[]{:S(2)}) %collective-permute-start.1) | collective-permute-done | bytes 65568 | tf_op jit(solution)/shard_map/ppermute | solution.py:50
  10.5 0.5 collective-permute-done.refs_1_
  11.0 0.0 copy-start
  11.0 0.0 copy-start.1
  11.0 0.1 collective-permute-start.3
  11.1 1.5 %collective-permute-done.3.next_ref = bf16[4,128,256]{2,1,0:T(8,128)(2,1)S(1)} collective-permute-done((bf16[4,128,256]{2,1,0:T(8,128)(2,1)S(1)}, bf16[4,128,256]{2,1,0:T(8,128)(2,1)S(1)}, u32[]{:S(2)}, u32[]{:S(2)}) %collective-permute-start.3) | collective-permute-done | bytes 262176 | tf_op jit(solution)/shard_map/ppermute | solution.py:40
  12.6 0.0 copy-done.3
  12.6 1.1 %shard_map.114 = (f32[128,256]{1,0:T(8,128)S(1)}, bf16[128,256]{1,0:T(8,128)(2,1)S(1)}, bf16[128,256]{1,0:T(8,128)(2,1)S(1)}, bf16[128,256]{1,0:T(8,128)(2,1)S(1)}) custom-call(s32[1,1,16]{2,1,0:T(1,128)S(1)} %copy-done.3, s32[1,1]{1,0:T(1,128)S(6)} %copy.12.count_ref, bf16[16,128,128]{2,1,0:T(8,128)(2,1)S(1)} %get-tuple-element.38.blocks_ref, ...), custom_call_target="tpu_custom_call" | custom-call | flops 1000000 | bytes 1000000 | tf_op jit(solution)/shard_map/pallas_call | solution.py:291
  13.7 2.7 %collective-permute-start.4 = (bf16[128,256]{1,0:T(8,128)(2,1)S(1)}, bf16[128,256]{1,0:T(8,128)(2,1)S(1)}, u32[]{:S(2)}, u32[]{:S(2)}) collective-permute-start(bf16[128,256]{1,0:T(8,128)(2,1)S(1)} %get-tuple-element.43), channel_id=1, source_target_pairs={{0,2},{1,3},{2,0},{3,1},{4,6},{5,7},{6,4},{7,5},{8,10},{9,11},{10,... | collective-permute-start | bytes 196616 | tf_op jit(solution)/shard_map/ppermute | solution.py:54
  16.4 1.3 %collective-permute-start.5 = (bf16[128,256]{1,0:T(8,128)(2,1)S(1)}, bf16[128,256]{1,0:T(8,128)(2,1)S(1)}, u32[]{:S(2)}, u32[]{:S(2)}) collective-permute-start(bf16[128,256]{1,0:T(8,128)(2,1)S(1)} %get-tuple-element.44), channel_id=1, source_target_pairs={{0,3},{1,2},{2,1},{3,0},{4,7},{5,6},{6,5},{7,4},{8,11},{9,10},{10,... | collective-permute-start | bytes 196616 | tf_op jit(solution)/shard_map/ppermute | solution.py:54
  17.7 0.0 collective-permute-start.6
  17.7 3.7 %collective-permute-done.4.refs_1_ = bf16[128,256]{1,0:T(8,128)(2,1)S(1)} collective-permute-done((bf16[128,256]{1,0:T(8,128)(2,1)S(1)}, bf16[128,256]{1,0:T(8,128)(2,1)S(1)}, u32[]{:S(2)}, u32[]{:S(2)}) %collective-permute-start.4) | collective-permute-done | bytes 65568 | tf_op jit(solution)/shard_map/ppermute | solution.py:54
  21.4 1.2 %collective-permute-done.5.refs_2_ = bf16[128,256]{1,0:T(8,128)(2,1)S(1)} collective-permute-done((bf16[128,256]{1,0:T(8,128)(2,1)S(1)}, bf16[128,256]{1,0:T(8,128)(2,1)S(1)}, u32[]{:S(2)}, u32[]{:S(2)}) %collective-permute-start.5) | collective-permute-done | bytes 65568 | tf_op jit(solution)/shard_map/ppermute | solution.py:54
  22.6 0.4 collective-permute-done.6.refs_3_
  23.1 0.0 copy-done
  23.1 0.0 copy-done.1
  23.1 0.2 shard_map.115
  23.3 2.9 %collective-permute-start.9 = (bf16[272,256]{1,0:T(8,128)(2,1)S(1)}, bf16[272,256]{1,0:T(8,128)(2,1)S(1)}, u32[]{:S(2)}, u32[]{:S(2)}) collective-permute-start(bf16[272,256]{1,0:T(8,128)(2,1)S(1)} %get-tuple-element.48.refs_0_), channel_id=1, source_target_pairs={{0,3},{1,2},{2,1},{3,0},{4,7},{5,6},{6,5},{7,4},{8,11},{9,10},{10,... | collective-permute-start | bytes 417800 | tf_op jit(solution)/shard_map/ppermute | solution.py:54
  26.2 0.0 collective-permute-start.8
  26.2 1.6 %collective-permute-start.7 = (bf16[272,256]{1,0:T(8,128)(2,1)S(1)}, bf16[272,256]{1,0:T(8,128)(2,1)S(1)}, u32[]{:S(2)}, u32[]{:S(2)}) collective-permute-start(bf16[272,256]{1,0:T(8,128)(2,1)S(1)} %get-tuple-element.48.refs_0_), channel_id=1, source_target_pairs={{0,1},{1,0},{2,3},{3,2},{4,5},{5,4},{6,7},{7,6},{8,9},{9,8},{10,11... | collective-permute-start | bytes 417800 | tf_op jit(solution)/shard_map/ppermute | solution.py:54
  27.8 4.1 %collective-permute-done.9.refs_3_ = bf16[272,256]{1,0:T(8,128)(2,1)S(1)} collective-permute-done((bf16[272,256]{1,0:T(8,128)(2,1)S(1)}, bf16[272,256]{1,0:T(8,128)(2,1)S(1)}, u32[]{:S(2)}, u32[]{:S(2)}) %collective-permute-start.9) | collective-permute-done | bytes 139296 | tf_op jit(solution)/shard_map/ppermute | solution.py:54
  31.8 6.6 %collective-permute-done.8.refs_2_ = bf16[272,256]{1,0:T(8,128)(2,1)S(1)} collective-permute-done((bf16[272,256]{1,0:T(8,128)(2,1)S(1)}, bf16[272,256]{1,0:T(8,128)(2,1)S(1)}, u32[]{:S(2)}, u32[]{:S(2)}) %collective-permute-start.8) | collective-permute-done | bytes 139296 | tf_op jit(solution)/shard_map/ppermute | solution.py:54
  38.4 0.0 collective-permute-done.7.refs_1_
  38.4 1.4 %shard_map.116 = (f32[4,128,256]{2,1,0:T(8,128)S(1)}, f32[128,256]{1,0:T(8,128)S(1)}, f32[1,256]{1,0:T(1,128)S(1)}, bf16[656,256]{1,0:T(8,128)(2,1)S(1)}) custom-call(s32[1,1,16]{2,1,0:T(1,128)S(1)} %copy-done.3, s32[1,1]{1,0:T(1,128)S(6)} %copy.12.count_ref, bf16[16,128,128]{2,1,0:T(8,128)(2,1)S(1)} %get-tuple-element.47.turned_ref, ...), custom_call_target="tpu_custom_call" | custom-call | flops 1000000 | bytes 1000000 | tf_op jit(solution)/shard_map/pallas_call | solution.py:307
  39.9 0.1 collective-permute-start.10
  39.9 1.6 %collective-permute-done.10.got_ref = bf16[656,256]{1,0:T(8,128)(2,1)S(1)} collective-permute-done((bf16[656,256]{1,0:T(8,128)(2,1)S(1)}, bf16[656,256]{1,0:T(8,128)(2,1)S(1)}, u32[]{:S(2)}, u32[]{:S(2)}) %collective-permute-start.10) | collective-permute-done | bytes 335904 | tf_op jit(solution)/shard_map/ppermute | solution.py:40
  41.6 0.1 shard_map.117
  41.6 1.4 %collective-permute-start.11 = (bf16[272,256]{1,0:T(8,128)(2,1)S(1)}, bf16[272,256]{1,0:T(8,128)(2,1)S(1)}, u32[]{:S(2)}, u32[]{:S(2)}) collective-permute-start(bf16[272,256]{1,0:T(8,128)(2,1)S(1)} %get-tuple-element.55), channel_id=1, source_target_pairs={{0,24},{4,28},{8,16},{12,20},{16,8},{20,12},{24,0},{28,4},{1,25},{... | collective-permute-start | bytes 417800 | tf_op jit(solution)/shard_map/ppermute | solution.py:50
  43.1 0.7 %collective-permute-start.12 = (bf16[272,256]{1,0:T(8,128)(2,1)S(1)}, bf16[272,256]{1,0:T(8,128)(2,1)S(1)}, u32[]{:S(2)}, u32[]{:S(2)}) collective-permute-start(bf16[272,256]{1,0:T(8,128)(2,1)S(1)} %get-tuple-element.56), channel_id=1, source_target_pairs={{0,16},{4,20},{8,24},{12,28},{16,0},{20,4},{24,8},{28,12},{1,17},{... | collective-permute-start | bytes 417800 | tf_op jit(solution)/shard_map/ppermute | solution.py:50
  43.8 1.4 %collective-permute-start.13 = (bf16[272,256]{1,0:T(8,128)(2,1)S(1)}, bf16[272,256]{1,0:T(8,128)(2,1)S(1)}, u32[]{:S(2)}, u32[]{:S(2)}) collective-permute-start(bf16[272,256]{1,0:T(8,128)(2,1)S(1)} %get-tuple-element.57), channel_id=1, source_target_pairs={{0,8},{4,12},{8,0},{12,4},{16,24},{20,28},{24,16},{28,20},{1,9},{5... | collective-permute-start | bytes 417800 | tf_op jit(solution)/shard_map/ppermute | solution.py:50
  45.2 4.0 %collective-permute-done.11.refs_0_ = bf16[272,256]{1,0:T(8,128)(2,1)S(1)} collective-permute-done((bf16[272,256]{1,0:T(8,128)(2,1)S(1)}, bf16[272,256]{1,0:T(8,128)(2,1)S(1)}, u32[]{:S(2)}, u32[]{:S(2)}) %collective-permute-start.11) | collective-permute-done | bytes 139296 | tf_op jit(solution)/shard_map/ppermute | solution.py:50
  49.2 2.1 %collective-permute-done.12.refs_1_ = bf16[272,256]{1,0:T(8,128)(2,1)S(1)} collective-permute-done((bf16[272,256]{1,0:T(8,128)(2,1)S(1)}, bf16[272,256]{1,0:T(8,128)(2,1)S(1)}, u32[]{:S(2)}, u32[]{:S(2)}) %collective-permute-start.12) | collective-permute-done | bytes 139296 | tf_op jit(solution)/shard_map/ppermute | solution.py:50
  51.3 0.0 collective-permute-done.13.refs_2_
  51.4 0.1 collective-permute-start.14
  51.4 1.3 %collective-permute-done.14.theirs_ref = f32[128,256]{1,0:T(8,128)S(1)} collective-permute-done((f32[128,256]{1,0:T(8,128)S(1)}, f32[128,256]{1,0:T(8,128)S(1)}, u32[]{:S(2)}, u32[]{:S(2)}) %collective-permute-start.14) | collective-permute-done | bytes 131104 | tf_op jit(solution)/shard_map/ppermute | solution.py:40
  52.8 0.8 %shard_map.119 = (bf16[128,256]{1,0:T(8,128)(2,1)}, bf16[128,256]{1,0:T(8,128)(2,1)}, f32[256,256]{1,0:T(8,128)}, f32[1,256]{1,0:T(1,128)}) custom-call(bf16[128,256]{1,0:T(8,128)(2,1)S(1)} %get-tuple-element.46.out_ref, f32[128,256]{1,0:T(8,128)S(1)} %get-tuple-element.35.inv_ref, f32[128,256]{1,0:T(8,128)S(1)} %get-tuple-element.53.own_ref, ...), custom_call_target="tpu_custom_call" | custom-call | flops 1000000 | bytes 1000000 | tf_op jit(solution)/shard_map/pallas_call | solution.py:338
  (5 shorter events, 0.1 us)
Async XLA Ops:
  0.6 0.7 %copy-start.4 = (s32[128]{0:T(128)S(1)}, s32[128]{0:T(128)}, u32[]{:S(2)}) copy-start(s32[128]{0:T(128)} %param.9) | copy-start | bytes 1540
  1.3 0.8 %copy-start.2 = (bf16[128,256]{1,0:T(8,128)(2,1)S(1)}, bf16[128,256]{1,0:T(8,128)(2,1)}, u32[]{:S(2)}) copy-start(bf16[128,256]{1,0:T(8,128)(2,1)} %features_ref.1) | copy-start | bytes 196612
  2.1 5.4 %copy-start.5 = (s32[1,1,16,512]{3,2,1,0:T(8,128)S(1)}, s32[1,1,16,512]{3,2,1,0:T(8,128)}, u32[]{:S(2)}) copy-start(s32[1,1,16,512]{3,2,1,0:T(8,128)} %edge_ref.1) | copy-start | bytes 98308
  2.2 6.7 %collective-permute-start.2 = (bf16[128,256]{1,0:T(8,128)(2,1)S(1)}, bf16[128,256]{1,0:T(8,128)(2,1)S(1)}, u32[]{:S(2)}, u32[]{:S(2)}) collective-permute-start(bf16[128,256]{1,0:T(8,128)(2,1)S(1)} %get-tuple-element.37.refs_0_), channel_id=1, source_target_pairs={{0,24},{4,28},{8,16},{12,20},{16,8},{20,12},{24,0},{28,4},{1,25},{... | collective-permute-start | bytes 196616 | tf_op jit(solution)/shard_map/ppermute | solution.py:50
  6.2 4.3 %collective-permute-start.1 = (bf16[128,256]{1,0:T(8,128)(2,1)S(1)}, bf16[128,256]{1,0:T(8,128)(2,1)S(1)}, u32[]{:S(2)}, u32[]{:S(2)}) collective-permute-start(bf16[128,256]{1,0:T(8,128)(2,1)S(1)} %get-tuple-element.37.refs_0_), channel_id=1, source_target_pairs={{0,16},{4,20},{8,24},{12,28},{16,0},{20,4},{24,8},{28,12},{1,17},{... | collective-permute-start | bytes 196616 | tf_op jit(solution)/shard_map/ppermute | solution.py:50
  6.7 4.3 %collective-permute-start = (bf16[128,256]{1,0:T(8,128)(2,1)S(1)}, bf16[128,256]{1,0:T(8,128)(2,1)S(1)}, u32[]{:S(2)}, u32[]{:S(2)}) collective-permute-start(bf16[128,256]{1,0:T(8,128)(2,1)S(1)} %get-tuple-element.37.refs_0_), channel_id=1, source_target_pairs={{0,8},{4,12},{8,0},{12,4},{16,24},{20,28},{24,16},{28,20},{1,9},{5... | collective-permute-start | bytes 196616 | tf_op jit(solution)/shard_map/ppermute | solution.py:50
  7.5 0.7 %copy-start.6 = (f32[256]{0:T(256)S(1)}, f32[256]{0:T(256)}, u32[]{:S(2)}) copy-start(f32[256]{0:T(256)} %param.11) | copy-start | bytes 3076
  11.0 1.7 %copy-start.3 = (s32[1,1,16]{2,1,0:T(1,128)S(1)}, s32[1,1,16]{2,1,0:T(1,128)}, u32[]{:S(2)}) copy-start(s32[1,1,16]{2,1,0:T(1,128)} %pos_hold_ref.3) | copy-start | bytes 196
  11.0 12.1 %copy-start = (bf16[256,256]{1,0:T(8,128)(2,1)S(1)}, bf16[256,256]{1,0:T(8,128)(2,1)}, u32[]{:S(2)}) copy-start(bf16[256,256]{1,0:T(8,128)(2,1)} %weight_ref.3) | copy-start | bytes 393220
  11.0 12.1 %copy-start.1 = (bf16[128,256]{1,0:T(8,128)(2,1)S(1)}, bf16[128,256]{1,0:T(8,128)(2,1)}, u32[]{:S(2)}) copy-start(bf16[128,256]{1,0:T(8,128)(2,1)} %cot_ref.1) | copy-start | bytes 196612
  11.0 1.6 %collective-permute-start.3 = (bf16[4,128,256]{2,1,0:T(8,128)(2,1)S(1)}, bf16[4,128,256]{2,1,0:T(8,128)(2,1)S(1)}, u32[]{:S(2)}, u32[]{:S(2)}) collective-permute-start(bf16[4,128,256]{2,1,0:T(8,128)(2,1)S(1)} %shard_map.113.near_ref), channel_id=1, source_target_pairs={{0,4},{4,0},{8,12},{12,8},{16,20},{20,16},{24,28},{28,24},{1,5},{5... | collective-permute-start | bytes 786440 | tf_op jit(solution)/shard_map/ppermute | solution.py:40
  13.7 7.7 %collective-permute-start.4 = (bf16[128,256]{1,0:T(8,128)(2,1)S(1)}, bf16[128,256]{1,0:T(8,128)(2,1)S(1)}, u32[]{:S(2)}, u32[]{:S(2)}) collective-permute-start(bf16[128,256]{1,0:T(8,128)(2,1)S(1)} %get-tuple-element.43), channel_id=1, source_target_pairs={{0,2},{1,3},{2,0},{3,1},{4,6},{5,7},{6,4},{7,5},{8,10},{9,11},{10,... | collective-permute-start | bytes 196616 | tf_op jit(solution)/shard_map/ppermute | solution.py:54
  16.4 6.3 %collective-permute-start.5 = (bf16[128,256]{1,0:T(8,128)(2,1)S(1)}, bf16[128,256]{1,0:T(8,128)(2,1)S(1)}, u32[]{:S(2)}, u32[]{:S(2)}) collective-permute-start(bf16[128,256]{1,0:T(8,128)(2,1)S(1)} %get-tuple-element.44), channel_id=1, source_target_pairs={{0,3},{1,2},{2,1},{3,0},{4,7},{5,6},{6,5},{7,4},{8,11},{9,10},{10,... | collective-permute-start | bytes 196616 | tf_op jit(solution)/shard_map/ppermute | solution.py:54
  17.7 5.4 %collective-permute-start.6 = (bf16[128,256]{1,0:T(8,128)(2,1)S(1)}, bf16[128,256]{1,0:T(8,128)(2,1)S(1)}, u32[]{:S(2)}, u32[]{:S(2)}) collective-permute-start(bf16[128,256]{1,0:T(8,128)(2,1)S(1)} %get-tuple-element.45), channel_id=1, source_target_pairs={{0,1},{1,0},{2,3},{3,2},{4,5},{5,4},{6,7},{7,6},{8,9},{9,8},{10,11... | collective-permute-start | bytes 196616 | tf_op jit(solution)/shard_map/ppermute | solution.py:54
  23.3 8.5 %collective-permute-start.9 = (bf16[272,256]{1,0:T(8,128)(2,1)S(1)}, bf16[272,256]{1,0:T(8,128)(2,1)S(1)}, u32[]{:S(2)}, u32[]{:S(2)}) collective-permute-start(bf16[272,256]{1,0:T(8,128)(2,1)S(1)} %get-tuple-element.48.refs_0_), channel_id=1, source_target_pairs={{0,3},{1,2},{2,1},{3,0},{4,7},{5,6},{6,5},{7,4},{8,11},{9,10},{10,... | collective-permute-start | bytes 417800 | tf_op jit(solution)/shard_map/ppermute | solution.py:54
  26.2 12.2 %collective-permute-start.8 = (bf16[272,256]{1,0:T(8,128)(2,1)S(1)}, bf16[272,256]{1,0:T(8,128)(2,1)S(1)}, u32[]{:S(2)}, u32[]{:S(2)}) collective-permute-start(bf16[272,256]{1,0:T(8,128)(2,1)S(1)} %get-tuple-element.48.refs_0_), channel_id=1, source_target_pairs={{0,2},{1,3},{2,0},{3,1},{4,6},{5,7},{6,4},{7,5},{8,10},{9,11},{10,... | collective-permute-start | bytes 417800 | tf_op jit(solution)/shard_map/ppermute | solution.py:54
  26.2 12.2 %collective-permute-start.7 = (bf16[272,256]{1,0:T(8,128)(2,1)S(1)}, bf16[272,256]{1,0:T(8,128)(2,1)S(1)}, u32[]{:S(2)}, u32[]{:S(2)}) collective-permute-start(bf16[272,256]{1,0:T(8,128)(2,1)S(1)} %get-tuple-element.48.refs_0_), channel_id=1, source_target_pairs={{0,1},{1,0},{2,3},{3,2},{4,5},{5,4},{6,7},{7,6},{8,9},{9,8},{10,11... | collective-permute-start | bytes 417800 | tf_op jit(solution)/shard_map/ppermute | solution.py:54
  39.9 1.7 %collective-permute-start.10 = (bf16[656,256]{1,0:T(8,128)(2,1)S(1)}, bf16[656,256]{1,0:T(8,128)(2,1)S(1)}, u32[]{:S(2)}, u32[]{:S(2)}) collective-permute-start(bf16[656,256]{1,0:T(8,128)(2,1)S(1)} %get-tuple-element.52), channel_id=1, source_target_pairs={{0,4},{4,0},{8,12},{12,8},{16,20},{20,16},{24,28},{28,24},{1,5},{5... | collective-permute-start | bytes 1007624 | tf_op jit(solution)/shard_map/ppermute | solution.py:40
  41.6 7.5 %collective-permute-start.11 = (bf16[272,256]{1,0:T(8,128)(2,1)S(1)}, bf16[272,256]{1,0:T(8,128)(2,1)S(1)}, u32[]{:S(2)}, u32[]{:S(2)}) collective-permute-start(bf16[272,256]{1,0:T(8,128)(2,1)S(1)} %get-tuple-element.55), channel_id=1, source_target_pairs={{0,24},{4,28},{8,16},{12,20},{16,8},{20,12},{24,0},{28,4},{1,25},{... | collective-permute-start | bytes 417800 | tf_op jit(solution)/shard_map/ppermute | solution.py:50
  43.1 8.2 %collective-permute-start.12 = (bf16[272,256]{1,0:T(8,128)(2,1)S(1)}, bf16[272,256]{1,0:T(8,128)(2,1)S(1)}, u32[]{:S(2)}, u32[]{:S(2)}) collective-permute-start(bf16[272,256]{1,0:T(8,128)(2,1)S(1)} %get-tuple-element.56), channel_id=1, source_target_pairs={{0,16},{4,20},{8,24},{12,28},{16,0},{20,4},{24,8},{28,12},{1,17},{... | collective-permute-start | bytes 417800 | tf_op jit(solution)/shard_map/ppermute | solution.py:50
  43.8 7.5 %collective-permute-start.13 = (bf16[272,256]{1,0:T(8,128)(2,1)S(1)}, bf16[272,256]{1,0:T(8,128)(2,1)S(1)}, u32[]{:S(2)}, u32[]{:S(2)}) collective-permute-start(bf16[272,256]{1,0:T(8,128)(2,1)S(1)} %get-tuple-element.57), channel_id=1, source_target_pairs={{0,8},{4,12},{8,0},{12,4},{16,24},{20,28},{24,16},{28,20},{1,9},{5... | collective-permute-start | bytes 417800 | tf_op jit(solution)/shard_map/ppermute | solution.py:50
  51.4 1.4 %collective-permute-start.14 = (f32[128,256]{1,0:T(8,128)S(1)}, f32[128,256]{1,0:T(8,128)S(1)}, u32[]{:S(2)}, u32[]{:S(2)}) collective-permute-start(f32[128,256]{1,0:T(8,128)S(1)} %get-tuple-element.58.mine_ref), channel_id=1, source_target_pairs={{0,4},{4,0},{8,12},{12,8},{16,20},{20,16},{24,28},{28,24},{1,5},{5... | collective-permute-start | bytes 393224 | tf_op jit(solution)/shard_map/ppermute | solution.py:40

commit v8 on v6

--- a/solution.py
+++ b/solution.py
@@ -162,22 +162,36 @@
     send_ref[half:] = pack_bias(bias_sum, EXTRA)
 
 
-def pair_sum_kernel(keep_ref, bias_keep_ref, got_ref, hidden_ref, out_ref):
-    owned, half = hidden_ref.shape[0], keep_ref.shape[0]
-    out_ref[:owned] = hidden_ref[...]
-    out_ref[owned : owned + half] = (keep_ref[...] + got_ref[:half].astype(F32)).astype(BF16)
-    out_ref[owned + half :] = pack_bias(bias_keep_ref[...] + add_bias(got_ref[half:]), EXTRA)
-
-
-def add_grads(half, a, b):
-    total = (a[:half].astype(F32) + b[:half].astype(F32)).astype(BF16)
-    return total, pack_bias(add_bias(a[half:]) + add_bias(b[half:]), EXTRA)
-
-
-def add_kernel(half, a_ref, b_ref, out_ref):
-    rows = half + EXTRA
-    a, b = (ref[ref.shape[0] - rows :] for ref in (a_ref, b_ref))
-    out_ref[:half], out_ref[half:] = add_grads(half, a, b)
+def pair_sum_kernel(keep_ref, bias_keep_ref, got_ref, out_ref):
+    half = keep_ref.shape[0]
+    out_ref[:half] = (keep_ref[...] + got_ref[:half].astype(F32)).astype(BF16)
+    out_ref[half:] = pack_bias(bias_keep_ref[...] + add_bias(got_ref[half:]), EXTRA)
+
+
+def total_of(n, me, refs, stage):
+    for k, ref in enumerate(refs):
+        owner = me ^ k if is_power(n) else lax.rem(me - k + n, n)
+        stage[owner] = ref[...]
+    half = stage.shape[1] - EXTRA
+    grads, bias = stage[0, :half].astype(F32), add_bias(stage[0, half:])
+    for i in range(1, n):
+        grads = grads + stage[i, :half].astype(F32)
+        bias = bias + add_bias(stage[i, half:])
+    return grads, bias
+
+
+def chip_sum_kernel(*refs):
+    *parts, out_ref, stage = refs
+    chip = lax.axis_index("row") // CORES
+    grads, bias = total_of(len(parts), chip, parts, stage)
+    half = grads.shape[0]
+    out_ref[:half] = grads.astype(BF16)
+    out_ref[half:] = pack_bias(bias, EXTRA)
+
+
+def col_sum_kernel(*refs):
+    *parts, half_ref, bias_ref, stage = refs
+    half_ref[...], bias_ref[...] = total_of(len(parts), lax.axis_index("col"), parts, stage)
 
 
 def collect_kernel(*refs):
@@ -187,14 +201,14 @@
 
 
 def backward_kernel(rows, cols, pos_hold_ref, count_ref, turned_ref, *refs):
-    own_ref, next_ref, far_ref, keep_ref, send_ref, hidden, acc, pos_ref, sem = refs
+    parts = refs[:cols]
+    keep_ref, send_ref, hidden, acc, pos_ref, sem = refs[cols:]
     fetch = pltpu.make_async_copy(pos_hold_ref, pos_ref, sem)
     fetch.start()
     chips = rows // CORES
     row, col = lax.axis_index("row"), lax.axis_index("col")
-    hidden[0] = own_ref[...]
-    hidden[1] = next_ref[:BLOCK]
-    hidden[2:] = far_ref[...]
+    for k, ref in enumerate(parts):
+        hidden[k] = ref[...]
     acc[...] = jnp.zeros_like(acc)
     fetch.wait()
 
@@ -211,32 +225,24 @@
     send_ref[...] = acc[chips:].astype(BF16)
 
 
-def merge_kernel(keep_ref, got_ref, grads_ref, own_ref, *send):
+def merge_kernel(keep_ref, got_ref, own_ref, *send):
     own_ref[...] = keep_ref[0] + got_ref[0].astype(F32)
     for k, ref in enumerate(send, 1):
-        ref[:BLOCK] = (keep_ref[k] + got_ref[k].astype(F32)).astype(BF16)
-        ref[BLOCK:] = grads_ref[...]
-
-
-def sum_grads_kernel(grads_ref, *refs):
-    *parts, half_ref, bias_ref = refs
-    half = half_ref.shape[0]
-    grads = grads_ref[:half].astype(F32)
-    bias = add_bias(grads_ref[half:])
-    for ref in parts:
-        grads = grads + ref[BLOCK : BLOCK + half].astype(F32)
-        bias = bias + add_bias(ref[BLOCK + half :])
-    half_ref[...] = grads
-    bias_ref[...] = bias
-
-
-def finish_kernel(norm, out_ref, inv_ref, own_ref, mine_ref, theirs_ref, bias_ref, *refs):
-    *parts, output_ref, grad_x_ref, grad_w_ref, grad_b_ref = refs
-    output_ref[...] = out_ref[...]
+        ref[...] = (keep_ref[k] + got_ref[k].astype(F32)).astype(BF16)
+
+
+def owned_sum_kernel(inv_ref, own_ref, *refs):
+    *parts, out_ref = refs
     total = own_ref[...]
     for ref in parts:
-        total = total + ref[:BLOCK].astype(F32)
-    grad_x_ref[...] = (total * inv_ref[...]).astype(BF16)
+        total = total + ref[...].astype(F32)
+    out_ref[...] = (total * inv_ref[...]).astype(BF16)
+
+
+def finish_kernel(norm, out_ref, x_ref, mine_ref, theirs_ref, bias_ref, *refs):
+    output_ref, grad_x_ref, grad_w_ref, grad_b_ref = refs
+    output_ref[...] = out_ref[...]
+    grad_x_ref[...] = x_ref[...]
     half = mine_ref.shape[0]
     first = lax.rem(lax.axis_index("row"), CORES) == 0
     mine, theirs = mine_ref[...] * norm, theirs_ref[...] * norm
@@ -297,47 +303,49 @@
         [(piece, BF16), (piece, BF16), ((half, width), F32), ((1, width), F32), (grads_shape, BF16)],
     )(weight, bias_vector, cotangent, inv, own, *parts)
 
-    half_got = to_core(half_send, rows)
-    far = [to_col(hidden, cols, k) for k in range(2, cols)]
-    message = call(
-        pair_sum_kernel, [VMEM] * 4, [((owned + half + EXTRA, width), BF16)], flops=LONG
-    )(keep, bias_keep, half_got, hidden)
-    next_to = to_col(message, cols, 1)
-    far = call(collect_kernel, [VMEM] * len(far), [((cols - 2,) + piece, BF16)], flops=LONG)(*far)
-    far, other = lax.optimization_barrier((far, next_to))
-    next_to, grads = other, message
-    add = call(functools.partial(add_kernel, half), [VMEM] * 2, [(grads_shape, BF16)], flops=LONG)
-    step = 2
-    while step < cols:
-        grads = add(grads, other)
-        other = to_col(grads, cols, step)
-        step *= 2
+    hidden_parts = {k: to_col(hidden, cols, k) for k in order}
+    grads = call(pair_sum_kernel, [VMEM] * 3, [(grads_shape, BF16)])(
+        keep, bias_keep, to_core(half_send, rows)
+    )
+    across = range(chips - 1, 0, -1)
+    grad_parts = {k: to_chip(grads, rows, k) for k in across}
+    grads = call(
+        chip_sum_kernel,
+        [VMEM] * chips,
+        [(grads_shape, BF16)],
+        [pltpu.VMEM((chips,) + grads_shape, BF16)],
+    )(grads, *(grad_parts[k] for k in range(1, chips)))
 
     col_keep, col_send = call(
         functools.partial(backward_kernel, rows, cols),
-        [VMEM, SMEM] + [VMEM] * 4,
+        [VMEM, SMEM, VMEM] + [VMEM] * cols,
         [((chips,) + piece, F32), ((chips,) + piece, BF16)],
         [pltpu.VMEM((cols,) + piece, BF16), pltpu.VMEM((rows,) + piece, F32), *fetched],
         flops=LONG,
-    )(block_pos, block_count, turned, hidden, next_to, far)
-    grads = add(grads, other)
+    )(block_pos, block_count, turned, hidden, *(hidden_parts[k] for k in range(1, cols)))
+    col_send, grads = lax.optimization_barrier((col_send, grads))
+    grad_parts = {k: to_col(grads, cols, k) for k in order}
     own_x, *send_x = call(
-        merge_kernel,
-        [VMEM] * 3,
-        [(piece, F32)] + [((owned + half + EXTRA, width), BF16)] * (chips - 1),
-    )(col_keep, to_core(col_send, rows), grads)
-    parts_x = [to_chip(send_x[k - 1], rows, k) for k in range(chips - 1, 0, -1)]
+        merge_kernel, [VMEM] * 2, [(piece, F32)] + [(piece, BF16)] * (chips - 1)
+    )(col_keep, to_core(col_send, rows))
+    parts_x = [to_chip(send_x[k - 1], rows, k) for k in across]
 
     mine, bias_sum = call(
-        sum_grads_kernel, [VMEM] * chips, [((half, width), F32), ((1, width), F32)]
-    )(grads, *parts_x)
+        col_sum_kernel,
+        [VMEM] * cols,
+        [((half, width), F32), ((1, width), F32)],
+        [pltpu.VMEM((cols,) + grads_shape, BF16)],
+    )(grads, *(grad_parts[k] for k in range(1, cols)))
     theirs = to_core(mine, rows)
+    x_piece = call(owned_sum_kernel, [VMEM] * (1 + chips), [(piece, BF16)], flops=LONG)(
+        inv, own_x, *parts_x
+    )
     norm = float((owned * rows * cols) ** -0.5)
     output, grad_x, grad_w, grad_b = call(
         functools.partial(finish_kernel, norm),
-        [VMEM] * (5 + chips),
+        [VMEM] * 5,
         [(piece, BF16), (piece, BF16), ((width, width), F32), ((1, width), F32)],
-    )(out_piece, inv, own_x, mine, theirs, bias_sum, *parts_x)
+    )(out_piece, x_piece, mine, theirs, bias_sum)
     return (output, grad_x, grad_w, grad_b.reshape(width))
 
 

time: 51.8 us -> 48.1 us (0.929)
  waiting for transfers between devices: 25.3 us -> 14.7 us
  starting transfers between devices: 18.1 us -> 24.9 us
    ppermute x7 -> x9, waiting for transfers between devices: 15.7 us -> 9.06 us  [to_col(): lax.ppermute(x, 'col', [(i, target(cols, i, k)) for i in range(cols)])]
    ppermute x7 -> x9, starting transfers between devices: 9.66 us -> 13.1 us  [to_col(): lax.ppermute(x, 'col', [(i, target(cols, i, k)) for i in range(cols)])]
    ppermute x6 -> x9, starting transfers between devices: 8.16 us -> 11.5 us  [to_chip(): return lax.ppermute(x, 'row', pairs)]
    ppermute x6 -> x9, waiting for transfers between devices: 6.7 us -> 3.64 us  [to_chip(): return lax.ppermute(x, 'row', pairs)]
    ppermute x4, waiting for transfers between devices: 2.86 us -> 1.97 us  [to_core(): return lax.ppermute(x, 'row', [(i, i ^ 1) for i in range(rows)])]
    pallas_call x8 -> x7, Pallas kernels: 2.13 us -> 2.18 us  [the longest x1 1.1 us: per_device(): call(functools.partial(backward_kernel, rows, cols), [VMEM, SMEM, VMEM] +...]
  transfers between devices with their start and end apart: 17 -> 22, of which waited for: 13 -> 14; matrix products, arithmetic and copies ran while one was open for 0% -> 0% of each run, Pallas kernels for 4% -> 4%
where the time goes in v8:
time: 48.1 us; the launch traced here: 47.7 us
  starting transfers between devices  24.9 us (52%)
  waiting for transfers between devices  14.7 us (31%)
  Pallas kernels  4.52 us (9%)
  local copies, waits for them, and re-layouts  2.17 us (5%)
  between operations  1.45 us (3%)
    ppermute x9, starting transfers between devices, to_col(): lax.ppermute(x, 'col', [(i, target(cols, i, k)) for i in range(cols)])  13.1 us
    ppermute x9, starting transfers between devices, to_chip(): return lax.ppermute(x, 'row', pairs)  11.5 us
    ppermute x9, waiting for transfers between devices, to_col(): lax.ppermute(x, 'col', [(i, target(cols, i, k)) for i in range(cols)])  9.06 us
    ppermute x9, waiting for transfers between devices, to_chip(): return lax.ppermute(x, 'row', pairs)  3.64 us
    unnamed x14, local copies, waits for them, and re-layouts  2.17 us
    ppermute x4, waiting for transfers between devices, to_core(): return lax.ppermute(x, 'row', [(i, i ^ 1) for i in range(rows)])  1.97 us
    pallas_call x1, Pallas kernels, per_device(): call(functools.partial(backward_kernel, rows, cols), [VMEM, SMEM, VMEM] +...  1.1 us
    pallas_call x1, Pallas kernels, per_device(): call(functools.partial(forward_kernel, rows, cols), [VMEM, SMEM, VMEM, VM...  1.07 us
  transfers between devices with their start and end apart: 22, of which 14 were waited for; matrix products, arithmetic and copies ran while one was open for 0% of the time, Pallas kernels for 4%

profile of v8, /device:TPU:0, one launch (start us, length us, event | category | flops | bytes accessed | tf_op | source)
XLA Modules:
  0.0 47.7 jit_solution(1284963790557469387)
XLA Ops:
  0.6 0.6 %copy-done.4 = s32[128]{0:T(128)S(1)} copy-done((s32[128]{0:T(128)S(1)}, s32[128]{0:T(128)}, u32[]{:S(2)}) %copy-start.4) | copy-done | bytes 536
  1.3 0.8 %copy-done.2 = bf16[128,256]{1,0:T(8,128)(2,1)S(1)} copy-done((bf16[128,256]{1,0:T(8,128)(2,1)S(1)}, bf16[128,256]{1,0:T(8,128)(2,1)}, u32[]{:S(2)}) %copy-start.2) | copy-done | bytes 65560
  2.1 0.1 shard_map.112
  2.2 4.0 %collective-permute-start.2 = (bf16[128,256]{1,0:T(8,128)(2,1)S(1)}, bf16[128,256]{1,0:T(8,128)(2,1)S(1)}, u32[]{:S(2)}, u32[]{:S(2)}) collective-permute-start(bf16[128,256]{1,0:T(8,128)(2,1)S(1)} %get-tuple-element.39.refs_0_), channel_id=1, source_target_pairs={{0,24},{4,28},{8,16},{12,20},{16,8},{20,12},{24,0},{28,4},{1,25},{... | collective-permute-start | bytes 196616 | tf_op jit(solution)/shard_map/ppermute | solution.py:50
  6.2 0.5 %collective-permute-start.1 = (bf16[128,256]{1,0:T(8,128)(2,1)S(1)}, bf16[128,256]{1,0:T(8,128)(2,1)S(1)}, u32[]{:S(2)}, u32[]{:S(2)}) collective-permute-start(bf16[128,256]{1,0:T(8,128)(2,1)S(1)} %get-tuple-element.39.refs_0_), channel_id=1, source_target_pairs={{0,16},{4,20},{8,24},{12,28},{16,0},{20,4},{24,8},{28,12},{1,17},{... | collective-permute-start | bytes 196616 | tf_op jit(solution)/shard_map/ppermute | solution.py:50
  6.7 0.1 collective-permute-start
  7.5 0.7 %copy-done.6 = f32[256]{0:T(256)S(1)} copy-done((f32[256]{0:T(256)S(1)}, f32[256]{0:T(256)}, u32[]{:S(2)}) %copy-start.6) | copy-done | bytes 1048
  8.2 0.8 %shard_map.111 = (bf16[16,128,128]{2,1,0:T(8,128)(2,1)S(1)}, bf16[16,128,128]{2,1,0:T(8,128)(2,1)S(1)}, f32[1,256]{1,0:T(1,128)S(1)}) custom-call(s32[1,1]{1,0:T(1,128)S(6)} %copy.12.count_ref, s32[1,1,16,512]{3,2,1,0:T(8,128)S(1)} %copy-done.5, f32[1,256]{1,0:T(1,128)S(1)} %bitcast.4), custom_call_target="tpu_custom_call" | custom-call | flops 4000000000 | bytes 1000000 | tf_op jit(solution)/shard_map/pallas_call | solution.py:281
  9.0 1.5 %collective-permute-done.1.refs_2_ = bf16[128,256]{1,0:T(8,128)(2,1)S(1)} collective-permute-done((bf16[128,256]{1,0:T(8,128)(2,1)S(1)}, bf16[128,256]{1,0:T(8,128)(2,1)S(1)}, u32[]{:S(2)}, u32[]{:S(2)}) %collective-permute-start.1) | collective-permute-done | bytes 65568 | tf_op jit(solution)/shard_map/ppermute | solution.py:50
  10.5 0.5 %collective-permute-done.refs_1_ = bf16[128,256]{1,0:T(8,128)(2,1)S(1)} collective-permute-done((bf16[128,256]{1,0:T(8,128)(2,1)S(1)}, bf16[128,256]{1,0:T(8,128)(2,1)S(1)}, u32[]{:S(2)}, u32[]{:S(2)}) %collective-permute-start) | collective-permute-done | bytes 65568 | tf_op jit(solution)/shard_map/ppermute | solution.py:50
  11.0 0.0 copy-start.1
  11.0 0.1 collective-permute-start.3
  11.1 1.5 %collective-permute-done.3.next_ref = bf16[4,128,256]{2,1,0:T(8,128)(2,1)S(1)} collective-permute-done((bf16[4,128,256]{2,1,0:T(8,128)(2,1)S(1)}, bf16[4,128,256]{2,1,0:T(8,128)(2,1)S(1)}, u32[]{:S(2)}, u32[]{:S(2)}) %collective-permute-start.3) | collective-permute-done | bytes 262176 | tf_op jit(solution)/shard_map/ppermute | solution.py:40
  12.6 1.1 %shard_map.114 = (f32[128,256]{1,0:T(8,128)S(1)}, bf16[128,256]{1,0:T(8,128)(2,1)S(1)}, bf16[128,256]{1,0:T(8,128)(2,1)S(1)}, bf16[128,256]{1,0:T(8,128)(2,1)S(1)}) custom-call(s32[1,1,16]{2,1,0:T(1,128)S(1)} %copy-done.3, s32[1,1]{1,0:T(1,128)S(6)} %copy.12.count_ref, bf16[16,128,128]{2,1,0:T(8,128)(2,1)S(1)} %get-tuple-element.40.blocks_ref, ...), custom_call_target="tpu_custom_call" | custom-call | flops 1000000 | bytes 1000000 | tf_op jit(solution)/shard_map/pallas_call | solution.py:291
  13.7 2.7 %collective-permute-start.4 = (bf16[128,256]{1,0:T(8,128)(2,1)S(1)}, bf16[128,256]{1,0:T(8,128)(2,1)S(1)}, u32[]{:S(2)}, u32[]{:S(2)}) collective-permute-start(bf16[128,256]{1,0:T(8,128)(2,1)S(1)} %get-tuple-element.45), channel_id=1, source_target_pairs={{0,2},{1,3},{2,0},{3,1},{4,6},{5,7},{6,4},{7,5},{8,10},{9,11},{10,... | collective-permute-start | bytes 196616 | tf_op jit(solution)/shard_map/ppermute | solution.py:54
  16.4 1.3 %collective-permute-start.5 = (bf16[128,256]{1,0:T(8,128)(2,1)S(1)}, bf16[128,256]{1,0:T(8,128)(2,1)S(1)}, u32[]{:S(2)}, u32[]{:S(2)}) collective-permute-start(bf16[128,256]{1,0:T(8,128)(2,1)S(1)} %get-tuple-element.46), channel_id=1, source_target_pairs={{0,3},{1,2},{2,1},{3,0},{4,7},{5,6},{6,5},{7,4},{8,11},{9,10},{10,... | collective-permute-start | bytes 196616 | tf_op jit(solution)/shard_map/ppermute | solution.py:54
  17.7 0.2 collective-permute-start.6
  17.9 3.5 %collective-permute-done.4.refs_1_ = bf16[128,256]{1,0:T(8,128)(2,1)S(1)} collective-permute-done((bf16[128,256]{1,0:T(8,128)(2,1)S(1)}, bf16[128,256]{1,0:T(8,128)(2,1)S(1)}, u32[]{:S(2)}, u32[]{:S(2)}) %collective-permute-start.4) | collective-permute-done | bytes 65568 | tf_op jit(solution)/shard_map/ppermute | solution.py:54
  21.4 1.2 %collective-permute-done.5.refs_2_ = bf16[128,256]{1,0:T(8,128)(2,1)S(1)} collective-permute-done((bf16[128,256]{1,0:T(8,128)(2,1)S(1)}, bf16[128,256]{1,0:T(8,128)(2,1)S(1)}, u32[]{:S(2)}, u32[]{:S(2)}) %collective-permute-start.5) | collective-permute-done | bytes 65568 | tf_op jit(solution)/shard_map/ppermute | solution.py:54
  22.6 0.4 collective-permute-done.6.refs_3_
  23.1 0.4 shard_map.115
  23.5 0.1 collective-permute-start.10
  23.6 2.9 %collective-permute-start.9 = (bf16[128,256]{1,0:T(8,128)(2,1)S(1)}, bf16[128,256]{1,0:T(8,128)(2,1)S(1)}, u32[]{:S(2)}, u32[]{:S(2)}) collective-permute-start(bf16[128,256]{1,0:T(8,128)(2,1)S(1)} %get-tuple-element.50.refs_0_), channel_id=1, source_target_pairs={{0,3},{1,2},{2,1},{3,0},{4,7},{5,6},{6,5},{7,4},{8,11},{9,10},{10,... | collective-permute-start | bytes 196616 | tf_op jit(solution)/shard_map/ppermute | solution.py:54
  26.4 1.6 %collective-permute-start.7 = (bf16[128,256]{1,0:T(8,128)(2,1)S(1)}, bf16[128,256]{1,0:T(8,128)(2,1)S(1)}, u32[]{:S(2)}, u32[]{:S(2)}) collective-permute-start(bf16[128,256]{1,0:T(8,128)(2,1)S(1)} %get-tuple-element.50.refs_0_), channel_id=1, source_target_pairs={{0,1},{1,0},{2,3},{3,2},{4,5},{5,4},{6,7},{7,6},{8,9},{9,8},{10,11... | collective-permute-start | bytes 196616 | tf_op jit(solution)/shard_map/ppermute | solution.py:54
  28.0 1.6 %collective-permute-start.13 = (bf16[144,256]{1,0:T(8,128)(2,1)S(1)}, bf16[144,256]{1,0:T(8,128)(2,1)S(1)}, u32[]{:S(2)}, u32[]{:S(2)}) collective-permute-start(bf16[144,256]{1,0:T(8,128)(2,1)S(1)} %shard_map.117.refs_0_), channel_id=1, source_target_pairs={{0,24},{4,28},{8,16},{12,20},{16,8},{20,12},{24,0},{28,4},{1,25},{... | collective-permute-start | bytes 221192 | tf_op jit(solution)/shard_map/ppermute | solution.py:50
  29.6 0.4 collective-permute-start.12
  30.1 0.2 collective-permute-done.9.refs_3_
  30.3 1.3 %collective-permute-start.11 = (bf16[144,256]{1,0:T(8,128)(2,1)S(1)}, bf16[144,256]{1,0:T(8,128)(2,1)S(1)}, u32[]{:S(2)}, u32[]{:S(2)}) collective-permute-start(bf16[144,256]{1,0:T(8,128)(2,1)S(1)} %shard_map.117.refs_0_), channel_id=1, source_target_pairs={{0,8},{4,12},{8,0},{12,4},{16,24},{20,28},{24,16},{28,20},{1,9},{5... | collective-permute-start | bytes 221192 | tf_op jit(solution)/shard_map/ppermute | solution.py:50
  31.6 1.3 %collective-permute-done.8.refs_2_ = bf16[128,256]{1,0:T(8,128)(2,1)S(1)} collective-permute-done((bf16[128,256]{1,0:T(8,128)(2,1)S(1)}, bf16[128,256]{1,0:T(8,128)(2,1)S(1)}, u32[]{:S(2)}, u32[]{:S(2)}) %collective-permute-start.8) | collective-permute-done | bytes 65568 | tf_op jit(solution)/shard_map/ppermute | solution.py:54
  32.9 1.1 %shard_map.116 = (f32[4,128,256]{2,1,0:T(8,128)S(1)}, bf16[4,128,256]{2,1,0:T(8,128)(2,1)S(1)}) custom-call(s32[1,1,16]{2,1,0:T(1,128)S(1)} %copy-done.3, s32[1,1]{1,0:T(1,128)S(6)} %copy.12.count_ref, bf16[16,128,128]{2,1,0:T(8,128)(2,1)S(1)} %get-tuple-element.49.turned_ref, bf16[128,256]{1,0:T(8,128)(2,1)S(1)} %get-tuple-element.50.refs_0_, ...), custom_call_target="tpu_custom_call" | custom-call | flops 4000000000 | bytes 1000000 | tf_op jit(solution)/shard_map/pallas_call | solution.py:319
  34.0 0.4 collective-permute-done.12.refs_2_
  34.4 0.4 collective-permute-done.11.refs_1_
  34.8 0.1 shard_map.118.refs_0_
  34.9 0.1 collective-permute-start.14
  34.9 2.9 %collective-permute-start.20 = (bf16[144,256]{1,0:T(8,128)(2,1)S(1)}, bf16[144,256]{1,0:T(8,128)(2,1)S(1)}, u32[]{:S(2)}, u32[]{:S(2)}) collective-permute-start(bf16[144,256]{1,0:T(8,128)(2,1)S(1)} %shard_map.118.refs_0_), channel_id=1, source_target_pairs={{0,3},{1,2},{2,1},{3,0},{4,7},{5,6},{6,5},{7,4},{8,11},{9,10},{10,... | collective-permute-start | bytes 221192 | tf_op jit(solution)/shard_map/ppermute | solution.py:54
  37.9 0.2 collective-permute-start.19
  38.1 1.3 %collective-permute-start.18 = (bf16[144,256]{1,0:T(8,128)(2,1)S(1)}, bf16[144,256]{1,0:T(8,128)(2,1)S(1)}, u32[]{:S(2)}, u32[]{:S(2)}) collective-permute-start(bf16[144,256]{1,0:T(8,128)(2,1)S(1)} %shard_map.118.refs_0_), channel_id=1, source_target_pairs={{0,1},{1,0},{2,3},{3,2},{4,5},{5,4},{6,7},{7,6},{8,9},{9,8},{10,11... | collective-permute-start | bytes 221192 | tf_op jit(solution)/shard_map/ppermute | solution.py:54
  39.4 0.1 shard_map.119
  39.5 2.6 %collective-permute-start.15 = (bf16[128,256]{1,0:T(8,128)(2,1)S(1)}, bf16[128,256]{1,0:T(8,128)(2,1)S(1)}, u32[]{:S(2)}, u32[]{:S(2)}) collective-permute-start(bf16[128,256]{1,0:T(8,128)(2,1)S(1)} %get-tuple-element.58), channel_id=1, source_target_pairs={{0,24},{4,28},{8,16},{12,20},{16,8},{20,12},{24,0},{28,4},{1,25},{... | collective-permute-start | bytes 196616 | tf_op jit(solution)/shard_map/ppermute | solution.py:50
  42.0 0.2 collective-permute-start.16
  42.2 0.8 %collective-permute-start.17 = (bf16[128,256]{1,0:T(8,128)(2,1)S(1)}, bf16[128,256]{1,0:T(8,128)(2,1)S(1)}, u32[]{:S(2)}, u32[]{:S(2)}) collective-permute-start(bf16[128,256]{1,0:T(8,128)(2,1)S(1)} %get-tuple-element.60), channel_id=1, source_target_pairs={{0,8},{4,12},{8,0},{12,4},{16,24},{20,28},{24,16},{28,20},{1,9},{5... | collective-permute-start | bytes 196616 | tf_op jit(solution)/shard_map/ppermute | solution.py:50
  43.0 2.4 %collective-permute-done.19.refs_2_ = bf16[144,256]{1,0:T(8,128)(2,1)S(1)} collective-permute-done((bf16[144,256]{1,0:T(8,128)(2,1)S(1)}, bf16[144,256]{1,0:T(8,128)(2,1)S(1)}, u32[]{:S(2)}, u32[]{:S(2)}) %collective-permute-start.19) | collective-permute-done | bytes 73760 | tf_op jit(solution)/shard_map/ppermute | solution.py:54
  45.4 0.1 shard_map.121
  45.5 0.1 collective-permute-start.21
  45.6 0.7 %collective-permute-done.16.refs_1_ = bf16[128,256]{1,0:T(8,128)(2,1)S(1)} collective-permute-done((bf16[128,256]{1,0:T(8,128)(2,1)S(1)}, bf16[128,256]{1,0:T(8,128)(2,1)S(1)}, u32[]{:S(2)}, u32[]{:S(2)}) %collective-permute-start.16) | collective-permute-done | bytes 65568 | tf_op jit(solution)/shard_map/ppermute | solution.py:50
  46.3 0.2 collective-permute-done.17.refs_2_
  46.5 0.4 collective-permute-done.21.theirs_ref
  46.9 0.8 %shard_map.122 = (bf16[128,256]{1,0:T(8,128)(2,1)}, bf16[128,256]{1,0:T(8,128)(2,1)}, f32[256,256]{1,0:T(8,128)}, f32[1,256]{1,0:T(1,128)}) custom-call(bf16[128,256]{1,0:T(8,128)(2,1)S(1)} %get-tuple-element.48.out_ref, bf16[128,256]{1,0:T(8,128)(2,1)S(1)} %shard_map.120.x_ref, f32[128,256]{1,0:T(8,128)S(1)} %get-tuple-element.62.mine_ref, ...), custom_call_target="tpu_custom_call" | custom-call | flops 1000000 | bytes 1000000 | tf_op jit(solution)/shard_map/pallas_call | solution.py:344
  (22 shorter events, 0.1 us)
Async XLA Ops:
  0.6 0.7 %copy-start.4 = (s32[128]{0:T(128)S(1)}, s32[128]{0:T(128)}, u32[]{:S(2)}) copy-start(s32[128]{0:T(128)} %param.9) | copy-start | bytes 1540
  1.3 0.8 %copy-start.2 = (bf16[128,256]{1,0:T(8,128)(2,1)S(1)}, bf16[128,256]{1,0:T(8,128)(2,1)}, u32[]{:S(2)}) copy-start(bf16[128,256]{1,0:T(8,128)(2,1)} %features_ref.1) | copy-start | bytes 196612
  2.1 5.4 %copy-start.5 = (s32[1,1,16,512]{3,2,1,0:T(8,128)S(1)}, s32[1,1,16,512]{3,2,1,0:T(8,128)}, u32[]{:S(2)}) copy-start(s32[1,1,16,512]{3,2,1,0:T(8,128)} %edge_ref.1) | copy-start | bytes 98308
  2.2 6.7 %collective-permute-start.2 = (bf16[128,256]{1,0:T(8,128)(2,1)S(1)}, bf16[128,256]{1,0:T(8,128)(2,1)S(1)}, u32[]{:S(2)}, u32[]{:S(2)}) collective-permute-start(bf16[128,256]{1,0:T(8,128)(2,1)S(1)} %get-tuple-element.39.refs_0_), channel_id=1, source_target_pairs={{0,24},{4,28},{8,16},{12,20},{16,8},{20,12},{24,0},{28,4},{1,25},{... | collective-permute-start | bytes 196616 | tf_op jit(solution)/shard_map/ppermute | solution.py:50
  6.2 4.3 %collective-permute-start.1 = (bf16[128,256]{1,0:T(8,128)(2,1)S(1)}, bf16[128,256]{1,0:T(8,128)(2,1)S(1)}, u32[]{:S(2)}, u32[]{:S(2)}) collective-permute-start(bf16[128,256]{1,0:T(8,128)(2,1)S(1)} %get-tuple-element.39.refs_0_), channel_id=1, source_target_pairs={{0,16},{4,20},{8,24},{12,28},{16,0},{20,4},{24,8},{28,12},{1,17},{... | collective-permute-start | bytes 196616 | tf_op jit(solution)/shard_map/ppermute | solution.py:50
  6.7 4.3 %collective-permute-start = (bf16[128,256]{1,0:T(8,128)(2,1)S(1)}, bf16[128,256]{1,0:T(8,128)(2,1)S(1)}, u32[]{:S(2)}, u32[]{:S(2)}) collective-permute-start(bf16[128,256]{1,0:T(8,128)(2,1)S(1)} %get-tuple-element.39.refs_0_), channel_id=1, source_target_pairs={{0,8},{4,12},{8,0},{12,4},{16,24},{20,28},{24,16},{28,20},{1,9},{5... | collective-permute-start | bytes 196616 | tf_op jit(solution)/shard_map/ppermute | solution.py:50
  7.5 0.7 %copy-start.6 = (f32[256]{0:T(256)S(1)}, f32[256]{0:T(256)}, u32[]{:S(2)}) copy-start(f32[256]{0:T(256)} %param.11) | copy-start | bytes 3076
  11.0 1.7 %copy-start.3 = (s32[1,1,16]{2,1,0:T(1,128)S(1)}, s32[1,1,16]{2,1,0:T(1,128)}, u32[]{:S(2)}) copy-start(s32[1,1,16]{2,1,0:T(1,128)} %pos_hold_ref.3) | copy-start | bytes 196
  11.0 12.1 %copy-start = (bf16[256,256]{1,0:T(8,128)(2,1)S(1)}, bf16[256,256]{1,0:T(8,128)(2,1)}, u32[]{:S(2)}) copy-start(bf16[256,256]{1,0:T(8,128)(2,1)} %weight_ref.1) | copy-start | bytes 393220
  11.0 12.1 %copy-start.1 = (bf16[128,256]{1,0:T(8,128)(2,1)S(1)}, bf16[128,256]{1,0:T(8,128)(2,1)}, u32[]{:S(2)}) copy-start(bf16[128,256]{1,0:T(8,128)(2,1)} %cot_ref.1) | copy-start | bytes 196612
  11.0 1.6 %collective-permute-start.3 = (bf16[4,128,256]{2,1,0:T(8,128)(2,1)S(1)}, bf16[4,128,256]{2,1,0:T(8,128)(2,1)S(1)}, u32[]{:S(2)}, u32[]{:S(2)}) collective-permute-start(bf16[4,128,256]{2,1,0:T(8,128)(2,1)S(1)} %shard_map.113.near_ref), channel_id=1, source_target_pairs={{0,4},{4,0},{8,12},{12,8},{16,20},{20,16},{24,28},{28,24},{1,5},{5... | collective-permute-start | bytes 786440 | tf_op jit(solution)/shard_map/ppermute | solution.py:40
  13.7 7.7 %collective-permute-start.4 = (bf16[128,256]{1,0:T(8,128)(2,1)S(1)}, bf16[128,256]{1,0:T(8,128)(2,1)S(1)}, u32[]{:S(2)}, u32[]{:S(2)}) collective-permute-start(bf16[128,256]{1,0:T(8,128)(2,1)S(1)} %get-tuple-element.45), channel_id=1, source_target_pairs={{0,2},{1,3},{2,0},{3,1},{4,6},{5,7},{6,4},{7,5},{8,10},{9,11},{10,... | collective-permute-start | bytes 196616 | tf_op jit(solution)/shard_map/ppermute | solution.py:54
  16.4 6.3 %collective-permute-start.5 = (bf16[128,256]{1,0:T(8,128)(2,1)S(1)}, bf16[128,256]{1,0:T(8,128)(2,1)S(1)}, u32[]{:S(2)}, u32[]{:S(2)}) collective-permute-start(bf16[128,256]{1,0:T(8,128)(2,1)S(1)} %get-tuple-element.46), channel_id=1, source_target_pairs={{0,3},{1,2},{2,1},{3,0},{4,7},{5,6},{6,5},{7,4},{8,11},{9,10},{10,... | collective-permute-start | bytes 196616 | tf_op jit(solution)/shard_map/ppermute | solution.py:54
  17.7 5.4 %collective-permute-start.6 = (bf16[128,256]{1,0:T(8,128)(2,1)S(1)}, bf16[128,256]{1,0:T(8,128)(2,1)S(1)}, u32[]{:S(2)}, u32[]{:S(2)}) collective-permute-start(bf16[128,256]{1,0:T(8,128)(2,1)S(1)} %get-tuple-element.47), channel_id=1, source_target_pairs={{0,1},{1,0},{2,3},{3,2},{4,5},{5,4},{6,7},{7,6},{8,9},{9,8},{10,11... | collective-permute-start | bytes 196616 | tf_op jit(solution)/shard_map/ppermute | solution.py:54
  23.5 4.5 %collective-permute-start.10 = (bf16[144,256]{1,0:T(8,128)(2,1)S(1)}, bf16[144,256]{1,0:T(8,128)(2,1)S(1)}, u32[]{:S(2)}, u32[]{:S(2)}) collective-permute-start(bf16[144,256]{1,0:T(8,128)(2,1)S(1)} %get-tuple-element.55), channel_id=1, source_target_pairs={{0,4},{4,0},{8,12},{12,8},{16,20},{20,16},{24,28},{28,24},{1,5},{5... | collective-permute-start | bytes 221192 | tf_op jit(solution)/shard_map/ppermute | solution.py:40
  23.6 6.8 %collective-permute-start.9 = (bf16[128,256]{1,0:T(8,128)(2,1)S(1)}, bf16[128,256]{1,0:T(8,128)(2,1)S(1)}, u32[]{:S(2)}, u32[]{:S(2)}) collective-permute-start(bf16[128,256]{1,0:T(8,128)(2,1)S(1)} %get-tuple-element.50.refs_0_), channel_id=1, source_target_pairs={{0,3},{1,2},{2,1},{3,0},{4,7},{5,6},{6,5},{7,4},{8,11},{9,10},{10,... | collective-permute-start | bytes 196616 | tf_op jit(solution)/shard_map/ppermute | solution.py:54
  26.4 6.4 %collective-permute-start.8 = (bf16[128,256]{1,0:T(8,128)(2,1)S(1)}, bf16[128,256]{1,0:T(8,128)(2,1)S(1)}, u32[]{:S(2)}, u32[]{:S(2)}) collective-permute-start(bf16[128,256]{1,0:T(8,128)(2,1)S(1)} %get-tuple-element.50.refs_0_), channel_id=1, source_target_pairs={{0,2},{1,3},{2,0},{3,1},{4,6},{5,7},{6,4},{7,5},{8,10},{9,11},{10,... | collective-permute-start | bytes 196616 | tf_op jit(solution)/shard_map/ppermute | solution.py:54
  26.4 6.4 %collective-permute-start.7 = (bf16[128,256]{1,0:T(8,128)(2,1)S(1)}, bf16[128,256]{1,0:T(8,128)(2,1)S(1)}, u32[]{:S(2)}, u32[]{:S(2)}) collective-permute-start(bf16[128,256]{1,0:T(8,128)(2,1)S(1)} %get-tuple-element.50.refs_0_), channel_id=1, source_target_pairs={{0,1},{1,0},{2,3},{3,2},{4,5},{5,4},{6,7},{7,6},{8,9},{9,8},{10,11... | collective-permute-start | bytes 196616 | tf_op jit(solution)/shard_map/ppermute | solution.py:54
  28.0 5.9 %collective-permute-start.13 = (bf16[144,256]{1,0:T(8,128)(2,1)S(1)}, bf16[144,256]{1,0:T(8,128)(2,1)S(1)}, u32[]{:S(2)}, u32[]{:S(2)}) collective-permute-start(bf16[144,256]{1,0:T(8,128)(2,1)S(1)} %shard_map.117.refs_0_), channel_id=1, source_target_pairs={{0,24},{4,28},{8,16},{12,20},{16,8},{20,12},{24,0},{28,4},{1,25},{... | collective-permute-start | bytes 221192 | tf_op jit(solution)/shard_map/ppermute | solution.py:50
  29.6 4.7 %collective-permute-start.12 = (bf16[144,256]{1,0:T(8,128)(2,1)S(1)}, bf16[144,256]{1,0:T(8,128)(2,1)S(1)}, u32[]{:S(2)}, u32[]{:S(2)}) collective-permute-start(bf16[144,256]{1,0:T(8,128)(2,1)S(1)} %shard_map.117.refs_0_), channel_id=1, source_target_pairs={{0,16},{4,20},{8,24},{12,28},{16,0},{20,4},{24,8},{28,12},{1,17},{... | collective-permute-start | bytes 221192 | tf_op jit(solution)/shard_map/ppermute | solution.py:50
  30.3 4.5 %collective-permute-start.11 = (bf16[144,256]{1,0:T(8,128)(2,1)S(1)}, bf16[144,256]{1,0:T(8,128)(2,1)S(1)}, u32[]{:S(2)}, u32[]{:S(2)}) collective-permute-start(bf16[144,256]{1,0:T(8,128)(2,1)S(1)} %shard_map.117.refs_0_), channel_id=1, source_target_pairs={{0,8},{4,12},{8,0},{12,4},{16,24},{20,28},{24,16},{28,20},{1,9},{5... | collective-permute-start | bytes 221192 | tf_op jit(solution)/shard_map/ppermute | solution.py:50
  34.9 4.5 %collective-permute-start.14 = (bf16[4,128,256]{2,1,0:T(8,128)(2,1)S(1)}, bf16[4,128,256]{2,1,0:T(8,128)(2,1)S(1)}, u32[]{:S(2)}, u32[]{:S(2)}) collective-permute-start(bf16[4,128,256]{2,1,0:T(8,128)(2,1)S(1)} %get-tuple-element.56), channel_id=1, source_target_pairs={{0,4},{4,0},{8,12},{12,8},{16,20},{20,16},{24,28},{28,24},{1,5},{5... | collective-permute-start | bytes 786440 | tf_op jit(solution)/shard_map/ppermute | solution.py:40
  34.9 7.2 %collective-permute-start.20 = (bf16[144,256]{1,0:T(8,128)(2,1)S(1)}, bf16[144,256]{1,0:T(8,128)(2,1)S(1)}, u32[]{:S(2)}, u32[]{:S(2)}) collective-permute-start(bf16[144,256]{1,0:T(8,128)(2,1)S(1)} %shard_map.118.refs_0_), channel_id=1, source_target_pairs={{0,3},{1,2},{2,1},{3,0},{4,7},{5,6},{6,5},{7,4},{8,11},{9,10},{10,... | collective-permute-start | bytes 221192 | tf_op jit(solution)/shard_map/ppermute | solution.py:54
  37.9 7.6 %collective-permute-start.19 = (bf16[144,256]{1,0:T(8,128)(2,1)S(1)}, bf16[144,256]{1,0:T(8,128)(2,1)S(1)}, u32[]{:S(2)}, u32[]{:S(2)}) collective-permute-start(bf16[144,256]{1,0:T(8,128)(2,1)S(1)} %shard_map.118.refs_0_), channel_id=1, source_target_pairs={{0,2},{1,3},{2,0},{3,1},{4,6},{5,7},{6,4},{7,5},{8,10},{9,11},{10,... | collective-permute-start | bytes 221192 | tf_op jit(solution)/shard_map/ppermute | solution.py:54
  38.1 7.3 %collective-permute-start.18 = (bf16[144,256]{1,0:T(8,128)(2,1)S(1)}, bf16[144,256]{1,0:T(8,128)(2,1)S(1)}, u32[]{:S(2)}, u32[]{:S(2)}) collective-permute-start(bf16[144,256]{1,0:T(8,128)(2,1)S(1)} %shard_map.118.refs_0_), channel_id=1, source_target_pairs={{0,1},{1,0},{2,3},{3,2},{4,5},{5,4},{6,7},{7,6},{8,9},{9,8},{10,11... | collective-permute-start | bytes 221192 | tf_op jit(solution)/shard_map/ppermute | solution.py:54
  39.5 6.1 %collective-permute-start.15 = (bf16[128,256]{1,0:T(8,128)(2,1)S(1)}, bf16[128,256]{1,0:T(8,128)(2,1)S(1)}, u32[]{:S(2)}, u32[]{:S(2)}) collective-permute-start(bf16[128,256]{1,0:T(8,128)(2,1)S(1)} %get-tuple-element.58), channel_id=1, source_target_pairs={{0,24},{4,28},{8,16},{12,20},{16,8},{20,12},{24,0},{28,4},{1,25},{... | collective-permute-start | bytes 196616 | tf_op jit(solution)/shard_map/ppermute | solution.py:50
  42.0 4.3 %collective-permute-start.16 = (bf16[128,256]{1,0:T(8,128)(2,1)S(1)}, bf16[128,256]{1,0:T(8,128)(2,1)S(1)}, u32[]{:S(2)}, u32[]{:S(2)}) collective-permute-start(bf16[128,256]{1,0:T(8,128)(2,1)S(1)} %get-tuple-element.59), channel_id=1, source_target_pairs={{0,16},{4,20},{8,24},{12,28},{16,0},{20,4},{24,8},{28,12},{1,17},{... | collective-permute-start | bytes 196616 | tf_op jit(solution)/shard_map/ppermute | solution.py:50
  42.2 4.3 %collective-permute-start.17 = (bf16[128,256]{1,0:T(8,128)(2,1)S(1)}, bf16[128,256]{1,0:T(8,128)(2,1)S(1)}, u32[]{:S(2)}, u32[]{:S(2)}) collective-permute-start(bf16[128,256]{1,0:T(8,128)(2,1)S(1)} %get-tuple-element.60), channel_id=1, source_target_pairs={{0,8},{4,12},{8,0},{12,4},{16,24},{20,28},{24,16},{28,20},{1,9},{5... | collective-permute-start | bytes 196616 | tf_op jit(solution)/shard_map/ppermute | solution.py:50
  45.5 1.4 %collective-permute-start.21 = (f32[128,256]{1,0:T(8,128)S(1)}, f32[128,256]{1,0:T(8,128)S(1)}, u32[]{:S(2)}, u32[]{:S(2)}) collective-permute-start(f32[128,256]{1,0:T(8,128)S(1)} %get-tuple-element.62.mine_ref), channel_id=1, source_target_pairs={{0,4},{4,0},{8,12},{12,8},{16,20},{20,16},{24,28},{28,24},{1,5},{5... | collective-permute-start | bytes 393224 | tf_op jit(solution)/shard_map/ppermute | solution.py:40

commit v9 on v8

--- a/solution.py
+++ b/solution.py
@@ -11,7 +11,7 @@
 CORES = 2
 EXTRA = 16
 LONG = 4_000_000_000
-GROUP = 4
+GROUP = 8
 VMEM = pl.BlockSpec(memory_space=pltpu.VMEM)
 SMEM = pl.BlockSpec(memory_space=pltpu.SMEM)
 NT = (((1,), (1,)), ((), ()))
@@ -67,17 +67,18 @@
     out_ref[...] = (features_ref[...].astype(F32) * inv).astype(BF16)
 
 
-def for_live(count_ref, slots, body):
-    count = count_ref[0, 0]
-    group = GROUP if slots % GROUP == 0 else 1
-
-    def step(i, carry):
-        for j in range(group):
-            slot = i * group + j
-            body(slot, slot < count)
-        return carry
-
-    lax.fori_loop(0, (count + group - 1) // group, step, 0)
+def group_of(slots):
+    return GROUP if slots % GROUP == 0 else 1
+
+
+def for_live(count, slots, body):
+    group = group_of(slots)
+    for start in range(0, slots, group):
+
+        @pl.when(start < count)
+        def _():
+            for slot in range(start, start + group):
+                body(slot)
 
 
 def build_kernel(count_ref, edge_ref, bias_ref, blocks_ref, turned_ref, bias_out_ref):
@@ -85,38 +86,44 @@
     slots, edges = edge_ref.shape[2], edge_ref.shape[3]
     node = lax.broadcasted_iota(jnp.int32, (BLOCK, edges), 0)
 
-    def build(s, live):
+    count = count_ref[0, 0]
+    group = group_of(slots)
+
+    def build(s):
         edge = edge_ref[0, 0, pl.ds(s, 1), :]
         row_hot = jnp.where(node == edge // BLOCK, 1.0, 0.0).astype(BF16)
         col_hot = jnp.where(node == edge % BLOCK, 1.0, 0.0).astype(BF16)
         counts = lax.dot_general(row_hot, col_hot, NT, preferred_element_type=F32)
-        block = jnp.where(live, counts, 0.0).astype(BF16)
+        block = jnp.where(s < count, counts, 0.0).astype(BF16)
         blocks_ref[s] = block
         turned_ref[s] = block.T
 
-    for_live(count_ref, slots, build)
-
-
-def forward_kernel(rows, cols, pos_hold_ref, count_ref, blocks_ref, near_ref, next_ref, *refs):
-    own_ref, *send, gathered, acc, pos_ref, sem = refs
-    fetch = pltpu.make_async_copy(pos_hold_ref, pos_ref, sem)
-    fetch.start()
+    def step(i, carry):
+        for j in range(group):
+            build(i * group + j)
+        return carry
+
+    lax.fori_loop(0, (count + group - 1) // group, step, 0)
+
+
+def forward_kernel(rows, cols, pos_ref, count_ref, blocks_ref, near_ref, next_ref, *refs):
+    own_ref, *send, gathered, acc = refs
     chips = rows // CORES
     row, col = lax.axis_index("row"), lax.axis_index("col")
     gathered[:chips] = near_ref[...]
     gathered[chips:] = next_ref[...]
     acc[...] = jnp.zeros_like(acc)
-    fetch.wait()
-
-    def add(s, live):
-        p = pos_ref[0, 0, s]
+    positions = pos_ref[0]
+
+    def add(s):
+        p = positions[0, s]
         u, v = p // rows, lax.rem(p, rows)
         k = offset_from(chips, row // CORES, v // CORES)
         src = (lax.rem(v, CORES) ^ lax.rem(row, CORES)) * chips + k
         dst = offset_to(cols, col, u)
         acc[dst] += jnp.dot(blocks_ref[s], gathered[src], preferred_element_type=F32)
 
-    for_live(count_ref, blocks_ref.shape[0], add)
+    for_live(count_ref[0, 0], blocks_ref.shape[0], add)
     own_ref[...] = acc[0]
     for k, ref in enumerate(send, 1):
         ref[...] = acc[k].astype(BF16)
@@ -200,27 +207,25 @@
         out_ref[n] = ref[...]
 
 
-def backward_kernel(rows, cols, pos_hold_ref, count_ref, turned_ref, *refs):
+def backward_kernel(rows, cols, pos_ref, count_ref, turned_ref, *refs):
     parts = refs[:cols]
-    keep_ref, send_ref, hidden, acc, pos_ref, sem = refs[cols:]
-    fetch = pltpu.make_async_copy(pos_hold_ref, pos_ref, sem)
-    fetch.start()
+    keep_ref, send_ref, hidden, acc = refs[cols:]
     chips = rows // CORES
     row, col = lax.axis_index("row"), lax.axis_index("col")
     for k, ref in enumerate(parts):
         hidden[k] = ref[...]
     acc[...] = jnp.zeros_like(acc)
-    fetch.wait()
-
-    def add(s, live):
-        p = pos_ref[0, 0, s]
+    positions = pos_ref[0]
+
+    def add(s):
+        p = positions[0, s]
         u, v = p // rows, lax.rem(p, rows)
         src = offset_from(cols, col, u)
         k = offset_to(chips, row // CORES, v // CORES)
         dst = (lax.rem(v, CORES) ^ lax.rem(row, CORES)) * chips + k
         acc[dst] += jnp.dot(turned_ref[s], hidden[src], preferred_element_type=F32)
 
-    for_live(count_ref, turned_ref.shape[0], add)
+    for_live(count_ref[0, 0], turned_ref.shape[0], add)
     keep_ref[...] = acc[:chips]
     send_ref[...] = acc[chips:].astype(BF16)
 
@@ -287,12 +292,11 @@
     blocks, *near = lax.optimization_barrier((blocks, *near))
     near = call(collect_kernel, [VMEM] * chips, [((chips,) + piece, BF16)])(scaled, *near)
 
-    fetched = [pltpu.SMEM(block_pos.shape, jnp.int32), pltpu.SemaphoreType.DMA]
     own, *send = call(
         functools.partial(forward_kernel, rows, cols),
         [VMEM, SMEM, VMEM, VMEM, VMEM],
         [(piece, F32)] + [(piece, BF16)] * (cols - 1),
-        [pltpu.VMEM((rows,) + piece, BF16), pltpu.VMEM((cols,) + piece, F32), *fetched],
+        [pltpu.VMEM((rows,) + piece, BF16), pltpu.VMEM((cols,) + piece, F32)],
     )(block_pos, block_count, blocks, near, to_core(near, rows))
     order = list(range(2, cols)) + [1]
     parts = [to_col(send[k - 1], cols, k) for k in order]
@@ -320,7 +324,7 @@
         functools.partial(backward_kernel, rows, cols),
         [VMEM, SMEM, VMEM] + [VMEM] * cols,
         [((chips,) + piece, F32), ((chips,) + piece, BF16)],
-        [pltpu.VMEM((cols,) + piece, BF16), pltpu.VMEM((rows,) + piece, F32), *fetched],
+        [pltpu.VMEM((cols,) + piece, BF16), pltpu.VMEM((rows,) + piece, F32)],
         flops=LONG,
     )(block_pos, block_count, turned, hidden, *(hidden_parts[k] for k in range(1, cols)))
     col_send, grads = lax.optimization_barrier((col_send, grads))

time: 48.1 us -> 47.8 us (level)
  Pallas kernels: 4.52 us -> 3.13 us
  waiting for transfers between devices: 14.7 us -> 15.7 us
    pallas_call x1, Pallas kernels: 1.07 us -> 0.49 us  [per_device(): call(functools.partial(forward_kernel, rows, cols), [VMEM, SMEM, VMEM, VM...]
    pallas_call x1, Pallas kernels: 1.1 us -> 0.53 us  [per_device(): call(functools.partial(backward_kernel, rows, cols), [VMEM, SMEM, VMEM] +...]
    ppermute x9, waiting for transfers between devices: 9.06 us -> 9.58 us  [to_col(): lax.ppermute(x, 'col', [(i, target(cols, i, k)) for i in range(cols)])]
  transfers between devices with their start and end apart: 22 -> 22, of which waited for: 14 -> 13; matrix products, arithmetic and copies ran while one was open for 0% -> 0% of each run, Pallas kernels for 4% -> 3%
where the time goes in v9:
time: 47.8 us; the launch traced here: 47.6 us
  starting transfers between devices  25.1 us (53%)
  waiting for transfers between devices  15.7 us (33%)
  Pallas kernels  3.13 us (7%)
  local copies, waits for them, and re-layouts  2.17 us (5%)
  between operations  1.45 us (3%)
    ppermute x9, starting transfers between devices, to_col(): lax.ppermute(x, 'col', [(i, target(cols, i, k)) for i in range(cols)])  13.1 us
    ppermute x9, starting transfers between devices, to_chip(): return lax.ppermute(x, 'row', pairs)  11.7 us
    ppermute x9, waiting for transfers between devices, to_col(): lax.ppermute(x, 'col', [(i, target(cols, i, k)) for i in range(cols)])  9.58 us
    ppermute x9, waiting for transfers between devices, to_chip(): return lax.ppermute(x, 'row', pairs)  3.7 us
    ppermute x4, waiting for transfers between devices, to_core(): return lax.ppermute(x, 'row', [(i, i ^ 1) for i in range(rows)])  2.42 us
    unnamed x14, local copies, waits for them, and re-layouts  2.17 us
  transfers between devices with their start and end apart: 22, of which 13 were waited for; matrix products, arithmetic and copies ran while one was open for 0% of the time, Pallas kernels for 3%

profile of v9, /device:TPU:0, one launch (start us, length us, event | category | flops | bytes accessed | tf_op | source)
XLA Modules:
  0.0 47.6 jit_solution(12178174541179630798)
XLA Ops:
  0.6 0.6 %copy-done.4 = s32[128]{0:T(128)S(1)} copy-done((s32[128]{0:T(128)S(1)}, s32[128]{0:T(128)}, u32[]{:S(2)}) %copy-start.4) | copy-done | bytes 536
  1.3 0.8 %copy-done.2 = bf16[128,256]{1,0:T(8,128)(2,1)S(1)} copy-done((bf16[128,256]{1,0:T(8,128)(2,1)S(1)}, bf16[128,256]{1,0:T(8,128)(2,1)}, u32[]{:S(2)}) %copy-start.2) | copy-done | bytes 65560
  2.1 0.1 shard_map.112
  2.2 4.0 %collective-permute-start.2 = (bf16[128,256]{1,0:T(8,128)(2,1)S(1)}, bf16[128,256]{1,0:T(8,128)(2,1)S(1)}, u32[]{:S(2)}, u32[]{:S(2)}) collective-permute-start(bf16[128,256]{1,0:T(8,128)(2,1)S(1)} %get-tuple-element.39.refs_0_), channel_id=1, source_target_pairs={{0,24},{4,28},{8,16},{12,20},{16,8},{20,12},{24,0},{28,4},{1,25},{... | collective-permute-start | bytes 196616 | tf_op jit(solution)/shard_map/ppermute | solution.py:50
  6.2 0.5 %collective-permute-start.1 = (bf16[128,256]{1,0:T(8,128)(2,1)S(1)}, bf16[128,256]{1,0:T(8,128)(2,1)S(1)}, u32[]{:S(2)}, u32[]{:S(2)}) collective-permute-start(bf16[128,256]{1,0:T(8,128)(2,1)S(1)} %get-tuple-element.39.refs_0_), channel_id=1, source_target_pairs={{0,16},{4,20},{8,24},{12,28},{16,0},{20,4},{24,8},{28,12},{1,17},{... | collective-permute-start | bytes 196616 | tf_op jit(solution)/shard_map/ppermute | solution.py:50
  6.7 0.1 collective-permute-start
  7.5 0.7 %copy-done.6 = f32[256]{0:T(256)S(1)} copy-done((f32[256]{0:T(256)S(1)}, f32[256]{0:T(256)}, u32[]{:S(2)}) %copy-start.6) | copy-done | bytes 1048
  8.2 0.5 %shard_map.111 = (bf16[16,128,128]{2,1,0:T(8,128)(2,1)S(1)}, bf16[16,128,128]{2,1,0:T(8,128)(2,1)S(1)}, f32[1,256]{1,0:T(1,128)S(1)}) custom-call(s32[1,1]{1,0:T(1,128)S(6)} %copy.12.count_ref, s32[1,1,16,512]{3,2,1,0:T(8,128)S(1)} %copy-done.5, f32[1,256]{1,0:T(1,128)S(1)} %bitcast.4), custom_call_target="tpu_custom_call" | custom-call | flops 4000000000 | bytes 1000000 | tf_op jit(solution)/shard_map/pallas_call | solution.py:286
  8.7 1.7 %collective-permute-done.1.refs_2_ = bf16[128,256]{1,0:T(8,128)(2,1)S(1)} collective-permute-done((bf16[128,256]{1,0:T(8,128)(2,1)S(1)}, bf16[128,256]{1,0:T(8,128)(2,1)S(1)}, u32[]{:S(2)}, u32[]{:S(2)}) %collective-permute-start.1) | collective-permute-done | bytes 65568 | tf_op jit(solution)/shard_map/ppermute | solution.py:50
  10.5 0.5 %collective-permute-done.refs_1_ = bf16[128,256]{1,0:T(8,128)(2,1)S(1)} collective-permute-done((bf16[128,256]{1,0:T(8,128)(2,1)S(1)}, bf16[128,256]{1,0:T(8,128)(2,1)S(1)}, u32[]{:S(2)}, u32[]{:S(2)}) %collective-permute-start) | collective-permute-done | bytes 65568 | tf_op jit(solution)/shard_map/ppermute | solution.py:50
  11.0 0.0 copy-start.1
  11.0 0.1 collective-permute-start.3
  11.1 1.5 %collective-permute-done.3.next_ref = bf16[4,128,256]{2,1,0:T(8,128)(2,1)S(1)} collective-permute-done((bf16[4,128,256]{2,1,0:T(8,128)(2,1)S(1)}, bf16[4,128,256]{2,1,0:T(8,128)(2,1)S(1)}, u32[]{:S(2)}, u32[]{:S(2)}) %collective-permute-start.3) | collective-permute-done | bytes 262176 | tf_op jit(solution)/shard_map/ppermute | solution.py:40
  12.6 0.5 %shard_map.114 = (f32[128,256]{1,0:T(8,128)S(1)}, bf16[128,256]{1,0:T(8,128)(2,1)S(1)}, bf16[128,256]{1,0:T(8,128)(2,1)S(1)}, bf16[128,256]{1,0:T(8,128)(2,1)S(1)}) custom-call(s32[1,1,16]{2,1,0:T(1,128)S(1)} %copy-done.3, s32[1,1]{1,0:T(1,128)S(6)} %copy.12.count_ref, bf16[16,128,128]{2,1,0:T(8,128)(2,1)S(1)} %get-tuple-element.40.blocks_ref, ...), custom_call_target="tpu_custom_call" | custom-call | flops 1000000 | bytes 1000000 | tf_op jit(solution)/shard_map/pallas_call | solution.py:295
  13.1 2.7 %collective-permute-start.4 = (bf16[128,256]{1,0:T(8,128)(2,1)S(1)}, bf16[128,256]{1,0:T(8,128)(2,1)S(1)}, u32[]{:S(2)}, u32[]{:S(2)}) collective-permute-start(bf16[128,256]{1,0:T(8,128)(2,1)S(1)} %get-tuple-element.45), channel_id=1, source_target_pairs={{0,2},{1,3},{2,0},{3,1},{4,6},{5,7},{6,4},{7,5},{8,10},{9,11},{10,... | collective-permute-start | bytes 196616 | tf_op jit(solution)/shard_map/ppermute | solution.py:54
  15.8 1.3 %collective-permute-start.5 = (bf16[128,256]{1,0:T(8,128)(2,1)S(1)}, bf16[128,256]{1,0:T(8,128)(2,1)S(1)}, u32[]{:S(2)}, u32[]{:S(2)}) collective-permute-start(bf16[128,256]{1,0:T(8,128)(2,1)S(1)} %get-tuple-element.46), channel_id=1, source_target_pairs={{0,3},{1,2},{2,1},{3,0},{4,7},{5,6},{6,5},{7,4},{8,11},{9,10},{10,... | collective-permute-start | bytes 196616 | tf_op jit(solution)/shard_map/ppermute | solution.py:54
  17.1 0.2 collective-permute-start.6
  17.4 3.5 %collective-permute-done.4.refs_1_ = bf16[128,256]{1,0:T(8,128)(2,1)S(1)} collective-permute-done((bf16[128,256]{1,0:T(8,128)(2,1)S(1)}, bf16[128,256]{1,0:T(8,128)(2,1)S(1)}, u32[]{:S(2)}, u32[]{:S(2)}) %collective-permute-start.4) | collective-permute-done | bytes 65568 | tf_op jit(solution)/shard_map/ppermute | solution.py:54
  20.9 1.3 %collective-permute-done.5.refs_2_ = bf16[128,256]{1,0:T(8,128)(2,1)S(1)} collective-permute-done((bf16[128,256]{1,0:T(8,128)(2,1)S(1)}, bf16[128,256]{1,0:T(8,128)(2,1)S(1)}, u32[]{:S(2)}, u32[]{:S(2)}) %collective-permute-start.5) | collective-permute-done | bytes 65568 | tf_op jit(solution)/shard_map/ppermute | solution.py:54
  22.2 0.3 collective-permute-done.6.refs_3_
  22.5 0.4 shard_map.115
  22.9 0.1 collective-permute-start.10
  23.0 3.2 %collective-permute-start.9 = (bf16[128,256]{1,0:T(8,128)(2,1)S(1)}, bf16[128,256]{1,0:T(8,128)(2,1)S(1)}, u32[]{:S(2)}, u32[]{:S(2)}) collective-permute-start(bf16[128,256]{1,0:T(8,128)(2,1)S(1)} %get-tuple-element.50.refs_0_), channel_id=1, source_target_pairs={{0,3},{1,2},{2,1},{3,0},{4,7},{5,6},{6,5},{7,4},{8,11},{9,10},{10,... | collective-permute-start | bytes 196616 | tf_op jit(solution)/shard_map/ppermute | solution.py:54
  26.2 1.2 %collective-permute-start.7 = (bf16[128,256]{1,0:T(8,128)(2,1)S(1)}, bf16[128,256]{1,0:T(8,128)(2,1)S(1)}, u32[]{:S(2)}, u32[]{:S(2)}) collective-permute-start(bf16[128,256]{1,0:T(8,128)(2,1)S(1)} %get-tuple-element.50.refs_0_), channel_id=1, source_target_pairs={{0,1},{1,0},{2,3},{3,2},{4,5},{5,4},{6,7},{7,6},{8,9},{9,8},{10,11... | collective-permute-start | bytes 196616 | tf_op jit(solution)/shard_map/ppermute | solution.py:54
  27.5 1.6 %collective-permute-start.13 = (bf16[144,256]{1,0:T(8,128)(2,1)S(1)}, bf16[144,256]{1,0:T(8,128)(2,1)S(1)}, u32[]{:S(2)}, u32[]{:S(2)}) collective-permute-start(bf16[144,256]{1,0:T(8,128)(2,1)S(1)} %shard_map.117.refs_0_), channel_id=1, source_target_pairs={{0,24},{4,28},{8,16},{12,20},{16,8},{20,12},{24,0},{28,4},{1,25},{... | collective-permute-start | bytes 221192 | tf_op jit(solution)/shard_map/ppermute | solution.py:50
  29.0 0.4 collective-permute-start.12
  29.5 0.0 collective-permute-done.9.refs_3_
  29.5 1.6 %collective-permute-start.11 = (bf16[144,256]{1,0:T(8,128)(2,1)S(1)}, bf16[144,256]{1,0:T(8,128)(2,1)S(1)}, u32[]{:S(2)}, u32[]{:S(2)}) collective-permute-start(bf16[144,256]{1,0:T(8,128)(2,1)S(1)} %shard_map.117.refs_0_), channel_id=1, source_target_pairs={{0,8},{4,12},{8,0},{12,4},{16,24},{20,28},{24,16},{28,20},{1,9},{5... | collective-permute-start | bytes 221192 | tf_op jit(solution)/shard_map/ppermute | solution.py:50
  31.0 1.5 %collective-permute-done.8.refs_2_ = bf16[128,256]{1,0:T(8,128)(2,1)S(1)} collective-permute-done((bf16[128,256]{1,0:T(8,128)(2,1)S(1)}, bf16[128,256]{1,0:T(8,128)(2,1)S(1)}, u32[]{:S(2)}, u32[]{:S(2)}) %collective-permute-start.8) | collective-permute-done | bytes 65568 | tf_op jit(solution)/shard_map/ppermute | solution.py:54
  32.5 0.5 %shard_map.116 = (f32[4,128,256]{2,1,0:T(8,128)S(1)}, bf16[4,128,256]{2,1,0:T(8,128)(2,1)S(1)}) custom-call(s32[1,1,16]{2,1,0:T(1,128)S(1)} %copy-done.3, s32[1,1]{1,0:T(1,128)S(6)} %copy.12.count_ref, bf16[16,128,128]{2,1,0:T(8,128)(2,1)S(1)} %get-tuple-element.49.turned_ref, bf16[128,256]{1,0:T(8,128)(2,1)S(1)} %get-tuple-element.50.refs_0_, ...), custom_call_target="tpu_custom_call" | custom-call | flops 4000000000 | bytes 1000000 | tf_op jit(solution)/shard_map/pallas_call | solution.py:323
  33.1 0.7 %collective-permute-done.12.refs_2_ = bf16[144,256]{1,0:T(8,128)(2,1)S(1)} collective-permute-done((bf16[144,256]{1,0:T(8,128)(2,1)S(1)}, bf16[144,256]{1,0:T(8,128)(2,1)S(1)}, u32[]{:S(2)}, u32[]{:S(2)}) %collective-permute-start.12) | collective-permute-done | bytes 73760 | tf_op jit(solution)/shard_map/ppermute | solution.py:50
  33.8 0.3 collective-permute-done.11.refs_1_
  34.1 0.1 shard_map.118.refs_0_
  34.2 0.1 collective-permute-start.14
  34.3 3.3 %collective-permute-start.20 = (bf16[144,256]{1,0:T(8,128)(2,1)S(1)}, bf16[144,256]{1,0:T(8,128)(2,1)S(1)}, u32[]{:S(2)}, u32[]{:S(2)}) collective-permute-start(bf16[144,256]{1,0:T(8,128)(2,1)S(1)} %shard_map.118.refs_0_), channel_id=1, source_target_pairs={{0,3},{1,2},{2,1},{3,0},{4,7},{5,6},{6,5},{7,4},{8,11},{9,10},{10,... | collective-permute-start | bytes 221192 | tf_op jit(solution)/shard_map/ppermute | solution.py:54
  37.6 0.4 collective-permute-start.19
  38.0 0.8 %collective-permute-start.18 = (bf16[144,256]{1,0:T(8,128)(2,1)S(1)}, bf16[144,256]{1,0:T(8,128)(2,1)S(1)}, u32[]{:S(2)}, u32[]{:S(2)}) collective-permute-start(bf16[144,256]{1,0:T(8,128)(2,1)S(1)} %shard_map.118.refs_0_), channel_id=1, source_target_pairs={{0,1},{1,0},{2,3},{3,2},{4,5},{5,4},{6,7},{7,6},{8,9},{9,8},{10,11... | collective-permute-start | bytes 221192 | tf_op jit(solution)/shard_map/ppermute | solution.py:54
  38.8 0.1 shard_map.119
  38.8 2.6 %collective-permute-start.15 = (bf16[128,256]{1,0:T(8,128)(2,1)S(1)}, bf16[128,256]{1,0:T(8,128)(2,1)S(1)}, u32[]{:S(2)}, u32[]{:S(2)}) collective-permute-start(bf16[128,256]{1,0:T(8,128)(2,1)S(1)} %get-tuple-element.58), channel_id=1, source_target_pairs={{0,24},{4,28},{8,16},{12,20},{16,8},{20,12},{24,0},{28,4},{1,25},{... | collective-permute-start | bytes 196616 | tf_op jit(solution)/shard_map/ppermute | solution.py:50
  41.4 0.2 collective-permute-start.16
  41.6 0.8 %collective-permute-start.17 = (bf16[128,256]{1,0:T(8,128)(2,1)S(1)}, bf16[128,256]{1,0:T(8,128)(2,1)S(1)}, u32[]{:S(2)}, u32[]{:S(2)}) collective-permute-start(bf16[128,256]{1,0:T(8,128)(2,1)S(1)} %get-tuple-element.60), channel_id=1, source_target_pairs={{0,8},{4,12},{8,0},{12,4},{16,24},{20,28},{24,16},{28,20},{1,9},{5... | collective-permute-start | bytes 196616 | tf_op jit(solution)/shard_map/ppermute | solution.py:50
  42.4 2.9 %collective-permute-done.19.refs_2_ = bf16[144,256]{1,0:T(8,128)(2,1)S(1)} collective-permute-done((bf16[144,256]{1,0:T(8,128)(2,1)S(1)}, bf16[144,256]{1,0:T(8,128)(2,1)S(1)}, u32[]{:S(2)}, u32[]{:S(2)}) %collective-permute-start.19) | collective-permute-done | bytes 73760 | tf_op jit(solution)/shard_map/ppermute | solution.py:54
  45.3 0.1 shard_map.121
  45.4 0.1 collective-permute-start.21
  45.5 0.2 collective-permute-done.16.refs_1_
  45.7 0.2 collective-permute-done.17.refs_2_
  45.9 0.9 %collective-permute-done.21.theirs_ref = f32[128,256]{1,0:T(8,128)S(1)} collective-permute-done((f32[128,256]{1,0:T(8,128)S(1)}, f32[128,256]{1,0:T(8,128)S(1)}, u32[]{:S(2)}, u32[]{:S(2)}) %collective-permute-start.21) | collective-permute-done | bytes 131104 | tf_op jit(solution)/shard_map/ppermute | solution.py:40
  46.8 0.8 %shard_map.122 = (bf16[128,256]{1,0:T(8,128)(2,1)}, bf16[128,256]{1,0:T(8,128)(2,1)}, f32[256,256]{1,0:T(8,128)}, f32[1,256]{1,0:T(1,128)}) custom-call(bf16[128,256]{1,0:T(8,128)(2,1)S(1)} %get-tuple-element.48.out_ref, bf16[128,256]{1,0:T(8,128)(2,1)S(1)} %shard_map.120.x_ref, f32[128,256]{1,0:T(8,128)S(1)} %get-tuple-element.62.mine_ref, ...), custom_call_target="tpu_custom_call" | custom-call | flops 1000000 | bytes 1000000 | tf_op jit(solution)/shard_map/pallas_call | solution.py:348
  (22 shorter events, 0.1 us)
Async XLA Ops:
  0.6 0.7 %copy-start.4 = (s32[128]{0:T(128)S(1)}, s32[128]{0:T(128)}, u32[]{:S(2)}) copy-start(s32[128]{0:T(128)} %param.9) | copy-start | bytes 1540
  1.3 0.8 %copy-start.2 = (bf16[128,256]{1,0:T(8,128)(2,1)S(1)}, bf16[128,256]{1,0:T(8,128)(2,1)}, u32[]{:S(2)}) copy-start(bf16[128,256]{1,0:T(8,128)(2,1)} %features_ref.1) | copy-start | bytes 196612
  2.1 5.4 %copy-start.5 = (s32[1,1,16,512]{3,2,1,0:T(8,128)S(1)}, s32[1,1,16,512]{3,2,1,0:T(8,128)}, u32[]{:S(2)}) copy-start(s32[1,1,16,512]{3,2,1,0:T(8,128)} %edge_ref.1) | copy-start | bytes 98308
  2.2 6.5 %collective-permute-start.2 = (bf16[128,256]{1,0:T(8,128)(2,1)S(1)}, bf16[128,256]{1,0:T(8,128)(2,1)S(1)}, u32[]{:S(2)}, u32[]{:S(2)}) collective-permute-start(bf16[128,256]{1,0:T(8,128)(2,1)S(1)} %get-tuple-element.39.refs_0_), channel_id=1, source_target_pairs={{0,24},{4,28},{8,16},{12,20},{16,8},{20,12},{24,0},{28,4},{1,25},{... | collective-permute-start | bytes 196616 | tf_op jit(solution)/shard_map/ppermute | solution.py:50
  6.2 4.3 %collective-permute-start.1 = (bf16[128,256]{1,0:T(8,128)(2,1)S(1)}, bf16[128,256]{1,0:T(8,128)(2,1)S(1)}, u32[]{:S(2)}, u32[]{:S(2)}) collective-permute-start(bf16[128,256]{1,0:T(8,128)(2,1)S(1)} %get-tuple-element.39.refs_0_), channel_id=1, source_target_pairs={{0,16},{4,20},{8,24},{12,28},{16,0},{20,4},{24,8},{28,12},{1,17},{... | collective-permute-start | bytes 196616 | tf_op jit(solution)/shard_map/ppermute | solution.py:50
  6.7 4.3 %collective-permute-start = (bf16[128,256]{1,0:T(8,128)(2,1)S(1)}, bf16[128,256]{1,0:T(8,128)(2,1)S(1)}, u32[]{:S(2)}, u32[]{:S(2)}) collective-permute-start(bf16[128,256]{1,0:T(8,128)(2,1)S(1)} %get-tuple-element.39.refs_0_), channel_id=1, source_target_pairs={{0,8},{4,12},{8,0},{12,4},{16,24},{20,28},{24,16},{28,20},{1,9},{5... | collective-permute-start | bytes 196616 | tf_op jit(solution)/shard_map/ppermute | solution.py:50
  7.5 0.7 %copy-start.6 = (f32[256]{0:T(256)S(1)}, f32[256]{0:T(256)}, u32[]{:S(2)}) copy-start(f32[256]{0:T(256)} %param.11) | copy-start | bytes 3076
  11.0 1.7 %copy-start.3 = (s32[1,1,16]{2,1,0:T(1,128)S(1)}, s32[1,1,16]{2,1,0:T(1,128)}, u32[]{:S(2)}) copy-start(s32[1,1,16]{2,1,0:T(1,128)} %pos_ref.3) | copy-start | bytes 196
  11.0 11.5 %copy-start = (bf16[256,256]{1,0:T(8,128)(2,1)S(1)}, bf16[256,256]{1,0:T(8,128)(2,1)}, u32[]{:S(2)}) copy-start(bf16[256,256]{1,0:T(8,128)(2,1)} %weight_ref.1) | copy-start | bytes 393220
  11.0 11.5 %copy-start.1 = (bf16[128,256]{1,0:T(8,128)(2,1)S(1)}, bf16[128,256]{1,0:T(8,128)(2,1)}, u32[]{:S(2)}) copy-start(bf16[128,256]{1,0:T(8,128)(2,1)} %cot_ref.1) | copy-start | bytes 196612
  11.0 1.6 %collective-permute-start.3 = (bf16[4,128,256]{2,1,0:T(8,128)(2,1)S(1)}, bf16[4,128,256]{2,1,0:T(8,128)(2,1)S(1)}, u32[]{:S(2)}, u32[]{:S(2)}) collective-permute-start(bf16[4,128,256]{2,1,0:T(8,128)(2,1)S(1)} %shard_map.113.near_ref), channel_id=1, source_target_pairs={{0,4},{4,0},{8,12},{12,8},{16,20},{20,16},{24,28},{28,24},{1,5},{5... | collective-permute-start | bytes 786440 | tf_op jit(solution)/shard_map/ppermute | solution.py:40
  13.1 7.8 %collective-permute-start.4 = (bf16[128,256]{1,0:T(8,128)(2,1)S(1)}, bf16[128,256]{1,0:T(8,128)(2,1)S(1)}, u32[]{:S(2)}, u32[]{:S(2)}) collective-permute-start(bf16[128,256]{1,0:T(8,128)(2,1)S(1)} %get-tuple-element.45), channel_id=1, source_target_pairs={{0,2},{1,3},{2,0},{3,1},{4,6},{5,7},{6,4},{7,5},{8,10},{9,11},{10,... | collective-permute-start | bytes 196616 | tf_op jit(solution)/shard_map/ppermute | solution.py:54
  15.8 6.4 %collective-permute-start.5 = (bf16[128,256]{1,0:T(8,128)(2,1)S(1)}, bf16[128,256]{1,0:T(8,128)(2,1)S(1)}, u32[]{:S(2)}, u32[]{:S(2)}) collective-permute-start(bf16[128,256]{1,0:T(8,128)(2,1)S(1)} %get-tuple-element.46), channel_id=1, source_target_pairs={{0,3},{1,2},{2,1},{3,0},{4,7},{5,6},{6,5},{7,4},{8,11},{9,10},{10,... | collective-permute-start | bytes 196616 | tf_op jit(solution)/shard_map/ppermute | solution.py:54
  17.1 5.4 %collective-permute-start.6 = (bf16[128,256]{1,0:T(8,128)(2,1)S(1)}, bf16[128,256]{1,0:T(8,128)(2,1)S(1)}, u32[]{:S(2)}, u32[]{:S(2)}) collective-permute-start(bf16[128,256]{1,0:T(8,128)(2,1)S(1)} %get-tuple-element.47), channel_id=1, source_target_pairs={{0,1},{1,0},{2,3},{3,2},{4,5},{5,4},{6,7},{7,6},{8,9},{9,8},{10,11... | collective-permute-start | bytes 196616 | tf_op jit(solution)/shard_map/ppermute | solution.py:54
  22.9 4.5 %collective-permute-start.10 = (bf16[144,256]{1,0:T(8,128)(2,1)S(1)}, bf16[144,256]{1,0:T(8,128)(2,1)S(1)}, u32[]{:S(2)}, u32[]{:S(2)}) collective-permute-start(bf16[144,256]{1,0:T(8,128)(2,1)S(1)} %get-tuple-element.55), channel_id=1, source_target_pairs={{0,4},{4,0},{8,12},{12,8},{16,20},{20,16},{24,28},{28,24},{1,5},{5... | collective-permute-start | bytes 221192 | tf_op jit(solution)/shard_map/ppermute | solution.py:40
  23.0 6.5 %collective-permute-start.9 = (bf16[128,256]{1,0:T(8,128)(2,1)S(1)}, bf16[128,256]{1,0:T(8,128)(2,1)S(1)}, u32[]{:S(2)}, u32[]{:S(2)}) collective-permute-start(bf16[128,256]{1,0:T(8,128)(2,1)S(1)} %get-tuple-element.50.refs_0_), channel_id=1, source_target_pairs={{0,3},{1,2},{2,1},{3,0},{4,7},{5,6},{6,5},{7,4},{8,11},{9,10},{10,... | collective-permute-start | bytes 196616 | tf_op jit(solution)/shard_map/ppermute | solution.py:54
  26.2 6.3 %collective-permute-start.8 = (bf16[128,256]{1,0:T(8,128)(2,1)S(1)}, bf16[128,256]{1,0:T(8,128)(2,1)S(1)}, u32[]{:S(2)}, u32[]{:S(2)}) collective-permute-start(bf16[128,256]{1,0:T(8,128)(2,1)S(1)} %get-tuple-element.50.refs_0_), channel_id=1, source_target_pairs={{0,2},{1,3},{2,0},{3,1},{4,6},{5,7},{6,4},{7,5},{8,10},{9,11},{10,... | collective-permute-start | bytes 196616 | tf_op jit(solution)/shard_map/ppermute | solution.py:54
  26.2 6.3 %collective-permute-start.7 = (bf16[128,256]{1,0:T(8,128)(2,1)S(1)}, bf16[128,256]{1,0:T(8,128)(2,1)S(1)}, u32[]{:S(2)}, u32[]{:S(2)}) collective-permute-start(bf16[128,256]{1,0:T(8,128)(2,1)S(1)} %get-tuple-element.50.refs_0_), channel_id=1, source_target_pairs={{0,1},{1,0},{2,3},{3,2},{4,5},{5,4},{6,7},{7,6},{8,9},{9,8},{10,11... | collective-permute-start | bytes 196616 | tf_op jit(solution)/shard_map/ppermute | solution.py:54
  27.5 5.6 %collective-permute-start.13 = (bf16[144,256]{1,0:T(8,128)(2,1)S(1)}, bf16[144,256]{1,0:T(8,128)(2,1)S(1)}, u32[]{:S(2)}, u32[]{:S(2)}) collective-permute-start(bf16[144,256]{1,0:T(8,128)(2,1)S(1)} %shard_map.117.refs_0_), channel_id=1, source_target_pairs={{0,24},{4,28},{8,16},{12,20},{16,8},{20,12},{24,0},{28,4},{1,25},{... | collective-permute-start | bytes 221192 | tf_op jit(solution)/shard_map/ppermute | solution.py:50
  29.0 4.8 %collective-permute-start.12 = (bf16[144,256]{1,0:T(8,128)(2,1)S(1)}, bf16[144,256]{1,0:T(8,128)(2,1)S(1)}, u32[]{:S(2)}, u32[]{:S(2)}) collective-permute-start(bf16[144,256]{1,0:T(8,128)(2,1)S(1)} %shard_map.117.refs_0_), channel_id=1, source_target_pairs={{0,16},{4,20},{8,24},{12,28},{16,0},{20,4},{24,8},{28,12},{1,17},{... | collective-permute-start | bytes 221192 | tf_op jit(solution)/shard_map/ppermute | solution.py:50
  29.5 4.7 %collective-permute-start.11 = (bf16[144,256]{1,0:T(8,128)(2,1)S(1)}, bf16[144,256]{1,0:T(8,128)(2,1)S(1)}, u32[]{:S(2)}, u32[]{:S(2)}) collective-permute-start(bf16[144,256]{1,0:T(8,128)(2,1)S(1)} %shard_map.117.refs_0_), channel_id=1, source_target_pairs={{0,8},{4,12},{8,0},{12,4},{16,24},{20,28},{24,16},{28,20},{1,9},{5... | collective-permute-start | bytes 221192 | tf_op jit(solution)/shard_map/ppermute | solution.py:50
  34.2 4.5 %collective-permute-start.14 = (bf16[4,128,256]{2,1,0:T(8,128)(2,1)S(1)}, bf16[4,128,256]{2,1,0:T(8,128)(2,1)S(1)}, u32[]{:S(2)}, u32[]{:S(2)}) collective-permute-start(bf16[4,128,256]{2,1,0:T(8,128)(2,1)S(1)} %get-tuple-element.56), channel_id=1, source_target_pairs={{0,4},{4,0},{8,12},{12,8},{16,20},{20,16},{24,28},{28,24},{1,5},{5... | collective-permute-start | bytes 786440 | tf_op jit(solution)/shard_map/ppermute | solution.py:40
  34.3 7.3 %collective-permute-start.20 = (bf16[144,256]{1,0:T(8,128)(2,1)S(1)}, bf16[144,256]{1,0:T(8,128)(2,1)S(1)}, u32[]{:S(2)}, u32[]{:S(2)}) collective-permute-start(bf16[144,256]{1,0:T(8,128)(2,1)S(1)} %shard_map.118.refs_0_), channel_id=1, source_target_pairs={{0,3},{1,2},{2,1},{3,0},{4,7},{5,6},{6,5},{7,4},{8,11},{9,10},{10,... | collective-permute-start | bytes 221192 | tf_op jit(solution)/shard_map/ppermute | solution.py:54
  37.6 7.7 %collective-permute-start.19 = (bf16[144,256]{1,0:T(8,128)(2,1)S(1)}, bf16[144,256]{1,0:T(8,128)(2,1)S(1)}, u32[]{:S(2)}, u32[]{:S(2)}) collective-permute-start(bf16[144,256]{1,0:T(8,128)(2,1)S(1)} %shard_map.118.refs_0_), channel_id=1, source_target_pairs={{0,2},{1,3},{2,0},{3,1},{4,6},{5,7},{6,4},{7,5},{8,10},{9,11},{10,... | collective-permute-start | bytes 221192 | tf_op jit(solution)/shard_map/ppermute | solution.py:54
  38.0 7.3 %collective-permute-start.18 = (bf16[144,256]{1,0:T(8,128)(2,1)S(1)}, bf16[144,256]{1,0:T(8,128)(2,1)S(1)}, u32[]{:S(2)}, u32[]{:S(2)}) collective-permute-start(bf16[144,256]{1,0:T(8,128)(2,1)S(1)} %shard_map.118.refs_0_), channel_id=1, source_target_pairs={{0,1},{1,0},{2,3},{3,2},{4,5},{5,4},{6,7},{7,6},{8,9},{9,8},{10,11... | collective-permute-start | bytes 221192 | tf_op jit(solution)/shard_map/ppermute | solution.py:54
  38.8 6.7 %collective-permute-start.15 = (bf16[128,256]{1,0:T(8,128)(2,1)S(1)}, bf16[128,256]{1,0:T(8,128)(2,1)S(1)}, u32[]{:S(2)}, u32[]{:S(2)}) collective-permute-start(bf16[128,256]{1,0:T(8,128)(2,1)S(1)} %get-tuple-element.58), channel_id=1, source_target_pairs={{0,24},{4,28},{8,16},{12,20},{16,8},{20,12},{24,0},{28,4},{1,25},{... | collective-permute-start | bytes 196616 | tf_op jit(solution)/shard_map/ppermute | solution.py:50
  41.4 4.3 %collective-permute-start.16 = (bf16[128,256]{1,0:T(8,128)(2,1)S(1)}, bf16[128,256]{1,0:T(8,128)(2,1)S(1)}, u32[]{:S(2)}, u32[]{:S(2)}) collective-permute-start(bf16[128,256]{1,0:T(8,128)(2,1)S(1)} %get-tuple-element.59), channel_id=1, source_target_pairs={{0,16},{4,20},{8,24},{12,28},{16,0},{20,4},{24,8},{28,12},{1,17},{... | collective-permute-start | bytes 196616 | tf_op jit(solution)/shard_map/ppermute | solution.py:50
  41.6 4.3 %collective-permute-start.17 = (bf16[128,256]{1,0:T(8,128)(2,1)S(1)}, bf16[128,256]{1,0:T(8,128)(2,1)S(1)}, u32[]{:S(2)}, u32[]{:S(2)}) collective-permute-start(bf16[128,256]{1,0:T(8,128)(2,1)S(1)} %get-tuple-element.60), channel_id=1, source_target_pairs={{0,8},{4,12},{8,0},{12,4},{16,24},{20,28},{24,16},{28,20},{1,9},{5... | collective-permute-start | bytes 196616 | tf_op jit(solution)/shard_map/ppermute | solution.py:50
  45.4 1.4 %collective-permute-start.21 = (f32[128,256]{1,0:T(8,128)S(1)}, f32[128,256]{1,0:T(8,128)S(1)}, u32[]{:S(2)}, u32[]{:S(2)}) collective-permute-start(f32[128,256]{1,0:T(8,128)S(1)} %get-tuple-element.62.mine_ref), channel_id=1, source_target_pairs={{0,4},{4,0},{8,12},{12,8},{16,20},{20,16},{24,28},{28,24},{1,5},{5... | collective-permute-start | bytes 393224 | tf_op jit(solution)/shard_map/ppermute | solution.py:40

commit v10 on v9

--- a/solution.py
+++ b/solution.py
@@ -196,9 +196,11 @@
     out_ref[half:] = pack_bias(bias, EXTRA)
 
 
-def col_sum_kernel(*refs):
+def col_sum_kernel(norm, *refs):
     *parts, half_ref, bias_ref, stage = refs
-    half_ref[...], bias_ref[...] = total_of(len(parts), lax.axis_index("col"), parts, stage)
+    grads, bias = total_of(len(parts), lax.axis_index("col"), parts, stage)
+    half_ref[...] = grads * norm
+    bias_ref[...] = bias * norm
 
 
 def collect_kernel(*refs):
@@ -244,26 +246,32 @@
     out_ref[...] = (total * inv_ref[...]).astype(BF16)
 
 
-def finish_kernel(norm, out_ref, x_ref, mine_ref, theirs_ref, bias_ref, *refs):
-    output_ref, grad_x_ref, grad_w_ref, grad_b_ref = refs
-    output_ref[...] = out_ref[...]
-    grad_x_ref[...] = x_ref[...]
+def finish_kernel(out_ref, x_ref, mine_ref, theirs_ref, bias_ref, *refs):
+    output_ref, grad_x_ref, grad_w_ref, grad_b_ref, sems = refs
     half = mine_ref.shape[0]
-    first = lax.rem(lax.axis_index("row"), CORES) == 0
-    mine, theirs = mine_ref[...] * norm, theirs_ref[...] * norm
-    grad_w_ref[:half] = jnp.where(first, mine, theirs)
-    grad_w_ref[half:] = jnp.where(first, theirs, mine)
-    grad_b_ref[...] = bias_ref[...] * norm
-
-
-def call(kernel, specs, outs, scratch=(), flops=1_000_000):
+    core = lax.rem(lax.axis_index("row"), CORES)
+    moves = [
+        (mine_ref, grad_w_ref.at[pl.ds(pl.multiple_of(core * half, half), half)]),
+        (theirs_ref, grad_w_ref.at[pl.ds(pl.multiple_of((1 - core) * half, half), half)]),
+        (out_ref, output_ref),
+        (x_ref, grad_x_ref),
+        (bias_ref, grad_b_ref),
+    ]
+    copies = [pltpu.make_async_copy(*move, sems.at[i]) for i, move in enumerate(moves)]
+    for copy in copies:
+        copy.start()
+    for copy in copies:
+        copy.wait()
+
+
+def call(kernel, specs, outs, scratch=(), flops=1_000_000, place=VMEM):
     shapes = [jax.ShapeDtypeStruct(shape, dtype) for shape, dtype in outs]
     single = len(shapes) == 1
     return pl.pallas_call(
         kernel,
         out_shape=shapes[0] if single else tuple(shapes),
         in_specs=specs,
-        out_specs=VMEM if single else tuple(VMEM for _ in shapes),
+        out_specs=place if single else tuple(place for _ in shapes),
         scratch_shapes=scratch,
         compiler_params=pltpu.CompilerParams(vmem_limit_bytes=40 * 1024 * 1024),
         cost_estimate=pl.CostEstimate(flops=flops, bytes_accessed=1_000_000, transcendentals=0),
@@ -334,8 +342,9 @@
     )(col_keep, to_core(col_send, rows))
     parts_x = [to_chip(send_x[k - 1], rows, k) for k in across]
 
+    norm = float((owned * rows * cols) ** -0.5)
     mine, bias_sum = call(
-        col_sum_kernel,
+        functools.partial(col_sum_kernel, norm),
         [VMEM] * cols,
         [((half, width), F32), ((1, width), F32)],
         [pltpu.VMEM((cols,) + grads_shape, BF16)],
@@ -344,11 +353,12 @@
     x_piece = call(owned_sum_kernel, [VMEM] * (1 + chips), [(piece, BF16)], flops=LONG)(
         inv, own_x, *parts_x
     )
-    norm = float((owned * rows * cols) ** -0.5)
     output, grad_x, grad_w, grad_b = call(
-        functools.partial(finish_kernel, norm),
+        finish_kernel,
         [VMEM] * 5,
         [(piece, BF16), (piece, BF16), ((width, width), F32), ((1, width), F32)],
+        [pltpu.SemaphoreType.DMA((5,))],
+        place=pl.BlockSpec(memory_space=pl.ANY),
     )(out_piece, x_piece, mine, theirs, bias_sum)
     return (output, grad_x, grad_w, grad_b.reshape(width))
 

time: 47.8 us -> 47.7 us (level)
  no operation moved by 1% of the time
where the time goes in v10:
time: 47.7 us; the launch traced here: 47.6 us
  starting transfers between devices  25.3 us (53%)
  waiting for transfers between devices  15.5 us (32%)
  Pallas kernels  3.15 us (7%)
  local copies, waits for them, and re-layouts  2.17 us (5%)
  between operations  1.43 us (3%)
    ppermute x9, starting transfers between devices, to_col(): lax.ppermute(x, 'col', [(i, target(cols, i, k)) for i in range(cols)])  13.1 us
    ppermute x9, starting transfers between devices, to_chip(): return lax.ppermute(x, 'row', pairs)  11.8 us
    ppermute x9, waiting for transfers between devices, to_col(): lax.ppermute(x, 'col', [(i, target(cols, i, k)) for i in range(cols)])  9.68 us
    ppermute x9, waiting for transfers between devices, to_chip(): return lax.ppermute(x, 'row', pairs)  3.45 us
    ppermute x4, waiting for transfers between devices, to_core(): return lax.ppermute(x, 'row', [(i, i ^ 1) for i in range(rows)])  2.41 us
    unnamed x14, local copies, waits for them, and re-layouts  2.17 us
  transfers between devices with their start and end apart: 22, of which 13 were waited for; matrix products, arithmetic and copies ran while one was open for 0% of the time, Pallas kernels for 3%

profile of v10, /device:TPU:0, one launch (start us, length us, event | category | flops | bytes accessed | tf_op | source)
XLA Modules:
  0.0 47.6 jit_solution(12792022709889481362)
XLA Ops:
  0.6 0.6 %copy-done.4 = s32[128]{0:T(128)S(1)} copy-done((s32[128]{0:T(128)S(1)}, s32[128]{0:T(128)}, u32[]{:S(2)}) %copy-start.4) | copy-done | bytes 536
  1.3 0.8 %copy-done.2 = bf16[128,256]{1,0:T(8,128)(2,1)S(1)} copy-done((bf16[128,256]{1,0:T(8,128)(2,1)S(1)}, bf16[128,256]{1,0:T(8,128)(2,1)}, u32[]{:S(2)}) %copy-start.2) | copy-done | bytes 65560
  2.1 0.1 shard_map.112
  2.2 4.0 %collective-permute-start.2 = (bf16[128,256]{1,0:T(8,128)(2,1)S(1)}, bf16[128,256]{1,0:T(8,128)(2,1)S(1)}, u32[]{:S(2)}, u32[]{:S(2)}) collective-permute-start(bf16[128,256]{1,0:T(8,128)(2,1)S(1)} %get-tuple-element.39.refs_0_), channel_id=1, source_target_pairs={{0,24},{4,28},{8,16},{12,20},{16,8},{20,12},{24,0},{28,4},{1,25},{... | collective-permute-start | bytes 196616 | tf_op jit(solution)/shard_map/ppermute | solution.py:50
  6.2 0.5 %collective-permute-start.1 = (bf16[128,256]{1,0:T(8,128)(2,1)S(1)}, bf16[128,256]{1,0:T(8,128)(2,1)S(1)}, u32[]{:S(2)}, u32[]{:S(2)}) collective-permute-start(bf16[128,256]{1,0:T(8,128)(2,1)S(1)} %get-tuple-element.39.refs_0_), channel_id=1, source_target_pairs={{0,16},{4,20},{8,24},{12,28},{16,0},{20,4},{24,8},{28,12},{1,17},{... | collective-permute-start | bytes 196616 | tf_op jit(solution)/shard_map/ppermute | solution.py:50
  6.7 0.1 collective-permute-start
  7.5 0.0 copy-start.6
  7.5 0.7 %copy-done.6 = f32[256]{0:T(256)S(1)} copy-done((f32[256]{0:T(256)S(1)}, f32[256]{0:T(256)}, u32[]{:S(2)}) %copy-start.6) | copy-done | bytes 1048
  8.2 0.5 %shard_map.111 = (bf16[16,128,128]{2,1,0:T(8,128)(2,1)S(1)}, bf16[16,128,128]{2,1,0:T(8,128)(2,1)S(1)}, f32[1,256]{1,0:T(1,128)S(1)}) custom-call(s32[1,1]{1,0:T(1,128)S(6)} %copy.12.count_ref, s32[1,1,16,512]{3,2,1,0:T(8,128)S(1)} %copy-done.5, f32[1,256]{1,0:T(1,128)S(1)} %bitcast.4), custom_call_target="tpu_custom_call" | custom-call | flops 4000000000 | bytes 1000000 | tf_op jit(solution)/shard_map/pallas_call | solution.py:294
  8.7 1.7 %collective-permute-done.1.refs_2_ = bf16[128,256]{1,0:T(8,128)(2,1)S(1)} collective-permute-done((bf16[128,256]{1,0:T(8,128)(2,1)S(1)}, bf16[128,256]{1,0:T(8,128)(2,1)S(1)}, u32[]{:S(2)}, u32[]{:S(2)}) %collective-permute-start.1) | collective-permute-done | bytes 65568 | tf_op jit(solution)/shard_map/ppermute | solution.py:50
  10.5 0.5 %collective-permute-done.refs_1_ = bf16[128,256]{1,0:T(8,128)(2,1)S(1)} collective-permute-done((bf16[128,256]{1,0:T(8,128)(2,1)S(1)}, bf16[128,256]{1,0:T(8,128)(2,1)S(1)}, u32[]{:S(2)}, u32[]{:S(2)}) %collective-permute-start) | collective-permute-done | bytes 65568 | tf_op jit(solution)/shard_map/ppermute | solution.py:50
  11.0 0.1 collective-permute-start.3
  11.1 1.5 %collective-permute-done.3.next_ref = bf16[4,128,256]{2,1,0:T(8,128)(2,1)S(1)} collective-permute-done((bf16[4,128,256]{2,1,0:T(8,128)(2,1)S(1)}, bf16[4,128,256]{2,1,0:T(8,128)(2,1)S(1)}, u32[]{:S(2)}, u32[]{:S(2)}) %collective-permute-start.3) | collective-permute-done | bytes 262176 | tf_op jit(solution)/shard_map/ppermute | solution.py:40
  12.6 0.5 %shard_map.114 = (f32[128,256]{1,0:T(8,128)S(1)}, bf16[128,256]{1,0:T(8,128)(2,1)S(1)}, bf16[128,256]{1,0:T(8,128)(2,1)S(1)}, bf16[128,256]{1,0:T(8,128)(2,1)S(1)}) custom-call(s32[1,1,16]{2,1,0:T(1,128)S(1)} %copy-done.3, s32[1,1]{1,0:T(1,128)S(6)} %copy.12.count_ref, bf16[16,128,128]{2,1,0:T(8,128)(2,1)S(1)} %get-tuple-element.40.blocks_ref, ...), custom_call_target="tpu_custom_call" | custom-call | flops 1000000 | bytes 1000000 | tf_op jit(solution)/shard_map/pallas_call | solution.py:303
  13.1 2.7 %collective-permute-start.4 = (bf16[128,256]{1,0:T(8,128)(2,1)S(1)}, bf16[128,256]{1,0:T(8,128)(2,1)S(1)}, u32[]{:S(2)}, u32[]{:S(2)}) collective-permute-start(bf16[128,256]{1,0:T(8,128)(2,1)S(1)} %get-tuple-element.45), channel_id=1, source_target_pairs={{0,2},{1,3},{2,0},{3,1},{4,6},{5,7},{6,4},{7,5},{8,10},{9,11},{10,... | collective-permute-start | bytes 196616 | tf_op jit(solution)/shard_map/ppermute | solution.py:54
  15.8 1.3 %collective-permute-start.5 = (bf16[128,256]{1,0:T(8,128)(2,1)S(1)}, bf16[128,256]{1,0:T(8,128)(2,1)S(1)}, u32[]{:S(2)}, u32[]{:S(2)}) collective-permute-start(bf16[128,256]{1,0:T(8,128)(2,1)S(1)} %get-tuple-element.46), channel_id=1, source_target_pairs={{0,3},{1,2},{2,1},{3,0},{4,7},{5,6},{6,5},{7,4},{8,11},{9,10},{10,... | collective-permute-start | bytes 196616 | tf_op jit(solution)/shard_map/ppermute | solution.py:54
  17.1 0.2 collective-permute-start.6
  17.4 3.5 %collective-permute-done.4.refs_1_ = bf16[128,256]{1,0:T(8,128)(2,1)S(1)} collective-permute-done((bf16[128,256]{1,0:T(8,128)(2,1)S(1)}, bf16[128,256]{1,0:T(8,128)(2,1)S(1)}, u32[]{:S(2)}, u32[]{:S(2)}) %collective-permute-start.4) | collective-permute-done | bytes 65568 | tf_op jit(solution)/shard_map/ppermute | solution.py:54
  20.9 1.3 %collective-permute-done.5.refs_2_ = bf16[128,256]{1,0:T(8,128)(2,1)S(1)} collective-permute-done((bf16[128,256]{1,0:T(8,128)(2,1)S(1)}, bf16[128,256]{1,0:T(8,128)(2,1)S(1)}, u32[]{:S(2)}, u32[]{:S(2)}) %collective-permute-start.5) | collective-permute-done | bytes 65568 | tf_op jit(solution)/shard_map/ppermute | solution.py:54
  22.2 0.3 collective-permute-done.6.refs_3_
  22.5 0.4 shard_map.115
  22.9 0.1 collective-permute-start.10
  23.0 3.2 %collective-permute-start.9 = (bf16[128,256]{1,0:T(8,128)(2,1)S(1)}, bf16[128,256]{1,0:T(8,128)(2,1)S(1)}, u32[]{:S(2)}, u32[]{:S(2)}) collective-permute-start(bf16[128,256]{1,0:T(8,128)(2,1)S(1)} %get-tuple-element.50.refs_0_), channel_id=1, source_target_pairs={{0,3},{1,2},{2,1},{3,0},{4,7},{5,6},{6,5},{7,4},{8,11},{9,10},{10,... | collective-permute-start | bytes 196616 | tf_op jit(solution)/shard_map/ppermute | solution.py:54
  26.2 1.2 %collective-permute-start.7 = (bf16[128,256]{1,0:T(8,128)(2,1)S(1)}, bf16[128,256]{1,0:T(8,128)(2,1)S(1)}, u32[]{:S(2)}, u32[]{:S(2)}) collective-permute-start(bf16[128,256]{1,0:T(8,128)(2,1)S(1)} %get-tuple-element.50.refs_0_), channel_id=1, source_target_pairs={{0,1},{1,0},{2,3},{3,2},{4,5},{5,4},{6,7},{7,6},{8,9},{9,8},{10,11... | collective-permute-start | bytes 196616 | tf_op jit(solution)/shard_map/ppermute | solution.py:54
  27.5 1.8 %collective-permute-start.13 = (bf16[144,256]{1,0:T(8,128)(2,1)S(1)}, bf16[144,256]{1,0:T(8,128)(2,1)S(1)}, u32[]{:S(2)}, u32[]{:S(2)}) collective-permute-start(bf16[144,256]{1,0:T(8,128)(2,1)S(1)} %shard_map.117.refs_0_), channel_id=1, source_target_pairs={{0,24},{4,28},{8,16},{12,20},{16,8},{20,12},{24,0},{28,4},{1,25},{... | collective-permute-start | bytes 221192 | tf_op jit(solution)/shard_map/ppermute | solution.py:50
  29.3 0.2 collective-permute-start.12
  29.5 0.0 collective-permute-done.9.refs_3_
  29.5 1.6 %collective-permute-start.11 = (bf16[144,256]{1,0:T(8,128)(2,1)S(1)}, bf16[144,256]{1,0:T(8,128)(2,1)S(1)}, u32[]{:S(2)}, u32[]{:S(2)}) collective-permute-start(bf16[144,256]{1,0:T(8,128)(2,1)S(1)} %shard_map.117.refs_0_), channel_id=1, source_target_pairs={{0,8},{4,12},{8,0},{12,4},{16,24},{20,28},{24,16},{28,20},{1,9},{5... | collective-permute-start | bytes 221192 | tf_op jit(solution)/shard_map/ppermute | solution.py:50
  31.0 1.5 %collective-permute-done.8.refs_2_ = bf16[128,256]{1,0:T(8,128)(2,1)S(1)} collective-permute-done((bf16[128,256]{1,0:T(8,128)(2,1)S(1)}, bf16[128,256]{1,0:T(8,128)(2,1)S(1)}, u32[]{:S(2)}, u32[]{:S(2)}) %collective-permute-start.8) | collective-permute-done | bytes 65568 | tf_op jit(solution)/shard_map/ppermute | solution.py:54
  32.5 0.5 %shard_map.116 = (f32[4,128,256]{2,1,0:T(8,128)S(1)}, bf16[4,128,256]{2,1,0:T(8,128)(2,1)S(1)}) custom-call(s32[1,1,16]{2,1,0:T(1,128)S(1)} %copy-done.3, s32[1,1]{1,0:T(1,128)S(6)} %copy.12.count_ref, bf16[16,128,128]{2,1,0:T(8,128)(2,1)S(1)} %get-tuple-element.49.turned_ref, bf16[128,256]{1,0:T(8,128)(2,1)S(1)} %get-tuple-element.50.refs_0_, ...), custom_call_target="tpu_custom_call" | custom-call | flops 4000000000 | bytes 1000000 | tf_op jit(solution)/shard_map/pallas_call | solution.py:331
  33.1 0.1 collective-permute-done.13.refs_3_
  33.2 0.6 %collective-permute-done.12.refs_2_ = bf16[144,256]{1,0:T(8,128)(2,1)S(1)} collective-permute-done((bf16[144,256]{1,0:T(8,128)(2,1)S(1)}, bf16[144,256]{1,0:T(8,128)(2,1)S(1)}, u32[]{:S(2)}, u32[]{:S(2)}) %collective-permute-start.12) | collective-permute-done | bytes 73760 | tf_op jit(solution)/shard_map/ppermute | solution.py:50
  33.8 0.1 collective-permute-done.11.refs_1_
  33.9 0.1 shard_map.118.refs_0_
  34.0 0.1 collective-permute-start.14
  34.1 3.5 %collective-permute-start.20 = (bf16[144,256]{1,0:T(8,128)(2,1)S(1)}, bf16[144,256]{1,0:T(8,128)(2,1)S(1)}, u32[]{:S(2)}, u32[]{:S(2)}) collective-permute-start(bf16[144,256]{1,0:T(8,128)(2,1)S(1)} %shard_map.118.refs_0_), channel_id=1, source_target_pairs={{0,3},{1,2},{2,1},{3,0},{4,7},{5,6},{6,5},{7,4},{8,11},{9,10},{10,... | collective-permute-start | bytes 221192 | tf_op jit(solution)/shard_map/ppermute | solution.py:54
  37.6 0.4 collective-permute-start.19
  38.0 0.6 %collective-permute-start.18 = (bf16[144,256]{1,0:T(8,128)(2,1)S(1)}, bf16[144,256]{1,0:T(8,128)(2,1)S(1)}, u32[]{:S(2)}, u32[]{:S(2)}) collective-permute-start(bf16[144,256]{1,0:T(8,128)(2,1)S(1)} %shard_map.118.refs_0_), channel_id=1, source_target_pairs={{0,1},{1,0},{2,3},{3,2},{4,5},{5,4},{6,7},{7,6},{8,9},{9,8},{10,11... | collective-permute-start | bytes 221192 | tf_op jit(solution)/shard_map/ppermute | solution.py:54
  38.5 0.1 shard_map.119
  38.6 2.5 %collective-permute-start.15 = (bf16[128,256]{1,0:T(8,128)(2,1)S(1)}, bf16[128,256]{1,0:T(8,128)(2,1)S(1)}, u32[]{:S(2)}, u32[]{:S(2)}) collective-permute-start(bf16[128,256]{1,0:T(8,128)(2,1)S(1)} %get-tuple-element.58), channel_id=1, source_target_pairs={{0,24},{4,28},{8,16},{12,20},{16,8},{20,12},{24,0},{28,4},{1,25},{... | collective-permute-start | bytes 196616 | tf_op jit(solution)/shard_map/ppermute | solution.py:50
  41.1 0.5 %collective-permute-start.16 = (bf16[128,256]{1,0:T(8,128)(2,1)S(1)}, bf16[128,256]{1,0:T(8,128)(2,1)S(1)}, u32[]{:S(2)}, u32[]{:S(2)}) collective-permute-start(bf16[128,256]{1,0:T(8,128)(2,1)S(1)} %get-tuple-element.59), channel_id=1, source_target_pairs={{0,16},{4,20},{8,24},{12,28},{16,0},{20,4},{24,8},{28,12},{1,17},{... | collective-permute-start | bytes 196616 | tf_op jit(solution)/shard_map/ppermute | solution.py:50
  41.6 0.7 %collective-permute-start.17 = (bf16[128,256]{1,0:T(8,128)(2,1)S(1)}, bf16[128,256]{1,0:T(8,128)(2,1)S(1)}, u32[]{:S(2)}, u32[]{:S(2)}) collective-permute-start(bf16[128,256]{1,0:T(8,128)(2,1)S(1)} %get-tuple-element.60), channel_id=1, source_target_pairs={{0,8},{4,12},{8,0},{12,4},{16,24},{20,28},{24,16},{28,20},{1,9},{5... | collective-permute-start | bytes 196616 | tf_op jit(solution)/shard_map/ppermute | solution.py:50
  42.3 3.0 %collective-permute-done.19.refs_2_ = bf16[144,256]{1,0:T(8,128)(2,1)S(1)} collective-permute-done((bf16[144,256]{1,0:T(8,128)(2,1)S(1)}, bf16[144,256]{1,0:T(8,128)(2,1)S(1)}, u32[]{:S(2)}, u32[]{:S(2)}) %collective-permute-start.19) | collective-permute-done | bytes 73760 | tf_op jit(solution)/shard_map/ppermute | solution.py:54
  45.3 0.1 shard_map.121
  45.4 0.1 collective-permute-start.21
  45.5 0.3 collective-permute-done.17.refs_2_
  45.9 0.9 %collective-permute-done.21.theirs_ref = f32[128,256]{1,0:T(8,128)S(1)} collective-permute-done((f32[128,256]{1,0:T(8,128)S(1)}, f32[128,256]{1,0:T(8,128)S(1)}, u32[]{:S(2)}, u32[]{:S(2)}) %collective-permute-start.21) | collective-permute-done | bytes 131104 | tf_op jit(solution)/shard_map/ppermute | solution.py:40
  46.8 0.8 %shard_map.122 = (bf16[128,256]{1,0:T(8,128)(2,1)}, bf16[128,256]{1,0:T(8,128)(2,1)}, f32[256,256]{1,0:T(8,128)}, f32[1,256]{1,0:T(1,128)}) custom-call(bf16[128,256]{1,0:T(8,128)(2,1)S(1)} %get-tuple-element.48.out_ref, bf16[128,256]{1,0:T(8,128)(2,1)S(1)} %shard_map.120.x_ref, f32[128,256]{1,0:T(8,128)S(1)} %get-tuple-element.62.mine_ref, ...), custom_call_target="tpu_custom_call" | custom-call | flops 1000000 | bytes 1000000 | tf_op jit(solution)/shard_map/pallas_call | solution.py:356
  (22 shorter events, 0.1 us)
Async XLA Ops:
  0.6 0.7 %copy-start.4 = (s32[128]{0:T(128)S(1)}, s32[128]{0:T(128)}, u32[]{:S(2)}) copy-start(s32[128]{0:T(128)} %param.9) | copy-start | bytes 1540
  1.3 0.8 %copy-start.2 = (bf16[128,256]{1,0:T(8,128)(2,1)S(1)}, bf16[128,256]{1,0:T(8,128)(2,1)}, u32[]{:S(2)}) copy-start(bf16[128,256]{1,0:T(8,128)(2,1)} %features_ref.1) | copy-start | bytes 196612
  2.1 5.4 %copy-start.5 = (s32[1,1,16,512]{3,2,1,0:T(8,128)S(1)}, s32[1,1,16,512]{3,2,1,0:T(8,128)}, u32[]{:S(2)}) copy-start(s32[1,1,16,512]{3,2,1,0:T(8,128)} %edge_ref.1) | copy-start | bytes 98308
  2.2 6.5 %collective-permute-start.2 = (bf16[128,256]{1,0:T(8,128)(2,1)S(1)}, bf16[128,256]{1,0:T(8,128)(2,1)S(1)}, u32[]{:S(2)}, u32[]{:S(2)}) collective-permute-start(bf16[128,256]{1,0:T(8,128)(2,1)S(1)} %get-tuple-element.39.refs_0_), channel_id=1, source_target_pairs={{0,24},{4,28},{8,16},{12,20},{16,8},{20,12},{24,0},{28,4},{1,25},{... | collective-permute-start | bytes 196616 | tf_op jit(solution)/shard_map/ppermute | solution.py:50
  6.2 4.3 %collective-permute-start.1 = (bf16[128,256]{1,0:T(8,128)(2,1)S(1)}, bf16[128,256]{1,0:T(8,128)(2,1)S(1)}, u32[]{:S(2)}, u32[]{:S(2)}) collective-permute-start(bf16[128,256]{1,0:T(8,128)(2,1)S(1)} %get-tuple-element.39.refs_0_), channel_id=1, source_target_pairs={{0,16},{4,20},{8,24},{12,28},{16,0},{20,4},{24,8},{28,12},{1,17},{... | collective-permute-start | bytes 196616 | tf_op jit(solution)/shard_map/ppermute | solution.py:50
  6.7 4.3 %collective-permute-start = (bf16[128,256]{1,0:T(8,128)(2,1)S(1)}, bf16[128,256]{1,0:T(8,128)(2,1)S(1)}, u32[]{:S(2)}, u32[]{:S(2)}) collective-permute-start(bf16[128,256]{1,0:T(8,128)(2,1)S(1)} %get-tuple-element.39.refs_0_), channel_id=1, source_target_pairs={{0,8},{4,12},{8,0},{12,4},{16,24},{20,28},{24,16},{28,20},{1,9},{5... | collective-permute-start | bytes 196616 | tf_op jit(solution)/shard_map/ppermute | solution.py:50
  7.5 0.7 %copy-start.6 = (f32[256]{0:T(256)S(1)}, f32[256]{0:T(256)}, u32[]{:S(2)}) copy-start(f32[256]{0:T(256)} %param.11) | copy-start | bytes 3076
  11.0 1.7 %copy-start.3 = (s32[1,1,16]{2,1,0:T(1,128)S(1)}, s32[1,1,16]{2,1,0:T(1,128)}, u32[]{:S(2)}) copy-start(s32[1,1,16]{2,1,0:T(1,128)} %pos_ref.3) | copy-start | bytes 196
  11.0 11.5 %copy-start = (bf16[256,256]{1,0:T(8,128)(2,1)S(1)}, bf16[256,256]{1,0:T(8,128)(2,1)}, u32[]{:S(2)}) copy-start(bf16[256,256]{1,0:T(8,128)(2,1)} %weight_ref.1) | copy-start | bytes 393220
  11.0 11.5 %copy-start.1 = (bf16[128,256]{1,0:T(8,128)(2,1)S(1)}, bf16[128,256]{1,0:T(8,128)(2,1)}, u32[]{:S(2)}) copy-start(bf16[128,256]{1,0:T(8,128)(2,1)} %cot_ref.1) | copy-start | bytes 196612
  11.0 1.6 %collective-permute-start.3 = (bf16[4,128,256]{2,1,0:T(8,128)(2,1)S(1)}, bf16[4,128,256]{2,1,0:T(8,128)(2,1)S(1)}, u32[]{:S(2)}, u32[]{:S(2)}) collective-permute-start(bf16[4,128,256]{2,1,0:T(8,128)(2,1)S(1)} %shard_map.113.near_ref), channel_id=1, source_target_pairs={{0,4},{4,0},{8,12},{12,8},{16,20},{20,16},{24,28},{28,24},{1,5},{5... | collective-permute-start | bytes 786440 | tf_op jit(solution)/shard_map/ppermute | solution.py:40
  13.1 7.8 %collective-permute-start.4 = (bf16[128,256]{1,0:T(8,128)(2,1)S(1)}, bf16[128,256]{1,0:T(8,128)(2,1)S(1)}, u32[]{:S(2)}, u32[]{:S(2)}) collective-permute-start(bf16[128,256]{1,0:T(8,128)(2,1)S(1)} %get-tuple-element.45), channel_id=1, source_target_pairs={{0,2},{1,3},{2,0},{3,1},{4,6},{5,7},{6,4},{7,5},{8,10},{9,11},{10,... | collective-permute-start | bytes 196616 | tf_op jit(solution)/shard_map/ppermute | solution.py:54
  15.8 6.4 %collective-permute-start.5 = (bf16[128,256]{1,0:T(8,128)(2,1)S(1)}, bf16[128,256]{1,0:T(8,128)(2,1)S(1)}, u32[]{:S(2)}, u32[]{:S(2)}) collective-permute-start(bf16[128,256]{1,0:T(8,128)(2,1)S(1)} %get-tuple-element.46), channel_id=1, source_target_pairs={{0,3},{1,2},{2,1},{3,0},{4,7},{5,6},{6,5},{7,4},{8,11},{9,10},{10,... | collective-permute-start | bytes 196616 | tf_op jit(solution)/shard_map/ppermute | solution.py:54
  17.1 5.4 %collective-permute-start.6 = (bf16[128,256]{1,0:T(8,128)(2,1)S(1)}, bf16[128,256]{1,0:T(8,128)(2,1)S(1)}, u32[]{:S(2)}, u32[]{:S(2)}) collective-permute-start(bf16[128,256]{1,0:T(8,128)(2,1)S(1)} %get-tuple-element.47), channel_id=1, source_target_pairs={{0,1},{1,0},{2,3},{3,2},{4,5},{5,4},{6,7},{7,6},{8,9},{9,8},{10,11... | collective-permute-start | bytes 196616 | tf_op jit(solution)/shard_map/ppermute | solution.py:54
  22.9 4.5 %collective-permute-start.10 = (bf16[144,256]{1,0:T(8,128)(2,1)S(1)}, bf16[144,256]{1,0:T(8,128)(2,1)S(1)}, u32[]{:S(2)}, u32[]{:S(2)}) collective-permute-start(bf16[144,256]{1,0:T(8,128)(2,1)S(1)} %get-tuple-element.55), channel_id=1, source_target_pairs={{0,4},{4,0},{8,12},{12,8},{16,20},{20,16},{24,28},{28,24},{1,5},{5... | collective-permute-start | bytes 221192 | tf_op jit(solution)/shard_map/ppermute | solution.py:40
  23.0 6.5 %collective-permute-start.9 = (bf16[128,256]{1,0:T(8,128)(2,1)S(1)}, bf16[128,256]{1,0:T(8,128)(2,1)S(1)}, u32[]{:S(2)}, u32[]{:S(2)}) collective-permute-start(bf16[128,256]{1,0:T(8,128)(2,1)S(1)} %get-tuple-element.50.refs_0_), channel_id=1, source_target_pairs={{0,3},{1,2},{2,1},{3,0},{4,7},{5,6},{6,5},{7,4},{8,11},{9,10},{10,... | collective-permute-start | bytes 196616 | tf_op jit(solution)/shard_map/ppermute | solution.py:54
  26.2 6.3 %collective-permute-start.8 = (bf16[128,256]{1,0:T(8,128)(2,1)S(1)}, bf16[128,256]{1,0:T(8,128)(2,1)S(1)}, u32[]{:S(2)}, u32[]{:S(2)}) collective-permute-start(bf16[128,256]{1,0:T(8,128)(2,1)S(1)} %get-tuple-element.50.refs_0_), channel_id=1, source_target_pairs={{0,2},{1,3},{2,0},{3,1},{4,6},{5,7},{6,4},{7,5},{8,10},{9,11},{10,... | collective-permute-start | bytes 196616 | tf_op jit(solution)/shard_map/ppermute | solution.py:54
  26.2 6.3 %collective-permute-start.7 = (bf16[128,256]{1,0:T(8,128)(2,1)S(1)}, bf16[128,256]{1,0:T(8,128)(2,1)S(1)}, u32[]{:S(2)}, u32[]{:S(2)}) collective-permute-start(bf16[128,256]{1,0:T(8,128)(2,1)S(1)} %get-tuple-element.50.refs_0_), channel_id=1, source_target_pairs={{0,1},{1,0},{2,3},{3,2},{4,5},{5,4},{6,7},{7,6},{8,9},{9,8},{10,11... | collective-permute-start | bytes 196616 | tf_op jit(solution)/shard_map/ppermute | solution.py:54
  27.5 5.7 %collective-permute-start.13 = (bf16[144,256]{1,0:T(8,128)(2,1)S(1)}, bf16[144,256]{1,0:T(8,128)(2,1)S(1)}, u32[]{:S(2)}, u32[]{:S(2)}) collective-permute-start(bf16[144,256]{1,0:T(8,128)(2,1)S(1)} %shard_map.117.refs_0_), channel_id=1, source_target_pairs={{0,24},{4,28},{8,16},{12,20},{16,8},{20,12},{24,0},{28,4},{1,25},{... | collective-permute-start | bytes 221192 | tf_op jit(solution)/shard_map/ppermute | solution.py:50
  29.3 4.5 %collective-permute-start.12 = (bf16[144,256]{1,0:T(8,128)(2,1)S(1)}, bf16[144,256]{1,0:T(8,128)(2,1)S(1)}, u32[]{:S(2)}, u32[]{:S(2)}) collective-permute-start(bf16[144,256]{1,0:T(8,128)(2,1)S(1)} %shard_map.117.refs_0_), channel_id=1, source_target_pairs={{0,16},{4,20},{8,24},{12,28},{16,0},{20,4},{24,8},{28,12},{1,17},{... | collective-permute-start | bytes 221192 | tf_op jit(solution)/shard_map/ppermute | solution.py:50
  29.5 4.4 %collective-permute-start.11 = (bf16[144,256]{1,0:T(8,128)(2,1)S(1)}, bf16[144,256]{1,0:T(8,128)(2,1)S(1)}, u32[]{:S(2)}, u32[]{:S(2)}) collective-permute-start(bf16[144,256]{1,0:T(8,128)(2,1)S(1)} %shard_map.117.refs_0_), channel_id=1, source_target_pairs={{0,8},{4,12},{8,0},{12,4},{16,24},{20,28},{24,16},{28,20},{1,9},{5... | collective-permute-start | bytes 221192 | tf_op jit(solution)/shard_map/ppermute | solution.py:50
  34.0 4.5 %collective-permute-start.14 = (bf16[4,128,256]{2,1,0:T(8,128)(2,1)S(1)}, bf16[4,128,256]{2,1,0:T(8,128)(2,1)S(1)}, u32[]{:S(2)}, u32[]{:S(2)}) collective-permute-start(bf16[4,128,256]{2,1,0:T(8,128)(2,1)S(1)} %get-tuple-element.56), channel_id=1, source_target_pairs={{0,4},{4,0},{8,12},{12,8},{16,20},{20,16},{24,28},{28,24},{1,5},{5... | collective-permute-start | bytes 786440 | tf_op jit(solution)/shard_map/ppermute | solution.py:40
  34.1 7.5 %collective-permute-start.20 = (bf16[144,256]{1,0:T(8,128)(2,1)S(1)}, bf16[144,256]{1,0:T(8,128)(2,1)S(1)}, u32[]{:S(2)}, u32[]{:S(2)}) collective-permute-start(bf16[144,256]{1,0:T(8,128)(2,1)S(1)} %shard_map.118.refs_0_), channel_id=1, source_target_pairs={{0,3},{1,2},{2,1},{3,0},{4,7},{5,6},{6,5},{7,4},{8,11},{9,10},{10,... | collective-permute-start | bytes 221192 | tf_op jit(solution)/shard_map/ppermute | solution.py:54
  37.6 7.7 %collective-permute-start.19 = (bf16[144,256]{1,0:T(8,128)(2,1)S(1)}, bf16[144,256]{1,0:T(8,128)(2,1)S(1)}, u32[]{:S(2)}, u32[]{:S(2)}) collective-permute-start(bf16[144,256]{1,0:T(8,128)(2,1)S(1)} %shard_map.118.refs_0_), channel_id=1, source_target_pairs={{0,2},{1,3},{2,0},{3,1},{4,6},{5,7},{6,4},{7,5},{8,10},{9,11},{10,... | collective-permute-start | bytes 221192 | tf_op jit(solution)/shard_map/ppermute | solution.py:54
  38.0 7.3 %collective-permute-start.18 = (bf16[144,256]{1,0:T(8,128)(2,1)S(1)}, bf16[144,256]{1,0:T(8,128)(2,1)S(1)}, u32[]{:S(2)}, u32[]{:S(2)}) collective-permute-start(bf16[144,256]{1,0:T(8,128)(2,1)S(1)} %shard_map.118.refs_0_), channel_id=1, source_target_pairs={{0,1},{1,0},{2,3},{3,2},{4,5},{5,4},{6,7},{7,6},{8,9},{9,8},{10,11... | collective-permute-start | bytes 221192 | tf_op jit(solution)/shard_map/ppermute | solution.py:54
  38.6 6.9 %collective-permute-start.15 = (bf16[128,256]{1,0:T(8,128)(2,1)S(1)}, bf16[128,256]{1,0:T(8,128)(2,1)S(1)}, u32[]{:S(2)}, u32[]{:S(2)}) collective-permute-start(bf16[128,256]{1,0:T(8,128)(2,1)S(1)} %get-tuple-element.58), channel_id=1, source_target_pairs={{0,24},{4,28},{8,16},{12,20},{16,8},{20,12},{24,0},{28,4},{1,25},{... | collective-permute-start | bytes 196616 | tf_op jit(solution)/shard_map/ppermute | solution.py:50
  41.1 4.4 %collective-permute-start.16 = (bf16[128,256]{1,0:T(8,128)(2,1)S(1)}, bf16[128,256]{1,0:T(8,128)(2,1)S(1)}, u32[]{:S(2)}, u32[]{:S(2)}) collective-permute-start(bf16[128,256]{1,0:T(8,128)(2,1)S(1)} %get-tuple-element.59), channel_id=1, source_target_pairs={{0,16},{4,20},{8,24},{12,28},{16,0},{20,4},{24,8},{28,12},{1,17},{... | collective-permute-start | bytes 196616 | tf_op jit(solution)/shard_map/ppermute | solution.py:50
  41.6 4.3 %collective-permute-start.17 = (bf16[128,256]{1,0:T(8,128)(2,1)S(1)}, bf16[128,256]{1,0:T(8,128)(2,1)S(1)}, u32[]{:S(2)}, u32[]{:S(2)}) collective-permute-start(bf16[128,256]{1,0:T(8,128)(2,1)S(1)} %get-tuple-element.60), channel_id=1, source_target_pairs={{0,8},{4,12},{8,0},{12,4},{16,24},{20,28},{24,16},{28,20},{1,9},{5... | collective-permute-start | bytes 196616 | tf_op jit(solution)/shard_map/ppermute | solution.py:50
  45.4 1.4 %collective-permute-start.21 = (f32[128,256]{1,0:T(8,128)S(1)}, f32[128,256]{1,0:T(8,128)S(1)}, u32[]{:S(2)}, u32[]{:S(2)}) collective-permute-start(f32[128,256]{1,0:T(8,128)S(1)} %get-tuple-element.62.mine_ref), channel_id=1, source_target_pairs={{0,4},{4,0},{8,12},{12,8},{16,20},{20,16},{24,28},{28,24},{1,5},{5... | collective-permute-start | bytes 393224 | tf_op jit(solution)/shard_map/ppermute | solution.py:40

commit v11 on v10

--- a/solution.py
+++ b/solution.py
@@ -34,6 +34,10 @@
 
 def offset_from(n, me, other):
     return me ^ other if is_power(n) else lax.rem(me - other + n, n)
+
+
+def col_order(cols):
+    return list(range(2, cols)) + [1]
 
 
 def to_core(x, rows):
@@ -175,8 +179,8 @@
     out_ref[half:] = pack_bias(bias_keep_ref[...] + add_bias(got_ref[half:]), EXTRA)
 
 
-def total_of(n, me, refs, stage):
-    for k, ref in enumerate(refs):
+def total_of(n, me, offsets, refs, stage):
+    for k, ref in zip(offsets, refs):
         owner = me ^ k if is_power(n) else lax.rem(me - k + n, n)
         stage[owner] = ref[...]
     half = stage.shape[1] - EXTRA
@@ -190,7 +194,7 @@
 def chip_sum_kernel(*refs):
     *parts, out_ref, stage = refs
     chip = lax.axis_index("row") // CORES
-    grads, bias = total_of(len(parts), chip, parts, stage)
+    grads, bias = total_of(len(parts), chip, range(len(parts)), parts, stage)
     half = grads.shape[0]
     out_ref[:half] = grads.astype(BF16)
     out_ref[half:] = pack_bias(bias, EXTRA)
@@ -198,7 +202,8 @@
 
 def col_sum_kernel(norm, *refs):
     *parts, half_ref, bias_ref, stage = refs
-    grads, bias = total_of(len(parts), lax.axis_index("col"), parts, stage)
+    cols = len(parts)
+    grads, bias = total_of(cols, lax.axis_index("col"), [0] + col_order(cols), parts, stage)
     half_ref[...] = grads * norm
     bias_ref[...] = bias * norm
 
@@ -214,7 +219,7 @@
     keep_ref, send_ref, hidden, acc = refs[cols:]
     chips = rows // CORES
     row, col = lax.axis_index("row"), lax.axis_index("col")
-    for k, ref in enumerate(parts):
+    for k, ref in zip([0] + col_order(cols), parts):
         hidden[k] = ref[...]
     acc[...] = jnp.zeros_like(acc)
     positions = pos_ref[0]
@@ -306,7 +311,7 @@
         [(piece, F32)] + [(piece, BF16)] * (cols - 1),
         [pltpu.VMEM((rows,) + piece, BF16), pltpu.VMEM((cols,) + piece, F32)],
     )(block_pos, block_count, blocks, near, to_core(near, rows))
-    order = list(range(2, cols)) + [1]
+    order = col_order(cols)
     parts = [to_col(send[k - 1], cols, k) for k in order]
 
     out_piece, hidden, keep, bias_keep, half_send = call(
@@ -315,7 +320,7 @@
         [(piece, BF16), (piece, BF16), ((half, width), F32), ((1, width), F32), (grads_shape, BF16)],
     )(weight, bias_vector, cotangent, inv, own, *parts)
 
-    hidden_parts = {k: to_col(hidden, cols, k) for k in order}
+    hidden_parts = [to_col(hidden, cols, k) for k in order]
     grads = call(pair_sum_kernel, [VMEM] * 3, [(grads_shape, BF16)])(
         keep, bias_keep, to_core(half_send, rows)
     )
@@ -334,9 +339,9 @@
         [((chips,) + piece, F32), ((chips,) + piece, BF16)],
         [pltpu.VMEM((cols,) + piece, BF16), pltpu.VMEM((rows,) + piece, F32)],
         flops=LONG,
-    )(block_pos, block_count, turned, hidden, *(hidden_parts[k] for k in range(1, cols)))
+    )(block_pos, block_count, turned, hidden, *hidden_parts)
     col_send, grads = lax.optimization_barrier((col_send, grads))
-    grad_parts = {k: to_col(grads, cols, k) for k in order}
+    grad_parts = [to_col(grads, cols, k) for k in order]
     own_x, *send_x = call(
         merge_kernel, [VMEM] * 2, [(piece, F32)] + [(piece, BF16)] * (chips - 1)
     )(col_keep, to_core(col_send, rows))
@@ -348,7 +353,7 @@
         [VMEM] * cols,
         [((half, width), F32), ((1, width), F32)],
         [pltpu.VMEM((cols,) + grads_shape, BF16)],
-    )(grads, *(grad_parts[k] for k in range(1, cols)))
+    )(grads, *grad_parts)
     theirs = to_core(mine, rows)
     x_piece = call(owned_sum_kernel, [VMEM] * (1 + chips), [(piece, BF16)], flops=LONG)(
         inv, own_x, *parts_x

time: 47.7 us -> 48 us (level)
  waiting for transfers between devices: 15.5 us -> 17 us
  starting transfers between devices: 25.3 us -> 24 us
    ppermute x9, waiting for transfers between devices: 9.68 us -> 12 us  [to_col(): lax.ppermute(x, 'col', [(i, target(cols, i, k)) for i in range(cols)])]
    ppermute x9, starting transfers between devices: 13.1 us -> 11.5 us  [to_col(): lax.ppermute(x, 'col', [(i, target(cols, i, k)) for i in range(cols)])]
    ppermute x9, waiting for transfers between devices: 3.45 us -> 2.26 us  [to_chip(): return lax.ppermute(x, 'row', pairs)]
  transfers between devices with their start and end apart: 22 -> 22, of which waited for: 13 -> 11; matrix products, arithmetic and copies ran while one was open for 0% -> 0% of each run, Pallas kernels for 3% -> 3%
where the time goes in v11:
time: 48 us; the launch traced here: 47.8 us
  starting transfers between devices  24 us (50%)
  waiting for transfers between devices  17 us (35%)
  Pallas kernels  3.16 us (7%)
  local copies, waits for them, and re-layouts  2.17 us (5%)
  between operations  1.46 us (3%)
    ppermute x9, waiting for transfers between devices, to_col(): lax.ppermute(x, 'col', [(i, target(cols, i, k)) for i in range(cols)])  12 us
    ppermute x9, starting transfers between devices, to_chip(): return lax.ppermute(x, 'row', pairs)  11.7 us
    ppermute x9, starting transfers between devices, to_col(): lax.ppermute(x, 'col', [(i, target(cols, i, k)) for i in range(cols)])  11.5 us
    ppermute x4, waiting for transfers between devices, to_core(): return lax.ppermute(x, 'row', [(i, i ^ 1) for i in range(rows)])  2.78 us
    ppermute x9, waiting for transfers between devices, to_chip(): return lax.ppermute(x, 'row', pairs)  2.26 us
    unnamed x14, local copies, waits for them, and re-layouts  2.17 us
  transfers between devices with their start and end apart: 22, of which 11 were waited for; matrix products, arithmetic and copies ran while one was open for 0% of the time, Pallas kernels for 3%

profile of v11, /device:TPU:0, one launch (start us, length us, event | category | flops | bytes accessed | tf_op | source)
XLA Modules:
  0.0 47.8 jit_solution(5210010937526393024)
XLA Ops:
  0.6 0.6 %copy-done.4 = s32[128]{0:T(128)S(1)} copy-done((s32[128]{0:T(128)S(1)}, s32[128]{0:T(128)}, u32[]{:S(2)}) %copy-start.4) | copy-done | bytes 536
  1.3 0.8 %copy-done.2 = bf16[128,256]{1,0:T(8,128)(2,1)S(1)} copy-done((bf16[128,256]{1,0:T(8,128)(2,1)S(1)}, bf16[128,256]{1,0:T(8,128)(2,1)}, u32[]{:S(2)}) %copy-start.2) | copy-done | bytes 65560
  2.1 0.1 shard_map.112
  2.2 4.0 %collective-permute-start.2 = (bf16[128,256]{1,0:T(8,128)(2,1)S(1)}, bf16[128,256]{1,0:T(8,128)(2,1)S(1)}, u32[]{:S(2)}, u32[]{:S(2)}) collective-permute-start(bf16[128,256]{1,0:T(8,128)(2,1)S(1)} %get-tuple-element.39.refs_0_), channel_id=1, source_target_pairs={{0,24},{4,28},{8,16},{12,20},{16,8},{20,12},{24,0},{28,4},{1,25},{... | collective-permute-start | bytes 196616 | tf_op jit(solution)/shard_map/ppermute | solution.py:54
  6.2 0.5 %collective-permute-start.1 = (bf16[128,256]{1,0:T(8,128)(2,1)S(1)}, bf16[128,256]{1,0:T(8,128)(2,1)S(1)}, u32[]{:S(2)}, u32[]{:S(2)}) collective-permute-start(bf16[128,256]{1,0:T(8,128)(2,1)S(1)} %get-tuple-element.39.refs_0_), channel_id=1, source_target_pairs={{0,16},{4,20},{8,24},{12,28},{16,0},{20,4},{24,8},{28,12},{1,17},{... | collective-permute-start | bytes 196616 | tf_op jit(solution)/shard_map/ppermute | solution.py:54
  6.7 0.1 collective-permute-start
  7.5 0.0 copy-start.6
  7.5 0.7 %copy-done.6 = f32[256]{0:T(256)S(1)} copy-done((f32[256]{0:T(256)S(1)}, f32[256]{0:T(256)}, u32[]{:S(2)}) %copy-start.6) | copy-done | bytes 1048
  8.2 0.5 %shard_map.111 = (bf16[16,128,128]{2,1,0:T(8,128)(2,1)S(1)}, bf16[16,128,128]{2,1,0:T(8,128)(2,1)S(1)}, f32[1,256]{1,0:T(1,128)S(1)}) custom-call(s32[1,1]{1,0:T(1,128)S(6)} %copy.12.count_ref, s32[1,1,16,512]{3,2,1,0:T(8,128)S(1)} %copy-done.5, f32[1,256]{1,0:T(1,128)S(1)} %bitcast.4), custom_call_target="tpu_custom_call" | custom-call | flops 4000000000 | bytes 1000000 | tf_op jit(solution)/shard_map/pallas_call | solution.py:299
  8.7 0.0 collective-permute-done.2.refs_3_
  8.7 1.7 %collective-permute-done.1.refs_2_ = bf16[128,256]{1,0:T(8,128)(2,1)S(1)} collective-permute-done((bf16[128,256]{1,0:T(8,128)(2,1)S(1)}, bf16[128,256]{1,0:T(8,128)(2,1)S(1)}, u32[]{:S(2)}, u32[]{:S(2)}) %collective-permute-start.1) | collective-permute-done | bytes 65568 | tf_op jit(solution)/shard_map/ppermute | solution.py:54
  10.5 0.5 %collective-permute-done.refs_1_ = bf16[128,256]{1,0:T(8,128)(2,1)S(1)} collective-permute-done((bf16[128,256]{1,0:T(8,128)(2,1)S(1)}, bf16[128,256]{1,0:T(8,128)(2,1)S(1)}, u32[]{:S(2)}, u32[]{:S(2)}) %collective-permute-start) | collective-permute-done | bytes 65568 | tf_op jit(solution)/shard_map/ppermute | solution.py:54
  11.0 0.0 copy-start
  11.0 0.0 copy-start.1
  11.0 0.1 collective-permute-start.3
  11.1 1.5 %collective-permute-done.3.next_ref = bf16[4,128,256]{2,1,0:T(8,128)(2,1)S(1)} collective-permute-done((bf16[4,128,256]{2,1,0:T(8,128)(2,1)S(1)}, bf16[4,128,256]{2,1,0:T(8,128)(2,1)S(1)}, u32[]{:S(2)}, u32[]{:S(2)}) %collective-permute-start.3) | collective-permute-done | bytes 262176 | tf_op jit(solution)/shard_map/ppermute | solution.py:44
  12.6 0.5 %shard_map.114 = (f32[128,256]{1,0:T(8,128)S(1)}, bf16[128,256]{1,0:T(8,128)(2,1)S(1)}, bf16[128,256]{1,0:T(8,128)(2,1)S(1)}, bf16[128,256]{1,0:T(8,128)(2,1)S(1)}) custom-call(s32[1,1,16]{2,1,0:T(1,128)S(1)} %copy-done.3, s32[1,1]{1,0:T(1,128)S(6)} %copy.12.count_ref, bf16[16,128,128]{2,1,0:T(8,128)(2,1)S(1)} %get-tuple-element.40.blocks_ref, ...), custom_call_target="tpu_custom_call" | custom-call | flops 1000000 | bytes 1000000 | tf_op jit(solution)/shard_map/pallas_call | solution.py:308
  13.1 2.7 %collective-permute-start.4 = (bf16[128,256]{1,0:T(8,128)(2,1)S(1)}, bf16[128,256]{1,0:T(8,128)(2,1)S(1)}, u32[]{:S(2)}, u32[]{:S(2)}) collective-permute-start(bf16[128,256]{1,0:T(8,128)(2,1)S(1)} %get-tuple-element.45), channel_id=1, source_target_pairs={{0,2},{1,3},{2,0},{3,1},{4,6},{5,7},{6,4},{7,5},{8,10},{9,11},{10,... | collective-permute-start | bytes 196616 | tf_op jit(solution)/shard_map/ppermute | solution.py:58
  15.8 1.3 %collective-permute-start.5 = (bf16[128,256]{1,0:T(8,128)(2,1)S(1)}, bf16[128,256]{1,0:T(8,128)(2,1)S(1)}, u32[]{:S(2)}, u32[]{:S(2)}) collective-permute-start(bf16[128,256]{1,0:T(8,128)(2,1)S(1)} %get-tuple-element.46), channel_id=1, source_target_pairs={{0,3},{1,2},{2,1},{3,0},{4,7},{5,6},{6,5},{7,4},{8,11},{9,10},{10,... | collective-permute-start | bytes 196616 | tf_op jit(solution)/shard_map/ppermute | solution.py:58
  17.1 0.2 collective-permute-start.6
  17.4 3.7 %collective-permute-done.4.refs_1_ = bf16[128,256]{1,0:T(8,128)(2,1)S(1)} collective-permute-done((bf16[128,256]{1,0:T(8,128)(2,1)S(1)}, bf16[128,256]{1,0:T(8,128)(2,1)S(1)}, u32[]{:S(2)}, u32[]{:S(2)}) %collective-permute-start.4) | collective-permute-done | bytes 65568 | tf_op jit(solution)/shard_map/ppermute | solution.py:58
  21.1 1.1 %collective-permute-done.5.refs_2_ = bf16[128,256]{1,0:T(8,128)(2,1)S(1)} collective-permute-done((bf16[128,256]{1,0:T(8,128)(2,1)S(1)}, bf16[128,256]{1,0:T(8,128)(2,1)S(1)}, u32[]{:S(2)}, u32[]{:S(2)}) %collective-permute-start.5) | collective-permute-done | bytes 65568 | tf_op jit(solution)/shard_map/ppermute | solution.py:58
  22.2 0.6 %collective-permute-done.6.refs_3_ = bf16[128,256]{1,0:T(8,128)(2,1)S(1)} collective-permute-done((bf16[128,256]{1,0:T(8,128)(2,1)S(1)}, bf16[128,256]{1,0:T(8,128)(2,1)S(1)}, u32[]{:S(2)}, u32[]{:S(2)}) %collective-permute-start.6) | collective-permute-done | bytes 65568 | tf_op jit(solution)/shard_map/ppermute | solution.py:58
  22.8 0.4 shard_map.115
  23.2 0.1 collective-permute-start.10
  23.3 0.7 %collective-permute-start.9 = (bf16[128,256]{1,0:T(8,128)(2,1)S(1)}, bf16[128,256]{1,0:T(8,128)(2,1)S(1)}, u32[]{:S(2)}, u32[]{:S(2)}) collective-permute-start(bf16[128,256]{1,0:T(8,128)(2,1)S(1)} %get-tuple-element.50.refs_0_), channel_id=1, source_target_pairs={{0,1},{1,0},{2,3},{3,2},{4,5},{5,4},{6,7},{7,6},{8,9},{9,8},{10,11... | collective-permute-start | bytes 196616 | tf_op jit(solution)/shard_map/ppermute | solution.py:58
  24.0 3.1 %collective-permute-start.8 = (bf16[128,256]{1,0:T(8,128)(2,1)S(1)}, bf16[128,256]{1,0:T(8,128)(2,1)S(1)}, u32[]{:S(2)}, u32[]{:S(2)}) collective-permute-start(bf16[128,256]{1,0:T(8,128)(2,1)S(1)} %get-tuple-element.50.refs_0_), channel_id=1, source_target_pairs={{0,3},{1,2},{2,1},{3,0},{4,7},{5,6},{6,5},{7,4},{8,11},{9,10},{10,... | collective-permute-start | bytes 196616 | tf_op jit(solution)/shard_map/ppermute | solution.py:58
  27.1 1.5 %collective-permute-start.13 = (bf16[144,256]{1,0:T(8,128)(2,1)S(1)}, bf16[144,256]{1,0:T(8,128)(2,1)S(1)}, u32[]{:S(2)}, u32[]{:S(2)}) collective-permute-start(bf16[144,256]{1,0:T(8,128)(2,1)S(1)} %shard_map.117.refs_0_), channel_id=1, source_target_pairs={{0,24},{4,28},{8,16},{12,20},{16,8},{20,12},{24,0},{28,4},{1,25},{... | collective-permute-start | bytes 221192 | tf_op jit(solution)/shard_map/ppermute | solution.py:54
  28.7 0.5 %collective-permute-start.12 = (bf16[144,256]{1,0:T(8,128)(2,1)S(1)}, bf16[144,256]{1,0:T(8,128)(2,1)S(1)}, u32[]{:S(2)}, u32[]{:S(2)}) collective-permute-start(bf16[144,256]{1,0:T(8,128)(2,1)S(1)} %shard_map.117.refs_0_), channel_id=1, source_target_pairs={{0,16},{4,20},{8,24},{12,28},{16,0},{20,4},{24,8},{28,12},{1,17},{... | collective-permute-start | bytes 221192 | tf_op jit(solution)/shard_map/ppermute | solution.py:54
  29.2 1.5 %collective-permute-start.11 = (bf16[144,256]{1,0:T(8,128)(2,1)S(1)}, bf16[144,256]{1,0:T(8,128)(2,1)S(1)}, u32[]{:S(2)}, u32[]{:S(2)}) collective-permute-start(bf16[144,256]{1,0:T(8,128)(2,1)S(1)} %shard_map.117.refs_0_), channel_id=1, source_target_pairs={{0,8},{4,12},{8,0},{12,4},{16,24},{20,28},{24,16},{28,20},{1,9},{5... | collective-permute-start | bytes 221192 | tf_op jit(solution)/shard_map/ppermute | solution.py:54
  30.7 0.8 %collective-permute-done.8.refs_2_ = bf16[128,256]{1,0:T(8,128)(2,1)S(1)} collective-permute-done((bf16[128,256]{1,0:T(8,128)(2,1)S(1)}, bf16[128,256]{1,0:T(8,128)(2,1)S(1)}, u32[]{:S(2)}, u32[]{:S(2)}) %collective-permute-start.8) | collective-permute-done | bytes 65568 | tf_op jit(solution)/shard_map/ppermute | solution.py:58
  31.4 2.3 %collective-permute-done.7.refs_1_ = bf16[128,256]{1,0:T(8,128)(2,1)S(1)} collective-permute-done((bf16[128,256]{1,0:T(8,128)(2,1)S(1)}, bf16[128,256]{1,0:T(8,128)(2,1)S(1)}, u32[]{:S(2)}, u32[]{:S(2)}) %collective-permute-start.7) | collective-permute-done | bytes 65568 | tf_op jit(solution)/shard_map/ppermute | solution.py:58
  33.7 0.5 %shard_map.116 = (f32[4,128,256]{2,1,0:T(8,128)S(1)}, bf16[4,128,256]{2,1,0:T(8,128)(2,1)S(1)}) custom-call(s32[1,1,16]{2,1,0:T(1,128)S(1)} %copy-done.3, s32[1,1]{1,0:T(1,128)S(6)} %copy.12.count_ref, bf16[16,128,128]{2,1,0:T(8,128)(2,1)S(1)} %get-tuple-element.49.turned_ref, bf16[128,256]{1,0:T(8,128)(2,1)S(1)} %get-tuple-element.50.refs_0_, ...), custom_call_target="tpu_custom_call" | custom-call | flops 4000000000 | bytes 1000000 | tf_op jit(solution)/shard_map/pallas_call | solution.py:336
  34.3 0.1 shard_map.118.refs_0_
  34.4 0.5 %collective-permute-start.14 = (bf16[4,128,256]{2,1,0:T(8,128)(2,1)S(1)}, bf16[4,128,256]{2,1,0:T(8,128)(2,1)S(1)}, u32[]{:S(2)}, u32[]{:S(2)}) collective-permute-start(bf16[4,128,256]{2,1,0:T(8,128)(2,1)S(1)} %get-tuple-element.56), channel_id=1, source_target_pairs={{0,4},{4,0},{8,12},{12,8},{16,20},{20,16},{24,28},{28,24},{1,5},{5... | collective-permute-start | bytes 786440 | tf_op jit(solution)/shard_map/ppermute | solution.py:44
  34.9 0.1 collective-permute-start.20
  34.9 3.2 %collective-permute-start.19 = (bf16[144,256]{1,0:T(8,128)(2,1)S(1)}, bf16[144,256]{1,0:T(8,128)(2,1)S(1)}, u32[]{:S(2)}, u32[]{:S(2)}) collective-permute-start(bf16[144,256]{1,0:T(8,128)(2,1)S(1)} %shard_map.118.refs_0_), channel_id=1, source_target_pairs={{0,3},{1,2},{2,1},{3,0},{4,7},{5,6},{6,5},{7,4},{8,11},{9,10},{10,... | collective-permute-start | bytes 221192 | tf_op jit(solution)/shard_map/ppermute | solution.py:58
  38.2 0.2 collective-permute-start.18
  38.4 0.1 shard_map.119
  38.4 2.3 %collective-permute-start.15 = (bf16[128,256]{1,0:T(8,128)(2,1)S(1)}, bf16[128,256]{1,0:T(8,128)(2,1)S(1)}, u32[]{:S(2)}, u32[]{:S(2)}) collective-permute-start(bf16[128,256]{1,0:T(8,128)(2,1)S(1)} %get-tuple-element.58), channel_id=1, source_target_pairs={{0,24},{4,28},{8,16},{12,20},{16,8},{20,12},{24,0},{28,4},{1,25},{... | collective-permute-start | bytes 196616 | tf_op jit(solution)/shard_map/ppermute | solution.py:54
  40.7 0.5 %collective-permute-start.16 = (bf16[128,256]{1,0:T(8,128)(2,1)S(1)}, bf16[128,256]{1,0:T(8,128)(2,1)S(1)}, u32[]{:S(2)}, u32[]{:S(2)}) collective-permute-start(bf16[128,256]{1,0:T(8,128)(2,1)S(1)} %get-tuple-element.59), channel_id=1, source_target_pairs={{0,16},{4,20},{8,24},{12,28},{16,0},{20,4},{24,8},{28,12},{1,17},{... | collective-permute-start | bytes 196616 | tf_op jit(solution)/shard_map/ppermute | solution.py:54
  41.3 0.7 %collective-permute-start.17 = (bf16[128,256]{1,0:T(8,128)(2,1)S(1)}, bf16[128,256]{1,0:T(8,128)(2,1)S(1)}, u32[]{:S(2)}, u32[]{:S(2)}) collective-permute-start(bf16[128,256]{1,0:T(8,128)(2,1)S(1)} %get-tuple-element.60), channel_id=1, source_target_pairs={{0,8},{4,12},{8,0},{12,4},{16,24},{20,28},{24,16},{28,20},{1,9},{5... | collective-permute-start | bytes 196616 | tf_op jit(solution)/shard_map/ppermute | solution.py:54
  42.0 0.9 %collective-permute-done.19.refs_2_ = bf16[144,256]{1,0:T(8,128)(2,1)S(1)} collective-permute-done((bf16[144,256]{1,0:T(8,128)(2,1)S(1)}, bf16[144,256]{1,0:T(8,128)(2,1)S(1)}, u32[]{:S(2)}, u32[]{:S(2)}) %collective-permute-start.19) | collective-permute-done | bytes 73760 | tf_op jit(solution)/shard_map/ppermute | solution.py:58
  42.9 2.6 %collective-permute-done.18.refs_1_ = bf16[144,256]{1,0:T(8,128)(2,1)S(1)} collective-permute-done((bf16[144,256]{1,0:T(8,128)(2,1)S(1)}, bf16[144,256]{1,0:T(8,128)(2,1)S(1)}, u32[]{:S(2)}, u32[]{:S(2)}) %collective-permute-start.18) | collective-permute-done | bytes 73760 | tf_op jit(solution)/shard_map/ppermute | solution.py:58
  45.5 0.1 shard_map.121
  45.6 0.1 collective-permute-start.21
  45.7 1.3 %collective-permute-done.21.theirs_ref = f32[128,256]{1,0:T(8,128)S(1)} collective-permute-done((f32[128,256]{1,0:T(8,128)S(1)}, f32[128,256]{1,0:T(8,128)S(1)}, u32[]{:S(2)}, u32[]{:S(2)}) %collective-permute-start.21) | collective-permute-done | bytes 131104 | tf_op jit(solution)/shard_map/ppermute | solution.py:44
  47.0 0.8 %shard_map.122 = (bf16[128,256]{1,0:T(8,128)(2,1)}, bf16[128,256]{1,0:T(8,128)(2,1)}, f32[256,256]{1,0:T(8,128)}, f32[1,256]{1,0:T(1,128)}) custom-call(bf16[128,256]{1,0:T(8,128)(2,1)S(1)} %get-tuple-element.48.out_ref, bf16[128,256]{1,0:T(8,128)(2,1)S(1)} %shard_map.120.x_ref, f32[128,256]{1,0:T(8,128)S(1)} %get-tuple-element.62.mine_ref, ...), custom_call_target="tpu_custom_call" | custom-call | flops 1000000 | bytes 1000000 | tf_op jit(solution)/shard_map/pallas_call | solution.py:361
  (22 shorter events, 0.1 us)
Async XLA Ops:
  0.6 0.7 %copy-start.4 = (s32[128]{0:T(128)S(1)}, s32[128]{0:T(128)}, u32[]{:S(2)}) copy-start(s32[128]{0:T(128)} %param.9) | copy-start | bytes 1540
  1.3 0.8 %copy-start.2 = (bf16[128,256]{1,0:T(8,128)(2,1)S(1)}, bf16[128,256]{1,0:T(8,128)(2,1)}, u32[]{:S(2)}) copy-start(bf16[128,256]{1,0:T(8,128)(2,1)} %features_ref.1) | copy-start | bytes 196612
  2.1 5.4 %copy-start.5 = (s32[1,1,16,512]{3,2,1,0:T(8,128)S(1)}, s32[1,1,16,512]{3,2,1,0:T(8,128)}, u32[]{:S(2)}) copy-start(s32[1,1,16,512]{3,2,1,0:T(8,128)} %edge_ref.1) | copy-start | bytes 98308
  2.2 6.5 %collective-permute-start.2 = (bf16[128,256]{1,0:T(8,128)(2,1)S(1)}, bf16[128,256]{1,0:T(8,128)(2,1)S(1)}, u32[]{:S(2)}, u32[]{:S(2)}) collective-permute-start(bf16[128,256]{1,0:T(8,128)(2,1)S(1)} %get-tuple-element.39.refs_0_), channel_id=1, source_target_pairs={{0,24},{4,28},{8,16},{12,20},{16,8},{20,12},{24,0},{28,4},{1,25},{... | collective-permute-start | bytes 196616 | tf_op jit(solution)/shard_map/ppermute | solution.py:54
  6.2 4.3 %collective-permute-start.1 = (bf16[128,256]{1,0:T(8,128)(2,1)S(1)}, bf16[128,256]{1,0:T(8,128)(2,1)S(1)}, u32[]{:S(2)}, u32[]{:S(2)}) collective-permute-start(bf16[128,256]{1,0:T(8,128)(2,1)S(1)} %get-tuple-element.39.refs_0_), channel_id=1, source_target_pairs={{0,16},{4,20},{8,24},{12,28},{16,0},{20,4},{24,8},{28,12},{1,17},{... | collective-permute-start | bytes 196616 | tf_op jit(solution)/shard_map/ppermute | solution.py:54
  6.7 4.3 %collective-permute-start = (bf16[128,256]{1,0:T(8,128)(2,1)S(1)}, bf16[128,256]{1,0:T(8,128)(2,1)S(1)}, u32[]{:S(2)}, u32[]{:S(2)}) collective-permute-start(bf16[128,256]{1,0:T(8,128)(2,1)S(1)} %get-tuple-element.39.refs_0_), channel_id=1, source_target_pairs={{0,8},{4,12},{8,0},{12,4},{16,24},{20,28},{24,16},{28,20},{1,9},{5... | collective-permute-start | bytes 196616 | tf_op jit(solution)/shard_map/ppermute | solution.py:54
  7.5 0.7 %copy-start.6 = (f32[256]{0:T(256)S(1)}, f32[256]{0:T(256)}, u32[]{:S(2)}) copy-start(f32[256]{0:T(256)} %param.11) | copy-start | bytes 3076
  11.0 1.7 %copy-start.3 = (s32[1,1,16]{2,1,0:T(1,128)S(1)}, s32[1,1,16]{2,1,0:T(1,128)}, u32[]{:S(2)}) copy-start(s32[1,1,16]{2,1,0:T(1,128)} %pos_ref.3) | copy-start | bytes 196
  11.0 11.8 %copy-start = (bf16[256,256]{1,0:T(8,128)(2,1)S(1)}, bf16[256,256]{1,0:T(8,128)(2,1)}, u32[]{:S(2)}) copy-start(bf16[256,256]{1,0:T(8,128)(2,1)} %weight_ref.1) | copy-start | bytes 393220
  11.0 11.8 %copy-start.1 = (bf16[128,256]{1,0:T(8,128)(2,1)S(1)}, bf16[128,256]{1,0:T(8,128)(2,1)}, u32[]{:S(2)}) copy-start(bf16[128,256]{1,0:T(8,128)(2,1)} %cot_ref.1) | copy-start | bytes 196612
  11.0 1.6 %collective-permute-start.3 = (bf16[4,128,256]{2,1,0:T(8,128)(2,1)S(1)}, bf16[4,128,256]{2,1,0:T(8,128)(2,1)S(1)}, u32[]{:S(2)}, u32[]{:S(2)}) collective-permute-start(bf16[4,128,256]{2,1,0:T(8,128)(2,1)S(1)} %shard_map.113.near_ref), channel_id=1, source_target_pairs={{0,4},{4,0},{8,12},{12,8},{16,20},{20,16},{24,28},{28,24},{1,5},{5... | collective-permute-start | bytes 786440 | tf_op jit(solution)/shard_map/ppermute | solution.py:44
  13.1 8.0 %collective-permute-start.4 = (bf16[128,256]{1,0:T(8,128)(2,1)S(1)}, bf16[128,256]{1,0:T(8,128)(2,1)S(1)}, u32[]{:S(2)}, u32[]{:S(2)}) collective-permute-start(bf16[128,256]{1,0:T(8,128)(2,1)S(1)} %get-tuple-element.45), channel_id=1, source_target_pairs={{0,2},{1,3},{2,0},{3,1},{4,6},{5,7},{6,4},{7,5},{8,10},{9,11},{10,... | collective-permute-start | bytes 196616 | tf_op jit(solution)/shard_map/ppermute | solution.py:58
  15.8 6.4 %collective-permute-start.5 = (bf16[128,256]{1,0:T(8,128)(2,1)S(1)}, bf16[128,256]{1,0:T(8,128)(2,1)S(1)}, u32[]{:S(2)}, u32[]{:S(2)}) collective-permute-start(bf16[128,256]{1,0:T(8,128)(2,1)S(1)} %get-tuple-element.46), channel_id=1, source_target_pairs={{0,3},{1,2},{2,1},{3,0},{4,7},{5,6},{6,5},{7,4},{8,11},{9,10},{10,... | collective-permute-start | bytes 196616 | tf_op jit(solution)/shard_map/ppermute | solution.py:58
  17.1 5.7 %collective-permute-start.6 = (bf16[128,256]{1,0:T(8,128)(2,1)S(1)}, bf16[128,256]{1,0:T(8,128)(2,1)S(1)}, u32[]{:S(2)}, u32[]{:S(2)}) collective-permute-start(bf16[128,256]{1,0:T(8,128)(2,1)S(1)} %get-tuple-element.47), channel_id=1, source_target_pairs={{0,1},{1,0},{2,3},{3,2},{4,5},{5,4},{6,7},{7,6},{8,9},{9,8},{10,11... | collective-permute-start | bytes 196616 | tf_op jit(solution)/shard_map/ppermute | solution.py:58
  23.2 3.9 %collective-permute-start.10 = (bf16[144,256]{1,0:T(8,128)(2,1)S(1)}, bf16[144,256]{1,0:T(8,128)(2,1)S(1)}, u32[]{:S(2)}, u32[]{:S(2)}) collective-permute-start(bf16[144,256]{1,0:T(8,128)(2,1)S(1)} %get-tuple-element.55), channel_id=1, source_target_pairs={{0,4},{4,0},{8,12},{12,8},{16,20},{20,16},{24,28},{28,24},{1,5},{5... | collective-permute-start | bytes 221192 | tf_op jit(solution)/shard_map/ppermute | solution.py:44
  23.3 5.9 %collective-permute-start.9 = (bf16[128,256]{1,0:T(8,128)(2,1)S(1)}, bf16[128,256]{1,0:T(8,128)(2,1)S(1)}, u32[]{:S(2)}, u32[]{:S(2)}) collective-permute-start(bf16[128,256]{1,0:T(8,128)(2,1)S(1)} %get-tuple-element.50.refs_0_), channel_id=1, source_target_pairs={{0,1},{1,0},{2,3},{3,2},{4,5},{5,4},{6,7},{7,6},{8,9},{9,8},{10,11... | collective-permute-start | bytes 196616 | tf_op jit(solution)/shard_map/ppermute | solution.py:58
  24.0 7.5 %collective-permute-start.8 = (bf16[128,256]{1,0:T(8,128)(2,1)S(1)}, bf16[128,256]{1,0:T(8,128)(2,1)S(1)}, u32[]{:S(2)}, u32[]{:S(2)}) collective-permute-start(bf16[128,256]{1,0:T(8,128)(2,1)S(1)} %get-tuple-element.50.refs_0_), channel_id=1, source_target_pairs={{0,3},{1,2},{2,1},{3,0},{4,7},{5,6},{6,5},{7,4},{8,11},{9,10},{10,... | collective-permute-start | bytes 196616 | tf_op jit(solution)/shard_map/ppermute | solution.py:58
  27.1 6.6 %collective-permute-start.7 = (bf16[128,256]{1,0:T(8,128)(2,1)S(1)}, bf16[128,256]{1,0:T(8,128)(2,1)S(1)}, u32[]{:S(2)}, u32[]{:S(2)}) collective-permute-start(bf16[128,256]{1,0:T(8,128)(2,1)S(1)} %get-tuple-element.50.refs_0_), channel_id=1, source_target_pairs={{0,2},{1,3},{2,0},{3,1},{4,6},{5,7},{6,4},{7,5},{8,10},{9,11},{10,... | collective-permute-start | bytes 196616 | tf_op jit(solution)/shard_map/ppermute | solution.py:58
  27.1 7.1 %collective-permute-start.13 = (bf16[144,256]{1,0:T(8,128)(2,1)S(1)}, bf16[144,256]{1,0:T(8,128)(2,1)S(1)}, u32[]{:S(2)}, u32[]{:S(2)}) collective-permute-start(bf16[144,256]{1,0:T(8,128)(2,1)S(1)} %shard_map.117.refs_0_), channel_id=1, source_target_pairs={{0,24},{4,28},{8,16},{12,20},{16,8},{20,12},{24,0},{28,4},{1,25},{... | collective-permute-start | bytes 221192 | tf_op jit(solution)/shard_map/ppermute | solution.py:54
  28.7 5.6 %collective-permute-start.12 = (bf16[144,256]{1,0:T(8,128)(2,1)S(1)}, bf16[144,256]{1,0:T(8,128)(2,1)S(1)}, u32[]{:S(2)}, u32[]{:S(2)}) collective-permute-start(bf16[144,256]{1,0:T(8,128)(2,1)S(1)} %shard_map.117.refs_0_), channel_id=1, source_target_pairs={{0,16},{4,20},{8,24},{12,28},{16,0},{20,4},{24,8},{28,12},{1,17},{... | collective-permute-start | bytes 221192 | tf_op jit(solution)/shard_map/ppermute | solution.py:54
  29.2 5.1 %collective-permute-start.11 = (bf16[144,256]{1,0:T(8,128)(2,1)S(1)}, bf16[144,256]{1,0:T(8,128)(2,1)S(1)}, u32[]{:S(2)}, u32[]{:S(2)}) collective-permute-start(bf16[144,256]{1,0:T(8,128)(2,1)S(1)} %shard_map.117.refs_0_), channel_id=1, source_target_pairs={{0,8},{4,12},{8,0},{12,4},{16,24},{20,28},{24,16},{28,20},{1,9},{5... | collective-permute-start | bytes 221192 | tf_op jit(solution)/shard_map/ppermute | solution.py:54
  34.4 4.0 %collective-permute-start.14 = (bf16[4,128,256]{2,1,0:T(8,128)(2,1)S(1)}, bf16[4,128,256]{2,1,0:T(8,128)(2,1)S(1)}, u32[]{:S(2)}, u32[]{:S(2)}) collective-permute-start(bf16[4,128,256]{2,1,0:T(8,128)(2,1)S(1)} %get-tuple-element.56), channel_id=1, source_target_pairs={{0,4},{4,0},{8,12},{12,8},{16,20},{20,16},{24,28},{28,24},{1,5},{5... | collective-permute-start | bytes 786440 | tf_op jit(solution)/shard_map/ppermute | solution.py:44
  34.9 6.4 %collective-permute-start.20 = (bf16[144,256]{1,0:T(8,128)(2,1)S(1)}, bf16[144,256]{1,0:T(8,128)(2,1)S(1)}, u32[]{:S(2)}, u32[]{:S(2)}) collective-permute-start(bf16[144,256]{1,0:T(8,128)(2,1)S(1)} %shard_map.118.refs_0_), channel_id=1, source_target_pairs={{0,1},{1,0},{2,3},{3,2},{4,5},{5,4},{6,7},{7,6},{8,9},{9,8},{10,11... | collective-permute-start | bytes 221192 | tf_op jit(solution)/shard_map/ppermute | solution.py:58
  34.9 7.9 %collective-permute-start.19 = (bf16[144,256]{1,0:T(8,128)(2,1)S(1)}, bf16[144,256]{1,0:T(8,128)(2,1)S(1)}, u32[]{:S(2)}, u32[]{:S(2)}) collective-permute-start(bf16[144,256]{1,0:T(8,128)(2,1)S(1)} %shard_map.118.refs_0_), channel_id=1, source_target_pairs={{0,3},{1,2},{2,1},{3,0},{4,7},{5,6},{6,5},{7,4},{8,11},{9,10},{10,... | collective-permute-start | bytes 221192 | tf_op jit(solution)/shard_map/ppermute | solution.py:58
  38.2 7.3 %collective-permute-start.18 = (bf16[144,256]{1,0:T(8,128)(2,1)S(1)}, bf16[144,256]{1,0:T(8,128)(2,1)S(1)}, u32[]{:S(2)}, u32[]{:S(2)}) collective-permute-start(bf16[144,256]{1,0:T(8,128)(2,1)S(1)} %shard_map.118.refs_0_), channel_id=1, source_target_pairs={{0,2},{1,3},{2,0},{3,1},{4,6},{5,7},{6,4},{7,5},{8,10},{9,11},{10,... | collective-permute-start | bytes 221192 | tf_op jit(solution)/shard_map/ppermute | solution.py:58
  38.4 7.2 %collective-permute-start.15 = (bf16[128,256]{1,0:T(8,128)(2,1)S(1)}, bf16[128,256]{1,0:T(8,128)(2,1)S(1)}, u32[]{:S(2)}, u32[]{:S(2)}) collective-permute-start(bf16[128,256]{1,0:T(8,128)(2,1)S(1)} %get-tuple-element.58), channel_id=1, source_target_pairs={{0,24},{4,28},{8,16},{12,20},{16,8},{20,12},{24,0},{28,4},{1,25},{... | collective-permute-start | bytes 196616 | tf_op jit(solution)/shard_map/ppermute | solution.py:54
  40.7 4.9 %collective-permute-start.16 = (bf16[128,256]{1,0:T(8,128)(2,1)S(1)}, bf16[128,256]{1,0:T(8,128)(2,1)S(1)}, u32[]{:S(2)}, u32[]{:S(2)}) collective-permute-start(bf16[128,256]{1,0:T(8,128)(2,1)S(1)} %get-tuple-element.59), channel_id=1, source_target_pairs={{0,16},{4,20},{8,24},{12,28},{16,0},{20,4},{24,8},{28,12},{1,17},{... | collective-permute-start | bytes 196616 | tf_op jit(solution)/shard_map/ppermute | solution.py:54
  41.3 4.4 %collective-permute-start.17 = (bf16[128,256]{1,0:T(8,128)(2,1)S(1)}, bf16[128,256]{1,0:T(8,128)(2,1)S(1)}, u32[]{:S(2)}, u32[]{:S(2)}) collective-permute-start(bf16[128,256]{1,0:T(8,128)(2,1)S(1)} %get-tuple-element.60), channel_id=1, source_target_pairs={{0,8},{4,12},{8,0},{12,4},{16,24},{20,28},{24,16},{28,20},{1,9},{5... | collective-permute-start | bytes 196616 | tf_op jit(solution)/shard_map/ppermute | solution.py:54
  45.6 1.4 %collective-permute-start.21 = (f32[128,256]{1,0:T(8,128)S(1)}, f32[128,256]{1,0:T(8,128)S(1)}, u32[]{:S(2)}, u32[]{:S(2)}) collective-permute-start(f32[128,256]{1,0:T(8,128)S(1)} %get-tuple-element.62.mine_ref), channel_id=1, source_target_pairs={{0,4},{4,0},{8,12},{12,8},{16,20},{20,16},{24,28},{28,24},{1,5},{5... | collective-permute-start | bytes 393224 | tf_op jit(solution)/shard_map/ppermute | solution.py:44

commit v12 on v11

--- a/solution.py
+++ b/solution.py
@@ -203,7 +203,7 @@
 def col_sum_kernel(norm, *refs):
     *parts, half_ref, bias_ref, stage = refs
     cols = len(parts)
-    grads, bias = total_of(cols, lax.axis_index("col"), [0] + col_order(cols), parts, stage)
+    grads, bias = total_of(cols, lax.axis_index("col"), [0] + col_order(cols)[::-1], parts, stage)
     half_ref[...] = grads * norm
     bias_ref[...] = bias * norm
 
@@ -219,7 +219,7 @@
     keep_ref, send_ref, hidden, acc = refs[cols:]
     chips = rows // CORES
     row, col = lax.axis_index("row"), lax.axis_index("col")
-    for k, ref in zip([0] + col_order(cols), parts):
+    for k, ref in zip([0] + col_order(cols)[::-1], parts):
         hidden[k] = ref[...]
     acc[...] = jnp.zeros_like(acc)
     positions = pos_ref[0]
@@ -320,7 +320,7 @@
         [(piece, BF16), (piece, BF16), ((half, width), F32), ((1, width), F32), (grads_shape, BF16)],
     )(weight, bias_vector, cotangent, inv, own, *parts)
 
-    hidden_parts = [to_col(hidden, cols, k) for k in order]
+    hidden_parts = [to_col(hidden, cols, k) for k in order[::-1]]
     grads = call(pair_sum_kernel, [VMEM] * 3, [(grads_shape, BF16)])(
         keep, bias_keep, to_core(half_send, rows)
     )
@@ -341,7 +341,7 @@
         flops=LONG,
     )(block_pos, block_count, turned, hidden, *hidden_parts)
     col_send, grads = lax.optimization_barrier((col_send, grads))
-    grad_parts = [to_col(grads, cols, k) for k in order]
+    grad_parts = [to_col(grads, cols, k) for k in order[::-1]]
     own_x, *send_x = call(
         merge_kernel, [VMEM] * 2, [(piece, F32)] + [(piece, BF16)] * (chips - 1)
     )(col_keep, to_core(col_send, rows))

time: 48 us -> 48.8 us (1.017)
  the two profiles are of different devices: /device:TPU:0 before, /device:TPU:4 now
where the time goes in v12:
time: 48.8 us; the launch traced here: 48.7 us
  waiting for transfers between devices  22.1 us (45%)
  starting transfers between devices  19.8 us (41%)
  Pallas kernels  3.17 us (6%)
  local copies, waits for them, and re-layouts  2.17 us (4%)
  between operations  1.47 us (3%)
    ppermute x9, waiting for transfers between devices, to_col(): lax.ppermute(x, 'col', [(i, target(cols, i, k)) for i in range(cols)])  13.2 us
    ppermute x9, starting transfers between devices, to_col(): lax.ppermute(x, 'col', [(i, target(cols, i, k)) for i in range(cols)])  11.9 us
    ppermute x9, starting transfers between devices, to_chip(): return lax.ppermute(x, 'row', pairs)  7.64 us
    ppermute x9, waiting for transfers between devices, to_chip(): return lax.ppermute(x, 'row', pairs)  7.3 us
    unnamed x14, local copies, waits for them, and re-layouts  2.17 us
    ppermute x4, waiting for transfers between devices, to_core(): return lax.ppermute(x, 'row', [(i, i ^ 1) for i in range(rows)])  1.53 us
  transfers between devices with their start and end apart: 22, of which 14 were waited for; matrix products, arithmetic and copies ran while one was open for 0% of the time, Pallas kernels for 3%

profile of v12, /device:TPU:4, one launch (start us, length us, event | category | flops | bytes accessed | tf_op | source)
XLA Modules:
  0.0 48.7 jit_solution(3558079601233899772)
XLA Ops:
  0.6 0.6 %copy-done.4 = s32[128]{0:T(128)S(1)} copy-done((s32[128]{0:T(128)S(1)}, s32[128]{0:T(128)}, u32[]{:S(2)}) %copy-start.4) | copy-done | bytes 536
  1.3 0.8 %copy-done.2 = bf16[128,256]{1,0:T(8,128)(2,1)S(1)} copy-done((bf16[128,256]{1,0:T(8,128)(2,1)S(1)}, bf16[128,256]{1,0:T(8,128)(2,1)}, u32[]{:S(2)}) %copy-start.2) | copy-done | bytes 65560
  2.1 0.1 shard_map.112
  2.2 1.5 %collective-permute-start.2 = (bf16[128,256]{1,0:T(8,128)(2,1)S(1)}, bf16[128,256]{1,0:T(8,128)(2,1)S(1)}, u32[]{:S(2)}, u32[]{:S(2)}) collective-permute-start(bf16[128,256]{1,0:T(8,128)(2,1)S(1)} %get-tuple-element.39.refs_0_), channel_id=1, source_target_pairs={{0,24},{4,28},{8,16},{12,20},{16,8},{20,12},{24,0},{28,4},{1,25},{... | collective-permute-start | bytes 196616 | tf_op jit(solution)/shard_map/ppermute | solution.py:54
  3.7 1.5 %collective-permute-start.1 = (bf16[128,256]{1,0:T(8,128)(2,1)S(1)}, bf16[128,256]{1,0:T(8,128)(2,1)S(1)}, u32[]{:S(2)}, u32[]{:S(2)}) collective-permute-start(bf16[128,256]{1,0:T(8,128)(2,1)S(1)} %get-tuple-element.39.refs_0_), channel_id=1, source_target_pairs={{0,16},{4,20},{8,24},{12,28},{16,0},{20,4},{24,8},{28,12},{1,17},{... | collective-permute-start | bytes 196616 | tf_op jit(solution)/shard_map/ppermute | solution.py:54
  5.3 0.5 %collective-permute-start = (bf16[128,256]{1,0:T(8,128)(2,1)S(1)}, bf16[128,256]{1,0:T(8,128)(2,1)S(1)}, u32[]{:S(2)}, u32[]{:S(2)}) collective-permute-start(bf16[128,256]{1,0:T(8,128)(2,1)S(1)} %get-tuple-element.39.refs_0_), channel_id=1, source_target_pairs={{0,8},{4,12},{8,0},{12,4},{16,24},{20,28},{24,16},{28,20},{1,9},{5... | collective-permute-start | bytes 196616 | tf_op jit(solution)/shard_map/ppermute | solution.py:54
  6.5 0.0 copy-start.6
  6.5 0.7 %copy-done.6 = f32[256]{0:T(256)S(1)} copy-done((f32[256]{0:T(256)S(1)}, f32[256]{0:T(256)}, u32[]{:S(2)}) %copy-start.6) | copy-done | bytes 1048
  7.1 0.5 %shard_map.111 = (bf16[16,128,128]{2,1,0:T(8,128)(2,1)S(1)}, bf16[16,128,128]{2,1,0:T(8,128)(2,1)S(1)}, f32[1,256]{1,0:T(1,128)S(1)}) custom-call(s32[1,1]{1,0:T(1,128)S(6)} %copy.12.count_ref, s32[1,1,16,512]{3,2,1,0:T(8,128)S(1)} %copy-done.5, f32[1,256]{1,0:T(1,128)S(1)} %bitcast.4), custom_call_target="tpu_custom_call" | custom-call | flops 4000000000 | bytes 1000000 | tf_op jit(solution)/shard_map/pallas_call | solution.py:299
  7.7 0.2 collective-permute-done.2.refs_3_
  7.9 0.6 %collective-permute-done.1.refs_2_ = bf16[128,256]{1,0:T(8,128)(2,1)S(1)} collective-permute-done((bf16[128,256]{1,0:T(8,128)(2,1)S(1)}, bf16[128,256]{1,0:T(8,128)(2,1)S(1)}, u32[]{:S(2)}, u32[]{:S(2)}) %collective-permute-start.1) | collective-permute-done | bytes 65568 | tf_op jit(solution)/shard_map/ppermute | solution.py:54
  8.4 1.1 %collective-permute-done.refs_1_ = bf16[128,256]{1,0:T(8,128)(2,1)S(1)} collective-permute-done((bf16[128,256]{1,0:T(8,128)(2,1)S(1)}, bf16[128,256]{1,0:T(8,128)(2,1)S(1)}, u32[]{:S(2)}, u32[]{:S(2)}) %collective-permute-start) | collective-permute-done | bytes 65568 | tf_op jit(solution)/shard_map/ppermute | solution.py:54
  9.6 0.0 copy-start
  9.6 0.1 collective-permute-start.3
  9.7 1.5 %collective-permute-done.3.next_ref = bf16[4,128,256]{2,1,0:T(8,128)(2,1)S(1)} collective-permute-done((bf16[4,128,256]{2,1,0:T(8,128)(2,1)S(1)}, bf16[4,128,256]{2,1,0:T(8,128)(2,1)S(1)}, u32[]{:S(2)}, u32[]{:S(2)}) %collective-permute-start.3) | collective-permute-done | bytes 262176 | tf_op jit(solution)/shard_map/ppermute | solution.py:44
  11.2 0.5 %shard_map.114 = (f32[128,256]{1,0:T(8,128)S(1)}, bf16[128,256]{1,0:T(8,128)(2,1)S(1)}, bf16[128,256]{1,0:T(8,128)(2,1)S(1)}, bf16[128,256]{1,0:T(8,128)(2,1)S(1)}) custom-call(s32[1,1,16]{2,1,0:T(1,128)S(1)} %copy-done.3, s32[1,1]{1,0:T(1,128)S(6)} %copy.12.count_ref, bf16[16,128,128]{2,1,0:T(8,128)(2,1)S(1)} %get-tuple-element.40.blocks_ref, ...), custom_call_target="tpu_custom_call" | custom-call | flops 1000000 | bytes 1000000 | tf_op jit(solution)/shard_map/pallas_call | solution.py:308
  11.7 2.7 %collective-permute-start.4 = (bf16[128,256]{1,0:T(8,128)(2,1)S(1)}, bf16[128,256]{1,0:T(8,128)(2,1)S(1)}, u32[]{:S(2)}, u32[]{:S(2)}) collective-permute-start(bf16[128,256]{1,0:T(8,128)(2,1)S(1)} %get-tuple-element.45), channel_id=1, source_target_pairs={{0,2},{1,3},{2,0},{3,1},{4,6},{5,7},{6,4},{7,5},{8,10},{9,11},{10,... | collective-permute-start | bytes 196616 | tf_op jit(solution)/shard_map/ppermute | solution.py:58
  14.3 1.3 %collective-permute-start.5 = (bf16[128,256]{1,0:T(8,128)(2,1)S(1)}, bf16[128,256]{1,0:T(8,128)(2,1)S(1)}, u32[]{:S(2)}, u32[]{:S(2)}) collective-permute-start(bf16[128,256]{1,0:T(8,128)(2,1)S(1)} %get-tuple-element.46), channel_id=1, source_target_pairs={{0,3},{1,2},{2,1},{3,0},{4,7},{5,6},{6,5},{7,4},{8,11},{9,10},{10,... | collective-permute-start | bytes 196616 | tf_op jit(solution)/shard_map/ppermute | solution.py:58
  15.7 0.2 collective-permute-start.6
  15.9 3.7 %collective-permute-done.4.refs_1_ = bf16[128,256]{1,0:T(8,128)(2,1)S(1)} collective-permute-done((bf16[128,256]{1,0:T(8,128)(2,1)S(1)}, bf16[128,256]{1,0:T(8,128)(2,1)S(1)}, u32[]{:S(2)}, u32[]{:S(2)}) %collective-permute-start.4) | collective-permute-done | bytes 65568 | tf_op jit(solution)/shard_map/ppermute | solution.py:58
  19.6 1.1 %collective-permute-done.5.refs_2_ = bf16[128,256]{1,0:T(8,128)(2,1)S(1)} collective-permute-done((bf16[128,256]{1,0:T(8,128)(2,1)S(1)}, bf16[128,256]{1,0:T(8,128)(2,1)S(1)}, u32[]{:S(2)}, u32[]{:S(2)}) %collective-permute-start.5) | collective-permute-done | bytes 65568 | tf_op jit(solution)/shard_map/ppermute | solution.py:58
  20.7 0.6 %collective-permute-done.6.refs_3_ = bf16[128,256]{1,0:T(8,128)(2,1)S(1)} collective-permute-done((bf16[128,256]{1,0:T(8,128)(2,1)S(1)}, bf16[128,256]{1,0:T(8,128)(2,1)S(1)}, u32[]{:S(2)}, u32[]{:S(2)}) %collective-permute-start.6) | collective-permute-done | bytes 65568 | tf_op jit(solution)/shard_map/ppermute | solution.py:58
  21.4 0.4 shard_map.115
  21.7 0.1 collective-permute-start.10
  21.8 2.3 %collective-permute-start.9 = (bf16[128,256]{1,0:T(8,128)(2,1)S(1)}, bf16[128,256]{1,0:T(8,128)(2,1)S(1)}, u32[]{:S(2)}, u32[]{:S(2)}) collective-permute-start(bf16[128,256]{1,0:T(8,128)(2,1)S(1)} %get-tuple-element.50.refs_0_), channel_id=1, source_target_pairs={{0,2},{1,3},{2,0},{3,1},{4,6},{5,7},{6,4},{7,5},{8,10},{9,11},{10,... | collective-permute-start | bytes 196616 | tf_op jit(solution)/shard_map/ppermute | solution.py:58
  24.2 0.7 %collective-permute-start.8 = (bf16[128,256]{1,0:T(8,128)(2,1)S(1)}, bf16[128,256]{1,0:T(8,128)(2,1)S(1)}, u32[]{:S(2)}, u32[]{:S(2)}) collective-permute-start(bf16[128,256]{1,0:T(8,128)(2,1)S(1)} %get-tuple-element.50.refs_0_), channel_id=1, source_target_pairs={{0,3},{1,2},{2,1},{3,0},{4,7},{5,6},{6,5},{7,4},{8,11},{9,10},{10,... | collective-permute-start | bytes 196616 | tf_op jit(solution)/shard_map/ppermute | solution.py:58
  24.9 0.5 %collective-permute-start.7 = (bf16[128,256]{1,0:T(8,128)(2,1)S(1)}, bf16[128,256]{1,0:T(8,128)(2,1)S(1)}, u32[]{:S(2)}, u32[]{:S(2)}) collective-permute-start(bf16[128,256]{1,0:T(8,128)(2,1)S(1)} %get-tuple-element.50.refs_0_), channel_id=1, source_target_pairs={{0,1},{1,0},{2,3},{3,2},{4,5},{5,4},{6,7},{7,6},{8,9},{9,8},{10,11... | collective-permute-start | bytes 196616 | tf_op jit(solution)/shard_map/ppermute | solution.py:58
  25.4 0.5 %collective-permute-start.13 = (bf16[144,256]{1,0:T(8,128)(2,1)S(1)}, bf16[144,256]{1,0:T(8,128)(2,1)S(1)}, u32[]{:S(2)}, u32[]{:S(2)}) collective-permute-start(bf16[144,256]{1,0:T(8,128)(2,1)S(1)} %shard_map.117.refs_0_), channel_id=1, source_target_pairs={{0,24},{4,28},{8,16},{12,20},{16,8},{20,12},{24,0},{28,4},{1,25},{... | collective-permute-start | bytes 221192 | tf_op jit(solution)/shard_map/ppermute | solution.py:54
  25.9 1.5 %collective-permute-start.12 = (bf16[144,256]{1,0:T(8,128)(2,1)S(1)}, bf16[144,256]{1,0:T(8,128)(2,1)S(1)}, u32[]{:S(2)}, u32[]{:S(2)}) collective-permute-start(bf16[144,256]{1,0:T(8,128)(2,1)S(1)} %shard_map.117.refs_0_), channel_id=1, source_target_pairs={{0,16},{4,20},{8,24},{12,28},{16,0},{20,4},{24,8},{28,12},{1,17},{... | collective-permute-start | bytes 221192 | tf_op jit(solution)/shard_map/ppermute | solution.py:54
  27.4 2.4 %collective-permute-done.9.refs_3_ = bf16[128,256]{1,0:T(8,128)(2,1)S(1)} collective-permute-done((bf16[128,256]{1,0:T(8,128)(2,1)S(1)}, bf16[128,256]{1,0:T(8,128)(2,1)S(1)}, u32[]{:S(2)}, u32[]{:S(2)}) %collective-permute-start.9) | collective-permute-done | bytes 65568 | tf_op jit(solution)/shard_map/ppermute | solution.py:58
  29.8 1.0 %collective-permute-done.8.refs_2_ = bf16[128,256]{1,0:T(8,128)(2,1)S(1)} collective-permute-done((bf16[128,256]{1,0:T(8,128)(2,1)S(1)}, bf16[128,256]{1,0:T(8,128)(2,1)S(1)}, u32[]{:S(2)}, u32[]{:S(2)}) %collective-permute-start.8) | collective-permute-done | bytes 65568 | tf_op jit(solution)/shard_map/ppermute | solution.py:58
  30.8 0.6 %collective-permute-done.7.refs_1_ = bf16[128,256]{1,0:T(8,128)(2,1)S(1)} collective-permute-done((bf16[128,256]{1,0:T(8,128)(2,1)S(1)}, bf16[128,256]{1,0:T(8,128)(2,1)S(1)}, u32[]{:S(2)}, u32[]{:S(2)}) %collective-permute-start.7) | collective-permute-done | bytes 65568 | tf_op jit(solution)/shard_map/ppermute | solution.py:58
  31.4 0.5 %shard_map.116 = (f32[4,128,256]{2,1,0:T(8,128)S(1)}, bf16[4,128,256]{2,1,0:T(8,128)(2,1)S(1)}) custom-call(s32[1,1,16]{2,1,0:T(1,128)S(1)} %copy-done.3, s32[1,1]{1,0:T(1,128)S(6)} %copy.12.count_ref, bf16[16,128,128]{2,1,0:T(8,128)(2,1)S(1)} %get-tuple-element.49.turned_ref, bf16[128,256]{1,0:T(8,128)(2,1)S(1)} %get-tuple-element.50.refs_0_, ...), custom_call_target="tpu_custom_call" | custom-call | flops 4000000000 | bytes 1000000 | tf_op jit(solution)/shard_map/pallas_call | solution.py:336
  32.0 2.2 %collective-permute-done.11.refs_1_ = bf16[144,256]{1,0:T(8,128)(2,1)S(1)} collective-permute-done((bf16[144,256]{1,0:T(8,128)(2,1)S(1)}, bf16[144,256]{1,0:T(8,128)(2,1)S(1)}, u32[]{:S(2)}, u32[]{:S(2)}) %collective-permute-start.11) | collective-permute-done | bytes 73760 | tf_op jit(solution)/shard_map/ppermute | solution.py:54
  34.2 0.1 shard_map.118.refs_0_
  34.3 0.1 collective-permute-start.14
  34.3 0.9 %collective-permute-start.20 = (bf16[144,256]{1,0:T(8,128)(2,1)S(1)}, bf16[144,256]{1,0:T(8,128)(2,1)S(1)}, u32[]{:S(2)}, u32[]{:S(2)}) collective-permute-start(bf16[144,256]{1,0:T(8,128)(2,1)S(1)} %shard_map.118.refs_0_), channel_id=1, source_target_pairs={{0,2},{1,3},{2,0},{3,1},{4,6},{5,7},{6,4},{7,5},{8,10},{9,11},{10,... | collective-permute-start | bytes 221192 | tf_op jit(solution)/shard_map/ppermute | solution.py:58
  35.3 2.7 %collective-permute-start.19 = (bf16[144,256]{1,0:T(8,128)(2,1)S(1)}, bf16[144,256]{1,0:T(8,128)(2,1)S(1)}, u32[]{:S(2)}, u32[]{:S(2)}) collective-permute-start(bf16[144,256]{1,0:T(8,128)(2,1)S(1)} %shard_map.118.refs_0_), channel_id=1, source_target_pairs={{0,3},{1,2},{2,1},{3,0},{4,7},{5,6},{6,5},{7,4},{8,11},{9,10},{10,... | collective-permute-start | bytes 221192 | tf_op jit(solution)/shard_map/ppermute | solution.py:58
  38.0 0.5 %collective-permute-start.18 = (bf16[144,256]{1,0:T(8,128)(2,1)S(1)}, bf16[144,256]{1,0:T(8,128)(2,1)S(1)}, u32[]{:S(2)}, u32[]{:S(2)}) collective-permute-start(bf16[144,256]{1,0:T(8,128)(2,1)S(1)} %shard_map.118.refs_0_), channel_id=1, source_target_pairs={{0,1},{1,0},{2,3},{3,2},{4,5},{5,4},{6,7},{7,6},{8,9},{9,8},{10,11... | collective-permute-start | bytes 221192 | tf_op jit(solution)/shard_map/ppermute | solution.py:58
  38.4 0.1 shard_map.119
  38.5 0.5 %collective-permute-start.15 = (bf16[128,256]{1,0:T(8,128)(2,1)S(1)}, bf16[128,256]{1,0:T(8,128)(2,1)S(1)}, u32[]{:S(2)}, u32[]{:S(2)}) collective-permute-start(bf16[128,256]{1,0:T(8,128)(2,1)S(1)} %get-tuple-element.58), channel_id=1, source_target_pairs={{0,24},{4,28},{8,16},{12,20},{16,8},{20,12},{24,0},{28,4},{1,25},{... | collective-permute-start | bytes 196616 | tf_op jit(solution)/shard_map/ppermute | solution.py:54
  39.1 1.5 %collective-permute-start.16 = (bf16[128,256]{1,0:T(8,128)(2,1)S(1)}, bf16[128,256]{1,0:T(8,128)(2,1)S(1)}, u32[]{:S(2)}, u32[]{:S(2)}) collective-permute-start(bf16[128,256]{1,0:T(8,128)(2,1)S(1)} %get-tuple-element.59), channel_id=1, source_target_pairs={{0,16},{4,20},{8,24},{12,28},{16,0},{20,4},{24,8},{28,12},{1,17},{... | collective-permute-start | bytes 196616 | tf_op jit(solution)/shard_map/ppermute | solution.py:54
  40.6 3.0 %collective-permute-done.20.refs_3_ = bf16[144,256]{1,0:T(8,128)(2,1)S(1)} collective-permute-done((bf16[144,256]{1,0:T(8,128)(2,1)S(1)}, bf16[144,256]{1,0:T(8,128)(2,1)S(1)}, u32[]{:S(2)}, u32[]{:S(2)}) %collective-permute-start.20) | collective-permute-done | bytes 73760 | tf_op jit(solution)/shard_map/ppermute | solution.py:58
  43.6 0.8 %collective-permute-done.18.refs_1_ = bf16[144,256]{1,0:T(8,128)(2,1)S(1)} collective-permute-done((bf16[144,256]{1,0:T(8,128)(2,1)S(1)}, bf16[144,256]{1,0:T(8,128)(2,1)S(1)}, u32[]{:S(2)}, u32[]{:S(2)}) %collective-permute-start.18) | collective-permute-done | bytes 73760 | tf_op jit(solution)/shard_map/ppermute | solution.py:58
  44.4 0.1 shard_map.121
  44.5 0.1 collective-permute-start.21
  44.6 3.2 %collective-permute-done.17.refs_2_ = bf16[128,256]{1,0:T(8,128)(2,1)S(1)} collective-permute-done((bf16[128,256]{1,0:T(8,128)(2,1)S(1)}, bf16[128,256]{1,0:T(8,128)(2,1)S(1)}, u32[]{:S(2)}, u32[]{:S(2)}) %collective-permute-start.17) | collective-permute-done | bytes 65568 | tf_op jit(solution)/shard_map/ppermute | solution.py:54
  47.9 0.8 %shard_map.122 = (bf16[128,256]{1,0:T(8,128)(2,1)}, bf16[128,256]{1,0:T(8,128)(2,1)}, f32[256,256]{1,0:T(8,128)}, f32[1,256]{1,0:T(1,128)}) custom-call(bf16[128,256]{1,0:T(8,128)(2,1)S(1)} %get-tuple-element.48.out_ref, bf16[128,256]{1,0:T(8,128)(2,1)S(1)} %shard_map.120.x_ref, f32[128,256]{1,0:T(8,128)S(1)} %get-tuple-element.62.mine_ref, ...), custom_call_target="tpu_custom_call" | custom-call | flops 1000000 | bytes 1000000 | tf_op jit(solution)/shard_map/pallas_call | solution.py:361
  (22 shorter events, 0.1 us)
Async XLA Ops:
  0.6 0.7 %copy-start.4 = (s32[128]{0:T(128)S(1)}, s32[128]{0:T(128)}, u32[]{:S(2)}) copy-start(s32[128]{0:T(128)} %param.9) | copy-start | bytes 1540
  1.3 0.8 %copy-start.2 = (bf16[128,256]{1,0:T(8,128)(2,1)S(1)}, bf16[128,256]{1,0:T(8,128)(2,1)}, u32[]{:S(2)}) copy-start(bf16[128,256]{1,0:T(8,128)(2,1)} %features_ref.1) | copy-start | bytes 196612
  2.1 4.3 %copy-start.5 = (s32[1,1,16,512]{3,2,1,0:T(8,128)S(1)}, s32[1,1,16,512]{3,2,1,0:T(8,128)}, u32[]{:S(2)}) copy-start(s32[1,1,16,512]{3,2,1,0:T(8,128)} %edge_ref.1) | copy-start | bytes 98308
  2.2 5.6 %collective-permute-start.2 = (bf16[128,256]{1,0:T(8,128)(2,1)S(1)}, bf16[128,256]{1,0:T(8,128)(2,1)S(1)}, u32[]{:S(2)}, u32[]{:S(2)}) collective-permute-start(bf16[128,256]{1,0:T(8,128)(2,1)S(1)} %get-tuple-element.39.refs_0_), channel_id=1, source_target_pairs={{0,24},{4,28},{8,16},{12,20},{16,8},{20,12},{24,0},{28,4},{1,25},{... | collective-permute-start | bytes 196616 | tf_op jit(solution)/shard_map/ppermute | solution.py:54
  3.7 4.7 %collective-permute-start.1 = (bf16[128,256]{1,0:T(8,128)(2,1)S(1)}, bf16[128,256]{1,0:T(8,128)(2,1)S(1)}, u32[]{:S(2)}, u32[]{:S(2)}) collective-permute-start(bf16[128,256]{1,0:T(8,128)(2,1)S(1)} %get-tuple-element.39.refs_0_), channel_id=1, source_target_pairs={{0,16},{4,20},{8,24},{12,28},{16,0},{20,4},{24,8},{28,12},{1,17},{... | collective-permute-start | bytes 196616 | tf_op jit(solution)/shard_map/ppermute | solution.py:54
  5.3 4.3 %collective-permute-start = (bf16[128,256]{1,0:T(8,128)(2,1)S(1)}, bf16[128,256]{1,0:T(8,128)(2,1)S(1)}, u32[]{:S(2)}, u32[]{:S(2)}) collective-permute-start(bf16[128,256]{1,0:T(8,128)(2,1)S(1)} %get-tuple-element.39.refs_0_), channel_id=1, source_target_pairs={{0,8},{4,12},{8,0},{12,4},{16,24},{20,28},{24,16},{28,20},{1,9},{5... | collective-permute-start | bytes 196616 | tf_op jit(solution)/shard_map/ppermute | solution.py:54
  6.5 0.7 %copy-start.6 = (f32[256]{0:T(256)S(1)}, f32[256]{0:T(256)}, u32[]{:S(2)}) copy-start(f32[256]{0:T(256)} %param.11) | copy-start | bytes 3076
  9.5 1.7 %copy-start.3 = (s32[1,1,16]{2,1,0:T(1,128)S(1)}, s32[1,1,16]{2,1,0:T(1,128)}, u32[]{:S(2)}) copy-start(s32[1,1,16]{2,1,0:T(1,128)} %pos_ref.3) | copy-start | bytes 196
  9.6 11.8 %copy-start = (bf16[256,256]{1,0:T(8,128)(2,1)S(1)}, bf16[256,256]{1,0:T(8,128)(2,1)}, u32[]{:S(2)}) copy-start(bf16[256,256]{1,0:T(8,128)(2,1)} %weight_ref.1) | copy-start | bytes 393220
  9.6 11.8 %copy-start.1 = (bf16[128,256]{1,0:T(8,128)(2,1)S(1)}, bf16[128,256]{1,0:T(8,128)(2,1)}, u32[]{:S(2)}) copy-start(bf16[128,256]{1,0:T(8,128)(2,1)} %cot_ref.1) | copy-start | bytes 196612
  9.6 1.6 %collective-permute-start.3 = (bf16[4,128,256]{2,1,0:T(8,128)(2,1)S(1)}, bf16[4,128,256]{2,1,0:T(8,128)(2,1)S(1)}, u32[]{:S(2)}, u32[]{:S(2)}) collective-permute-start(bf16[4,128,256]{2,1,0:T(8,128)(2,1)S(1)} %shard_map.113.near_ref), channel_id=1, source_target_pairs={{0,4},{4,0},{8,12},{12,8},{16,20},{20,16},{24,28},{28,24},{1,5},{5... | collective-permute-start | bytes 786440 | tf_op jit(solution)/shard_map/ppermute | solution.py:44
  11.7 8.0 %collective-permute-start.4 = (bf16[128,256]{1,0:T(8,128)(2,1)S(1)}, bf16[128,256]{1,0:T(8,128)(2,1)S(1)}, u32[]{:S(2)}, u32[]{:S(2)}) collective-permute-start(bf16[128,256]{1,0:T(8,128)(2,1)S(1)} %get-tuple-element.45), channel_id=1, source_target_pairs={{0,2},{1,3},{2,0},{3,1},{4,6},{5,7},{6,4},{7,5},{8,10},{9,11},{10,... | collective-permute-start | bytes 196616 | tf_op jit(solution)/shard_map/ppermute | solution.py:58
  14.3 6.4 %collective-permute-start.5 = (bf16[128,256]{1,0:T(8,128)(2,1)S(1)}, bf16[128,256]{1,0:T(8,128)(2,1)S(1)}, u32[]{:S(2)}, u32[]{:S(2)}) collective-permute-start(bf16[128,256]{1,0:T(8,128)(2,1)S(1)} %get-tuple-element.46), channel_id=1, source_target_pairs={{0,3},{1,2},{2,1},{3,0},{4,7},{5,6},{6,5},{7,4},{8,11},{9,10},{10,... | collective-permute-start | bytes 196616 | tf_op jit(solution)/shard_map/ppermute | solution.py:58
  15.7 5.7 %collective-permute-start.6 = (bf16[128,256]{1,0:T(8,128)(2,1)S(1)}, bf16[128,256]{1,0:T(8,128)(2,1)S(1)}, u32[]{:S(2)}, u32[]{:S(2)}) collective-permute-start(bf16[128,256]{1,0:T(8,128)(2,1)S(1)} %get-tuple-element.47), channel_id=1, source_target_pairs={{0,1},{1,0},{2,3},{3,2},{4,5},{5,4},{6,7},{7,6},{8,9},{9,8},{10,11... | collective-permute-start | bytes 196616 | tf_op jit(solution)/shard_map/ppermute | solution.py:58
  21.7 3.6 %collective-permute-start.10 = (bf16[144,256]{1,0:T(8,128)(2,1)S(1)}, bf16[144,256]{1,0:T(8,128)(2,1)S(1)}, u32[]{:S(2)}, u32[]{:S(2)}) collective-permute-start(bf16[144,256]{1,0:T(8,128)(2,1)S(1)} %get-tuple-element.55), channel_id=1, source_target_pairs={{0,4},{4,0},{8,12},{12,8},{16,20},{20,16},{24,28},{28,24},{1,5},{5... | collective-permute-start | bytes 221192 | tf_op jit(solution)/shard_map/ppermute | solution.py:44
  21.8 8.0 %collective-permute-start.9 = (bf16[128,256]{1,0:T(8,128)(2,1)S(1)}, bf16[128,256]{1,0:T(8,128)(2,1)S(1)}, u32[]{:S(2)}, u32[]{:S(2)}) collective-permute-start(bf16[128,256]{1,0:T(8,128)(2,1)S(1)} %get-tuple-element.50.refs_0_), channel_id=1, source_target_pairs={{0,2},{1,3},{2,0},{3,1},{4,6},{5,7},{6,4},{7,5},{8,10},{9,11},{10,... | collective-permute-start | bytes 196616 | tf_op jit(solution)/shard_map/ppermute | solution.py:58
  24.2 6.7 %collective-permute-start.8 = (bf16[128,256]{1,0:T(8,128)(2,1)S(1)}, bf16[128,256]{1,0:T(8,128)(2,1)S(1)}, u32[]{:S(2)}, u32[]{:S(2)}) collective-permute-start(bf16[128,256]{1,0:T(8,128)(2,1)S(1)} %get-tuple-element.50.refs_0_), channel_id=1, source_target_pairs={{0,3},{1,2},{2,1},{3,0},{4,7},{5,6},{6,5},{7,4},{8,11},{9,10},{10,... | collective-permute-start | bytes 196616 | tf_op jit(solution)/shard_map/ppermute | solution.py:58
  24.9 6.5 %collective-permute-start.7 = (bf16[128,256]{1,0:T(8,128)(2,1)S(1)}, bf16[128,256]{1,0:T(8,128)(2,1)S(1)}, u32[]{:S(2)}, u32[]{:S(2)}) collective-permute-start(bf16[128,256]{1,0:T(8,128)(2,1)S(1)} %get-tuple-element.50.refs_0_), channel_id=1, source_target_pairs={{0,1},{1,0},{2,3},{3,2},{4,5},{5,4},{6,7},{7,6},{8,9},{9,8},{10,11... | collective-permute-start | bytes 196616 | tf_op jit(solution)/shard_map/ppermute | solution.py:58
  25.4 6.5 %collective-permute-start.13 = (bf16[144,256]{1,0:T(8,128)(2,1)S(1)}, bf16[144,256]{1,0:T(8,128)(2,1)S(1)}, u32[]{:S(2)}, u32[]{:S(2)}) collective-permute-start(bf16[144,256]{1,0:T(8,128)(2,1)S(1)} %shard_map.117.refs_0_), channel_id=1, source_target_pairs={{0,24},{4,28},{8,16},{12,20},{16,8},{20,12},{24,0},{28,4},{1,25},{... | collective-permute-start | bytes 221192 | tf_op jit(solution)/shard_map/ppermute | solution.py:54
  25.9 6.0 %collective-permute-start.12 = (bf16[144,256]{1,0:T(8,128)(2,1)S(1)}, bf16[144,256]{1,0:T(8,128)(2,1)S(1)}, u32[]{:S(2)}, u32[]{:S(2)}) collective-permute-start(bf16[144,256]{1,0:T(8,128)(2,1)S(1)} %shard_map.117.refs_0_), channel_id=1, source_target_pairs={{0,16},{4,20},{8,24},{12,28},{16,0},{20,4},{24,8},{28,12},{1,17},{... | collective-permute-start | bytes 221192 | tf_op jit(solution)/shard_map/ppermute | solution.py:54
  29.8 4.4 %collective-permute-start.11 = (bf16[144,256]{1,0:T(8,128)(2,1)S(1)}, bf16[144,256]{1,0:T(8,128)(2,1)S(1)}, u32[]{:S(2)}, u32[]{:S(2)}) collective-permute-start(bf16[144,256]{1,0:T(8,128)(2,1)S(1)} %shard_map.117.refs_0_), channel_id=1, source_target_pairs={{0,8},{4,12},{8,0},{12,4},{16,24},{20,28},{24,16},{28,20},{1,9},{5... | collective-permute-start | bytes 221192 | tf_op jit(solution)/shard_map/ppermute | solution.py:54
  34.3 4.2 %collective-permute-start.14 = (bf16[4,128,256]{2,1,0:T(8,128)(2,1)S(1)}, bf16[4,128,256]{2,1,0:T(8,128)(2,1)S(1)}, u32[]{:S(2)}, u32[]{:S(2)}) collective-permute-start(bf16[4,128,256]{2,1,0:T(8,128)(2,1)S(1)} %get-tuple-element.56), channel_id=1, source_target_pairs={{0,4},{4,0},{8,12},{12,8},{16,20},{20,16},{24,28},{28,24},{1,5},{5... | collective-permute-start | bytes 786440 | tf_op jit(solution)/shard_map/ppermute | solution.py:44
  34.3 9.2 %collective-permute-start.20 = (bf16[144,256]{1,0:T(8,128)(2,1)S(1)}, bf16[144,256]{1,0:T(8,128)(2,1)S(1)}, u32[]{:S(2)}, u32[]{:S(2)}) collective-permute-start(bf16[144,256]{1,0:T(8,128)(2,1)S(1)} %shard_map.118.refs_0_), channel_id=1, source_target_pairs={{0,2},{1,3},{2,0},{3,1},{4,6},{5,7},{6,4},{7,5},{8,10},{9,11},{10,... | collective-permute-start | bytes 221192 | tf_op jit(solution)/shard_map/ppermute | solution.py:58
  35.3 8.3 %collective-permute-start.19 = (bf16[144,256]{1,0:T(8,128)(2,1)S(1)}, bf16[144,256]{1,0:T(8,128)(2,1)S(1)}, u32[]{:S(2)}, u32[]{:S(2)}) collective-permute-start(bf16[144,256]{1,0:T(8,128)(2,1)S(1)} %shard_map.118.refs_0_), channel_id=1, source_target_pairs={{0,3},{1,2},{2,1},{3,0},{4,7},{5,6},{6,5},{7,4},{8,11},{9,10},{10,... | collective-permute-start | bytes 221192 | tf_op jit(solution)/shard_map/ppermute | solution.py:58
  38.0 6.5 %collective-permute-start.18 = (bf16[144,256]{1,0:T(8,128)(2,1)S(1)}, bf16[144,256]{1,0:T(8,128)(2,1)S(1)}, u32[]{:S(2)}, u32[]{:S(2)}) collective-permute-start(bf16[144,256]{1,0:T(8,128)(2,1)S(1)} %shard_map.118.refs_0_), channel_id=1, source_target_pairs={{0,1},{1,0},{2,3},{3,2},{4,5},{5,4},{6,7},{7,6},{8,9},{9,8},{10,11... | collective-permute-start | bytes 221192 | tf_op jit(solution)/shard_map/ppermute | solution.py:58
  38.5 6.1 %collective-permute-start.15 = (bf16[128,256]{1,0:T(8,128)(2,1)S(1)}, bf16[128,256]{1,0:T(8,128)(2,1)S(1)}, u32[]{:S(2)}, u32[]{:S(2)}) collective-permute-start(bf16[128,256]{1,0:T(8,128)(2,1)S(1)} %get-tuple-element.58), channel_id=1, source_target_pairs={{0,24},{4,28},{8,16},{12,20},{16,8},{20,12},{24,0},{28,4},{1,25},{... | collective-permute-start | bytes 196616 | tf_op jit(solution)/shard_map/ppermute | solution.py:54
  39.1 5.5 %collective-permute-start.16 = (bf16[128,256]{1,0:T(8,128)(2,1)S(1)}, bf16[128,256]{1,0:T(8,128)(2,1)S(1)}, u32[]{:S(2)}, u32[]{:S(2)}) collective-permute-start(bf16[128,256]{1,0:T(8,128)(2,1)S(1)} %get-tuple-element.59), channel_id=1, source_target_pairs={{0,16},{4,20},{8,24},{12,28},{16,0},{20,4},{24,8},{28,12},{1,17},{... | collective-permute-start | bytes 196616 | tf_op jit(solution)/shard_map/ppermute | solution.py:54
  43.6 4.3 %collective-permute-start.17 = (bf16[128,256]{1,0:T(8,128)(2,1)S(1)}, bf16[128,256]{1,0:T(8,128)(2,1)S(1)}, u32[]{:S(2)}, u32[]{:S(2)}) collective-permute-start(bf16[128,256]{1,0:T(8,128)(2,1)S(1)} %get-tuple-element.60), channel_id=1, source_target_pairs={{0,8},{4,12},{8,0},{12,4},{16,24},{20,28},{24,16},{28,20},{1,9},{5... | collective-permute-start | bytes 196616 | tf_op jit(solution)/shard_map/ppermute | solution.py:54
  44.5 3.4 %collective-permute-start.21 = (f32[128,256]{1,0:T(8,128)S(1)}, f32[128,256]{1,0:T(8,128)S(1)}, u32[]{:S(2)}, u32[]{:S(2)}) collective-permute-start(f32[128,256]{1,0:T(8,128)S(1)} %get-tuple-element.62.mine_ref), channel_id=1, source_target_pairs={{0,4},{4,0},{8,12},{12,8},{16,20},{20,16},{24,28},{28,24},{1,5},{5... | collective-permute-start | bytes 393224 | tf_op jit(solution)/shard_map/ppermute | solution.py:44

commit v13 on v10

--- a/solution.py
+++ b/solution.py
@@ -210,12 +210,12 @@
 
 
 def backward_kernel(rows, cols, pos_ref, count_ref, turned_ref, *refs):
-    parts = refs[:cols]
-    keep_ref, send_ref, hidden, acc = refs[cols:]
+    own_ref, next_ref, far_ref, keep_ref, send_ref, hidden, acc = refs
     chips = rows // CORES
     row, col = lax.axis_index("row"), lax.axis_index("col")
-    for k, ref in enumerate(parts):
-        hidden[k] = ref[...]
+    hidden[0] = own_ref[...]
+    hidden[1] = next_ref[...]
+    hidden[2:] = far_ref[...]
     acc[...] = jnp.zeros_like(acc)
     positions = pos_ref[0]
 
@@ -315,27 +315,31 @@
         [(piece, BF16), (piece, BF16), ((half, width), F32), ((1, width), F32), (grads_shape, BF16)],
     )(weight, bias_vector, cotangent, inv, own, *parts)
 
-    hidden_parts = {k: to_col(hidden, cols, k) for k in order}
+    far = [to_col(hidden, cols, k) for k in range(2, cols)]
     grads = call(pair_sum_kernel, [VMEM] * 3, [(grads_shape, BF16)])(
         keep, bias_keep, to_core(half_send, rows)
     )
+    nearby, grads = lax.optimization_barrier((hidden, grads))
+    next_to = to_col(nearby, cols, 1)
+    far = call(collect_kernel, [VMEM] * len(far), [((cols - 2,) + piece, BF16)], flops=LONG)(*far)
     across = range(chips - 1, 0, -1)
     grad_parts = {k: to_chip(grads, rows, k) for k in across}
+    grads, far = lax.optimization_barrier((grads, far))
     grads = call(
         chip_sum_kernel,
         [VMEM] * chips,
         [(grads_shape, BF16)],
         [pltpu.VMEM((chips,) + grads_shape, BF16)],
     )(grads, *(grad_parts[k] for k in range(1, chips)))
+    next_to, grads = lax.optimization_barrier((next_to, grads))
 
     col_keep, col_send = call(
         functools.partial(backward_kernel, rows, cols),
-        [VMEM, SMEM, VMEM] + [VMEM] * cols,
+        [VMEM, SMEM, VMEM] + [VMEM] * 3,
         [((chips,) + piece, F32), ((chips,) + piece, BF16)],
         [pltpu.VMEM((cols,) + piece, BF16), pltpu.VMEM((rows,) + piece, F32)],
         flops=LONG,
-    )(block_pos, block_count, turned, hidden, *(hidden_parts[k] for k in range(1, cols)))
-    col_send, grads = lax.optimization_barrier((col_send, grads))
+    )(block_pos, block_count, turned, hidden, next_to, far)
     grad_parts = {k: to_col(grads, cols, k) for k in order}
     own_x, *send_x = call(
         merge_kernel, [VMEM] * 2, [(piece, F32)] + [(piece, BF16)] * (chips - 1)

time: 47.7 us -> 48.4 us (1.015)
  starting transfers between devices: 25.3 us -> 26.3 us
    ppermute x9, starting transfers between devices: 13.1 us -> 14.2 us  [to_col(): lax.ppermute(x, 'col', [(i, target(cols, i, k)) for i in range(cols)])]
    ppermute x9, waiting for transfers between devices: 3.45 us -> 2.9 us  [to_chip(): return lax.ppermute(x, 'row', pairs)]
  transfers between devices with their start and end apart: 22 -> 22, of which waited for: 13 -> 12; matrix products, arithmetic and copies ran while one was open for 0% -> 0% of each run, Pallas kernels for 3% -> 2%
where the time goes in v13:
time: 48.4 us; the launch traced here: 48.3 us
  starting transfers between devices  26.3 us (54%)
  waiting for transfers between devices  15.3 us (32%)
  Pallas kernels  3.17 us (7%)
  local copies, waits for them, and re-layouts  2.17 us (4%)
  between operations  1.45 us (3%)
    ppermute x9, starting transfers between devices, to_col(): lax.ppermute(x, 'col', [(i, target(cols, i, k)) for i in range(cols)])  14.2 us
    ppermute x9, starting transfers between devices, to_chip(): return lax.ppermute(x, 'row', pairs)  11.7 us
    ppermute x9, waiting for transfers between devices, to_col(): lax.ppermute(x, 'col', [(i, target(cols, i, k)) for i in range(cols)])  9.61 us
    ppermute x9, waiting for transfers between devices, to_chip(): return lax.ppermute(x, 'row', pairs)  2.9 us
    ppermute x4, waiting for transfers between devices, to_core(): return lax.ppermute(x, 'row', [(i, i ^ 1) for i in range(rows)])  2.75 us
    unnamed x14, local copies, waits for them, and re-layouts  2.17 us
  transfers between devices with their start and end apart: 22, of which 12 were waited for; matrix products, arithmetic and copies ran while one was open for 0% of the time, Pallas kernels for 2%

profile of v13, /device:TPU:0, one launch (start us, length us, event | category | flops | bytes accessed | tf_op | source)
XLA Modules:
  0.0 48.3 jit_solution(8414907340707407022)
XLA Ops:
  0.6 0.6 %copy-done.4 = s32[128]{0:T(128)S(1)} copy-done((s32[128]{0:T(128)S(1)}, s32[128]{0:T(128)}, u32[]{:S(2)}) %copy-start.4) | copy-done | bytes 536
  1.3 0.8 %copy-done.2 = bf16[128,256]{1,0:T(8,128)(2,1)S(1)} copy-done((bf16[128,256]{1,0:T(8,128)(2,1)S(1)}, bf16[128,256]{1,0:T(8,128)(2,1)}, u32[]{:S(2)}) %copy-start.2) | copy-done | bytes 65560
  2.1 0.1 shard_map.112
  2.2 4.0 %collective-permute-start.2 = (bf16[128,256]{1,0:T(8,128)(2,1)S(1)}, bf16[128,256]{1,0:T(8,128)(2,1)S(1)}, u32[]{:S(2)}, u32[]{:S(2)}) collective-permute-start(bf16[128,256]{1,0:T(8,128)(2,1)S(1)} %get-tuple-element.43.refs_0_), channel_id=1, source_target_pairs={{0,24},{4,28},{8,16},{12,20},{16,8},{20,12},{24,0},{28,4},{1,25},{... | collective-permute-start | bytes 196616 | tf_op jit(solution)/shard_map/ppermute | solution.py:50
  6.2 0.5 %collective-permute-start.1 = (bf16[128,256]{1,0:T(8,128)(2,1)S(1)}, bf16[128,256]{1,0:T(8,128)(2,1)S(1)}, u32[]{:S(2)}, u32[]{:S(2)}) collective-permute-start(bf16[128,256]{1,0:T(8,128)(2,1)S(1)} %get-tuple-element.43.refs_0_), channel_id=1, source_target_pairs={{0,16},{4,20},{8,24},{12,28},{16,0},{20,4},{24,8},{28,12},{1,17},{... | collective-permute-start | bytes 196616 | tf_op jit(solution)/shard_map/ppermute | solution.py:50
  6.7 0.1 collective-permute-start
  7.5 0.0 copy-start.6
  7.5 0.7 %copy-done.6 = f32[256]{0:T(256)S(1)} copy-done((f32[256]{0:T(256)S(1)}, f32[256]{0:T(256)}, u32[]{:S(2)}) %copy-start.6) | copy-done | bytes 1048
  8.2 0.5 %shard_map.111 = (bf16[16,128,128]{2,1,0:T(8,128)(2,1)S(1)}, bf16[16,128,128]{2,1,0:T(8,128)(2,1)S(1)}, f32[1,256]{1,0:T(1,128)S(1)}) custom-call(s32[1,1]{1,0:T(1,128)S(6)} %copy.12.count_ref, s32[1,1,16,512]{3,2,1,0:T(8,128)S(1)} %copy-done.5, f32[1,256]{1,0:T(1,128)S(1)} %bitcast.4), custom_call_target="tpu_custom_call" | custom-call | flops 4000000000 | bytes 1000000 | tf_op jit(solution)/shard_map/pallas_call | solution.py:294
  8.7 1.7 %collective-permute-done.1.refs_2_ = bf16[128,256]{1,0:T(8,128)(2,1)S(1)} collective-permute-done((bf16[128,256]{1,0:T(8,128)(2,1)S(1)}, bf16[128,256]{1,0:T(8,128)(2,1)S(1)}, u32[]{:S(2)}, u32[]{:S(2)}) %collective-permute-start.1) | collective-permute-done | bytes 65568 | tf_op jit(solution)/shard_map/ppermute | solution.py:50
  10.5 0.5 %collective-permute-done.refs_1_ = bf16[128,256]{1,0:T(8,128)(2,1)S(1)} collective-permute-done((bf16[128,256]{1,0:T(8,128)(2,1)S(1)}, bf16[128,256]{1,0:T(8,128)(2,1)S(1)}, u32[]{:S(2)}, u32[]{:S(2)}) %collective-permute-start) | collective-permute-done | bytes 65568 | tf_op jit(solution)/shard_map/ppermute | solution.py:50
  11.0 0.0 copy-start
  11.0 0.0 copy-start.1
  11.0 0.1 collective-permute-start.3
  11.1 1.5 %collective-permute-done.3.next_ref = bf16[4,128,256]{2,1,0:T(8,128)(2,1)S(1)} collective-permute-done((bf16[4,128,256]{2,1,0:T(8,128)(2,1)S(1)}, bf16[4,128,256]{2,1,0:T(8,128)(2,1)S(1)}, u32[]{:S(2)}, u32[]{:S(2)}) %collective-permute-start.3) | collective-permute-done | bytes 262176 | tf_op jit(solution)/shard_map/ppermute | solution.py:40
  12.6 0.5 %shard_map.114 = (f32[128,256]{1,0:T(8,128)S(1)}, bf16[128,256]{1,0:T(8,128)(2,1)S(1)}, bf16[128,256]{1,0:T(8,128)(2,1)S(1)}, bf16[128,256]{1,0:T(8,128)(2,1)S(1)}) custom-call(s32[1,1,16]{2,1,0:T(1,128)S(1)} %copy-done.3, s32[1,1]{1,0:T(1,128)S(6)} %copy.12.count_ref, bf16[16,128,128]{2,1,0:T(8,128)(2,1)S(1)} %get-tuple-element.44.blocks_ref, ...), custom_call_target="tpu_custom_call" | custom-call | flops 1000000 | bytes 1000000 | tf_op jit(solution)/shard_map/pallas_call | solution.py:303
  13.1 2.7 %collective-permute-start.4 = (bf16[128,256]{1,0:T(8,128)(2,1)S(1)}, bf16[128,256]{1,0:T(8,128)(2,1)S(1)}, u32[]{:S(2)}, u32[]{:S(2)}) collective-permute-start(bf16[128,256]{1,0:T(8,128)(2,1)S(1)} %get-tuple-element.49), channel_id=1, source_target_pairs={{0,2},{1,3},{2,0},{3,1},{4,6},{5,7},{6,4},{7,5},{8,10},{9,11},{10,... | collective-permute-start | bytes 196616 | tf_op jit(solution)/shard_map/ppermute | solution.py:54
  15.8 1.8 %collective-permute-start.5 = (bf16[128,256]{1,0:T(8,128)(2,1)S(1)}, bf16[128,256]{1,0:T(8,128)(2,1)S(1)}, u32[]{:S(2)}, u32[]{:S(2)}) collective-permute-start(bf16[128,256]{1,0:T(8,128)(2,1)S(1)} %get-tuple-element.50), channel_id=1, source_target_pairs={{0,3},{1,2},{2,1},{3,0},{4,7},{5,6},{6,5},{7,4},{8,11},{9,10},{10,... | collective-permute-start | bytes 196616 | tf_op jit(solution)/shard_map/ppermute | solution.py:54
  17.5 1.5 %collective-permute-done.4.refs_1_ = bf16[128,256]{1,0:T(8,128)(2,1)S(1)} collective-permute-done((bf16[128,256]{1,0:T(8,128)(2,1)S(1)}, bf16[128,256]{1,0:T(8,128)(2,1)S(1)}, u32[]{:S(2)}, u32[]{:S(2)}) %collective-permute-start.4) | collective-permute-done | bytes 65568 | tf_op jit(solution)/shard_map/ppermute | solution.py:54
  19.1 3.2 %collective-permute-done.5.refs_2_ = bf16[128,256]{1,0:T(8,128)(2,1)S(1)} collective-permute-done((bf16[128,256]{1,0:T(8,128)(2,1)S(1)}, bf16[128,256]{1,0:T(8,128)(2,1)S(1)}, u32[]{:S(2)}, u32[]{:S(2)}) %collective-permute-start.5) | collective-permute-done | bytes 65568 | tf_op jit(solution)/shard_map/ppermute | solution.py:54
  22.2 0.3 collective-permute-done.6.refs_3_
  22.5 0.4 shard_map.115
  22.9 0.1 collective-permute-start.7
  23.0 3.2 %collective-permute-start.10 = (bf16[128,256]{1,0:T(8,128)(2,1)S(1)}, bf16[128,256]{1,0:T(8,128)(2,1)S(1)}, u32[]{:S(2)}, u32[]{:S(2)}) collective-permute-start(bf16[128,256]{1,0:T(8,128)(2,1)S(1)} %get-tuple-element.58.refs_0_), channel_id=1, source_target_pairs={{0,3},{1,2},{2,1},{3,0},{4,7},{5,6},{6,5},{7,4},{8,11},{9,10},{10,... | collective-permute-start | bytes 196616 | tf_op jit(solution)/shard_map/ppermute | solution.py:54
  26.3 1.6 %collective-permute-start.13 = (bf16[144,256]{1,0:T(8,128)(2,1)S(1)}, bf16[144,256]{1,0:T(8,128)(2,1)S(1)}, u32[]{:S(2)}, u32[]{:S(2)}) collective-permute-start(bf16[144,256]{1,0:T(8,128)(2,1)S(1)} %shard_map.116.refs_0_), channel_id=1, source_target_pairs={{0,24},{4,28},{8,16},{12,20},{16,8},{20,12},{24,0},{28,4},{1,25},{... | collective-permute-start | bytes 221192 | tf_op jit(solution)/shard_map/ppermute | solution.py:50
  27.8 0.5 %collective-permute-start.12 = (bf16[144,256]{1,0:T(8,128)(2,1)S(1)}, bf16[144,256]{1,0:T(8,128)(2,1)S(1)}, u32[]{:S(2)}, u32[]{:S(2)}) collective-permute-start(bf16[144,256]{1,0:T(8,128)(2,1)S(1)} %shard_map.116.refs_0_), channel_id=1, source_target_pairs={{0,16},{4,20},{8,24},{12,28},{16,0},{20,4},{24,8},{28,12},{1,17},{... | collective-permute-start | bytes 221192 | tf_op jit(solution)/shard_map/ppermute | solution.py:50
  28.3 1.5 %collective-permute-start.11 = (bf16[144,256]{1,0:T(8,128)(2,1)S(1)}, bf16[144,256]{1,0:T(8,128)(2,1)S(1)}, u32[]{:S(2)}, u32[]{:S(2)}) collective-permute-start(bf16[144,256]{1,0:T(8,128)(2,1)S(1)} %shard_map.116.refs_0_), channel_id=1, source_target_pairs={{0,8},{4,12},{8,0},{12,4},{16,24},{20,28},{24,16},{28,20},{1,9},{5... | collective-permute-start | bytes 221192 | tf_op jit(solution)/shard_map/ppermute | solution.py:50
  29.8 2.1 %collective-permute-start.8 = (bf16[128,256]{1,0:T(8,128)(2,1)S(1)}, bf16[128,256]{1,0:T(8,128)(2,1)S(1)}, u32[]{:S(2)}, u32[]{:S(2)}) collective-permute-start(bf16[128,256]{1,0:T(8,128)(2,1)S(1)} %get-tuple-element.58.refs_0_), channel_id=1, source_target_pairs={{0,1},{1,0},{2,3},{3,2},{4,5},{5,4},{6,7},{7,6},{8,9},{9,8},{10,11... | collective-permute-start | bytes 196616 | tf_op jit(solution)/shard_map/ppermute | solution.py:54
  31.9 0.6 %collective-permute-done.9.refs_0_ = bf16[128,256]{1,0:T(8,128)(2,1)S(1)} collective-permute-done((bf16[128,256]{1,0:T(8,128)(2,1)S(1)}, bf16[128,256]{1,0:T(8,128)(2,1)S(1)}, u32[]{:S(2)}, u32[]{:S(2)}) %collective-permute-start.9) | collective-permute-done | bytes 65568 | tf_op jit(solution)/shard_map/ppermute | solution.py:54
  32.6 0.6 %collective-permute-done.12.refs_2_ = bf16[144,256]{1,0:T(8,128)(2,1)S(1)} collective-permute-done((bf16[144,256]{1,0:T(8,128)(2,1)S(1)}, bf16[144,256]{1,0:T(8,128)(2,1)S(1)}, u32[]{:S(2)}, u32[]{:S(2)}) %collective-permute-start.12) | collective-permute-done | bytes 73760 | tf_op jit(solution)/shard_map/ppermute | solution.py:50
  33.1 0.1 collective-permute-done.11.refs_1_
  33.2 0.1 shard_map.118.refs_0_
  33.3 0.9 %collective-permute-done.8.refs_1_ = bf16[128,256]{1,0:T(8,128)(2,1)S(1)} collective-permute-done((bf16[128,256]{1,0:T(8,128)(2,1)S(1)}, bf16[128,256]{1,0:T(8,128)(2,1)S(1)}, u32[]{:S(2)}, u32[]{:S(2)}) %collective-permute-start.8) | collective-permute-done | bytes 65568 | tf_op jit(solution)/shard_map/ppermute | solution.py:54
  34.2 0.5 %shard_map.119 = (f32[4,128,256]{2,1,0:T(8,128)S(1)}, bf16[4,128,256]{2,1,0:T(8,128)(2,1)S(1)}) custom-call(s32[1,1,16]{2,1,0:T(1,128)S(1)} %copy-done.3, s32[1,1]{1,0:T(1,128)S(6)} %copy.12.count_ref, bf16[16,128,128]{2,1,0:T(8,128)(2,1)S(1)} %get-tuple-element.53.turned_ref, bf16[128,256]{1,0:T(8,128)(2,1)S(1)} %get-tuple-element.58.refs_0_, ...), custom_call_target="tpu_custom_call" | custom-call | flops 4000000000 | bytes 1000000 | tf_op jit(solution)/shard_map/pallas_call | solution.py:336
  34.7 0.1 collective-permute-start.14
  34.8 3.1 %collective-permute-start.20 = (bf16[144,256]{1,0:T(8,128)(2,1)S(1)}, bf16[144,256]{1,0:T(8,128)(2,1)S(1)}, u32[]{:S(2)}, u32[]{:S(2)}) collective-permute-start(bf16[144,256]{1,0:T(8,128)(2,1)S(1)} %shard_map.118.refs_0_), channel_id=1, source_target_pairs={{0,3},{1,2},{2,1},{3,0},{4,7},{5,6},{6,5},{7,4},{8,11},{9,10},{10,... | collective-permute-start | bytes 221192 | tf_op jit(solution)/shard_map/ppermute | solution.py:54
  37.9 0.8 %collective-permute-start.19 = (bf16[144,256]{1,0:T(8,128)(2,1)S(1)}, bf16[144,256]{1,0:T(8,128)(2,1)S(1)}, u32[]{:S(2)}, u32[]{:S(2)}) collective-permute-start(bf16[144,256]{1,0:T(8,128)(2,1)S(1)} %shard_map.118.refs_0_), channel_id=1, source_target_pairs={{0,2},{1,3},{2,0},{3,1},{4,6},{5,7},{6,4},{7,5},{8,10},{9,11},{10,... | collective-permute-start | bytes 221192 | tf_op jit(solution)/shard_map/ppermute | solution.py:54
  38.8 0.5 %collective-permute-start.18 = (bf16[144,256]{1,0:T(8,128)(2,1)S(1)}, bf16[144,256]{1,0:T(8,128)(2,1)S(1)}, u32[]{:S(2)}, u32[]{:S(2)}) collective-permute-start(bf16[144,256]{1,0:T(8,128)(2,1)S(1)} %shard_map.118.refs_0_), channel_id=1, source_target_pairs={{0,1},{1,0},{2,3},{3,2},{4,5},{5,4},{6,7},{7,6},{8,9},{9,8},{10,11... | collective-permute-start | bytes 221192 | tf_op jit(solution)/shard_map/ppermute | solution.py:54
  39.3 0.1 shard_map.120
  39.3 1.6 %collective-permute-start.15 = (bf16[128,256]{1,0:T(8,128)(2,1)S(1)}, bf16[128,256]{1,0:T(8,128)(2,1)S(1)}, u32[]{:S(2)}, u32[]{:S(2)}) collective-permute-start(bf16[128,256]{1,0:T(8,128)(2,1)S(1)} %get-tuple-element.66), channel_id=1, source_target_pairs={{0,24},{4,28},{8,16},{12,20},{16,8},{20,12},{24,0},{28,4},{1,25},{... | collective-permute-start | bytes 196616 | tf_op jit(solution)/shard_map/ppermute | solution.py:50
  40.9 0.5 %collective-permute-start.16 = (bf16[128,256]{1,0:T(8,128)(2,1)S(1)}, bf16[128,256]{1,0:T(8,128)(2,1)S(1)}, u32[]{:S(2)}, u32[]{:S(2)}) collective-permute-start(bf16[128,256]{1,0:T(8,128)(2,1)S(1)} %get-tuple-element.67), channel_id=1, source_target_pairs={{0,16},{4,20},{8,24},{12,28},{16,0},{20,4},{24,8},{28,12},{1,17},{... | collective-permute-start | bytes 196616 | tf_op jit(solution)/shard_map/ppermute | solution.py:50
  41.4 0.0 collective-permute-done.20.refs_3_
  41.4 1.5 %collective-permute-start.17 = (bf16[128,256]{1,0:T(8,128)(2,1)S(1)}, bf16[128,256]{1,0:T(8,128)(2,1)S(1)}, u32[]{:S(2)}, u32[]{:S(2)}) collective-permute-start(bf16[128,256]{1,0:T(8,128)(2,1)S(1)} %get-tuple-element.68), channel_id=1, source_target_pairs={{0,8},{4,12},{8,0},{12,4},{16,24},{20,28},{24,16},{28,20},{1,9},{5... | collective-permute-start | bytes 196616 | tf_op jit(solution)/shard_map/ppermute | solution.py:50
  42.9 3.1 %collective-permute-done.19.refs_2_ = bf16[144,256]{1,0:T(8,128)(2,1)S(1)} collective-permute-done((bf16[144,256]{1,0:T(8,128)(2,1)S(1)}, bf16[144,256]{1,0:T(8,128)(2,1)S(1)}, u32[]{:S(2)}, u32[]{:S(2)}) %collective-permute-start.19) | collective-permute-done | bytes 73760 | tf_op jit(solution)/shard_map/ppermute | solution.py:54
  46.0 0.1 shard_map.122
  46.1 0.1 collective-permute-start.21
  46.3 1.2 %collective-permute-done.21.theirs_ref = f32[128,256]{1,0:T(8,128)S(1)} collective-permute-done((f32[128,256]{1,0:T(8,128)S(1)}, f32[128,256]{1,0:T(8,128)S(1)}, u32[]{:S(2)}, u32[]{:S(2)}) %collective-permute-start.21) | collective-permute-done | bytes 131104 | tf_op jit(solution)/shard_map/ppermute | solution.py:40
  47.5 0.8 %shard_map.123 = (bf16[128,256]{1,0:T(8,128)(2,1)}, bf16[128,256]{1,0:T(8,128)(2,1)}, f32[256,256]{1,0:T(8,128)}, f32[1,256]{1,0:T(1,128)}) custom-call(bf16[128,256]{1,0:T(8,128)(2,1)S(1)} %get-tuple-element.52.out_ref, bf16[128,256]{1,0:T(8,128)(2,1)S(1)} %shard_map.121.x_ref, f32[128,256]{1,0:T(8,128)S(1)} %get-tuple-element.70.mine_ref, ...), custom_call_target="tpu_custom_call" | custom-call | flops 1000000 | bytes 1000000 | tf_op jit(solution)/shard_map/pallas_call | solution.py:360
  (23 shorter events, 0.2 us)
Async XLA Ops:
  0.6 0.7 %copy-start.4 = (s32[128]{0:T(128)S(1)}, s32[128]{0:T(128)}, u32[]{:S(2)}) copy-start(s32[128]{0:T(128)} %param.9) | copy-start | bytes 1540
  1.3 0.8 %copy-start.2 = (bf16[128,256]{1,0:T(8,128)(2,1)S(1)}, bf16[128,256]{1,0:T(8,128)(2,1)}, u32[]{:S(2)}) copy-start(bf16[128,256]{1,0:T(8,128)(2,1)} %features_ref.1) | copy-start | bytes 196612
  2.1 5.4 %copy-start.5 = (s32[1,1,16,512]{3,2,1,0:T(8,128)S(1)}, s32[1,1,16,512]{3,2,1,0:T(8,128)}, u32[]{:S(2)}) copy-start(s32[1,1,16,512]{3,2,1,0:T(8,128)} %edge_ref.1) | copy-start | bytes 98308
  2.2 6.5 %collective-permute-start.2 = (bf16[128,256]{1,0:T(8,128)(2,1)S(1)}, bf16[128,256]{1,0:T(8,128)(2,1)S(1)}, u32[]{:S(2)}, u32[]{:S(2)}) collective-permute-start(bf16[128,256]{1,0:T(8,128)(2,1)S(1)} %get-tuple-element.43.refs_0_), channel_id=1, source_target_pairs={{0,24},{4,28},{8,16},{12,20},{16,8},{20,12},{24,0},{28,4},{1,25},{... | collective-permute-start | bytes 196616 | tf_op jit(solution)/shard_map/ppermute | solution.py:50
  6.2 4.3 %collective-permute-start.1 = (bf16[128,256]{1,0:T(8,128)(2,1)S(1)}, bf16[128,256]{1,0:T(8,128)(2,1)S(1)}, u32[]{:S(2)}, u32[]{:S(2)}) collective-permute-start(bf16[128,256]{1,0:T(8,128)(2,1)S(1)} %get-tuple-element.43.refs_0_), channel_id=1, source_target_pairs={{0,16},{4,20},{8,24},{12,28},{16,0},{20,4},{24,8},{28,12},{1,17},{... | collective-permute-start | bytes 196616 | tf_op jit(solution)/shard_map/ppermute | solution.py:50
  6.7 4.3 %collective-permute-start = (bf16[128,256]{1,0:T(8,128)(2,1)S(1)}, bf16[128,256]{1,0:T(8,128)(2,1)S(1)}, u32[]{:S(2)}, u32[]{:S(2)}) collective-permute-start(bf16[128,256]{1,0:T(8,128)(2,1)S(1)} %get-tuple-element.43.refs_0_), channel_id=1, source_target_pairs={{0,8},{4,12},{8,0},{12,4},{16,24},{20,28},{24,16},{28,20},{1,9},{5... | collective-permute-start | bytes 196616 | tf_op jit(solution)/shard_map/ppermute | solution.py:50
  7.5 0.7 %copy-start.6 = (f32[256]{0:T(256)S(1)}, f32[256]{0:T(256)}, u32[]{:S(2)}) copy-start(f32[256]{0:T(256)} %param.11) | copy-start | bytes 3076
  11.0 1.7 %copy-start.3 = (s32[1,1,16]{2,1,0:T(1,128)S(1)}, s32[1,1,16]{2,1,0:T(1,128)}, u32[]{:S(2)}) copy-start(s32[1,1,16]{2,1,0:T(1,128)} %pos_ref.3) | copy-start | bytes 196
  11.0 11.5 %copy-start = (bf16[256,256]{1,0:T(8,128)(2,1)S(1)}, bf16[256,256]{1,0:T(8,128)(2,1)}, u32[]{:S(2)}) copy-start(bf16[256,256]{1,0:T(8,128)(2,1)} %weight_ref.1) | copy-start | bytes 393220
  11.0 11.5 %copy-start.1 = (bf16[128,256]{1,0:T(8,128)(2,1)S(1)}, bf16[128,256]{1,0:T(8,128)(2,1)}, u32[]{:S(2)}) copy-start(bf16[128,256]{1,0:T(8,128)(2,1)} %cot_ref.1) | copy-start | bytes 196612
  11.0 1.6 %collective-permute-start.3 = (bf16[4,128,256]{2,1,0:T(8,128)(2,1)S(1)}, bf16[4,128,256]{2,1,0:T(8,128)(2,1)S(1)}, u32[]{:S(2)}, u32[]{:S(2)}) collective-permute-start(bf16[4,128,256]{2,1,0:T(8,128)(2,1)S(1)} %shard_map.113.near_ref), channel_id=1, source_target_pairs={{0,4},{4,0},{8,12},{12,8},{16,20},{20,16},{24,28},{28,24},{1,5},{5... | collective-permute-start | bytes 786440 | tf_op jit(solution)/shard_map/ppermute | solution.py:40
  13.1 5.9 %collective-permute-start.4 = (bf16[128,256]{1,0:T(8,128)(2,1)S(1)}, bf16[128,256]{1,0:T(8,128)(2,1)S(1)}, u32[]{:S(2)}, u32[]{:S(2)}) collective-permute-start(bf16[128,256]{1,0:T(8,128)(2,1)S(1)} %get-tuple-element.49), channel_id=1, source_target_pairs={{0,2},{1,3},{2,0},{3,1},{4,6},{5,7},{6,4},{7,5},{8,10},{9,11},{10,... | collective-permute-start | bytes 196616 | tf_op jit(solution)/shard_map/ppermute | solution.py:54
  15.8 6.5 %collective-permute-start.5 = (bf16[128,256]{1,0:T(8,128)(2,1)S(1)}, bf16[128,256]{1,0:T(8,128)(2,1)S(1)}, u32[]{:S(2)}, u32[]{:S(2)}) collective-permute-start(bf16[128,256]{1,0:T(8,128)(2,1)S(1)} %get-tuple-element.50), channel_id=1, source_target_pairs={{0,3},{1,2},{2,1},{3,0},{4,7},{5,6},{6,5},{7,4},{8,11},{9,10},{10,... | collective-permute-start | bytes 196616 | tf_op jit(solution)/shard_map/ppermute | solution.py:54
  17.5 5.0 %collective-permute-start.6 = (bf16[128,256]{1,0:T(8,128)(2,1)S(1)}, bf16[128,256]{1,0:T(8,128)(2,1)S(1)}, u32[]{:S(2)}, u32[]{:S(2)}) collective-permute-start(bf16[128,256]{1,0:T(8,128)(2,1)S(1)} %get-tuple-element.51), channel_id=1, source_target_pairs={{0,1},{1,0},{2,3},{3,2},{4,5},{5,4},{6,7},{7,6},{8,9},{9,8},{10,11... | collective-permute-start | bytes 196616 | tf_op jit(solution)/shard_map/ppermute | solution.py:54
  22.9 3.3 %collective-permute-start.7 = (bf16[144,256]{1,0:T(8,128)(2,1)S(1)}, bf16[144,256]{1,0:T(8,128)(2,1)S(1)}, u32[]{:S(2)}, u32[]{:S(2)}) collective-permute-start(bf16[144,256]{1,0:T(8,128)(2,1)S(1)} %get-tuple-element.57), channel_id=1, source_target_pairs={{0,4},{4,0},{8,12},{12,8},{16,20},{20,16},{24,28},{28,24},{1,5},{5... | collective-permute-start | bytes 221192 | tf_op jit(solution)/shard_map/ppermute | solution.py:40
  23.0 6.8 %collective-permute-start.10 = (bf16[128,256]{1,0:T(8,128)(2,1)S(1)}, bf16[128,256]{1,0:T(8,128)(2,1)S(1)}, u32[]{:S(2)}, u32[]{:S(2)}) collective-permute-start(bf16[128,256]{1,0:T(8,128)(2,1)S(1)} %get-tuple-element.58.refs_0_), channel_id=1, source_target_pairs={{0,3},{1,2},{2,1},{3,0},{4,7},{5,6},{6,5},{7,4},{8,11},{9,10},{10,... | collective-permute-start | bytes 196616 | tf_op jit(solution)/shard_map/ppermute | solution.py:54
  26.2 6.3 %collective-permute-start.9 = (bf16[128,256]{1,0:T(8,128)(2,1)S(1)}, bf16[128,256]{1,0:T(8,128)(2,1)S(1)}, u32[]{:S(2)}, u32[]{:S(2)}) collective-permute-start(bf16[128,256]{1,0:T(8,128)(2,1)S(1)} %get-tuple-element.58.refs_0_), channel_id=1, source_target_pairs={{0,2},{1,3},{2,0},{3,1},{4,6},{5,7},{6,4},{7,5},{8,10},{9,11},{10,... | collective-permute-start | bytes 196616 | tf_op jit(solution)/shard_map/ppermute | solution.py:54
  26.3 6.3 %collective-permute-start.13 = (bf16[144,256]{1,0:T(8,128)(2,1)S(1)}, bf16[144,256]{1,0:T(8,128)(2,1)S(1)}, u32[]{:S(2)}, u32[]{:S(2)}) collective-permute-start(bf16[144,256]{1,0:T(8,128)(2,1)S(1)} %shard_map.116.refs_0_), channel_id=1, source_target_pairs={{0,24},{4,28},{8,16},{12,20},{16,8},{20,12},{24,0},{28,4},{1,25},{... | collective-permute-start | bytes 221192 | tf_op jit(solution)/shard_map/ppermute | solution.py:50
  27.8 5.3 %collective-permute-start.12 = (bf16[144,256]{1,0:T(8,128)(2,1)S(1)}, bf16[144,256]{1,0:T(8,128)(2,1)S(1)}, u32[]{:S(2)}, u32[]{:S(2)}) collective-permute-start(bf16[144,256]{1,0:T(8,128)(2,1)S(1)} %shard_map.116.refs_0_), channel_id=1, source_target_pairs={{0,16},{4,20},{8,24},{12,28},{16,0},{20,4},{24,8},{28,12},{1,17},{... | collective-permute-start | bytes 221192 | tf_op jit(solution)/shard_map/ppermute | solution.py:50
  28.3 4.9 %collective-permute-start.11 = (bf16[144,256]{1,0:T(8,128)(2,1)S(1)}, bf16[144,256]{1,0:T(8,128)(2,1)S(1)}, u32[]{:S(2)}, u32[]{:S(2)}) collective-permute-start(bf16[144,256]{1,0:T(8,128)(2,1)S(1)} %shard_map.116.refs_0_), channel_id=1, source_target_pairs={{0,8},{4,12},{8,0},{12,4},{16,24},{20,28},{24,16},{28,20},{1,9},{5... | collective-permute-start | bytes 221192 | tf_op jit(solution)/shard_map/ppermute | solution.py:50
  29.8 4.4 %collective-permute-start.8 = (bf16[128,256]{1,0:T(8,128)(2,1)S(1)}, bf16[128,256]{1,0:T(8,128)(2,1)S(1)}, u32[]{:S(2)}, u32[]{:S(2)}) collective-permute-start(bf16[128,256]{1,0:T(8,128)(2,1)S(1)} %get-tuple-element.58.refs_0_), channel_id=1, source_target_pairs={{0,1},{1,0},{2,3},{3,2},{4,5},{5,4},{6,7},{7,6},{8,9},{9,8},{10,11... | collective-permute-start | bytes 196616 | tf_op jit(solution)/shard_map/ppermute | solution.py:54
  34.7 4.5 %collective-permute-start.14 = (bf16[4,128,256]{2,1,0:T(8,128)(2,1)S(1)}, bf16[4,128,256]{2,1,0:T(8,128)(2,1)S(1)}, u32[]{:S(2)}, u32[]{:S(2)}) collective-permute-start(bf16[4,128,256]{2,1,0:T(8,128)(2,1)S(1)} %get-tuple-element.64), channel_id=1, source_target_pairs={{0,4},{4,0},{8,12},{12,8},{16,20},{20,16},{24,28},{28,24},{1,5},{5... | collective-permute-start | bytes 786440 | tf_op jit(solution)/shard_map/ppermute | solution.py:40
  34.8 6.6 %collective-permute-start.20 = (bf16[144,256]{1,0:T(8,128)(2,1)S(1)}, bf16[144,256]{1,0:T(8,128)(2,1)S(1)}, u32[]{:S(2)}, u32[]{:S(2)}) collective-permute-start(bf16[144,256]{1,0:T(8,128)(2,1)S(1)} %shard_map.118.refs_0_), channel_id=1, source_target_pairs={{0,3},{1,2},{2,1},{3,0},{4,7},{5,6},{6,5},{7,4},{8,11},{9,10},{10,... | collective-permute-start | bytes 221192 | tf_op jit(solution)/shard_map/ppermute | solution.py:54
  37.9 8.1 %collective-permute-start.19 = (bf16[144,256]{1,0:T(8,128)(2,1)S(1)}, bf16[144,256]{1,0:T(8,128)(2,1)S(1)}, u32[]{:S(2)}, u32[]{:S(2)}) collective-permute-start(bf16[144,256]{1,0:T(8,128)(2,1)S(1)} %shard_map.118.refs_0_), channel_id=1, source_target_pairs={{0,2},{1,3},{2,0},{3,1},{4,6},{5,7},{6,4},{7,5},{8,10},{9,11},{10,... | collective-permute-start | bytes 221192 | tf_op jit(solution)/shard_map/ppermute | solution.py:54
  38.8 7.3 %collective-permute-start.18 = (bf16[144,256]{1,0:T(8,128)(2,1)S(1)}, bf16[144,256]{1,0:T(8,128)(2,1)S(1)}, u32[]{:S(2)}, u32[]{:S(2)}) collective-permute-start(bf16[144,256]{1,0:T(8,128)(2,1)S(1)} %shard_map.118.refs_0_), channel_id=1, source_target_pairs={{0,1},{1,0},{2,3},{3,2},{4,5},{5,4},{6,7},{7,6},{8,9},{9,8},{10,11... | collective-permute-start | bytes 221192 | tf_op jit(solution)/shard_map/ppermute | solution.py:54
  39.3 6.9 %collective-permute-start.15 = (bf16[128,256]{1,0:T(8,128)(2,1)S(1)}, bf16[128,256]{1,0:T(8,128)(2,1)S(1)}, u32[]{:S(2)}, u32[]{:S(2)}) collective-permute-start(bf16[128,256]{1,0:T(8,128)(2,1)S(1)} %get-tuple-element.66), channel_id=1, source_target_pairs={{0,24},{4,28},{8,16},{12,20},{16,8},{20,12},{24,0},{28,4},{1,25},{... | collective-permute-start | bytes 196616 | tf_op jit(solution)/shard_map/ppermute | solution.py:50
  40.9 5.4 %collective-permute-start.16 = (bf16[128,256]{1,0:T(8,128)(2,1)S(1)}, bf16[128,256]{1,0:T(8,128)(2,1)S(1)}, u32[]{:S(2)}, u32[]{:S(2)}) collective-permute-start(bf16[128,256]{1,0:T(8,128)(2,1)S(1)} %get-tuple-element.67), channel_id=1, source_target_pairs={{0,16},{4,20},{8,24},{12,28},{16,0},{20,4},{24,8},{28,12},{1,17},{... | collective-permute-start | bytes 196616 | tf_op jit(solution)/shard_map/ppermute | solution.py:50
  41.4 4.9 %collective-permute-start.17 = (bf16[128,256]{1,0:T(8,128)(2,1)S(1)}, bf16[128,256]{1,0:T(8,128)(2,1)S(1)}, u32[]{:S(2)}, u32[]{:S(2)}) collective-permute-start(bf16[128,256]{1,0:T(8,128)(2,1)S(1)} %get-tuple-element.68), channel_id=1, source_target_pairs={{0,8},{4,12},{8,0},{12,4},{16,24},{20,28},{24,16},{28,20},{1,9},{5... | collective-permute-start | bytes 196616 | tf_op jit(solution)/shard_map/ppermute | solution.py:50
  46.1 1.4 %collective-permute-start.21 = (f32[128,256]{1,0:T(8,128)S(1)}, f32[128,256]{1,0:T(8,128)S(1)}, u32[]{:S(2)}, u32[]{:S(2)}) collective-permute-start(f32[128,256]{1,0:T(8,128)S(1)} %get-tuple-element.70.mine_ref), channel_id=1, source_target_pairs={{0,4},{4,0},{8,12},{12,8},{16,20},{20,16},{24,28},{28,24},{1,5},{5... | collective-permute-start | bytes 393224 | tf_op jit(solution)/shard_map/ppermute | solution.py:40

commit v14 on v10

--- a/solution.py
+++ b/solution.py
@@ -61,9 +61,17 @@
     return jnp.concatenate([tall] * (width // BLOCK), axis=1)
 
 
-def scale_kernel(features_ref, degree_ref, out_ref, inv_ref):
+def scale_kernel(features_hbm, degree_hbm, out_ref, inv_ref, features_ref, degree_ref, sems):
+    copies = [
+        pltpu.make_async_copy(degree_hbm, degree_ref, sems.at[0]),
+        pltpu.make_async_copy(features_hbm, features_ref, sems.at[1]),
+    ]
+    for copy in copies:
+        copy.start()
+    copies[0].wait()
     inv = spread_inv(degree_ref, features_ref.shape[1])
     inv_ref[...] = inv
+    copies[1].wait()
     out_ref[...] = (features_ref[...].astype(F32) * inv).astype(BF16)
 
 
@@ -289,7 +297,15 @@
     degree = degree.reshape(1, owned)
     bias_vector = bias_vector.reshape(1, width)
 
-    scaled, inv = call(scale_kernel, [VMEM, VMEM], [(piece, BF16), (piece, F32)])(features, degree)
+    features, degree = (
+        pltpu.with_memory_space_constraint(x, pltpu.HBM) for x in (features, degree)
+    )
+    scaled, inv = call(
+        scale_kernel,
+        [pl.BlockSpec(memory_space=pltpu.HBM)] * 2,
+        [(piece, BF16), (piece, F32)],
+        [pltpu.VMEM(piece, BF16), pltpu.VMEM((1, owned), jnp.int32), pltpu.SemaphoreType.DMA((2,))],
+    )(features, degree)
     near = [to_chip(scaled, rows, k) for k in range(1, chips)]
     blocks, turned, bias_vector = call(
         build_kernel,

time: 47.7 us -> 47 us (0.985)
  local copies, waits for them, and re-layouts: 2.17 us -> 0.68 us
  Pallas kernels: 3.15 us -> 3.95 us
  starting transfers between devices: 25.3 us -> 24.7 us
    unnamed x14 -> x10, local copies, waits for them, and re-layouts: 2.17 us -> 0.68 us
    ppermute x9, waiting for transfers between devices: 3.45 us -> 4.56 us  [to_chip(): return lax.ppermute(x, 'row', pairs)]
    pallas_call x1, Pallas kernels: 0.11 us -> 0.89 us  [per_device(): call(scale_kernel, [pl.BlockSpec(memory_space=pltpu.HBM)] * 2, [(piece, B...]
    ppermute x4, waiting for transfers between devices: 2.41 us -> 1.88 us  [to_core(): return lax.ppermute(x, 'row', [(i, i ^ 1) for i in range(rows)])]
    ppermute x9, starting transfers between devices: 11.8 us -> 11.3 us  [to_chip(): return lax.ppermute(x, 'row', pairs)]
  transfers between devices with their start and end apart: 22 -> 22, of which waited for: 13 -> 15; matrix products, arithmetic and copies ran while one was open for 0% -> 0% of each run, Pallas kernels for 3% -> 3%
where the time goes in v14:
time: 47 us; the launch traced here: 46.6 us
  starting transfers between devices  24.7 us (53%)
  waiting for transfers between devices  15.8 us (34%)
  Pallas kernels  3.95 us (8%)
  between operations  1.45 us (3%)
  local copies, waits for them, and re-layouts  0.68 us (1%)
    ppermute x9, starting transfers between devices, to_col(): lax.ppermute(x, 'col', [(i, target(cols, i, k)) for i in range(cols)])  13.1 us
    ppermute x9, starting transfers between devices, to_chip(): return lax.ppermute(x, 'row', pairs)  11.3 us
    ppermute x9, waiting for transfers between devices, to_col(): lax.ppermute(x, 'col', [(i, target(cols, i, k)) for i in range(cols)])  9.4 us
    ppermute x9, waiting for transfers between devices, to_chip(): return lax.ppermute(x, 'row', pairs)  4.56 us
    ppermute x4, waiting for transfers between devices, to_core(): return lax.ppermute(x, 'row', [(i, i ^ 1) for i in range(rows)])  1.88 us
  transfers between devices with their start and end apart: 22, of which 15 were waited for; matrix products, arithmetic and copies ran while one was open for 0% of the time, Pallas kernels for 3%

profile of v14, /device:TPU:0, one launch (start us, length us, event | category | flops | bytes accessed | tf_op | source)
XLA Modules:
  0.0 46.6 jit_solution(11804867457629920618)
XLA Ops:
  0.6 0.9 %shard_map.112 = (bf16[128,256]{1,0:T(8,128)(2,1)S(1)}, f32[128,256]{1,0:T(8,128)S(1)}) custom-call(bf16[128,256]{1,0:T(8,128)(2,1)} %features_hbm.1, s32[1,128]{1,0:T(1,128)} %bitcast.4), custom_call_target="tpu_custom_call" | custom-call | flops 1000000 | bytes 1000000 | tf_op jit(solution)/shard_map/pallas_call | solution.py:303
  1.5 4.0 %collective-permute-start.2 = (bf16[128,256]{1,0:T(8,128)(2,1)S(1)}, bf16[128,256]{1,0:T(8,128)(2,1)S(1)}, u32[]{:S(2)}, u32[]{:S(2)}) collective-permute-start(bf16[128,256]{1,0:T(8,128)(2,1)S(1)} %get-tuple-element.39.refs_0_), channel_id=1, source_target_pairs={{0,24},{4,28},{8,16},{12,20},{16,8},{20,12},{24,0},{28,4},{1,25},{... | collective-permute-start | bytes 196616 | tf_op jit(solution)/shard_map/ppermute | solution.py:50
  5.5 0.5 %collective-permute-start.1 = (bf16[128,256]{1,0:T(8,128)(2,1)S(1)}, bf16[128,256]{1,0:T(8,128)(2,1)S(1)}, u32[]{:S(2)}, u32[]{:S(2)}) collective-permute-start(bf16[128,256]{1,0:T(8,128)(2,1)S(1)} %get-tuple-element.39.refs_0_), channel_id=1, source_target_pairs={{0,16},{4,20},{8,24},{12,28},{16,0},{20,4},{24,8},{28,12},{1,17},{... | collective-permute-start | bytes 196616 | tf_op jit(solution)/shard_map/ppermute | solution.py:50
  6.0 0.1 collective-permute-start
  6.8 0.0 copy-start.4
  6.8 0.7 %copy-done.4 = f32[256]{0:T(256)S(1)} copy-done((f32[256]{0:T(256)S(1)}, f32[256]{0:T(256)}, u32[]{:S(2)}) %copy-start.4) | copy-done | bytes 1048
  7.5 0.5 %shard_map.111 = (bf16[16,128,128]{2,1,0:T(8,128)(2,1)S(1)}, bf16[16,128,128]{2,1,0:T(8,128)(2,1)S(1)}, f32[1,256]{1,0:T(1,128)S(1)}) custom-call(s32[1,1]{1,0:T(1,128)S(6)} %copy.12.count_ref, s32[1,1,16,512]{3,2,1,0:T(8,128)S(1)} %copy-done.3, f32[1,256]{1,0:T(1,128)S(1)} %bitcast.3), custom_call_target="tpu_custom_call" | custom-call | flops 4000000000 | bytes 1000000 | tf_op jit(solution)/shard_map/pallas_call | solution.py:310
  8.0 1.7 %collective-permute-done.1.refs_2_ = bf16[128,256]{1,0:T(8,128)(2,1)S(1)} collective-permute-done((bf16[128,256]{1,0:T(8,128)(2,1)S(1)}, bf16[128,256]{1,0:T(8,128)(2,1)S(1)}, u32[]{:S(2)}, u32[]{:S(2)}) %collective-permute-start.1) | collective-permute-done | bytes 65568 | tf_op jit(solution)/shard_map/ppermute | solution.py:50
  9.8 0.5 %collective-permute-done.refs_1_ = bf16[128,256]{1,0:T(8,128)(2,1)S(1)} collective-permute-done((bf16[128,256]{1,0:T(8,128)(2,1)S(1)}, bf16[128,256]{1,0:T(8,128)(2,1)S(1)}, u32[]{:S(2)}, u32[]{:S(2)}) %collective-permute-start) | collective-permute-done | bytes 65568 | tf_op jit(solution)/shard_map/ppermute | solution.py:50
  10.3 0.0 copy-start
  10.3 0.1 collective-permute-start.3
  10.4 1.5 %collective-permute-done.3.next_ref = bf16[4,128,256]{2,1,0:T(8,128)(2,1)S(1)} collective-permute-done((bf16[4,128,256]{2,1,0:T(8,128)(2,1)S(1)}, bf16[4,128,256]{2,1,0:T(8,128)(2,1)S(1)}, u32[]{:S(2)}, u32[]{:S(2)}) %collective-permute-start.3) | collective-permute-done | bytes 262176 | tf_op jit(solution)/shard_map/ppermute | solution.py:40
  11.9 0.5 %shard_map.114 = (f32[128,256]{1,0:T(8,128)S(1)}, bf16[128,256]{1,0:T(8,128)(2,1)S(1)}, bf16[128,256]{1,0:T(8,128)(2,1)S(1)}, bf16[128,256]{1,0:T(8,128)(2,1)S(1)}) custom-call(s32[1,1,16]{2,1,0:T(1,128)S(1)} %copy-done.2, s32[1,1]{1,0:T(1,128)S(6)} %copy.12.count_ref, bf16[16,128,128]{2,1,0:T(8,128)(2,1)S(1)} %get-tuple-element.40.blocks_ref, ...), custom_call_target="tpu_custom_call" | custom-call | flops 1000000 | bytes 1000000 | tf_op jit(solution)/shard_map/pallas_call | solution.py:319
  12.4 2.7 %collective-permute-start.4 = (bf16[128,256]{1,0:T(8,128)(2,1)S(1)}, bf16[128,256]{1,0:T(8,128)(2,1)S(1)}, u32[]{:S(2)}, u32[]{:S(2)}) collective-permute-start(bf16[128,256]{1,0:T(8,128)(2,1)S(1)} %get-tuple-element.45), channel_id=1, source_target_pairs={{0,2},{1,3},{2,0},{3,1},{4,6},{5,7},{6,4},{7,5},{8,10},{9,11},{10,... | collective-permute-start | bytes 196616 | tf_op jit(solution)/shard_map/ppermute | solution.py:54
  15.1 1.3 %collective-permute-start.5 = (bf16[128,256]{1,0:T(8,128)(2,1)S(1)}, bf16[128,256]{1,0:T(8,128)(2,1)S(1)}, u32[]{:S(2)}, u32[]{:S(2)}) collective-permute-start(bf16[128,256]{1,0:T(8,128)(2,1)S(1)} %get-tuple-element.46), channel_id=1, source_target_pairs={{0,3},{1,2},{2,1},{3,0},{4,7},{5,6},{6,5},{7,4},{8,11},{9,10},{10,... | collective-permute-start | bytes 196616 | tf_op jit(solution)/shard_map/ppermute | solution.py:54
  16.4 0.2 collective-permute-start.6
  16.7 3.7 %collective-permute-done.4.refs_1_ = bf16[128,256]{1,0:T(8,128)(2,1)S(1)} collective-permute-done((bf16[128,256]{1,0:T(8,128)(2,1)S(1)}, bf16[128,256]{1,0:T(8,128)(2,1)S(1)}, u32[]{:S(2)}, u32[]{:S(2)}) %collective-permute-start.4) | collective-permute-done | bytes 65568 | tf_op jit(solution)/shard_map/ppermute | solution.py:54
  20.4 1.1 %collective-permute-done.5.refs_2_ = bf16[128,256]{1,0:T(8,128)(2,1)S(1)} collective-permute-done((bf16[128,256]{1,0:T(8,128)(2,1)S(1)}, bf16[128,256]{1,0:T(8,128)(2,1)S(1)}, u32[]{:S(2)}, u32[]{:S(2)}) %collective-permute-start.5) | collective-permute-done | bytes 65568 | tf_op jit(solution)/shard_map/ppermute | solution.py:54
  21.5 0.6 %collective-permute-done.6.refs_3_ = bf16[128,256]{1,0:T(8,128)(2,1)S(1)} collective-permute-done((bf16[128,256]{1,0:T(8,128)(2,1)S(1)}, bf16[128,256]{1,0:T(8,128)(2,1)S(1)}, u32[]{:S(2)}, u32[]{:S(2)}) %collective-permute-start.6) | collective-permute-done | bytes 65568 | tf_op jit(solution)/shard_map/ppermute | solution.py:54
  22.1 0.4 shard_map.115
  22.5 0.1 collective-permute-start.10
  22.6 2.9 %collective-permute-start.9 = (bf16[128,256]{1,0:T(8,128)(2,1)S(1)}, bf16[128,256]{1,0:T(8,128)(2,1)S(1)}, u32[]{:S(2)}, u32[]{:S(2)}) collective-permute-start(bf16[128,256]{1,0:T(8,128)(2,1)S(1)} %get-tuple-element.50.refs_0_), channel_id=1, source_target_pairs={{0,3},{1,2},{2,1},{3,0},{4,7},{5,6},{6,5},{7,4},{8,11},{9,10},{10,... | collective-permute-start | bytes 196616 | tf_op jit(solution)/shard_map/ppermute | solution.py:54
  25.5 1.5 %collective-permute-start.7 = (bf16[128,256]{1,0:T(8,128)(2,1)S(1)}, bf16[128,256]{1,0:T(8,128)(2,1)S(1)}, u32[]{:S(2)}, u32[]{:S(2)}) collective-permute-start(bf16[128,256]{1,0:T(8,128)(2,1)S(1)} %get-tuple-element.50.refs_0_), channel_id=1, source_target_pairs={{0,1},{1,0},{2,3},{3,2},{4,5},{5,4},{6,7},{7,6},{8,9},{9,8},{10,11... | collective-permute-start | bytes 196616 | tf_op jit(solution)/shard_map/ppermute | solution.py:54
  27.1 1.3 %collective-permute-start.13 = (bf16[144,256]{1,0:T(8,128)(2,1)S(1)}, bf16[144,256]{1,0:T(8,128)(2,1)S(1)}, u32[]{:S(2)}, u32[]{:S(2)}) collective-permute-start(bf16[144,256]{1,0:T(8,128)(2,1)S(1)} %shard_map.117.refs_0_), channel_id=1, source_target_pairs={{0,24},{4,28},{8,16},{12,20},{16,8},{20,12},{24,0},{28,4},{1,25},{... | collective-permute-start | bytes 221192 | tf_op jit(solution)/shard_map/ppermute | solution.py:50
  28.3 0.4 collective-permute-start.12
  28.8 0.6 %collective-permute-done.9.refs_3_ = bf16[128,256]{1,0:T(8,128)(2,1)S(1)} collective-permute-done((bf16[128,256]{1,0:T(8,128)(2,1)S(1)}, bf16[128,256]{1,0:T(8,128)(2,1)S(1)}, u32[]{:S(2)}, u32[]{:S(2)}) %collective-permute-start.9) | collective-permute-done | bytes 65568 | tf_op jit(solution)/shard_map/ppermute | solution.py:54
  29.4 1.2 %collective-permute-start.11 = (bf16[144,256]{1,0:T(8,128)(2,1)S(1)}, bf16[144,256]{1,0:T(8,128)(2,1)S(1)}, u32[]{:S(2)}, u32[]{:S(2)}) collective-permute-start(bf16[144,256]{1,0:T(8,128)(2,1)S(1)} %shard_map.117.refs_0_), channel_id=1, source_target_pairs={{0,8},{4,12},{8,0},{12,4},{16,24},{20,28},{24,16},{28,20},{1,9},{5... | collective-permute-start | bytes 221192 | tf_op jit(solution)/shard_map/ppermute | solution.py:50
  30.6 1.2 %collective-permute-done.8.refs_2_ = bf16[128,256]{1,0:T(8,128)(2,1)S(1)} collective-permute-done((bf16[128,256]{1,0:T(8,128)(2,1)S(1)}, bf16[128,256]{1,0:T(8,128)(2,1)S(1)}, u32[]{:S(2)}, u32[]{:S(2)}) %collective-permute-start.8) | collective-permute-done | bytes 65568 | tf_op jit(solution)/shard_map/ppermute | solution.py:54
  31.8 0.5 %shard_map.116 = (f32[4,128,256]{2,1,0:T(8,128)S(1)}, bf16[4,128,256]{2,1,0:T(8,128)(2,1)S(1)}) custom-call(s32[1,1,16]{2,1,0:T(1,128)S(1)} %copy-done.2, s32[1,1]{1,0:T(1,128)S(6)} %copy.12.count_ref, bf16[16,128,128]{2,1,0:T(8,128)(2,1)S(1)} %get-tuple-element.49.turned_ref, bf16[128,256]{1,0:T(8,128)(2,1)S(1)} %get-tuple-element.50.refs_0_, ...), custom_call_target="tpu_custom_call" | custom-call | flops 4000000000 | bytes 1000000 | tf_op jit(solution)/shard_map/pallas_call | solution.py:347
  32.3 0.6 %collective-permute-done.13.refs_3_ = bf16[144,256]{1,0:T(8,128)(2,1)S(1)} collective-permute-done((bf16[144,256]{1,0:T(8,128)(2,1)S(1)}, bf16[144,256]{1,0:T(8,128)(2,1)S(1)}, u32[]{:S(2)}, u32[]{:S(2)}) %collective-permute-start.13) | collective-permute-done | bytes 73760 | tf_op jit(solution)/shard_map/ppermute | solution.py:50
  32.9 0.4 collective-permute-done.12.refs_2_
  33.4 0.3 collective-permute-done.11.refs_1_
  33.7 0.1 shard_map.118.refs_0_
  33.8 0.1 collective-permute-start.14
  33.9 3.0 %collective-permute-start.20 = (bf16[144,256]{1,0:T(8,128)(2,1)S(1)}, bf16[144,256]{1,0:T(8,128)(2,1)S(1)}, u32[]{:S(2)}, u32[]{:S(2)}) collective-permute-start(bf16[144,256]{1,0:T(8,128)(2,1)S(1)} %shard_map.118.refs_0_), channel_id=1, source_target_pairs={{0,3},{1,2},{2,1},{3,0},{4,7},{5,6},{6,5},{7,4},{8,11},{9,10},{10,... | collective-permute-start | bytes 221192 | tf_op jit(solution)/shard_map/ppermute | solution.py:54
  36.9 0.1 collective-permute-start.19
  37.0 1.3 %collective-permute-start.18 = (bf16[144,256]{1,0:T(8,128)(2,1)S(1)}, bf16[144,256]{1,0:T(8,128)(2,1)S(1)}, u32[]{:S(2)}, u32[]{:S(2)}) collective-permute-start(bf16[144,256]{1,0:T(8,128)(2,1)S(1)} %shard_map.118.refs_0_), channel_id=1, source_target_pairs={{0,1},{1,0},{2,3},{3,2},{4,5},{5,4},{6,7},{7,6},{8,9},{9,8},{10,11... | collective-permute-start | bytes 221192 | tf_op jit(solution)/shard_map/ppermute | solution.py:54
  38.4 0.1 shard_map.119
  38.4 2.0 %collective-permute-start.15 = (bf16[128,256]{1,0:T(8,128)(2,1)S(1)}, bf16[128,256]{1,0:T(8,128)(2,1)S(1)}, u32[]{:S(2)}, u32[]{:S(2)}) collective-permute-start(bf16[128,256]{1,0:T(8,128)(2,1)S(1)} %get-tuple-element.58), channel_id=1, source_target_pairs={{0,24},{4,28},{8,16},{12,20},{16,8},{20,12},{24,0},{28,4},{1,25},{... | collective-permute-start | bytes 196616 | tf_op jit(solution)/shard_map/ppermute | solution.py:50
  40.4 0.8 %collective-permute-start.16 = (bf16[128,256]{1,0:T(8,128)(2,1)S(1)}, bf16[128,256]{1,0:T(8,128)(2,1)S(1)}, u32[]{:S(2)}, u32[]{:S(2)}) collective-permute-start(bf16[128,256]{1,0:T(8,128)(2,1)S(1)} %get-tuple-element.59), channel_id=1, source_target_pairs={{0,16},{4,20},{8,24},{12,28},{16,0},{20,4},{24,8},{28,12},{1,17},{... | collective-permute-start | bytes 196616 | tf_op jit(solution)/shard_map/ppermute | solution.py:50
  41.2 1.0 %collective-permute-start.17 = (bf16[128,256]{1,0:T(8,128)(2,1)S(1)}, bf16[128,256]{1,0:T(8,128)(2,1)S(1)}, u32[]{:S(2)}, u32[]{:S(2)}) collective-permute-start(bf16[128,256]{1,0:T(8,128)(2,1)S(1)} %get-tuple-element.60), channel_id=1, source_target_pairs={{0,8},{4,12},{8,0},{12,4},{16,24},{20,28},{24,16},{28,20},{1,9},{5... | collective-permute-start | bytes 196616 | tf_op jit(solution)/shard_map/ppermute | solution.py:50
  42.2 2.2 %collective-permute-done.19.refs_2_ = bf16[144,256]{1,0:T(8,128)(2,1)S(1)} collective-permute-done((bf16[144,256]{1,0:T(8,128)(2,1)S(1)}, bf16[144,256]{1,0:T(8,128)(2,1)S(1)}, u32[]{:S(2)}, u32[]{:S(2)}) %collective-permute-start.19) | collective-permute-done | bytes 73760 | tf_op jit(solution)/shard_map/ppermute | solution.py:54
  44.4 0.1 shard_map.121
  44.4 0.1 collective-permute-start.21
  44.5 0.1 collective-permute-done.16.refs_1_
  44.7 0.8 %collective-permute-done.17.refs_2_ = bf16[128,256]{1,0:T(8,128)(2,1)S(1)} collective-permute-done((bf16[128,256]{1,0:T(8,128)(2,1)S(1)}, bf16[128,256]{1,0:T(8,128)(2,1)S(1)}, u32[]{:S(2)}, u32[]{:S(2)}) %collective-permute-start.17) | collective-permute-done | bytes 65568 | tf_op jit(solution)/shard_map/ppermute | solution.py:50
  45.5 0.4 collective-permute-done.21.theirs_ref
  45.9 0.8 %shard_map.122 = (bf16[128,256]{1,0:T(8,128)(2,1)}, bf16[128,256]{1,0:T(8,128)(2,1)}, f32[256,256]{1,0:T(8,128)}, f32[1,256]{1,0:T(1,128)}) custom-call(bf16[128,256]{1,0:T(8,128)(2,1)S(1)} %get-tuple-element.48.out_ref, bf16[128,256]{1,0:T(8,128)(2,1)S(1)} %shard_map.120.x_ref, f32[128,256]{1,0:T(8,128)S(1)} %get-tuple-element.62.mine_ref, ...), custom_call_target="tpu_custom_call" | custom-call | flops 1000000 | bytes 1000000 | tf_op jit(solution)/shard_map/pallas_call | solution.py:372
  (18 shorter events, 0.1 us)
Async XLA Ops:
  0.6 6.2 %copy-start.3 = (s32[1,1,16,512]{3,2,1,0:T(8,128)S(1)}, s32[1,1,16,512]{3,2,1,0:T(8,128)}, u32[]{:S(2)}) copy-start(s32[1,1,16,512]{3,2,1,0:T(8,128)} %edge_ref.1) | copy-start | bytes 98308
  1.5 6.5 %collective-permute-start.2 = (bf16[128,256]{1,0:T(8,128)(2,1)S(1)}, bf16[128,256]{1,0:T(8,128)(2,1)S(1)}, u32[]{:S(2)}, u32[]{:S(2)}) collective-permute-start(bf16[128,256]{1,0:T(8,128)(2,1)S(1)} %get-tuple-element.39.refs_0_), channel_id=1, source_target_pairs={{0,24},{4,28},{8,16},{12,20},{16,8},{20,12},{24,0},{28,4},{1,25},{... | collective-permute-start | bytes 196616 | tf_op jit(solution)/shard_map/ppermute | solution.py:50
  5.5 4.3 %collective-permute-start.1 = (bf16[128,256]{1,0:T(8,128)(2,1)S(1)}, bf16[128,256]{1,0:T(8,128)(2,1)S(1)}, u32[]{:S(2)}, u32[]{:S(2)}) collective-permute-start(bf16[128,256]{1,0:T(8,128)(2,1)S(1)} %get-tuple-element.39.refs_0_), channel_id=1, source_target_pairs={{0,16},{4,20},{8,24},{12,28},{16,0},{20,4},{24,8},{28,12},{1,17},{... | collective-permute-start | bytes 196616 | tf_op jit(solution)/shard_map/ppermute | solution.py:50
  6.0 4.3 %collective-permute-start = (bf16[128,256]{1,0:T(8,128)(2,1)S(1)}, bf16[128,256]{1,0:T(8,128)(2,1)S(1)}, u32[]{:S(2)}, u32[]{:S(2)}) collective-permute-start(bf16[128,256]{1,0:T(8,128)(2,1)S(1)} %get-tuple-element.39.refs_0_), channel_id=1, source_target_pairs={{0,8},{4,12},{8,0},{12,4},{16,24},{20,28},{24,16},{28,20},{1,9},{5... | collective-permute-start | bytes 196616 | tf_op jit(solution)/shard_map/ppermute | solution.py:50
  6.8 0.7 %copy-start.4 = (f32[256]{0:T(256)S(1)}, f32[256]{0:T(256)}, u32[]{:S(2)}) copy-start(f32[256]{0:T(256)} %param.11) | copy-start | bytes 3076
  10.3 1.7 %copy-start.2 = (s32[1,1,16]{2,1,0:T(1,128)S(1)}, s32[1,1,16]{2,1,0:T(1,128)}, u32[]{:S(2)}) copy-start(s32[1,1,16]{2,1,0:T(1,128)} %pos_ref.3) | copy-start | bytes 196
  10.3 11.8 %copy-start = (bf16[256,256]{1,0:T(8,128)(2,1)S(1)}, bf16[256,256]{1,0:T(8,128)(2,1)}, u32[]{:S(2)}) copy-start(bf16[256,256]{1,0:T(8,128)(2,1)} %weight_ref.1) | copy-start | bytes 393220
  10.3 11.8 %copy-start.1 = (bf16[128,256]{1,0:T(8,128)(2,1)S(1)}, bf16[128,256]{1,0:T(8,128)(2,1)}, u32[]{:S(2)}) copy-start(bf16[128,256]{1,0:T(8,128)(2,1)} %cot_ref.1) | copy-start | bytes 196612
  10.3 1.6 %collective-permute-start.3 = (bf16[4,128,256]{2,1,0:T(8,128)(2,1)S(1)}, bf16[4,128,256]{2,1,0:T(8,128)(2,1)S(1)}, u32[]{:S(2)}, u32[]{:S(2)}) collective-permute-start(bf16[4,128,256]{2,1,0:T(8,128)(2,1)S(1)} %shard_map.113.near_ref), channel_id=1, source_target_pairs={{0,4},{4,0},{8,12},{12,8},{16,20},{20,16},{24,28},{28,24},{1,5},{5... | collective-permute-start | bytes 786440 | tf_op jit(solution)/shard_map/ppermute | solution.py:40
  12.4 8.0 %collective-permute-start.4 = (bf16[128,256]{1,0:T(8,128)(2,1)S(1)}, bf16[128,256]{1,0:T(8,128)(2,1)S(1)}, u32[]{:S(2)}, u32[]{:S(2)}) collective-permute-start(bf16[128,256]{1,0:T(8,128)(2,1)S(1)} %get-tuple-element.45), channel_id=1, source_target_pairs={{0,2},{1,3},{2,0},{3,1},{4,6},{5,7},{6,4},{7,5},{8,10},{9,11},{10,... | collective-permute-start | bytes 196616 | tf_op jit(solution)/shard_map/ppermute | solution.py:54
  15.1 6.4 %collective-permute-start.5 = (bf16[128,256]{1,0:T(8,128)(2,1)S(1)}, bf16[128,256]{1,0:T(8,128)(2,1)S(1)}, u32[]{:S(2)}, u32[]{:S(2)}) collective-permute-start(bf16[128,256]{1,0:T(8,128)(2,1)S(1)} %get-tuple-element.46), channel_id=1, source_target_pairs={{0,3},{1,2},{2,1},{3,0},{4,7},{5,6},{6,5},{7,4},{8,11},{9,10},{10,... | collective-permute-start | bytes 196616 | tf_op jit(solution)/shard_map/ppermute | solution.py:54
  16.4 5.7 %collective-permute-start.6 = (bf16[128,256]{1,0:T(8,128)(2,1)S(1)}, bf16[128,256]{1,0:T(8,128)(2,1)S(1)}, u32[]{:S(2)}, u32[]{:S(2)}) collective-permute-start(bf16[128,256]{1,0:T(8,128)(2,1)S(1)} %get-tuple-element.47), channel_id=1, source_target_pairs={{0,1},{1,0},{2,3},{3,2},{4,5},{5,4},{6,7},{7,6},{8,9},{9,8},{10,11... | collective-permute-start | bytes 196616 | tf_op jit(solution)/shard_map/ppermute | solution.py:54
  22.5 4.5 %collective-permute-start.10 = (bf16[144,256]{1,0:T(8,128)(2,1)S(1)}, bf16[144,256]{1,0:T(8,128)(2,1)S(1)}, u32[]{:S(2)}, u32[]{:S(2)}) collective-permute-start(bf16[144,256]{1,0:T(8,128)(2,1)S(1)} %get-tuple-element.55), channel_id=1, source_target_pairs={{0,4},{4,0},{8,12},{12,8},{16,20},{20,16},{24,28},{28,24},{1,5},{5... | collective-permute-start | bytes 221192 | tf_op jit(solution)/shard_map/ppermute | solution.py:40
  22.6 6.8 %collective-permute-start.9 = (bf16[128,256]{1,0:T(8,128)(2,1)S(1)}, bf16[128,256]{1,0:T(8,128)(2,1)S(1)}, u32[]{:S(2)}, u32[]{:S(2)}) collective-permute-start(bf16[128,256]{1,0:T(8,128)(2,1)S(1)} %get-tuple-element.50.refs_0_), channel_id=1, source_target_pairs={{0,3},{1,2},{2,1},{3,0},{4,7},{5,6},{6,5},{7,4},{8,11},{9,10},{10,... | collective-permute-start | bytes 196616 | tf_op jit(solution)/shard_map/ppermute | solution.py:54
  25.5 6.3 %collective-permute-start.8 = (bf16[128,256]{1,0:T(8,128)(2,1)S(1)}, bf16[128,256]{1,0:T(8,128)(2,1)S(1)}, u32[]{:S(2)}, u32[]{:S(2)}) collective-permute-start(bf16[128,256]{1,0:T(8,128)(2,1)S(1)} %get-tuple-element.50.refs_0_), channel_id=1, source_target_pairs={{0,2},{1,3},{2,0},{3,1},{4,6},{5,7},{6,4},{7,5},{8,10},{9,11},{10,... | collective-permute-start | bytes 196616 | tf_op jit(solution)/shard_map/ppermute | solution.py:54
  25.5 6.3 %collective-permute-start.7 = (bf16[128,256]{1,0:T(8,128)(2,1)S(1)}, bf16[128,256]{1,0:T(8,128)(2,1)S(1)}, u32[]{:S(2)}, u32[]{:S(2)}) collective-permute-start(bf16[128,256]{1,0:T(8,128)(2,1)S(1)} %get-tuple-element.50.refs_0_), channel_id=1, source_target_pairs={{0,1},{1,0},{2,3},{3,2},{4,5},{5,4},{6,7},{7,6},{8,9},{9,8},{10,11... | collective-permute-start | bytes 196616 | tf_op jit(solution)/shard_map/ppermute | solution.py:54
  27.1 5.9 %collective-permute-start.13 = (bf16[144,256]{1,0:T(8,128)(2,1)S(1)}, bf16[144,256]{1,0:T(8,128)(2,1)S(1)}, u32[]{:S(2)}, u32[]{:S(2)}) collective-permute-start(bf16[144,256]{1,0:T(8,128)(2,1)S(1)} %shard_map.117.refs_0_), channel_id=1, source_target_pairs={{0,24},{4,28},{8,16},{12,20},{16,8},{20,12},{24,0},{28,4},{1,25},{... | collective-permute-start | bytes 221192 | tf_op jit(solution)/shard_map/ppermute | solution.py:50
  28.3 5.0 %collective-permute-start.12 = (bf16[144,256]{1,0:T(8,128)(2,1)S(1)}, bf16[144,256]{1,0:T(8,128)(2,1)S(1)}, u32[]{:S(2)}, u32[]{:S(2)}) collective-permute-start(bf16[144,256]{1,0:T(8,128)(2,1)S(1)} %shard_map.117.refs_0_), channel_id=1, source_target_pairs={{0,16},{4,20},{8,24},{12,28},{16,0},{20,4},{24,8},{28,12},{1,17},{... | collective-permute-start | bytes 221192 | tf_op jit(solution)/shard_map/ppermute | solution.py:50
  29.4 4.4 %collective-permute-start.11 = (bf16[144,256]{1,0:T(8,128)(2,1)S(1)}, bf16[144,256]{1,0:T(8,128)(2,1)S(1)}, u32[]{:S(2)}, u32[]{:S(2)}) collective-permute-start(bf16[144,256]{1,0:T(8,128)(2,1)S(1)} %shard_map.117.refs_0_), channel_id=1, source_target_pairs={{0,8},{4,12},{8,0},{12,4},{16,24},{20,28},{24,16},{28,20},{1,9},{5... | collective-permute-start | bytes 221192 | tf_op jit(solution)/shard_map/ppermute | solution.py:50
  33.8 4.5 %collective-permute-start.14 = (bf16[4,128,256]{2,1,0:T(8,128)(2,1)S(1)}, bf16[4,128,256]{2,1,0:T(8,128)(2,1)S(1)}, u32[]{:S(2)}, u32[]{:S(2)}) collective-permute-start(bf16[4,128,256]{2,1,0:T(8,128)(2,1)S(1)} %get-tuple-element.56), channel_id=1, source_target_pairs={{0,4},{4,0},{8,12},{12,8},{16,20},{20,16},{24,28},{28,24},{1,5},{5... | collective-permute-start | bytes 786440 | tf_op jit(solution)/shard_map/ppermute | solution.py:40
  33.9 7.3 %collective-permute-start.20 = (bf16[144,256]{1,0:T(8,128)(2,1)S(1)}, bf16[144,256]{1,0:T(8,128)(2,1)S(1)}, u32[]{:S(2)}, u32[]{:S(2)}) collective-permute-start(bf16[144,256]{1,0:T(8,128)(2,1)S(1)} %shard_map.118.refs_0_), channel_id=1, source_target_pairs={{0,3},{1,2},{2,1},{3,0},{4,7},{5,6},{6,5},{7,4},{8,11},{9,10},{10,... | collective-permute-start | bytes 221192 | tf_op jit(solution)/shard_map/ppermute | solution.py:54
  36.9 7.5 %collective-permute-start.19 = (bf16[144,256]{1,0:T(8,128)(2,1)S(1)}, bf16[144,256]{1,0:T(8,128)(2,1)S(1)}, u32[]{:S(2)}, u32[]{:S(2)}) collective-permute-start(bf16[144,256]{1,0:T(8,128)(2,1)S(1)} %shard_map.118.refs_0_), channel_id=1, source_target_pairs={{0,2},{1,3},{2,0},{3,1},{4,6},{5,7},{6,4},{7,5},{8,10},{9,11},{10,... | collective-permute-start | bytes 221192 | tf_op jit(solution)/shard_map/ppermute | solution.py:54
  37.0 7.3 %collective-permute-start.18 = (bf16[144,256]{1,0:T(8,128)(2,1)S(1)}, bf16[144,256]{1,0:T(8,128)(2,1)S(1)}, u32[]{:S(2)}, u32[]{:S(2)}) collective-permute-start(bf16[144,256]{1,0:T(8,128)(2,1)S(1)} %shard_map.118.refs_0_), channel_id=1, source_target_pairs={{0,1},{1,0},{2,3},{3,2},{4,5},{5,4},{6,7},{7,6},{8,9},{9,8},{10,11... | collective-permute-start | bytes 221192 | tf_op jit(solution)/shard_map/ppermute | solution.py:54
  38.4 6.1 %collective-permute-start.15 = (bf16[128,256]{1,0:T(8,128)(2,1)S(1)}, bf16[128,256]{1,0:T(8,128)(2,1)S(1)}, u32[]{:S(2)}, u32[]{:S(2)}) collective-permute-start(bf16[128,256]{1,0:T(8,128)(2,1)S(1)} %get-tuple-element.58), channel_id=1, source_target_pairs={{0,24},{4,28},{8,16},{12,20},{16,8},{20,12},{24,0},{28,4},{1,25},{... | collective-permute-start | bytes 196616 | tf_op jit(solution)/shard_map/ppermute | solution.py:50
  40.4 4.3 %collective-permute-start.16 = (bf16[128,256]{1,0:T(8,128)(2,1)S(1)}, bf16[128,256]{1,0:T(8,128)(2,1)S(1)}, u32[]{:S(2)}, u32[]{:S(2)}) collective-permute-start(bf16[128,256]{1,0:T(8,128)(2,1)S(1)} %get-tuple-element.59), channel_id=1, source_target_pairs={{0,16},{4,20},{8,24},{12,28},{16,0},{20,4},{24,8},{28,12},{1,17},{... | collective-permute-start | bytes 196616 | tf_op jit(solution)/shard_map/ppermute | solution.py:50
  41.2 4.3 %collective-permute-start.17 = (bf16[128,256]{1,0:T(8,128)(2,1)S(1)}, bf16[128,256]{1,0:T(8,128)(2,1)S(1)}, u32[]{:S(2)}, u32[]{:S(2)}) collective-permute-start(bf16[128,256]{1,0:T(8,128)(2,1)S(1)} %get-tuple-element.60), channel_id=1, source_target_pairs={{0,8},{4,12},{8,0},{12,4},{16,24},{20,28},{24,16},{28,20},{1,9},{5... | collective-permute-start | bytes 196616 | tf_op jit(solution)/shard_map/ppermute | solution.py:50
  44.4 1.4 %collective-permute-start.21 = (f32[128,256]{1,0:T(8,128)S(1)}, f32[128,256]{1,0:T(8,128)S(1)}, u32[]{:S(2)}, u32[]{:S(2)}) collective-permute-start(f32[128,256]{1,0:T(8,128)S(1)} %get-tuple-element.62.mine_ref), channel_id=1, source_target_pairs={{0,4},{4,0},{8,12},{12,8},{16,20},{20,16},{24,28},{28,24},{1,5},{5... | collective-permute-start | bytes 393224 | tf_op jit(solution)/shard_map/ppermute | solution.py:40

commit v15 on v14

--- a/solution.py
+++ b/solution.py
@@ -11,6 +11,7 @@
 CORES = 2
 EXTRA = 16
 LONG = 4_000_000_000
+SHORT = 1_000_000_000
 GROUP = 8
 VMEM = pl.BlockSpec(memory_space=pltpu.VMEM)
 SMEM = pl.BlockSpec(memory_space=pltpu.SMEM)
@@ -151,7 +152,8 @@
 
 def pointwise_kernel(cols, weight_ref, bias_ref, cot_ref, inv_ref, *refs):
     own_ref, *parts = refs[:cols]
-    out_ref, hidden_ref, keep_ref, bias_keep_ref, send_ref = refs[cols:]
+    out_ref, hidden_ref, keep_ref, send_ref = refs[cols:]
+    owned = out_ref.shape[0]
     width = out_ref.shape[1]
     half = width // CORES
     core = lax.rem(lax.axis_index("row"), CORES)
@@ -166,49 +168,43 @@
     out_ref[...] = (preact * sig).astype(BF16)
     grad_pre = (cot_ref[...].astype(F32) * sig * (1.0 + preact * (1.0 - sig))).astype(BF16)
     hidden = lax.dot_general(grad_pre, weight, NT, preferred_element_type=F32)
-    hidden_ref[...] = (hidden * inv).astype(BF16)
+    hidden_ref[:owned] = (hidden * inv).astype(BF16)
     term = lax.dot_general(agg, grad_pre, TN, preferred_element_type=F32)
     low, high = term[:half], term[half:]
     first = core == 0
     keep_ref[...] = jnp.where(first, low, high)
-    send_ref[:half] = jnp.where(first, high, low).astype(BF16)
+    send_ref[...] = jnp.where(first, high, low).astype(BF16)
     bias_sum = jnp.sum(grad_pre.astype(F32), axis=0, keepdims=True)
-    bias_keep_ref[...] = bias_sum
-    send_ref[half:] = pack_bias(bias_sum, EXTRA)
-
-
-def pair_sum_kernel(keep_ref, bias_keep_ref, got_ref, out_ref):
-    half = keep_ref.shape[0]
-    out_ref[:half] = (keep_ref[...] + got_ref[:half].astype(F32)).astype(BF16)
-    out_ref[half:] = pack_bias(bias_keep_ref[...] + add_bias(got_ref[half:]), EXTRA)
-
-
-def total_of(n, me, refs, stage):
-    for k, ref in enumerate(refs):
-        owner = me ^ k if is_power(n) else lax.rem(me - k + n, n)
-        stage[owner] = ref[...]
-    half = stage.shape[1] - EXTRA
-    grads, bias = stage[0, :half].astype(F32), add_bias(stage[0, half:])
+    hidden_ref[owned:] = pack_bias(bias_sum, EXTRA)
+
+
+def pair_sum_kernel(keep_ref, got_ref, out_ref):
+    out_ref[...] = (keep_ref[...] + got_ref[...].astype(F32)).astype(BF16)
+
+
+def owner_of(n, me, k):
+    return me ^ k if is_power(n) else lax.rem(me - k + n, n)
+
+
+def total_of(n, me, pieces, stage):
+    for k, piece in enumerate(pieces):
+        stage[owner_of(n, me, k)] = piece
+    total = stage[0].astype(F32)
     for i in range(1, n):
-        grads = grads + stage[i, :half].astype(F32)
-        bias = bias + add_bias(stage[i, half:])
-    return grads, bias
+        total = total + stage[i].astype(F32)
+    return total
 
 
 def chip_sum_kernel(*refs):
     *parts, out_ref, stage = refs
     chip = lax.axis_index("row") // CORES
-    grads, bias = total_of(len(parts), chip, parts, stage)
-    half = grads.shape[0]
-    out_ref[:half] = grads.astype(BF16)
-    out_ref[half:] = pack_bias(bias, EXTRA)
+    out_ref[...] = total_of(len(parts), chip, [ref[...] for ref in parts], stage).astype(BF16)
 
 
 def col_sum_kernel(norm, *refs):
-    *parts, half_ref, bias_ref, stage = refs
-    grads, bias = total_of(len(parts), lax.axis_index("col"), parts, stage)
-    half_ref[...] = grads * norm
-    bias_ref[...] = bias * norm
+    *parts, half_ref, stage = refs
+    total = total_of(len(parts), lax.axis_index("col"), [ref[...] for ref in parts], stage)
+    half_ref[...] = total * norm
 
 
 def collect_kernel(*refs):
@@ -219,11 +215,12 @@
 
 def backward_kernel(rows, cols, pos_ref, count_ref, turned_ref, *refs):
     parts = refs[:cols]
-    keep_ref, send_ref, hidden, acc = refs[cols:]
+    keep_ref, bias_ref, send_ref, hidden, acc, stage = refs[cols:]
+    owned = acc.shape[1]
     chips = rows // CORES
     row, col = lax.axis_index("row"), lax.axis_index("col")
     for k, ref in enumerate(parts):
-        hidden[k] = ref[...]
+        hidden[k] = ref[:owned]
     acc[...] = jnp.zeros_like(acc)
     positions = pos_ref[0]
 
@@ -237,21 +234,38 @@
 
     for_live(count_ref[0, 0], turned_ref.shape[0], add)
     keep_ref[...] = acc[:chips]
-    send_ref[...] = acc[chips:].astype(BF16)
-
-
-def merge_kernel(keep_ref, got_ref, own_ref, *send):
-    own_ref[...] = keep_ref[0] + got_ref[0].astype(F32)
+    for k in range(chips):
+        send_ref[k * owned : (k + 1) * owned] = acc[chips + k].astype(BF16)
+    bias = total_of(cols, col, [ref[owned:] for ref in parts], stage)
+    packed = pack_bias(jnp.sum(bias, axis=0, keepdims=True), EXTRA)
+    bias_ref[...] = packed
+    send_ref[chips * owned :] = packed
+
+
+def merge_kernel(keep_ref, bias_ref, got_ref, own_ref, pair_ref, *send):
+    chips, owned = keep_ref.shape[:2]
+    packed = pack_bias(add_bias(bias_ref[...]) + add_bias(got_ref[chips * owned :]), EXTRA)
+    pair_ref[...] = packed
+    own_ref[...] = keep_ref[0] + got_ref[:owned].astype(F32)
     for k, ref in enumerate(send, 1):
-        ref[...] = (keep_ref[k] + got_ref[k].astype(F32)).astype(BF16)
-
-
-def owned_sum_kernel(inv_ref, own_ref, *refs):
-    *parts, out_ref = refs
+        part = got_ref[k * owned : (k + 1) * owned].astype(F32)
+        ref[:owned] = (keep_ref[k] + part).astype(BF16)
+        ref[owned:] = packed
+
+
+def owned_sum_kernel(norm, offsets, inv_ref, own_ref, pair_ref, *refs):
+    *parts, out_ref, grad_b_ref, stage = refs
+    owned = own_ref.shape[0]
+    chips = len(parts) + 1
     total = own_ref[...]
-    for ref in parts:
-        total = total + ref[...].astype(F32)
+    biases = {0: pair_ref[...]}
+    for k, ref in zip(offsets, parts):
+        total = total + ref[:owned].astype(F32)
+        biases[k] = ref[owned:]
     out_ref[...] = (total * inv_ref[...]).astype(BF16)
+    chip = lax.axis_index("row") // CORES
+    bias = total_of(chips, chip, [biases[k] for k in range(chips)], stage)
+    grad_b_ref[...] = jnp.sum(bias, axis=0, keepdims=True) * norm
 
 
 def finish_kernel(out_ref, x_ref, mine_ref, theirs_ref, bias_ref, *refs):
@@ -293,7 +307,9 @@
     slots = block_pos.shape[2]
     half = width // CORES
     piece = (owned, width)
-    grads_shape = (half + EXTRA, width)
+    grads_shape = (half, width)
+    bias_shape = (EXTRA, width)
+    norm = float((owned * rows * cols) ** -0.5)
     degree = degree.reshape(1, owned)
     bias_vector = bias_vector.reshape(1, width)
 
@@ -325,15 +341,14 @@
     order = list(range(2, cols)) + [1]
     parts = [to_col(send[k - 1], cols, k) for k in order]
 
-    out_piece, hidden, keep, bias_keep, half_send = call(
+    out_piece, hidden, keep, half_send = call(
         functools.partial(pointwise_kernel, cols),
         [VMEM] * (4 + cols),
-        [(piece, BF16), (piece, BF16), ((half, width), F32), ((1, width), F32), (grads_shape, BF16)],
+        [(piece, BF16), ((owned + EXTRA, width), BF16), (grads_shape, F32), (grads_shape, BF16)],
     )(weight, bias_vector, cotangent, inv, own, *parts)
-
     hidden_parts = {k: to_col(hidden, cols, k) for k in order}
-    grads = call(pair_sum_kernel, [VMEM] * 3, [(grads_shape, BF16)])(
-        keep, bias_keep, to_core(half_send, rows)
+    grads = call(pair_sum_kernel, [VMEM] * 2, [(grads_shape, BF16)])(
+        keep, to_core(half_send, rows)
     )
     across = range(chips - 1, 0, -1)
     grad_parts = {k: to_chip(grads, rows, k) for k in across}
@@ -344,31 +359,40 @@
         [pltpu.VMEM((chips,) + grads_shape, BF16)],
     )(grads, *(grad_parts[k] for k in range(1, chips)))
 
-    col_keep, col_send = call(
+    col_keep, bias, col_send = call(
         functools.partial(backward_kernel, rows, cols),
         [VMEM, SMEM, VMEM] + [VMEM] * cols,
-        [((chips,) + piece, F32), ((chips,) + piece, BF16)],
-        [pltpu.VMEM((cols,) + piece, BF16), pltpu.VMEM((rows,) + piece, F32)],
+        [((chips,) + piece, F32), (bias_shape, BF16), ((chips * owned + EXTRA, width), BF16)],
+        [
+            pltpu.VMEM((cols,) + piece, BF16),
+            pltpu.VMEM((rows,) + piece, F32),
+            pltpu.VMEM((cols,) + bias_shape, BF16),
+        ],
         flops=LONG,
     )(block_pos, block_count, turned, hidden, *(hidden_parts[k] for k in range(1, cols)))
     col_send, grads = lax.optimization_barrier((col_send, grads))
     grad_parts = {k: to_col(grads, cols, k) for k in order}
-    own_x, *send_x = call(
-        merge_kernel, [VMEM] * 2, [(piece, F32)] + [(piece, BF16)] * (chips - 1)
-    )(col_keep, to_core(col_send, rows))
+    own_x, bias, *send_x = call(
+        merge_kernel,
+        [VMEM] * 3,
+        [(piece, F32), (bias_shape, BF16)] + [((owned + EXTRA, width), BF16)] * (chips - 1),
+    )(col_keep, bias, to_core(col_send, rows))
     parts_x = [to_chip(send_x[k - 1], rows, k) for k in across]
 
-    norm = float((owned * rows * cols) ** -0.5)
-    mine, bias_sum = call(
+    mine = call(
         functools.partial(col_sum_kernel, norm),
         [VMEM] * cols,
-        [((half, width), F32), ((1, width), F32)],
+        [(grads_shape, F32)],
         [pltpu.VMEM((cols,) + grads_shape, BF16)],
     )(grads, *(grad_parts[k] for k in range(1, cols)))
     theirs = to_core(mine, rows)
-    x_piece = call(owned_sum_kernel, [VMEM] * (1 + chips), [(piece, BF16)], flops=LONG)(
-        inv, own_x, *parts_x
-    )
+    x_piece, bias_sum = call(
+        functools.partial(owned_sum_kernel, norm, list(across)),
+        [VMEM] * (2 + chips),
+        [(piece, BF16), ((1, width), F32)],
+        [pltpu.VMEM((chips,) + bias_shape, BF16)],
+        flops=SHORT,
+    )(inv, own_x, bias, *parts_x)
     output, grad_x, grad_w, grad_b = call(
         finish_kernel,
         [VMEM] * 5,

time: 47 us -> 47.4 us (level)
    ppermute x9, waiting for transfers between devices: 9.4 us -> 7.04 us  [to_col(): lax.ppermute(x, 'col', [(i, target(cols, i, k)) for i in range(cols)])]
    ppermute x9, waiting for transfers between devices: 4.56 us -> 6.23 us  [to_chip(): return lax.ppermute(x, 'row', pairs)]
    ppermute x4, waiting for transfers between devices: 1.88 us -> 2.78 us  [to_core(): return lax.ppermute(x, 'row', [(i, i ^ 1) for i in range(rows)])]
where the time goes in v15:
time: 47.4 us; the launch traced here: 47.2 us
  starting transfers between devices  25.1 us (53%)
  waiting for transfers between devices  16.1 us (34%)
  Pallas kernels  3.96 us (8%)
  between operations  1.44 us (3%)
  local copies, waits for them, and re-layouts  0.68 us (1%)
    ppermute x9, starting transfers between devices, to_col(): lax.ppermute(x, 'col', [(i, target(cols, i, k)) for i in range(cols)])  13.1 us
    ppermute x9, starting transfers between devices, to_chip(): return lax.ppermute(x, 'row', pairs)  11.7 us
    ppermute x9, waiting for transfers between devices, to_col(): lax.ppermute(x, 'col', [(i, target(cols, i, k)) for i in range(cols)])  7.04 us
    ppermute x9, waiting for transfers between devices, to_chip(): return lax.ppermute(x, 'row', pairs)  6.23 us
    ppermute x4, waiting for transfers between devices, to_core(): return lax.ppermute(x, 'row', [(i, i ^ 1) for i in range(rows)])  2.78 us
  transfers between devices with their start and end apart: 22, of which 15 were waited for; matrix products, arithmetic and copies ran while one was open for 0% of the time, Pallas kernels for 3%

profile of v15, /device:TPU:0, one launch (start us, length us, event | category | flops | bytes accessed | tf_op | source)
XLA Modules:
  0.0 47.2 jit_solution(4120481615922034637)
XLA Ops:
  0.6 0.9 %shard_map.112 = (bf16[128,256]{1,0:T(8,128)(2,1)S(1)}, f32[128,256]{1,0:T(8,128)S(1)}) custom-call(bf16[128,256]{1,0:T(8,128)(2,1)} %features_hbm.1, s32[1,128]{1,0:T(1,128)} %bitcast.4), custom_call_target="tpu_custom_call" | custom-call | flops 1000000 | bytes 1000000 | tf_op jit(solution)/shard_map/pallas_call | solution.py:319
  1.5 4.0 %collective-permute-start.2 = (bf16[128,256]{1,0:T(8,128)(2,1)S(1)}, bf16[128,256]{1,0:T(8,128)(2,1)S(1)}, u32[]{:S(2)}, u32[]{:S(2)}) collective-permute-start(bf16[128,256]{1,0:T(8,128)(2,1)S(1)} %get-tuple-element.40.refs_0_), channel_id=1, source_target_pairs={{0,24},{4,28},{8,16},{12,20},{16,8},{20,12},{24,0},{28,4},{1,25},{... | collective-permute-start | bytes 196616 | tf_op jit(solution)/shard_map/ppermute | solution.py:51
  5.5 0.5 %collective-permute-start.1 = (bf16[128,256]{1,0:T(8,128)(2,1)S(1)}, bf16[128,256]{1,0:T(8,128)(2,1)S(1)}, u32[]{:S(2)}, u32[]{:S(2)}) collective-permute-start(bf16[128,256]{1,0:T(8,128)(2,1)S(1)} %get-tuple-element.40.refs_0_), channel_id=1, source_target_pairs={{0,16},{4,20},{8,24},{12,28},{16,0},{20,4},{24,8},{28,12},{1,17},{... | collective-permute-start | bytes 196616 | tf_op jit(solution)/shard_map/ppermute | solution.py:51
  6.0 0.1 collective-permute-start
  6.8 0.0 copy-start.4
  6.8 0.7 %copy-done.4 = f32[256]{0:T(256)S(1)} copy-done((f32[256]{0:T(256)S(1)}, f32[256]{0:T(256)}, u32[]{:S(2)}) %copy-start.4) | copy-done | bytes 1048
  7.5 0.5 %shard_map.111 = (bf16[16,128,128]{2,1,0:T(8,128)(2,1)S(1)}, bf16[16,128,128]{2,1,0:T(8,128)(2,1)S(1)}, f32[1,256]{1,0:T(1,128)S(1)}) custom-call(s32[1,1]{1,0:T(1,128)S(6)} %copy.12.count_ref, s32[1,1,16,512]{3,2,1,0:T(8,128)S(1)} %copy-done.3, f32[1,256]{1,0:T(1,128)S(1)} %bitcast.3), custom_call_target="tpu_custom_call" | custom-call | flops 4000000000 | bytes 1000000 | tf_op jit(solution)/shard_map/pallas_call | solution.py:326
  8.0 1.7 %collective-permute-done.1.refs_2_ = bf16[128,256]{1,0:T(8,128)(2,1)S(1)} collective-permute-done((bf16[128,256]{1,0:T(8,128)(2,1)S(1)}, bf16[128,256]{1,0:T(8,128)(2,1)S(1)}, u32[]{:S(2)}, u32[]{:S(2)}) %collective-permute-start.1) | collective-permute-done | bytes 65568 | tf_op jit(solution)/shard_map/ppermute | solution.py:51
  9.8 0.5 %collective-permute-done.refs_1_ = bf16[128,256]{1,0:T(8,128)(2,1)S(1)} collective-permute-done((bf16[128,256]{1,0:T(8,128)(2,1)S(1)}, bf16[128,256]{1,0:T(8,128)(2,1)S(1)}, u32[]{:S(2)}, u32[]{:S(2)}) %collective-permute-start) | collective-permute-done | bytes 65568 | tf_op jit(solution)/shard_map/ppermute | solution.py:51
  10.3 0.0 copy-start
  10.3 0.0 copy-start.1
  10.3 0.1 collective-permute-start.3
  10.4 1.5 %collective-permute-done.3.next_ref = bf16[4,128,256]{2,1,0:T(8,128)(2,1)S(1)} collective-permute-done((bf16[4,128,256]{2,1,0:T(8,128)(2,1)S(1)}, bf16[4,128,256]{2,1,0:T(8,128)(2,1)S(1)}, u32[]{:S(2)}, u32[]{:S(2)}) %collective-permute-start.3) | collective-permute-done | bytes 262176 | tf_op jit(solution)/shard_map/ppermute | solution.py:41
  11.9 0.5 %shard_map.114 = (f32[128,256]{1,0:T(8,128)S(1)}, bf16[128,256]{1,0:T(8,128)(2,1)S(1)}, bf16[128,256]{1,0:T(8,128)(2,1)S(1)}, bf16[128,256]{1,0:T(8,128)(2,1)S(1)}) custom-call(s32[1,1,16]{2,1,0:T(1,128)S(1)} %copy-done.2, s32[1,1]{1,0:T(1,128)S(6)} %copy.12.count_ref, bf16[16,128,128]{2,1,0:T(8,128)(2,1)S(1)} %get-tuple-element.41.blocks_ref, ...), custom_call_target="tpu_custom_call" | custom-call | flops 1000000 | bytes 1000000 | tf_op jit(solution)/shard_map/pallas_call | solution.py:335
  12.4 2.7 %collective-permute-start.4 = (bf16[128,256]{1,0:T(8,128)(2,1)S(1)}, bf16[128,256]{1,0:T(8,128)(2,1)S(1)}, u32[]{:S(2)}, u32[]{:S(2)}) collective-permute-start(bf16[128,256]{1,0:T(8,128)(2,1)S(1)} %get-tuple-element.46), channel_id=1, source_target_pairs={{0,2},{1,3},{2,0},{3,1},{4,6},{5,7},{6,4},{7,5},{8,10},{9,11},{10,... | collective-permute-start | bytes 196616 | tf_op jit(solution)/shard_map/ppermute | solution.py:55
  15.1 1.3 %collective-permute-start.5 = (bf16[128,256]{1,0:T(8,128)(2,1)S(1)}, bf16[128,256]{1,0:T(8,128)(2,1)S(1)}, u32[]{:S(2)}, u32[]{:S(2)}) collective-permute-start(bf16[128,256]{1,0:T(8,128)(2,1)S(1)} %get-tuple-element.47), channel_id=1, source_target_pairs={{0,3},{1,2},{2,1},{3,0},{4,7},{5,6},{6,5},{7,4},{8,11},{9,10},{10,... | collective-permute-start | bytes 196616 | tf_op jit(solution)/shard_map/ppermute | solution.py:55
  16.4 0.2 collective-permute-start.6
  16.7 3.5 %collective-permute-done.4.refs_1_ = bf16[128,256]{1,0:T(8,128)(2,1)S(1)} collective-permute-done((bf16[128,256]{1,0:T(8,128)(2,1)S(1)}, bf16[128,256]{1,0:T(8,128)(2,1)S(1)}, u32[]{:S(2)}, u32[]{:S(2)}) %collective-permute-start.4) | collective-permute-done | bytes 65568 | tf_op jit(solution)/shard_map/ppermute | solution.py:55
  20.2 1.3 %collective-permute-done.5.refs_2_ = bf16[128,256]{1,0:T(8,128)(2,1)S(1)} collective-permute-done((bf16[128,256]{1,0:T(8,128)(2,1)S(1)}, bf16[128,256]{1,0:T(8,128)(2,1)S(1)}, u32[]{:S(2)}, u32[]{:S(2)}) %collective-permute-start.5) | collective-permute-done | bytes 65568 | tf_op jit(solution)/shard_map/ppermute | solution.py:55
  21.5 0.3 collective-permute-done.6.refs_3_
  21.8 0.4 shard_map.115
  22.2 3.2 %collective-permute-start.9 = (bf16[144,256]{1,0:T(8,128)(2,1)S(1)}, bf16[144,256]{1,0:T(8,128)(2,1)S(1)}, u32[]{:S(2)}, u32[]{:S(2)}) collective-permute-start(bf16[144,256]{1,0:T(8,128)(2,1)S(1)} %get-tuple-element.51.refs_0_), channel_id=1, source_target_pairs={{0,3},{1,2},{2,1},{3,0},{4,7},{5,6},{6,5},{7,4},{8,11},{9,10},{10,... | collective-permute-start | bytes 221192 | tf_op jit(solution)/shard_map/ppermute | solution.py:55
  25.4 1.2 %collective-permute-start.7 = (bf16[144,256]{1,0:T(8,128)(2,1)S(1)}, bf16[144,256]{1,0:T(8,128)(2,1)S(1)}, u32[]{:S(2)}, u32[]{:S(2)}) collective-permute-start(bf16[144,256]{1,0:T(8,128)(2,1)S(1)} %get-tuple-element.51.refs_0_), channel_id=1, source_target_pairs={{0,1},{1,0},{2,3},{3,2},{4,5},{5,4},{6,7},{7,6},{8,9},{9,8},{10,11... | collective-permute-start | bytes 221192 | tf_op jit(solution)/shard_map/ppermute | solution.py:55
  26.7 1.3 %collective-permute-done.10.got_ref = bf16[128,256]{1,0:T(8,128)(2,1)S(1)} collective-permute-done((bf16[128,256]{1,0:T(8,128)(2,1)S(1)}, bf16[128,256]{1,0:T(8,128)(2,1)S(1)}, u32[]{:S(2)}, u32[]{:S(2)}) %collective-permute-start.10) | collective-permute-done | bytes 65568 | tf_op jit(solution)/shard_map/ppermute | solution.py:41
  27.9 1.6 %collective-permute-start.13 = (bf16[128,256]{1,0:T(8,128)(2,1)S(1)}, bf16[128,256]{1,0:T(8,128)(2,1)S(1)}, u32[]{:S(2)}, u32[]{:S(2)}) collective-permute-start(bf16[128,256]{1,0:T(8,128)(2,1)S(1)} %shard_map.117.refs_0_), channel_id=1, source_target_pairs={{0,24},{4,28},{8,16},{12,20},{16,8},{20,12},{24,0},{28,4},{1,25},{... | collective-permute-start | bytes 196616 | tf_op jit(solution)/shard_map/ppermute | solution.py:51
  29.5 0.4 collective-permute-start.12
  29.9 1.6 %collective-permute-start.11 = (bf16[128,256]{1,0:T(8,128)(2,1)S(1)}, bf16[128,256]{1,0:T(8,128)(2,1)S(1)}, u32[]{:S(2)}, u32[]{:S(2)}) collective-permute-start(bf16[128,256]{1,0:T(8,128)(2,1)S(1)} %shard_map.117.refs_0_), channel_id=1, source_target_pairs={{0,8},{4,12},{8,0},{12,4},{16,24},{20,28},{24,16},{28,20},{1,9},{5... | collective-permute-start | bytes 196616 | tf_op jit(solution)/shard_map/ppermute | solution.py:51
  31.5 0.5 %collective-permute-done.8.refs_2_ = bf16[144,256]{1,0:T(8,128)(2,1)S(1)} collective-permute-done((bf16[144,256]{1,0:T(8,128)(2,1)S(1)}, bf16[144,256]{1,0:T(8,128)(2,1)S(1)}, u32[]{:S(2)}, u32[]{:S(2)}) %collective-permute-start.8) | collective-permute-done | bytes 73760 | tf_op jit(solution)/shard_map/ppermute | solution.py:55
  32.0 0.6 %shard_map.116 = (f32[4,128,256]{2,1,0:T(8,128)S(1)}, bf16[16,256]{1,0:T(8,128)(2,1)S(1)}, bf16[528,256]{1,0:T(8,128)(2,1)S(1)}) custom-call(s32[1,1,16]{2,1,0:T(1,128)S(1)} %copy-done.2, s32[1,1]{1,0:T(1,128)S(6)} %copy.12.count_ref, bf16[16,128,128]{2,1,0:T(8,128)(2,1)S(1)} %get-tuple-element.50.turned_ref, ...), custom_call_target="tpu_custom_call" | custom-call | flops 4000000000 | bytes 1000000 | tf_op jit(solution)/shard_map/pallas_call | solution.py:362
  32.6 0.7 %collective-permute-done.13.refs_3_ = bf16[128,256]{1,0:T(8,128)(2,1)S(1)} collective-permute-done((bf16[128,256]{1,0:T(8,128)(2,1)S(1)}, bf16[128,256]{1,0:T(8,128)(2,1)S(1)}, u32[]{:S(2)}, u32[]{:S(2)}) %collective-permute-start.13) | collective-permute-done | bytes 65568 | tf_op jit(solution)/shard_map/ppermute | solution.py:51
  33.2 1.2 %collective-permute-done.12.refs_2_ = bf16[128,256]{1,0:T(8,128)(2,1)S(1)} collective-permute-done((bf16[128,256]{1,0:T(8,128)(2,1)S(1)}, bf16[128,256]{1,0:T(8,128)(2,1)S(1)}, u32[]{:S(2)}, u32[]{:S(2)}) %collective-permute-start.12) | collective-permute-done | bytes 65568 | tf_op jit(solution)/shard_map/ppermute | solution.py:51
  34.5 0.2 collective-permute-done.11.refs_1_
  34.7 0.1 shard_map.118.refs_0_
  34.8 0.1 collective-permute-start.14
  34.9 3.0 %collective-permute-start.20 = (bf16[128,256]{1,0:T(8,128)(2,1)S(1)}, bf16[128,256]{1,0:T(8,128)(2,1)S(1)}, u32[]{:S(2)}, u32[]{:S(2)}) collective-permute-start(bf16[128,256]{1,0:T(8,128)(2,1)S(1)} %shard_map.118.refs_0_), channel_id=1, source_target_pairs={{0,3},{1,2},{2,1},{3,0},{4,7},{5,6},{6,5},{7,4},{8,11},{9,10},{10,... | collective-permute-start | bytes 196616 | tf_op jit(solution)/shard_map/ppermute | solution.py:55
  37.9 1.4 %collective-permute-start.18 = (bf16[128,256]{1,0:T(8,128)(2,1)S(1)}, bf16[128,256]{1,0:T(8,128)(2,1)S(1)}, u32[]{:S(2)}, u32[]{:S(2)}) collective-permute-start(bf16[128,256]{1,0:T(8,128)(2,1)S(1)} %shard_map.118.refs_0_), channel_id=1, source_target_pairs={{0,1},{1,0},{2,3},{3,2},{4,5},{5,4},{6,7},{7,6},{8,9},{9,8},{10,11... | collective-permute-start | bytes 196616 | tf_op jit(solution)/shard_map/ppermute | solution.py:55
  39.3 0.1 shard_map.119
  39.4 2.3 %collective-permute-start.15 = (bf16[144,256]{1,0:T(8,128)(2,1)S(1)}, bf16[144,256]{1,0:T(8,128)(2,1)S(1)}, u32[]{:S(2)}, u32[]{:S(2)}) collective-permute-start(bf16[144,256]{1,0:T(8,128)(2,1)S(1)} %get-tuple-element.60), channel_id=1, source_target_pairs={{0,24},{4,28},{8,16},{12,20},{16,8},{20,12},{24,0},{28,4},{1,25},{... | collective-permute-start | bytes 221192 | tf_op jit(solution)/shard_map/ppermute | solution.py:51
  41.7 0.3 collective-permute-start.16
  42.0 1.0 %collective-permute-start.17 = (bf16[144,256]{1,0:T(8,128)(2,1)S(1)}, bf16[144,256]{1,0:T(8,128)(2,1)S(1)}, u32[]{:S(2)}, u32[]{:S(2)}) collective-permute-start(bf16[144,256]{1,0:T(8,128)(2,1)S(1)} %get-tuple-element.62), channel_id=1, source_target_pairs={{0,8},{4,12},{8,0},{12,4},{16,24},{20,28},{24,16},{28,20},{1,9},{5... | collective-permute-start | bytes 221192 | tf_op jit(solution)/shard_map/ppermute | solution.py:51
  42.9 1.4 %collective-permute-done.19.refs_2_ = bf16[128,256]{1,0:T(8,128)(2,1)S(1)} collective-permute-done((bf16[128,256]{1,0:T(8,128)(2,1)S(1)}, bf16[128,256]{1,0:T(8,128)(2,1)S(1)}, u32[]{:S(2)}, u32[]{:S(2)}) %collective-permute-start.19) | collective-permute-done | bytes 65568 | tf_op jit(solution)/shard_map/ppermute | solution.py:55
  44.3 0.1 shard_map.121.mine_ref
  44.4 0.1 collective-permute-start.21
  44.5 0.3 collective-permute-done.15.refs_0_
  44.8 1.2 %collective-permute-done.16.refs_1_ = bf16[144,256]{1,0:T(8,128)(2,1)S(1)} collective-permute-done((bf16[144,256]{1,0:T(8,128)(2,1)S(1)}, bf16[144,256]{1,0:T(8,128)(2,1)S(1)}, u32[]{:S(2)}, u32[]{:S(2)}) %collective-permute-start.16) | collective-permute-done | bytes 73760 | tf_op jit(solution)/shard_map/ppermute | solution.py:51
  46.0 0.3 collective-permute-done.17.refs_2_
  46.3 0.1 shard_map.120
  46.4 0.8 %shard_map.122 = (bf16[128,256]{1,0:T(8,128)(2,1)}, bf16[128,256]{1,0:T(8,128)(2,1)}, f32[256,256]{1,0:T(8,128)}, f32[1,256]{1,0:T(1,128)}) custom-call(bf16[128,256]{1,0:T(8,128)(2,1)S(1)} %get-tuple-element.49.out_ref, bf16[128,256]{1,0:T(8,128)(2,1)S(1)} %get-tuple-element.63.x_ref, f32[128,256]{1,0:T(8,128)S(1)} %shard_map.121.mine_ref, ...), custom_call_target="tpu_custom_call" | custom-call | flops 1000000 | bytes 1000000 | tf_op jit(solution)/shard_map/pallas_call | solution.py:396
  (18 shorter events, 0.1 us)
Async XLA Ops:
  0.6 6.2 %copy-start.3 = (s32[1,1,16,512]{3,2,1,0:T(8,128)S(1)}, s32[1,1,16,512]{3,2,1,0:T(8,128)}, u32[]{:S(2)}) copy-start(s32[1,1,16,512]{3,2,1,0:T(8,128)} %edge_ref.1) | copy-start | bytes 98308
  1.5 6.5 %collective-permute-start.2 = (bf16[128,256]{1,0:T(8,128)(2,1)S(1)}, bf16[128,256]{1,0:T(8,128)(2,1)S(1)}, u32[]{:S(2)}, u32[]{:S(2)}) collective-permute-start(bf16[128,256]{1,0:T(8,128)(2,1)S(1)} %get-tuple-element.40.refs_0_), channel_id=1, source_target_pairs={{0,24},{4,28},{8,16},{12,20},{16,8},{20,12},{24,0},{28,4},{1,25},{... | collective-permute-start | bytes 196616 | tf_op jit(solution)/shard_map/ppermute | solution.py:51
  5.5 4.3 %collective-permute-start.1 = (bf16[128,256]{1,0:T(8,128)(2,1)S(1)}, bf16[128,256]{1,0:T(8,128)(2,1)S(1)}, u32[]{:S(2)}, u32[]{:S(2)}) collective-permute-start(bf16[128,256]{1,0:T(8,128)(2,1)S(1)} %get-tuple-element.40.refs_0_), channel_id=1, source_target_pairs={{0,16},{4,20},{8,24},{12,28},{16,0},{20,4},{24,8},{28,12},{1,17},{... | collective-permute-start | bytes 196616 | tf_op jit(solution)/shard_map/ppermute | solution.py:51
  6.0 4.3 %collective-permute-start = (bf16[128,256]{1,0:T(8,128)(2,1)S(1)}, bf16[128,256]{1,0:T(8,128)(2,1)S(1)}, u32[]{:S(2)}, u32[]{:S(2)}) collective-permute-start(bf16[128,256]{1,0:T(8,128)(2,1)S(1)} %get-tuple-element.40.refs_0_), channel_id=1, source_target_pairs={{0,8},{4,12},{8,0},{12,4},{16,24},{20,28},{24,16},{28,20},{1,9},{5... | collective-permute-start | bytes 196616 | tf_op jit(solution)/shard_map/ppermute | solution.py:51
  6.8 0.7 %copy-start.4 = (f32[256]{0:T(256)S(1)}, f32[256]{0:T(256)}, u32[]{:S(2)}) copy-start(f32[256]{0:T(256)} %param.11) | copy-start | bytes 3076
  10.3 1.7 %copy-start.2 = (s32[1,1,16]{2,1,0:T(1,128)S(1)}, s32[1,1,16]{2,1,0:T(1,128)}, u32[]{:S(2)}) copy-start(s32[1,1,16]{2,1,0:T(1,128)} %pos_ref.3) | copy-start | bytes 196
  10.3 11.5 %copy-start = (bf16[256,256]{1,0:T(8,128)(2,1)S(1)}, bf16[256,256]{1,0:T(8,128)(2,1)}, u32[]{:S(2)}) copy-start(bf16[256,256]{1,0:T(8,128)(2,1)} %weight_ref.1) | copy-start | bytes 393220
  10.3 11.5 %copy-start.1 = (bf16[128,256]{1,0:T(8,128)(2,1)S(1)}, bf16[128,256]{1,0:T(8,128)(2,1)}, u32[]{:S(2)}) copy-start(bf16[128,256]{1,0:T(8,128)(2,1)} %cot_ref.1) | copy-start | bytes 196612
  10.3 1.6 %collective-permute-start.3 = (bf16[4,128,256]{2,1,0:T(8,128)(2,1)S(1)}, bf16[4,128,256]{2,1,0:T(8,128)(2,1)S(1)}, u32[]{:S(2)}, u32[]{:S(2)}) collective-permute-start(bf16[4,128,256]{2,1,0:T(8,128)(2,1)S(1)} %shard_map.113.near_ref), channel_id=1, source_target_pairs={{0,4},{4,0},{8,12},{12,8},{16,20},{20,16},{24,28},{28,24},{1,5},{5... | collective-permute-start | bytes 786440 | tf_op jit(solution)/shard_map/ppermute | solution.py:41
  12.4 7.8 %collective-permute-start.4 = (bf16[128,256]{1,0:T(8,128)(2,1)S(1)}, bf16[128,256]{1,0:T(8,128)(2,1)S(1)}, u32[]{:S(2)}, u32[]{:S(2)}) collective-permute-start(bf16[128,256]{1,0:T(8,128)(2,1)S(1)} %get-tuple-element.46), channel_id=1, source_target_pairs={{0,2},{1,3},{2,0},{3,1},{4,6},{5,7},{6,4},{7,5},{8,10},{9,11},{10,... | collective-permute-start | bytes 196616 | tf_op jit(solution)/shard_map/ppermute | solution.py:55
  15.1 6.4 %collective-permute-start.5 = (bf16[128,256]{1,0:T(8,128)(2,1)S(1)}, bf16[128,256]{1,0:T(8,128)(2,1)S(1)}, u32[]{:S(2)}, u32[]{:S(2)}) collective-permute-start(bf16[128,256]{1,0:T(8,128)(2,1)S(1)} %get-tuple-element.47), channel_id=1, source_target_pairs={{0,3},{1,2},{2,1},{3,0},{4,7},{5,6},{6,5},{7,4},{8,11},{9,10},{10,... | collective-permute-start | bytes 196616 | tf_op jit(solution)/shard_map/ppermute | solution.py:55
  16.4 5.4 %collective-permute-start.6 = (bf16[128,256]{1,0:T(8,128)(2,1)S(1)}, bf16[128,256]{1,0:T(8,128)(2,1)S(1)}, u32[]{:S(2)}, u32[]{:S(2)}) collective-permute-start(bf16[128,256]{1,0:T(8,128)(2,1)S(1)} %get-tuple-element.48), channel_id=1, source_target_pairs={{0,1},{1,0},{2,3},{3,2},{4,5},{5,4},{6,7},{7,6},{8,9},{9,8},{10,11... | collective-permute-start | bytes 196616 | tf_op jit(solution)/shard_map/ppermute | solution.py:55
  22.2 7.7 %collective-permute-start.9 = (bf16[144,256]{1,0:T(8,128)(2,1)S(1)}, bf16[144,256]{1,0:T(8,128)(2,1)S(1)}, u32[]{:S(2)}, u32[]{:S(2)}) collective-permute-start(bf16[144,256]{1,0:T(8,128)(2,1)S(1)} %get-tuple-element.51.refs_0_), channel_id=1, source_target_pairs={{0,3},{1,2},{2,1},{3,0},{4,7},{5,6},{6,5},{7,4},{8,11},{9,10},{10,... | collective-permute-start | bytes 221192 | tf_op jit(solution)/shard_map/ppermute | solution.py:55
  25.4 6.6 %collective-permute-start.8 = (bf16[144,256]{1,0:T(8,128)(2,1)S(1)}, bf16[144,256]{1,0:T(8,128)(2,1)S(1)}, u32[]{:S(2)}, u32[]{:S(2)}) collective-permute-start(bf16[144,256]{1,0:T(8,128)(2,1)S(1)} %get-tuple-element.51.refs_0_), channel_id=1, source_target_pairs={{0,2},{1,3},{2,0},{3,1},{4,6},{5,7},{6,4},{7,5},{8,10},{9,11},{10,... | collective-permute-start | bytes 221192 | tf_op jit(solution)/shard_map/ppermute | solution.py:55
  25.4 6.6 %collective-permute-start.7 = (bf16[144,256]{1,0:T(8,128)(2,1)S(1)}, bf16[144,256]{1,0:T(8,128)(2,1)S(1)}, u32[]{:S(2)}, u32[]{:S(2)}) collective-permute-start(bf16[144,256]{1,0:T(8,128)(2,1)S(1)} %get-tuple-element.51.refs_0_), channel_id=1, source_target_pairs={{0,1},{1,0},{2,3},{3,2},{4,5},{5,4},{6,7},{7,6},{8,9},{9,8},{10,11... | collective-permute-start | bytes 221192 | tf_op jit(solution)/shard_map/ppermute | solution.py:55
  26.7 1.3 %collective-permute-start.10 = (bf16[128,256]{1,0:T(8,128)(2,1)S(1)}, bf16[128,256]{1,0:T(8,128)(2,1)S(1)}, u32[]{:S(2)}, u32[]{:S(2)}) collective-permute-start(bf16[128,256]{1,0:T(8,128)(2,1)S(1)} %get-tuple-element.56), channel_id=1, source_target_pairs={{0,4},{4,0},{8,12},{12,8},{16,20},{20,16},{24,28},{28,24},{1,5},{5... | collective-permute-start | bytes 196616 | tf_op jit(solution)/shard_map/ppermute | solution.py:41
  27.9 5.3 %collective-permute-start.13 = (bf16[128,256]{1,0:T(8,128)(2,1)S(1)}, bf16[128,256]{1,0:T(8,128)(2,1)S(1)}, u32[]{:S(2)}, u32[]{:S(2)}) collective-permute-start(bf16[128,256]{1,0:T(8,128)(2,1)S(1)} %shard_map.117.refs_0_), channel_id=1, source_target_pairs={{0,24},{4,28},{8,16},{12,20},{16,8},{20,12},{24,0},{28,4},{1,25},{... | collective-permute-start | bytes 196616 | tf_op jit(solution)/shard_map/ppermute | solution.py:51
  29.5 5.0 %collective-permute-start.12 = (bf16[128,256]{1,0:T(8,128)(2,1)S(1)}, bf16[128,256]{1,0:T(8,128)(2,1)S(1)}, u32[]{:S(2)}, u32[]{:S(2)}) collective-permute-start(bf16[128,256]{1,0:T(8,128)(2,1)S(1)} %shard_map.117.refs_0_), channel_id=1, source_target_pairs={{0,16},{4,20},{8,24},{12,28},{16,0},{20,4},{24,8},{28,12},{1,17},{... | collective-permute-start | bytes 196616 | tf_op jit(solution)/shard_map/ppermute | solution.py:51
  29.9 4.8 %collective-permute-start.11 = (bf16[128,256]{1,0:T(8,128)(2,1)S(1)}, bf16[128,256]{1,0:T(8,128)(2,1)S(1)}, u32[]{:S(2)}, u32[]{:S(2)}) collective-permute-start(bf16[128,256]{1,0:T(8,128)(2,1)S(1)} %shard_map.117.refs_0_), channel_id=1, source_target_pairs={{0,8},{4,12},{8,0},{12,4},{16,24},{20,28},{24,16},{28,20},{1,9},{5... | collective-permute-start | bytes 196616 | tf_op jit(solution)/shard_map/ppermute | solution.py:51
  34.8 4.5 %collective-permute-start.14 = (bf16[528,256]{1,0:T(8,128)(2,1)S(1)}, bf16[528,256]{1,0:T(8,128)(2,1)S(1)}, u32[]{:S(2)}, u32[]{:S(2)}) collective-permute-start(bf16[528,256]{1,0:T(8,128)(2,1)S(1)} %get-tuple-element.57), channel_id=1, source_target_pairs={{0,4},{4,0},{8,12},{12,8},{16,20},{20,16},{24,28},{28,24},{1,5},{5... | collective-permute-start | bytes 811016 | tf_op jit(solution)/shard_map/ppermute | solution.py:41
  34.9 7.1 %collective-permute-start.20 = (bf16[128,256]{1,0:T(8,128)(2,1)S(1)}, bf16[128,256]{1,0:T(8,128)(2,1)S(1)}, u32[]{:S(2)}, u32[]{:S(2)}) collective-permute-start(bf16[128,256]{1,0:T(8,128)(2,1)S(1)} %shard_map.118.refs_0_), channel_id=1, source_target_pairs={{0,3},{1,2},{2,1},{3,0},{4,7},{5,6},{6,5},{7,4},{8,11},{9,10},{10,... | collective-permute-start | bytes 196616 | tf_op jit(solution)/shard_map/ppermute | solution.py:55
  37.9 6.4 %collective-permute-start.19 = (bf16[128,256]{1,0:T(8,128)(2,1)S(1)}, bf16[128,256]{1,0:T(8,128)(2,1)S(1)}, u32[]{:S(2)}, u32[]{:S(2)}) collective-permute-start(bf16[128,256]{1,0:T(8,128)(2,1)S(1)} %shard_map.118.refs_0_), channel_id=1, source_target_pairs={{0,2},{1,3},{2,0},{3,1},{4,6},{5,7},{6,4},{7,5},{8,10},{9,11},{10,... | collective-permute-start | bytes 196616 | tf_op jit(solution)/shard_map/ppermute | solution.py:55
  37.9 6.4 %collective-permute-start.18 = (bf16[128,256]{1,0:T(8,128)(2,1)S(1)}, bf16[128,256]{1,0:T(8,128)(2,1)S(1)}, u32[]{:S(2)}, u32[]{:S(2)}) collective-permute-start(bf16[128,256]{1,0:T(8,128)(2,1)S(1)} %shard_map.118.refs_0_), channel_id=1, source_target_pairs={{0,1},{1,0},{2,3},{3,2},{4,5},{5,4},{6,7},{7,6},{8,9},{9,8},{10,11... | collective-permute-start | bytes 196616 | tf_op jit(solution)/shard_map/ppermute | solution.py:55
  39.4 5.4 %collective-permute-start.15 = (bf16[144,256]{1,0:T(8,128)(2,1)S(1)}, bf16[144,256]{1,0:T(8,128)(2,1)S(1)}, u32[]{:S(2)}, u32[]{:S(2)}) collective-permute-start(bf16[144,256]{1,0:T(8,128)(2,1)S(1)} %get-tuple-element.60), channel_id=1, source_target_pairs={{0,24},{4,28},{8,16},{12,20},{16,8},{20,12},{24,0},{28,4},{1,25},{... | collective-permute-start | bytes 221192 | tf_op jit(solution)/shard_map/ppermute | solution.py:51
  41.7 4.4 %collective-permute-start.16 = (bf16[144,256]{1,0:T(8,128)(2,1)S(1)}, bf16[144,256]{1,0:T(8,128)(2,1)S(1)}, u32[]{:S(2)}, u32[]{:S(2)}) collective-permute-start(bf16[144,256]{1,0:T(8,128)(2,1)S(1)} %get-tuple-element.61), channel_id=1, source_target_pairs={{0,16},{4,20},{8,24},{12,28},{16,0},{20,4},{24,8},{28,12},{1,17},{... | collective-permute-start | bytes 221192 | tf_op jit(solution)/shard_map/ppermute | solution.py:51
  42.0 4.4 %collective-permute-start.17 = (bf16[144,256]{1,0:T(8,128)(2,1)S(1)}, bf16[144,256]{1,0:T(8,128)(2,1)S(1)}, u32[]{:S(2)}, u32[]{:S(2)}) collective-permute-start(bf16[144,256]{1,0:T(8,128)(2,1)S(1)} %get-tuple-element.62), channel_id=1, source_target_pairs={{0,8},{4,12},{8,0},{12,4},{16,24},{20,28},{24,16},{28,20},{1,9},{5... | collective-permute-start | bytes 221192 | tf_op jit(solution)/shard_map/ppermute | solution.py:51
  44.4 2.0 %collective-permute-start.21 = (f32[128,256]{1,0:T(8,128)S(1)}, f32[128,256]{1,0:T(8,128)S(1)}, u32[]{:S(2)}, u32[]{:S(2)}) collective-permute-start(f32[128,256]{1,0:T(8,128)S(1)} %shard_map.121.mine_ref), channel_id=1, source_target_pairs={{0,4},{4,0},{8,12},{12,8},{16,20},{20,16},{24,28},{28,24},{1,5},{5... | collective-permute-start | bytes 393224 | tf_op jit(solution)/shard_map/ppermute | solution.py:41

commit v16 on v15

--- a/solution.py
+++ b/solution.py
@@ -347,7 +347,7 @@
         [(piece, BF16), ((owned + EXTRA, width), BF16), (grads_shape, F32), (grads_shape, BF16)],
     )(weight, bias_vector, cotangent, inv, own, *parts)
     hidden_parts = {k: to_col(hidden, cols, k) for k in order}
-    grads = call(pair_sum_kernel, [VMEM] * 2, [(grads_shape, BF16)])(
+    grads = call(pair_sum_kernel, [VMEM] * 2, [(grads_shape, BF16)], flops=LONG)(
         keep, to_core(half_send, rows)
     )
     across = range(chips - 1, 0, -1)

time: 47.4 us -> 46.6 us (0.983)
  waiting for transfers between devices: 16.1 us -> 15.3 us
    ppermute x9, waiting for transfers between devices: 7.04 us -> 9.98 us  [to_col(): lax.ppermute(x, 'col', [(i, target(cols, i, k)) for i in range(cols)])]
    ppermute x9, waiting for transfers between devices: 6.23 us -> 3.47 us  [to_chip(): return lax.ppermute(x, 'row', pairs)]
    ppermute x4, waiting for transfers between devices: 2.78 us -> 1.87 us  [to_core(): return lax.ppermute(x, 'row', [(i, i ^ 1) for i in range(rows)])]
  transfers between devices with their start and end apart: 22 -> 22, of which waited for: 15 -> 13; matrix products, arithmetic and copies ran while one was open for 0% -> 0% of each run, Pallas kernels for 3% -> 3%
where the time goes in v16:
time: 46.6 us; the launch traced here: 46.3 us
  starting transfers between devices  24.9 us (53%)
  waiting for transfers between devices  15.3 us (33%)
  Pallas kernels  3.94 us (8%)
  between operations  1.46 us (3%)
  local copies, waits for them, and re-layouts  0.68 us (1%)
    ppermute x9, starting transfers between devices, to_col(): lax.ppermute(x, 'col', [(i, target(cols, i, k)) for i in range(cols)])  13.3 us
    ppermute x9, starting transfers between devices, to_chip(): return lax.ppermute(x, 'row', pairs)  11.3 us
    ppermute x9, waiting for transfers between devices, to_col(): lax.ppermute(x, 'col', [(i, target(cols, i, k)) for i in range(cols)])  9.98 us
    ppermute x9, waiting for transfers between devices, to_chip(): return lax.ppermute(x, 'row', pairs)  3.47 us
    ppermute x4, waiting for transfers between devices, to_core(): return lax.ppermute(x, 'row', [(i, i ^ 1) for i in range(rows)])  1.87 us
  transfers between devices with their start and end apart: 22, of which 13 were waited for; matrix products, arithmetic and copies ran while one was open for 0% of the time, Pallas kernels for 3%

profile of v16, /device:TPU:0, one launch (start us, length us, event | category | flops | bytes accessed | tf_op | source)
XLA Modules:
  0.0 46.3 jit_solution(5127772827892229369)
XLA Ops:
  0.6 0.9 %shard_map.112 = (bf16[128,256]{1,0:T(8,128)(2,1)S(1)}, f32[128,256]{1,0:T(8,128)S(1)}) custom-call(bf16[128,256]{1,0:T(8,128)(2,1)} %features_hbm.1, s32[1,128]{1,0:T(1,128)} %bitcast.4), custom_call_target="tpu_custom_call" | custom-call | flops 1000000 | bytes 1000000 | tf_op jit(solution)/shard_map/pallas_call | solution.py:319
  1.5 4.0 %collective-permute-start.2 = (bf16[128,256]{1,0:T(8,128)(2,1)S(1)}, bf16[128,256]{1,0:T(8,128)(2,1)S(1)}, u32[]{:S(2)}, u32[]{:S(2)}) collective-permute-start(bf16[128,256]{1,0:T(8,128)(2,1)S(1)} %get-tuple-element.40.refs_0_), channel_id=1, source_target_pairs={{0,24},{4,28},{8,16},{12,20},{16,8},{20,12},{24,0},{28,4},{1,25},{... | collective-permute-start | bytes 196616 | tf_op jit(solution)/shard_map/ppermute | solution.py:51
  5.5 0.5 %collective-permute-start.1 = (bf16[128,256]{1,0:T(8,128)(2,1)S(1)}, bf16[128,256]{1,0:T(8,128)(2,1)S(1)}, u32[]{:S(2)}, u32[]{:S(2)}) collective-permute-start(bf16[128,256]{1,0:T(8,128)(2,1)S(1)} %get-tuple-element.40.refs_0_), channel_id=1, source_target_pairs={{0,16},{4,20},{8,24},{12,28},{16,0},{20,4},{24,8},{28,12},{1,17},{... | collective-permute-start | bytes 196616 | tf_op jit(solution)/shard_map/ppermute | solution.py:51
  6.0 0.1 collective-permute-start
  6.8 0.0 copy-start.4
  6.8 0.7 %copy-done.4 = f32[256]{0:T(256)S(1)} copy-done((f32[256]{0:T(256)S(1)}, f32[256]{0:T(256)}, u32[]{:S(2)}) %copy-start.4) | copy-done | bytes 1048
  7.5 0.5 %shard_map.111 = (bf16[16,128,128]{2,1,0:T(8,128)(2,1)S(1)}, bf16[16,128,128]{2,1,0:T(8,128)(2,1)S(1)}, f32[1,256]{1,0:T(1,128)S(1)}) custom-call(s32[1,1]{1,0:T(1,128)S(6)} %copy.12.count_ref, s32[1,1,16,512]{3,2,1,0:T(8,128)S(1)} %copy-done.3, f32[1,256]{1,0:T(1,128)S(1)} %bitcast.3), custom_call_target="tpu_custom_call" | custom-call | flops 4000000000 | bytes 1000000 | tf_op jit(solution)/shard_map/pallas_call | solution.py:326
  8.0 1.7 %collective-permute-done.1.refs_2_ = bf16[128,256]{1,0:T(8,128)(2,1)S(1)} collective-permute-done((bf16[128,256]{1,0:T(8,128)(2,1)S(1)}, bf16[128,256]{1,0:T(8,128)(2,1)S(1)}, u32[]{:S(2)}, u32[]{:S(2)}) %collective-permute-start.1) | collective-permute-done | bytes 65568 | tf_op jit(solution)/shard_map/ppermute | solution.py:51
  9.8 0.5 %collective-permute-done.refs_1_ = bf16[128,256]{1,0:T(8,128)(2,1)S(1)} collective-permute-done((bf16[128,256]{1,0:T(8,128)(2,1)S(1)}, bf16[128,256]{1,0:T(8,128)(2,1)S(1)}, u32[]{:S(2)}, u32[]{:S(2)}) %collective-permute-start) | collective-permute-done | bytes 65568 | tf_op jit(solution)/shard_map/ppermute | solution.py:51
  10.3 0.0 copy-start
  10.3 0.0 copy-start.1
  10.3 0.1 collective-permute-start.3
  10.4 1.5 %collective-permute-done.3.next_ref = bf16[4,128,256]{2,1,0:T(8,128)(2,1)S(1)} collective-permute-done((bf16[4,128,256]{2,1,0:T(8,128)(2,1)S(1)}, bf16[4,128,256]{2,1,0:T(8,128)(2,1)S(1)}, u32[]{:S(2)}, u32[]{:S(2)}) %collective-permute-start.3) | collective-permute-done | bytes 262176 | tf_op jit(solution)/shard_map/ppermute | solution.py:41
  11.9 0.5 %shard_map.114 = (f32[128,256]{1,0:T(8,128)S(1)}, bf16[128,256]{1,0:T(8,128)(2,1)S(1)}, bf16[128,256]{1,0:T(8,128)(2,1)S(1)}, bf16[128,256]{1,0:T(8,128)(2,1)S(1)}) custom-call(s32[1,1,16]{2,1,0:T(1,128)S(1)} %copy-done.2, s32[1,1]{1,0:T(1,128)S(6)} %copy.12.count_ref, bf16[16,128,128]{2,1,0:T(8,128)(2,1)S(1)} %get-tuple-element.41.blocks_ref, ...), custom_call_target="tpu_custom_call" | custom-call | flops 1000000 | bytes 1000000 | tf_op jit(solution)/shard_map/pallas_call | solution.py:335
  12.4 2.7 %collective-permute-start.4 = (bf16[128,256]{1,0:T(8,128)(2,1)S(1)}, bf16[128,256]{1,0:T(8,128)(2,1)S(1)}, u32[]{:S(2)}, u32[]{:S(2)}) collective-permute-start(bf16[128,256]{1,0:T(8,128)(2,1)S(1)} %get-tuple-element.46), channel_id=1, source_target_pairs={{0,2},{1,3},{2,0},{3,1},{4,6},{5,7},{6,4},{7,5},{8,10},{9,11},{10,... | collective-permute-start | bytes 196616 | tf_op jit(solution)/shard_map/ppermute | solution.py:55
  15.1 1.3 %collective-permute-start.5 = (bf16[128,256]{1,0:T(8,128)(2,1)S(1)}, bf16[128,256]{1,0:T(8,128)(2,1)S(1)}, u32[]{:S(2)}, u32[]{:S(2)}) collective-permute-start(bf16[128,256]{1,0:T(8,128)(2,1)S(1)} %get-tuple-element.47), channel_id=1, source_target_pairs={{0,3},{1,2},{2,1},{3,0},{4,7},{5,6},{6,5},{7,4},{8,11},{9,10},{10,... | collective-permute-start | bytes 196616 | tf_op jit(solution)/shard_map/ppermute | solution.py:55
  16.4 0.2 collective-permute-start.6
  16.7 3.5 %collective-permute-done.4.refs_1_ = bf16[128,256]{1,0:T(8,128)(2,1)S(1)} collective-permute-done((bf16[128,256]{1,0:T(8,128)(2,1)S(1)}, bf16[128,256]{1,0:T(8,128)(2,1)S(1)}, u32[]{:S(2)}, u32[]{:S(2)}) %collective-permute-start.4) | collective-permute-done | bytes 65568 | tf_op jit(solution)/shard_map/ppermute | solution.py:55
  20.2 1.3 %collective-permute-done.5.refs_2_ = bf16[128,256]{1,0:T(8,128)(2,1)S(1)} collective-permute-done((bf16[128,256]{1,0:T(8,128)(2,1)S(1)}, bf16[128,256]{1,0:T(8,128)(2,1)S(1)}, u32[]{:S(2)}, u32[]{:S(2)}) %collective-permute-start.5) | collective-permute-done | bytes 65568 | tf_op jit(solution)/shard_map/ppermute | solution.py:55
  21.5 0.3 collective-permute-done.6.refs_3_
  21.8 0.4 shard_map.115
  22.2 0.1 collective-permute-start.10
  22.3 3.2 %collective-permute-start.9 = (bf16[144,256]{1,0:T(8,128)(2,1)S(1)}, bf16[144,256]{1,0:T(8,128)(2,1)S(1)}, u32[]{:S(2)}, u32[]{:S(2)}) collective-permute-start(bf16[144,256]{1,0:T(8,128)(2,1)S(1)} %get-tuple-element.51.refs_0_), channel_id=1, source_target_pairs={{0,3},{1,2},{2,1},{3,0},{4,7},{5,6},{6,5},{7,4},{8,11},{9,10},{10,... | collective-permute-start | bytes 221192 | tf_op jit(solution)/shard_map/ppermute | solution.py:55
  25.5 1.2 %collective-permute-start.7 = (bf16[144,256]{1,0:T(8,128)(2,1)S(1)}, bf16[144,256]{1,0:T(8,128)(2,1)S(1)}, u32[]{:S(2)}, u32[]{:S(2)}) collective-permute-start(bf16[144,256]{1,0:T(8,128)(2,1)S(1)} %get-tuple-element.51.refs_0_), channel_id=1, source_target_pairs={{0,1},{1,0},{2,3},{3,2},{4,5},{5,4},{6,7},{7,6},{8,9},{9,8},{10,11... | collective-permute-start | bytes 221192 | tf_op jit(solution)/shard_map/ppermute | solution.py:55
  26.8 1.8 %collective-permute-start.13 = (bf16[128,256]{1,0:T(8,128)(2,1)S(1)}, bf16[128,256]{1,0:T(8,128)(2,1)S(1)}, u32[]{:S(2)}, u32[]{:S(2)}) collective-permute-start(bf16[128,256]{1,0:T(8,128)(2,1)S(1)} %shard_map.117.refs_0_), channel_id=1, source_target_pairs={{0,24},{4,28},{8,16},{12,20},{16,8},{20,12},{24,0},{28,4},{1,25},{... | collective-permute-start | bytes 196616 | tf_op jit(solution)/shard_map/ppermute | solution.py:51
  28.6 0.2 collective-permute-start.12
  28.8 0.4 collective-permute-done.9.refs_3_
  29.1 1.2 %collective-permute-start.11 = (bf16[128,256]{1,0:T(8,128)(2,1)S(1)}, bf16[128,256]{1,0:T(8,128)(2,1)S(1)}, u32[]{:S(2)}, u32[]{:S(2)}) collective-permute-start(bf16[128,256]{1,0:T(8,128)(2,1)S(1)} %shard_map.117.refs_0_), channel_id=1, source_target_pairs={{0,8},{4,12},{8,0},{12,4},{16,24},{20,28},{24,16},{28,20},{1,9},{5... | collective-permute-start | bytes 196616 | tf_op jit(solution)/shard_map/ppermute | solution.py:51
  30.3 2.2 %collective-permute-done.8.refs_2_ = bf16[144,256]{1,0:T(8,128)(2,1)S(1)} collective-permute-done((bf16[144,256]{1,0:T(8,128)(2,1)S(1)}, bf16[144,256]{1,0:T(8,128)(2,1)S(1)}, u32[]{:S(2)}, u32[]{:S(2)}) %collective-permute-start.8) | collective-permute-done | bytes 73760 | tf_op jit(solution)/shard_map/ppermute | solution.py:55
  32.5 0.6 %shard_map.116 = (f32[4,128,256]{2,1,0:T(8,128)S(1)}, bf16[16,256]{1,0:T(8,128)(2,1)S(1)}, bf16[528,256]{1,0:T(8,128)(2,1)S(1)}) custom-call(s32[1,1,16]{2,1,0:T(1,128)S(1)} %copy-done.2, s32[1,1]{1,0:T(1,128)S(6)} %copy.12.count_ref, bf16[16,128,128]{2,1,0:T(8,128)(2,1)S(1)} %get-tuple-element.50.turned_ref, ...), custom_call_target="tpu_custom_call" | custom-call | flops 4000000000 | bytes 1000000 | tf_op jit(solution)/shard_map/pallas_call | solution.py:362
  33.1 0.3 collective-permute-done.11.refs_1_
  33.4 0.1 shard_map.118.refs_0_
  33.5 0.1 collective-permute-start.14
  33.6 3.4 %collective-permute-start.20 = (bf16[128,256]{1,0:T(8,128)(2,1)S(1)}, bf16[128,256]{1,0:T(8,128)(2,1)S(1)}, u32[]{:S(2)}, u32[]{:S(2)}) collective-permute-start(bf16[128,256]{1,0:T(8,128)(2,1)S(1)} %shard_map.118.refs_0_), channel_id=1, source_target_pairs={{0,3},{1,2},{2,1},{3,0},{4,7},{5,6},{6,5},{7,4},{8,11},{9,10},{10,... | collective-permute-start | bytes 196616 | tf_op jit(solution)/shard_map/ppermute | solution.py:55
  37.0 0.7 %collective-permute-start.19 = (bf16[128,256]{1,0:T(8,128)(2,1)S(1)}, bf16[128,256]{1,0:T(8,128)(2,1)S(1)}, u32[]{:S(2)}, u32[]{:S(2)}) collective-permute-start(bf16[128,256]{1,0:T(8,128)(2,1)S(1)} %shard_map.118.refs_0_), channel_id=1, source_target_pairs={{0,2},{1,3},{2,0},{3,1},{4,6},{5,7},{6,4},{7,5},{8,10},{9,11},{10,... | collective-permute-start | bytes 196616 | tf_op jit(solution)/shard_map/ppermute | solution.py:55
  37.7 0.5 %collective-permute-start.18 = (bf16[128,256]{1,0:T(8,128)(2,1)S(1)}, bf16[128,256]{1,0:T(8,128)(2,1)S(1)}, u32[]{:S(2)}, u32[]{:S(2)}) collective-permute-start(bf16[128,256]{1,0:T(8,128)(2,1)S(1)} %shard_map.118.refs_0_), channel_id=1, source_target_pairs={{0,1},{1,0},{2,3},{3,2},{4,5},{5,4},{6,7},{7,6},{8,9},{9,8},{10,11... | collective-permute-start | bytes 196616 | tf_op jit(solution)/shard_map/ppermute | solution.py:55
  38.2 0.1 shard_map.119
  38.3 2.0 %collective-permute-start.15 = (bf16[144,256]{1,0:T(8,128)(2,1)S(1)}, bf16[144,256]{1,0:T(8,128)(2,1)S(1)}, u32[]{:S(2)}, u32[]{:S(2)}) collective-permute-start(bf16[144,256]{1,0:T(8,128)(2,1)S(1)} %get-tuple-element.60), channel_id=1, source_target_pairs={{0,24},{4,28},{8,16},{12,20},{16,8},{20,12},{24,0},{28,4},{1,25},{... | collective-permute-start | bytes 221192 | tf_op jit(solution)/shard_map/ppermute | solution.py:51
  40.3 0.5 %collective-permute-start.16 = (bf16[144,256]{1,0:T(8,128)(2,1)S(1)}, bf16[144,256]{1,0:T(8,128)(2,1)S(1)}, u32[]{:S(2)}, u32[]{:S(2)}) collective-permute-start(bf16[144,256]{1,0:T(8,128)(2,1)S(1)} %get-tuple-element.61), channel_id=1, source_target_pairs={{0,16},{4,20},{8,24},{12,28},{16,0},{20,4},{24,8},{28,12},{1,17},{... | collective-permute-start | bytes 221192 | tf_op jit(solution)/shard_map/ppermute | solution.py:51
  40.8 1.0 %collective-permute-start.17 = (bf16[144,256]{1,0:T(8,128)(2,1)S(1)}, bf16[144,256]{1,0:T(8,128)(2,1)S(1)}, u32[]{:S(2)}, u32[]{:S(2)}) collective-permute-start(bf16[144,256]{1,0:T(8,128)(2,1)S(1)} %get-tuple-element.62), channel_id=1, source_target_pairs={{0,8},{4,12},{8,0},{12,4},{16,24},{20,28},{24,16},{28,20},{1,9},{5... | collective-permute-start | bytes 221192 | tf_op jit(solution)/shard_map/ppermute | solution.py:51
  41.8 2.2 %collective-permute-done.19.refs_2_ = bf16[128,256]{1,0:T(8,128)(2,1)S(1)} collective-permute-done((bf16[128,256]{1,0:T(8,128)(2,1)S(1)}, bf16[128,256]{1,0:T(8,128)(2,1)S(1)}, u32[]{:S(2)}, u32[]{:S(2)}) %collective-permute-start.19) | collective-permute-done | bytes 65568 | tf_op jit(solution)/shard_map/ppermute | solution.py:55
  44.1 0.1 shard_map.121.mine_ref
  44.2 0.1 collective-permute-start.21
  44.2 0.6 %collective-permute-done.16.refs_1_ = bf16[144,256]{1,0:T(8,128)(2,1)S(1)} collective-permute-done((bf16[144,256]{1,0:T(8,128)(2,1)S(1)}, bf16[144,256]{1,0:T(8,128)(2,1)S(1)}, u32[]{:S(2)}, u32[]{:S(2)}) %collective-permute-start.16) | collective-permute-done | bytes 73760 | tf_op jit(solution)/shard_map/ppermute | solution.py:51
  44.9 0.3 collective-permute-done.17.refs_2_
  45.2 0.1 shard_map.120
  45.2 0.3 collective-permute-done.21.theirs_ref
  45.6 0.8 %shard_map.122 = (bf16[128,256]{1,0:T(8,128)(2,1)}, bf16[128,256]{1,0:T(8,128)(2,1)}, f32[256,256]{1,0:T(8,128)}, f32[1,256]{1,0:T(1,128)}) custom-call(bf16[128,256]{1,0:T(8,128)(2,1)S(1)} %get-tuple-element.49.out_ref, bf16[128,256]{1,0:T(8,128)(2,1)S(1)} %get-tuple-element.63.x_ref, f32[128,256]{1,0:T(8,128)S(1)} %shard_map.121.mine_ref, ...), custom_call_target="tpu_custom_call" | custom-call | flops 1000000 | bytes 1000000 | tf_op jit(solution)/shard_map/pallas_call | solution.py:396
  (18 shorter events, 0.1 us)
Async XLA Ops:
  0.6 6.2 %copy-start.3 = (s32[1,1,16,512]{3,2,1,0:T(8,128)S(1)}, s32[1,1,16,512]{3,2,1,0:T(8,128)}, u32[]{:S(2)}) copy-start(s32[1,1,16,512]{3,2,1,0:T(8,128)} %edge_ref.1) | copy-start | bytes 98308
  1.5 6.5 %collective-permute-start.2 = (bf16[128,256]{1,0:T(8,128)(2,1)S(1)}, bf16[128,256]{1,0:T(8,128)(2,1)S(1)}, u32[]{:S(2)}, u32[]{:S(2)}) collective-permute-start(bf16[128,256]{1,0:T(8,128)(2,1)S(1)} %get-tuple-element.40.refs_0_), channel_id=1, source_target_pairs={{0,24},{4,28},{8,16},{12,20},{16,8},{20,12},{24,0},{28,4},{1,25},{... | collective-permute-start | bytes 196616 | tf_op jit(solution)/shard_map/ppermute | solution.py:51
  5.5 4.3 %collective-permute-start.1 = (bf16[128,256]{1,0:T(8,128)(2,1)S(1)}, bf16[128,256]{1,0:T(8,128)(2,1)S(1)}, u32[]{:S(2)}, u32[]{:S(2)}) collective-permute-start(bf16[128,256]{1,0:T(8,128)(2,1)S(1)} %get-tuple-element.40.refs_0_), channel_id=1, source_target_pairs={{0,16},{4,20},{8,24},{12,28},{16,0},{20,4},{24,8},{28,12},{1,17},{... | collective-permute-start | bytes 196616 | tf_op jit(solution)/shard_map/ppermute | solution.py:51
  6.0 4.3 %collective-permute-start = (bf16[128,256]{1,0:T(8,128)(2,1)S(1)}, bf16[128,256]{1,0:T(8,128)(2,1)S(1)}, u32[]{:S(2)}, u32[]{:S(2)}) collective-permute-start(bf16[128,256]{1,0:T(8,128)(2,1)S(1)} %get-tuple-element.40.refs_0_), channel_id=1, source_target_pairs={{0,8},{4,12},{8,0},{12,4},{16,24},{20,28},{24,16},{28,20},{1,9},{5... | collective-permute-start | bytes 196616 | tf_op jit(solution)/shard_map/ppermute | solution.py:51
  6.8 0.7 %copy-start.4 = (f32[256]{0:T(256)S(1)}, f32[256]{0:T(256)}, u32[]{:S(2)}) copy-start(f32[256]{0:T(256)} %param.11) | copy-start | bytes 3076
  10.3 1.7 %copy-start.2 = (s32[1,1,16]{2,1,0:T(1,128)S(1)}, s32[1,1,16]{2,1,0:T(1,128)}, u32[]{:S(2)}) copy-start(s32[1,1,16]{2,1,0:T(1,128)} %pos_ref.3) | copy-start | bytes 196
  10.3 11.5 %copy-start = (bf16[256,256]{1,0:T(8,128)(2,1)S(1)}, bf16[256,256]{1,0:T(8,128)(2,1)}, u32[]{:S(2)}) copy-start(bf16[256,256]{1,0:T(8,128)(2,1)} %weight_ref.1) | copy-start | bytes 393220
  10.3 11.5 %copy-start.1 = (bf16[128,256]{1,0:T(8,128)(2,1)S(1)}, bf16[128,256]{1,0:T(8,128)(2,1)}, u32[]{:S(2)}) copy-start(bf16[128,256]{1,0:T(8,128)(2,1)} %cot_ref.1) | copy-start | bytes 196612
  10.3 1.6 %collective-permute-start.3 = (bf16[4,128,256]{2,1,0:T(8,128)(2,1)S(1)}, bf16[4,128,256]{2,1,0:T(8,128)(2,1)S(1)}, u32[]{:S(2)}, u32[]{:S(2)}) collective-permute-start(bf16[4,128,256]{2,1,0:T(8,128)(2,1)S(1)} %shard_map.113.near_ref), channel_id=1, source_target_pairs={{0,4},{4,0},{8,12},{12,8},{16,20},{20,16},{24,28},{28,24},{1,5},{5... | collective-permute-start | bytes 786440 | tf_op jit(solution)/shard_map/ppermute | solution.py:41
  12.4 7.8 %collective-permute-start.4 = (bf16[128,256]{1,0:T(8,128)(2,1)S(1)}, bf16[128,256]{1,0:T(8,128)(2,1)S(1)}, u32[]{:S(2)}, u32[]{:S(2)}) collective-permute-start(bf16[128,256]{1,0:T(8,128)(2,1)S(1)} %get-tuple-element.46), channel_id=1, source_target_pairs={{0,2},{1,3},{2,0},{3,1},{4,6},{5,7},{6,4},{7,5},{8,10},{9,11},{10,... | collective-permute-start | bytes 196616 | tf_op jit(solution)/shard_map/ppermute | solution.py:55
  15.1 6.4 %collective-permute-start.5 = (bf16[128,256]{1,0:T(8,128)(2,1)S(1)}, bf16[128,256]{1,0:T(8,128)(2,1)S(1)}, u32[]{:S(2)}, u32[]{:S(2)}) collective-permute-start(bf16[128,256]{1,0:T(8,128)(2,1)S(1)} %get-tuple-element.47), channel_id=1, source_target_pairs={{0,3},{1,2},{2,1},{3,0},{4,7},{5,6},{6,5},{7,4},{8,11},{9,10},{10,... | collective-permute-start | bytes 196616 | tf_op jit(solution)/shard_map/ppermute | solution.py:55
  16.4 5.4 %collective-permute-start.6 = (bf16[128,256]{1,0:T(8,128)(2,1)S(1)}, bf16[128,256]{1,0:T(8,128)(2,1)S(1)}, u32[]{:S(2)}, u32[]{:S(2)}) collective-permute-start(bf16[128,256]{1,0:T(8,128)(2,1)S(1)} %get-tuple-element.48), channel_id=1, source_target_pairs={{0,1},{1,0},{2,3},{3,2},{4,5},{5,4},{6,7},{7,6},{8,9},{9,8},{10,11... | collective-permute-start | bytes 196616 | tf_op jit(solution)/shard_map/ppermute | solution.py:55
  22.2 4.5 %collective-permute-start.10 = (bf16[128,256]{1,0:T(8,128)(2,1)S(1)}, bf16[128,256]{1,0:T(8,128)(2,1)S(1)}, u32[]{:S(2)}, u32[]{:S(2)}) collective-permute-start(bf16[128,256]{1,0:T(8,128)(2,1)S(1)} %get-tuple-element.56), channel_id=1, source_target_pairs={{0,4},{4,0},{8,12},{12,8},{16,20},{20,16},{24,28},{28,24},{1,5},{5... | collective-permute-start | bytes 196616 | tf_op jit(solution)/shard_map/ppermute | solution.py:41
  22.3 6.8 %collective-permute-start.9 = (bf16[144,256]{1,0:T(8,128)(2,1)S(1)}, bf16[144,256]{1,0:T(8,128)(2,1)S(1)}, u32[]{:S(2)}, u32[]{:S(2)}) collective-permute-start(bf16[144,256]{1,0:T(8,128)(2,1)S(1)} %get-tuple-element.51.refs_0_), channel_id=1, source_target_pairs={{0,3},{1,2},{2,1},{3,0},{4,7},{5,6},{6,5},{7,4},{8,11},{9,10},{10,... | collective-permute-start | bytes 221192 | tf_op jit(solution)/shard_map/ppermute | solution.py:55
  25.5 7.0 %collective-permute-start.8 = (bf16[144,256]{1,0:T(8,128)(2,1)S(1)}, bf16[144,256]{1,0:T(8,128)(2,1)S(1)}, u32[]{:S(2)}, u32[]{:S(2)}) collective-permute-start(bf16[144,256]{1,0:T(8,128)(2,1)S(1)} %get-tuple-element.51.refs_0_), channel_id=1, source_target_pairs={{0,2},{1,3},{2,0},{3,1},{4,6},{5,7},{6,4},{7,5},{8,10},{9,11},{10,... | collective-permute-start | bytes 221192 | tf_op jit(solution)/shard_map/ppermute | solution.py:55
  25.5 7.0 %collective-permute-start.7 = (bf16[144,256]{1,0:T(8,128)(2,1)S(1)}, bf16[144,256]{1,0:T(8,128)(2,1)S(1)}, u32[]{:S(2)}, u32[]{:S(2)}) collective-permute-start(bf16[144,256]{1,0:T(8,128)(2,1)S(1)} %get-tuple-element.51.refs_0_), channel_id=1, source_target_pairs={{0,1},{1,0},{2,3},{3,2},{4,5},{5,4},{6,7},{7,6},{8,9},{9,8},{10,11... | collective-permute-start | bytes 221192 | tf_op jit(solution)/shard_map/ppermute | solution.py:55
  26.8 6.3 %collective-permute-start.13 = (bf16[128,256]{1,0:T(8,128)(2,1)S(1)}, bf16[128,256]{1,0:T(8,128)(2,1)S(1)}, u32[]{:S(2)}, u32[]{:S(2)}) collective-permute-start(bf16[128,256]{1,0:T(8,128)(2,1)S(1)} %shard_map.117.refs_0_), channel_id=1, source_target_pairs={{0,24},{4,28},{8,16},{12,20},{16,8},{20,12},{24,0},{28,4},{1,25},{... | collective-permute-start | bytes 196616 | tf_op jit(solution)/shard_map/ppermute | solution.py:51
  28.6 4.5 %collective-permute-start.12 = (bf16[128,256]{1,0:T(8,128)(2,1)S(1)}, bf16[128,256]{1,0:T(8,128)(2,1)S(1)}, u32[]{:S(2)}, u32[]{:S(2)}) collective-permute-start(bf16[128,256]{1,0:T(8,128)(2,1)S(1)} %shard_map.117.refs_0_), channel_id=1, source_target_pairs={{0,16},{4,20},{8,24},{12,28},{16,0},{20,4},{24,8},{28,12},{1,17},{... | collective-permute-start | bytes 196616 | tf_op jit(solution)/shard_map/ppermute | solution.py:51
  29.1 4.3 %collective-permute-start.11 = (bf16[128,256]{1,0:T(8,128)(2,1)S(1)}, bf16[128,256]{1,0:T(8,128)(2,1)S(1)}, u32[]{:S(2)}, u32[]{:S(2)}) collective-permute-start(bf16[128,256]{1,0:T(8,128)(2,1)S(1)} %shard_map.117.refs_0_), channel_id=1, source_target_pairs={{0,8},{4,12},{8,0},{12,4},{16,24},{20,28},{24,16},{28,20},{1,9},{5... | collective-permute-start | bytes 196616 | tf_op jit(solution)/shard_map/ppermute | solution.py:51
  33.5 4.7 %collective-permute-start.14 = (bf16[528,256]{1,0:T(8,128)(2,1)S(1)}, bf16[528,256]{1,0:T(8,128)(2,1)S(1)}, u32[]{:S(2)}, u32[]{:S(2)}) collective-permute-start(bf16[528,256]{1,0:T(8,128)(2,1)S(1)} %get-tuple-element.57), channel_id=1, source_target_pairs={{0,4},{4,0},{8,12},{12,8},{16,20},{20,16},{24,28},{28,24},{1,5},{5... | collective-permute-start | bytes 811016 | tf_op jit(solution)/shard_map/ppermute | solution.py:41
  33.6 7.3 %collective-permute-start.20 = (bf16[128,256]{1,0:T(8,128)(2,1)S(1)}, bf16[128,256]{1,0:T(8,128)(2,1)S(1)}, u32[]{:S(2)}, u32[]{:S(2)}) collective-permute-start(bf16[128,256]{1,0:T(8,128)(2,1)S(1)} %shard_map.118.refs_0_), channel_id=1, source_target_pairs={{0,3},{1,2},{2,1},{3,0},{4,7},{5,6},{6,5},{7,4},{8,11},{9,10},{10,... | collective-permute-start | bytes 196616 | tf_op jit(solution)/shard_map/ppermute | solution.py:55
  37.0 7.1 %collective-permute-start.19 = (bf16[128,256]{1,0:T(8,128)(2,1)S(1)}, bf16[128,256]{1,0:T(8,128)(2,1)S(1)}, u32[]{:S(2)}, u32[]{:S(2)}) collective-permute-start(bf16[128,256]{1,0:T(8,128)(2,1)S(1)} %shard_map.118.refs_0_), channel_id=1, source_target_pairs={{0,2},{1,3},{2,0},{3,1},{4,6},{5,7},{6,4},{7,5},{8,10},{9,11},{10,... | collective-permute-start | bytes 196616 | tf_op jit(solution)/shard_map/ppermute | solution.py:55
  37.7 6.4 %collective-permute-start.18 = (bf16[128,256]{1,0:T(8,128)(2,1)S(1)}, bf16[128,256]{1,0:T(8,128)(2,1)S(1)}, u32[]{:S(2)}, u32[]{:S(2)}) collective-permute-start(bf16[128,256]{1,0:T(8,128)(2,1)S(1)} %shard_map.118.refs_0_), channel_id=1, source_target_pairs={{0,1},{1,0},{2,3},{3,2},{4,5},{5,4},{6,7},{7,6},{8,9},{9,8},{10,11... | collective-permute-start | bytes 196616 | tf_op jit(solution)/shard_map/ppermute | solution.py:55
  38.3 6.0 %collective-permute-start.15 = (bf16[144,256]{1,0:T(8,128)(2,1)S(1)}, bf16[144,256]{1,0:T(8,128)(2,1)S(1)}, u32[]{:S(2)}, u32[]{:S(2)}) collective-permute-start(bf16[144,256]{1,0:T(8,128)(2,1)S(1)} %get-tuple-element.60), channel_id=1, source_target_pairs={{0,24},{4,28},{8,16},{12,20},{16,8},{20,12},{24,0},{28,4},{1,25},{... | collective-permute-start | bytes 221192 | tf_op jit(solution)/shard_map/ppermute | solution.py:51
  40.3 4.6 %collective-permute-start.16 = (bf16[144,256]{1,0:T(8,128)(2,1)S(1)}, bf16[144,256]{1,0:T(8,128)(2,1)S(1)}, u32[]{:S(2)}, u32[]{:S(2)}) collective-permute-start(bf16[144,256]{1,0:T(8,128)(2,1)S(1)} %get-tuple-element.61), channel_id=1, source_target_pairs={{0,16},{4,20},{8,24},{12,28},{16,0},{20,4},{24,8},{28,12},{1,17},{... | collective-permute-start | bytes 221192 | tf_op jit(solution)/shard_map/ppermute | solution.py:51
  40.8 4.4 %collective-permute-start.17 = (bf16[144,256]{1,0:T(8,128)(2,1)S(1)}, bf16[144,256]{1,0:T(8,128)(2,1)S(1)}, u32[]{:S(2)}, u32[]{:S(2)}) collective-permute-start(bf16[144,256]{1,0:T(8,128)(2,1)S(1)} %get-tuple-element.62), channel_id=1, source_target_pairs={{0,8},{4,12},{8,0},{12,4},{16,24},{20,28},{24,16},{28,20},{1,9},{5... | collective-permute-start | bytes 221192 | tf_op jit(solution)/shard_map/ppermute | solution.py:51
  44.2 1.4 %collective-permute-start.21 = (f32[128,256]{1,0:T(8,128)S(1)}, f32[128,256]{1,0:T(8,128)S(1)}, u32[]{:S(2)}, u32[]{:S(2)}) collective-permute-start(f32[128,256]{1,0:T(8,128)S(1)} %shard_map.121.mine_ref), channel_id=1, source_target_pairs={{0,4},{4,0},{8,12},{12,8},{16,20},{20,16},{24,28},{28,24},{1,5},{5... | collective-permute-start | bytes 393224 | tf_op jit(solution)/shard_map/ppermute | solution.py:41

commit v17 on v16

--- a/solution.py
+++ b/solution.py
@@ -203,7 +203,10 @@
 
 def col_sum_kernel(norm, *refs):
     *parts, half_ref, stage = refs
-    total = total_of(len(parts), lax.axis_index("col"), [ref[...] for ref in parts], stage)
+    cols = len(parts)
+    by_offset = dict(zip([0] + list(range(2, cols)) + [1], parts))
+    pieces = [by_offset[k][...] for k in range(cols)]
+    total = total_of(cols, lax.axis_index("col"), pieces, stage)
     half_ref[...] = total * norm
 
 
@@ -384,7 +387,7 @@
         [VMEM] * cols,
         [(grads_shape, F32)],
         [pltpu.VMEM((cols,) + grads_shape, BF16)],
-    )(grads, *(grad_parts[k] for k in range(1, cols)))
+    )(grads, *(grad_parts[k] for k in order))
     theirs = to_core(mine, rows)
     x_piece, bias_sum = call(
         functools.partial(owned_sum_kernel, norm, list(across)),

time: 46.6 us -> 48.2 us (1.034)
  starting transfers between devices: 24.9 us -> 25.9 us
  waiting for transfers between devices: 15.3 us -> 16 us
    ppermute x9, waiting for transfers between devices: 3.47 us -> 2.56 us  [to_chip(): return lax.ppermute(x, 'row', pairs)]
    ppermute x9, starting transfers between devices: 13.3 us -> 14.2 us  [to_col(): lax.ppermute(x, 'col', [(i, target(cols, i, k)) for i in range(cols)])]
    ppermute x4, waiting for transfers between devices: 1.87 us -> 2.77 us  [to_core(): return lax.ppermute(x, 'row', [(i, i ^ 1) for i in range(rows)])]
    ppermute x9, waiting for transfers between devices: 9.98 us -> 10.7 us  [to_col(): lax.ppermute(x, 'col', [(i, target(cols, i, k)) for i in range(cols)])]
  transfers between devices with their start and end apart: 22 -> 22, of which waited for: 13 -> 12; matrix products, arithmetic and copies ran while one was open for 0% -> 0% of each run, Pallas kernels for 3% -> 3%
where the time goes in v17:
time: 48.2 us; the launch traced here: 48 us
  starting transfers between devices  25.9 us (54%)
  waiting for transfers between devices  16 us (33%)
  Pallas kernels  3.94 us (8%)
  between operations  1.46 us (3%)
  local copies, waits for them, and re-layouts  0.68 us (1%)
    ppermute x9, starting transfers between devices, to_col(): lax.ppermute(x, 'col', [(i, target(cols, i, k)) for i in range(cols)])  14.2 us
    ppermute x9, starting transfers between devices, to_chip(): return lax.ppermute(x, 'row', pairs)  11.4 us
    ppermute x9, waiting for transfers between devices, to_col(): lax.ppermute(x, 'col', [(i, target(cols, i, k)) for i in range(cols)])  10.7 us
    ppermute x4, waiting for transfers between devices, to_core(): return lax.ppermute(x, 'row', [(i, i ^ 1) for i in range(rows)])  2.77 us
    ppermute x9, waiting for transfers between devices, to_chip(): return lax.ppermute(x, 'row', pairs)  2.56 us
  transfers between devices with their start and end apart: 22, of which 12 were waited for; matrix products, arithmetic and copies ran while one was open for 0% of the time, Pallas kernels for 3%

profile of v17, /device:TPU:0, one launch (start us, length us, event | category | flops | bytes accessed | tf_op | source)
XLA Modules:
  0.0 48.0 jit_solution(10238024750061744943)
XLA Ops:
  0.6 0.9 %shard_map.112 = (bf16[128,256]{1,0:T(8,128)(2,1)S(1)}, f32[128,256]{1,0:T(8,128)S(1)}) custom-call(bf16[128,256]{1,0:T(8,128)(2,1)} %features_hbm.1, s32[1,128]{1,0:T(1,128)} %bitcast.4), custom_call_target="tpu_custom_call" | custom-call | flops 1000000 | bytes 1000000 | tf_op jit(solution)/shard_map/pallas_call | solution.py:322
  1.5 4.0 %collective-permute-start.2 = (bf16[128,256]{1,0:T(8,128)(2,1)S(1)}, bf16[128,256]{1,0:T(8,128)(2,1)S(1)}, u32[]{:S(2)}, u32[]{:S(2)}) collective-permute-start(bf16[128,256]{1,0:T(8,128)(2,1)S(1)} %get-tuple-element.40.refs_0_), channel_id=1, source_target_pairs={{0,24},{4,28},{8,16},{12,20},{16,8},{20,12},{24,0},{28,4},{1,25},{... | collective-permute-start | bytes 196616 | tf_op jit(solution)/shard_map/ppermute | solution.py:51
  5.5 0.5 %collective-permute-start.1 = (bf16[128,256]{1,0:T(8,128)(2,1)S(1)}, bf16[128,256]{1,0:T(8,128)(2,1)S(1)}, u32[]{:S(2)}, u32[]{:S(2)}) collective-permute-start(bf16[128,256]{1,0:T(8,128)(2,1)S(1)} %get-tuple-element.40.refs_0_), channel_id=1, source_target_pairs={{0,16},{4,20},{8,24},{12,28},{16,0},{20,4},{24,8},{28,12},{1,17},{... | collective-permute-start | bytes 196616 | tf_op jit(solution)/shard_map/ppermute | solution.py:51
  6.0 0.1 collective-permute-start
  6.8 0.0 copy-start.4
  6.8 0.7 %copy-done.4 = f32[256]{0:T(256)S(1)} copy-done((f32[256]{0:T(256)S(1)}, f32[256]{0:T(256)}, u32[]{:S(2)}) %copy-start.4) | copy-done | bytes 1048
  7.5 0.5 %shard_map.111 = (bf16[16,128,128]{2,1,0:T(8,128)(2,1)S(1)}, bf16[16,128,128]{2,1,0:T(8,128)(2,1)S(1)}, f32[1,256]{1,0:T(1,128)S(1)}) custom-call(s32[1,1]{1,0:T(1,128)S(6)} %copy.12.count_ref, s32[1,1,16,512]{3,2,1,0:T(8,128)S(1)} %copy-done.3, f32[1,256]{1,0:T(1,128)S(1)} %bitcast.3), custom_call_target="tpu_custom_call" | custom-call | flops 4000000000 | bytes 1000000 | tf_op jit(solution)/shard_map/pallas_call | solution.py:329
  8.0 0.0 collective-permute-done.2.refs_3_
  8.0 1.7 %collective-permute-done.1.refs_2_ = bf16[128,256]{1,0:T(8,128)(2,1)S(1)} collective-permute-done((bf16[128,256]{1,0:T(8,128)(2,1)S(1)}, bf16[128,256]{1,0:T(8,128)(2,1)S(1)}, u32[]{:S(2)}, u32[]{:S(2)}) %collective-permute-start.1) | collective-permute-done | bytes 65568 | tf_op jit(solution)/shard_map/ppermute | solution.py:51
  9.8 0.5 %collective-permute-done.refs_1_ = bf16[128,256]{1,0:T(8,128)(2,1)S(1)} collective-permute-done((bf16[128,256]{1,0:T(8,128)(2,1)S(1)}, bf16[128,256]{1,0:T(8,128)(2,1)S(1)}, u32[]{:S(2)}, u32[]{:S(2)}) %collective-permute-start) | collective-permute-done | bytes 65568 | tf_op jit(solution)/shard_map/ppermute | solution.py:51
  10.3 0.0 copy-start
  10.3 0.0 copy-start.1
  10.3 0.1 collective-permute-start.3
  10.4 1.5 %collective-permute-done.3.next_ref = bf16[4,128,256]{2,1,0:T(8,128)(2,1)S(1)} collective-permute-done((bf16[4,128,256]{2,1,0:T(8,128)(2,1)S(1)}, bf16[4,128,256]{2,1,0:T(8,128)(2,1)S(1)}, u32[]{:S(2)}, u32[]{:S(2)}) %collective-permute-start.3) | collective-permute-done | bytes 262176 | tf_op jit(solution)/shard_map/ppermute | solution.py:41
  11.9 0.5 %shard_map.114 = (f32[128,256]{1,0:T(8,128)S(1)}, bf16[128,256]{1,0:T(8,128)(2,1)S(1)}, bf16[128,256]{1,0:T(8,128)(2,1)S(1)}, bf16[128,256]{1,0:T(8,128)(2,1)S(1)}) custom-call(s32[1,1,16]{2,1,0:T(1,128)S(1)} %copy-done.2, s32[1,1]{1,0:T(1,128)S(6)} %copy.12.count_ref, bf16[16,128,128]{2,1,0:T(8,128)(2,1)S(1)} %get-tuple-element.41.blocks_ref, ...), custom_call_target="tpu_custom_call" | custom-call | flops 1000000 | bytes 1000000 | tf_op jit(solution)/shard_map/pallas_call | solution.py:338
  12.4 2.7 %collective-permute-start.4 = (bf16[128,256]{1,0:T(8,128)(2,1)S(1)}, bf16[128,256]{1,0:T(8,128)(2,1)S(1)}, u32[]{:S(2)}, u32[]{:S(2)}) collective-permute-start(bf16[128,256]{1,0:T(8,128)(2,1)S(1)} %get-tuple-element.46), channel_id=1, source_target_pairs={{0,2},{1,3},{2,0},{3,1},{4,6},{5,7},{6,4},{7,5},{8,10},{9,11},{10,... | collective-permute-start | bytes 196616 | tf_op jit(solution)/shard_map/ppermute | solution.py:55
  15.1 1.3 %collective-permute-start.5 = (bf16[128,256]{1,0:T(8,128)(2,1)S(1)}, bf16[128,256]{1,0:T(8,128)(2,1)S(1)}, u32[]{:S(2)}, u32[]{:S(2)}) collective-permute-start(bf16[128,256]{1,0:T(8,128)(2,1)S(1)} %get-tuple-element.47), channel_id=1, source_target_pairs={{0,3},{1,2},{2,1},{3,0},{4,7},{5,6},{6,5},{7,4},{8,11},{9,10},{10,... | collective-permute-start | bytes 196616 | tf_op jit(solution)/shard_map/ppermute | solution.py:55
  16.4 0.2 collective-permute-start.6
  16.7 3.5 %collective-permute-done.4.refs_1_ = bf16[128,256]{1,0:T(8,128)(2,1)S(1)} collective-permute-done((bf16[128,256]{1,0:T(8,128)(2,1)S(1)}, bf16[128,256]{1,0:T(8,128)(2,1)S(1)}, u32[]{:S(2)}, u32[]{:S(2)}) %collective-permute-start.4) | collective-permute-done | bytes 65568 | tf_op jit(solution)/shard_map/ppermute | solution.py:55
  20.2 1.3 %collective-permute-done.5.refs_2_ = bf16[128,256]{1,0:T(8,128)(2,1)S(1)} collective-permute-done((bf16[128,256]{1,0:T(8,128)(2,1)S(1)}, bf16[128,256]{1,0:T(8,128)(2,1)S(1)}, u32[]{:S(2)}, u32[]{:S(2)}) %collective-permute-start.5) | collective-permute-done | bytes 65568 | tf_op jit(solution)/shard_map/ppermute | solution.py:55
  21.5 0.3 collective-permute-done.6.refs_3_
  21.8 0.4 shard_map.115
  22.2 0.1 collective-permute-start.10
  22.3 3.2 %collective-permute-start.9 = (bf16[144,256]{1,0:T(8,128)(2,1)S(1)}, bf16[144,256]{1,0:T(8,128)(2,1)S(1)}, u32[]{:S(2)}, u32[]{:S(2)}) collective-permute-start(bf16[144,256]{1,0:T(8,128)(2,1)S(1)} %get-tuple-element.51.refs_0_), channel_id=1, source_target_pairs={{0,3},{1,2},{2,1},{3,0},{4,7},{5,6},{6,5},{7,4},{8,11},{9,10},{10,... | collective-permute-start | bytes 221192 | tf_op jit(solution)/shard_map/ppermute | solution.py:55
  25.5 0.0 collective-permute-start.8
  25.5 1.2 %collective-permute-start.7 = (bf16[144,256]{1,0:T(8,128)(2,1)S(1)}, bf16[144,256]{1,0:T(8,128)(2,1)S(1)}, u32[]{:S(2)}, u32[]{:S(2)}) collective-permute-start(bf16[144,256]{1,0:T(8,128)(2,1)S(1)} %get-tuple-element.51.refs_0_), channel_id=1, source_target_pairs={{0,1},{1,0},{2,3},{3,2},{4,5},{5,4},{6,7},{7,6},{8,9},{9,8},{10,11... | collective-permute-start | bytes 221192 | tf_op jit(solution)/shard_map/ppermute | solution.py:55
  26.8 1.6 %collective-permute-start.13 = (bf16[128,256]{1,0:T(8,128)(2,1)S(1)}, bf16[128,256]{1,0:T(8,128)(2,1)S(1)}, u32[]{:S(2)}, u32[]{:S(2)}) collective-permute-start(bf16[128,256]{1,0:T(8,128)(2,1)S(1)} %shard_map.117.refs_0_), channel_id=1, source_target_pairs={{0,24},{4,28},{8,16},{12,20},{16,8},{20,12},{24,0},{28,4},{1,25},{... | collective-permute-start | bytes 196616 | tf_op jit(solution)/shard_map/ppermute | solution.py:51
  28.3 0.5 %collective-permute-start.12 = (bf16[128,256]{1,0:T(8,128)(2,1)S(1)}, bf16[128,256]{1,0:T(8,128)(2,1)S(1)}, u32[]{:S(2)}, u32[]{:S(2)}) collective-permute-start(bf16[128,256]{1,0:T(8,128)(2,1)S(1)} %shard_map.117.refs_0_), channel_id=1, source_target_pairs={{0,16},{4,20},{8,24},{12,28},{16,0},{20,4},{24,8},{28,12},{1,17},{... | collective-permute-start | bytes 196616 | tf_op jit(solution)/shard_map/ppermute | solution.py:51
  28.8 0.3 collective-permute-done.9.refs_3_
  29.1 1.2 %collective-permute-start.11 = (bf16[128,256]{1,0:T(8,128)(2,1)S(1)}, bf16[128,256]{1,0:T(8,128)(2,1)S(1)}, u32[]{:S(2)}, u32[]{:S(2)}) collective-permute-start(bf16[128,256]{1,0:T(8,128)(2,1)S(1)} %shard_map.117.refs_0_), channel_id=1, source_target_pairs={{0,8},{4,12},{8,0},{12,4},{16,24},{20,28},{24,16},{28,20},{1,9},{5... | collective-permute-start | bytes 196616 | tf_op jit(solution)/shard_map/ppermute | solution.py:51
  30.3 2.2 %collective-permute-done.8.refs_2_ = bf16[144,256]{1,0:T(8,128)(2,1)S(1)} collective-permute-done((bf16[144,256]{1,0:T(8,128)(2,1)S(1)}, bf16[144,256]{1,0:T(8,128)(2,1)S(1)}, u32[]{:S(2)}, u32[]{:S(2)}) %collective-permute-start.8) | collective-permute-done | bytes 73760 | tf_op jit(solution)/shard_map/ppermute | solution.py:55
  32.5 0.6 %shard_map.116 = (f32[4,128,256]{2,1,0:T(8,128)S(1)}, bf16[16,256]{1,0:T(8,128)(2,1)S(1)}, bf16[528,256]{1,0:T(8,128)(2,1)S(1)}) custom-call(s32[1,1,16]{2,1,0:T(1,128)S(1)} %copy-done.2, s32[1,1]{1,0:T(1,128)S(6)} %copy.12.count_ref, bf16[16,128,128]{2,1,0:T(8,128)(2,1)S(1)} %get-tuple-element.50.turned_ref, ...), custom_call_target="tpu_custom_call" | custom-call | flops 4000000000 | bytes 1000000 | tf_op jit(solution)/shard_map/pallas_call | solution.py:365
  33.1 0.3 collective-permute-done.11.refs_1_
  33.4 0.1 shard_map.118.refs_0_
  33.5 0.1 collective-permute-start.14
  33.6 2.7 %collective-permute-start.20 = (bf16[128,256]{1,0:T(8,128)(2,1)S(1)}, bf16[128,256]{1,0:T(8,128)(2,1)S(1)}, u32[]{:S(2)}, u32[]{:S(2)}) collective-permute-start(bf16[128,256]{1,0:T(8,128)(2,1)S(1)} %shard_map.118.refs_0_), channel_id=1, source_target_pairs={{0,1},{1,0},{2,3},{3,2},{4,5},{5,4},{6,7},{7,6},{8,9},{9,8},{10,11... | collective-permute-start | bytes 196616 | tf_op jit(solution)/shard_map/ppermute | solution.py:55
  36.2 2.8 %collective-permute-start.19 = (bf16[128,256]{1,0:T(8,128)(2,1)S(1)}, bf16[128,256]{1,0:T(8,128)(2,1)S(1)}, u32[]{:S(2)}, u32[]{:S(2)}) collective-permute-start(bf16[128,256]{1,0:T(8,128)(2,1)S(1)} %shard_map.118.refs_0_), channel_id=1, source_target_pairs={{0,3},{1,2},{2,1},{3,0},{4,7},{5,6},{6,5},{7,4},{8,11},{9,10},{10,... | collective-permute-start | bytes 196616 | tf_op jit(solution)/shard_map/ppermute | solution.py:55
  39.1 0.1 shard_map.119
  39.2 1.6 %collective-permute-start.15 = (bf16[144,256]{1,0:T(8,128)(2,1)S(1)}, bf16[144,256]{1,0:T(8,128)(2,1)S(1)}, u32[]{:S(2)}, u32[]{:S(2)}) collective-permute-start(bf16[144,256]{1,0:T(8,128)(2,1)S(1)} %get-tuple-element.60), channel_id=1, source_target_pairs={{0,24},{4,28},{8,16},{12,20},{16,8},{20,12},{24,0},{28,4},{1,25},{... | collective-permute-start | bytes 221192 | tf_op jit(solution)/shard_map/ppermute | solution.py:51
  40.7 0.3 collective-permute-start.16
  41.0 1.7 %collective-permute-start.17 = (bf16[144,256]{1,0:T(8,128)(2,1)S(1)}, bf16[144,256]{1,0:T(8,128)(2,1)S(1)}, u32[]{:S(2)}, u32[]{:S(2)}) collective-permute-start(bf16[144,256]{1,0:T(8,128)(2,1)S(1)} %get-tuple-element.62), channel_id=1, source_target_pairs={{0,8},{4,12},{8,0},{12,4},{16,24},{20,28},{24,16},{28,20},{1,9},{5... | collective-permute-start | bytes 221192 | tf_op jit(solution)/shard_map/ppermute | solution.py:51
  42.7 0.7 %collective-permute-done.19.refs_2_ = bf16[128,256]{1,0:T(8,128)(2,1)S(1)} collective-permute-done((bf16[128,256]{1,0:T(8,128)(2,1)S(1)}, bf16[128,256]{1,0:T(8,128)(2,1)S(1)}, u32[]{:S(2)}, u32[]{:S(2)}) %collective-permute-start.19) | collective-permute-done | bytes 65568 | tf_op jit(solution)/shard_map/ppermute | solution.py:55
  43.5 2.3 %collective-permute-done.18.refs_1_ = bf16[128,256]{1,0:T(8,128)(2,1)S(1)} collective-permute-done((bf16[128,256]{1,0:T(8,128)(2,1)S(1)}, bf16[128,256]{1,0:T(8,128)(2,1)S(1)}, u32[]{:S(2)}, u32[]{:S(2)}) %collective-permute-start.18) | collective-permute-done | bytes 65568 | tf_op jit(solution)/shard_map/ppermute | solution.py:55
  45.7 0.1 shard_map.121.mine_ref
  45.8 0.1 collective-permute-start.21
  45.9 0.1 shard_map.120
  46.0 1.2 %collective-permute-done.21.theirs_ref = f32[128,256]{1,0:T(8,128)S(1)} collective-permute-done((f32[128,256]{1,0:T(8,128)S(1)}, f32[128,256]{1,0:T(8,128)S(1)}, u32[]{:S(2)}, u32[]{:S(2)}) %collective-permute-start.21) | collective-permute-done | bytes 131104 | tf_op jit(solution)/shard_map/ppermute | solution.py:41
  47.2 0.8 %shard_map.122 = (bf16[128,256]{1,0:T(8,128)(2,1)}, bf16[128,256]{1,0:T(8,128)(2,1)}, f32[256,256]{1,0:T(8,128)}, f32[1,256]{1,0:T(1,128)}) custom-call(bf16[128,256]{1,0:T(8,128)(2,1)S(1)} %get-tuple-element.49.out_ref, bf16[128,256]{1,0:T(8,128)(2,1)S(1)} %get-tuple-element.63.x_ref, f32[128,256]{1,0:T(8,128)S(1)} %shard_map.121.mine_ref, ...), custom_call_target="tpu_custom_call" | custom-call | flops 1000000 | bytes 1000000 | tf_op jit(solution)/shard_map/pallas_call | solution.py:399
  (18 shorter events, 0.1 us)
Async XLA Ops:
  0.6 6.2 %copy-start.3 = (s32[1,1,16,512]{3,2,1,0:T(8,128)S(1)}, s32[1,1,16,512]{3,2,1,0:T(8,128)}, u32[]{:S(2)}) copy-start(s32[1,1,16,512]{3,2,1,0:T(8,128)} %edge_ref.1) | copy-start | bytes 98308
  1.5 6.5 %collective-permute-start.2 = (bf16[128,256]{1,0:T(8,128)(2,1)S(1)}, bf16[128,256]{1,0:T(8,128)(2,1)S(1)}, u32[]{:S(2)}, u32[]{:S(2)}) collective-permute-start(bf16[128,256]{1,0:T(8,128)(2,1)S(1)} %get-tuple-element.40.refs_0_), channel_id=1, source_target_pairs={{0,24},{4,28},{8,16},{12,20},{16,8},{20,12},{24,0},{28,4},{1,25},{... | collective-permute-start | bytes 196616 | tf_op jit(solution)/shard_map/ppermute | solution.py:51
  5.5 4.3 %collective-permute-start.1 = (bf16[128,256]{1,0:T(8,128)(2,1)S(1)}, bf16[128,256]{1,0:T(8,128)(2,1)S(1)}, u32[]{:S(2)}, u32[]{:S(2)}) collective-permute-start(bf16[128,256]{1,0:T(8,128)(2,1)S(1)} %get-tuple-element.40.refs_0_), channel_id=1, source_target_pairs={{0,16},{4,20},{8,24},{12,28},{16,0},{20,4},{24,8},{28,12},{1,17},{... | collective-permute-start | bytes 196616 | tf_op jit(solution)/shard_map/ppermute | solution.py:51
  6.0 4.3 %collective-permute-start = (bf16[128,256]{1,0:T(8,128)(2,1)S(1)}, bf16[128,256]{1,0:T(8,128)(2,1)S(1)}, u32[]{:S(2)}, u32[]{:S(2)}) collective-permute-start(bf16[128,256]{1,0:T(8,128)(2,1)S(1)} %get-tuple-element.40.refs_0_), channel_id=1, source_target_pairs={{0,8},{4,12},{8,0},{12,4},{16,24},{20,28},{24,16},{28,20},{1,9},{5... | collective-permute-start | bytes 196616 | tf_op jit(solution)/shard_map/ppermute | solution.py:51
  6.8 0.7 %copy-start.4 = (f32[256]{0:T(256)S(1)}, f32[256]{0:T(256)}, u32[]{:S(2)}) copy-start(f32[256]{0:T(256)} %param.11) | copy-start | bytes 3076
  10.3 1.7 %copy-start.2 = (s32[1,1,16]{2,1,0:T(1,128)S(1)}, s32[1,1,16]{2,1,0:T(1,128)}, u32[]{:S(2)}) copy-start(s32[1,1,16]{2,1,0:T(1,128)} %pos_ref.3) | copy-start | bytes 196
  10.3 11.5 %copy-start = (bf16[256,256]{1,0:T(8,128)(2,1)S(1)}, bf16[256,256]{1,0:T(8,128)(2,1)}, u32[]{:S(2)}) copy-start(bf16[256,256]{1,0:T(8,128)(2,1)} %weight_ref.1) | copy-start | bytes 393220
  10.3 11.5 %copy-start.1 = (bf16[128,256]{1,0:T(8,128)(2,1)S(1)}, bf16[128,256]{1,0:T(8,128)(2,1)}, u32[]{:S(2)}) copy-start(bf16[128,256]{1,0:T(8,128)(2,1)} %cot_ref.1) | copy-start | bytes 196612
  10.3 1.6 %collective-permute-start.3 = (bf16[4,128,256]{2,1,0:T(8,128)(2,1)S(1)}, bf16[4,128,256]{2,1,0:T(8,128)(2,1)S(1)}, u32[]{:S(2)}, u32[]{:S(2)}) collective-permute-start(bf16[4,128,256]{2,1,0:T(8,128)(2,1)S(1)} %shard_map.113.near_ref), channel_id=1, source_target_pairs={{0,4},{4,0},{8,12},{12,8},{16,20},{20,16},{24,28},{28,24},{1,5},{5... | collective-permute-start | bytes 786440 | tf_op jit(solution)/shard_map/ppermute | solution.py:41
  12.4 7.8 %collective-permute-start.4 = (bf16[128,256]{1,0:T(8,128)(2,1)S(1)}, bf16[128,256]{1,0:T(8,128)(2,1)S(1)}, u32[]{:S(2)}, u32[]{:S(2)}) collective-permute-start(bf16[128,256]{1,0:T(8,128)(2,1)S(1)} %get-tuple-element.46), channel_id=1, source_target_pairs={{0,2},{1,3},{2,0},{3,1},{4,6},{5,7},{6,4},{7,5},{8,10},{9,11},{10,... | collective-permute-start | bytes 196616 | tf_op jit(solution)/shard_map/ppermute | solution.py:55
  15.1 6.4 %collective-permute-start.5 = (bf16[128,256]{1,0:T(8,128)(2,1)S(1)}, bf16[128,256]{1,0:T(8,128)(2,1)S(1)}, u32[]{:S(2)}, u32[]{:S(2)}) collective-permute-start(bf16[128,256]{1,0:T(8,128)(2,1)S(1)} %get-tuple-element.47), channel_id=1, source_target_pairs={{0,3},{1,2},{2,1},{3,0},{4,7},{5,6},{6,5},{7,4},{8,11},{9,10},{10,... | collective-permute-start | bytes 196616 | tf_op jit(solution)/shard_map/ppermute | solution.py:55
  16.4 5.4 %collective-permute-start.6 = (bf16[128,256]{1,0:T(8,128)(2,1)S(1)}, bf16[128,256]{1,0:T(8,128)(2,1)S(1)}, u32[]{:S(2)}, u32[]{:S(2)}) collective-permute-start(bf16[128,256]{1,0:T(8,128)(2,1)S(1)} %get-tuple-element.48), channel_id=1, source_target_pairs={{0,1},{1,0},{2,3},{3,2},{4,5},{5,4},{6,7},{7,6},{8,9},{9,8},{10,11... | collective-permute-start | bytes 196616 | tf_op jit(solution)/shard_map/ppermute | solution.py:55
  22.2 4.5 %collective-permute-start.10 = (bf16[128,256]{1,0:T(8,128)(2,1)S(1)}, bf16[128,256]{1,0:T(8,128)(2,1)S(1)}, u32[]{:S(2)}, u32[]{:S(2)}) collective-permute-start(bf16[128,256]{1,0:T(8,128)(2,1)S(1)} %get-tuple-element.56), channel_id=1, source_target_pairs={{0,4},{4,0},{8,12},{12,8},{16,20},{20,16},{24,28},{28,24},{1,5},{5... | collective-permute-start | bytes 196616 | tf_op jit(solution)/shard_map/ppermute | solution.py:41
  22.3 6.8 %collective-permute-start.9 = (bf16[144,256]{1,0:T(8,128)(2,1)S(1)}, bf16[144,256]{1,0:T(8,128)(2,1)S(1)}, u32[]{:S(2)}, u32[]{:S(2)}) collective-permute-start(bf16[144,256]{1,0:T(8,128)(2,1)S(1)} %get-tuple-element.51.refs_0_), channel_id=1, source_target_pairs={{0,3},{1,2},{2,1},{3,0},{4,7},{5,6},{6,5},{7,4},{8,11},{9,10},{10,... | collective-permute-start | bytes 221192 | tf_op jit(solution)/shard_map/ppermute | solution.py:55
  25.5 7.0 %collective-permute-start.8 = (bf16[144,256]{1,0:T(8,128)(2,1)S(1)}, bf16[144,256]{1,0:T(8,128)(2,1)S(1)}, u32[]{:S(2)}, u32[]{:S(2)}) collective-permute-start(bf16[144,256]{1,0:T(8,128)(2,1)S(1)} %get-tuple-element.51.refs_0_), channel_id=1, source_target_pairs={{0,2},{1,3},{2,0},{3,1},{4,6},{5,7},{6,4},{7,5},{8,10},{9,11},{10,... | collective-permute-start | bytes 221192 | tf_op jit(solution)/shard_map/ppermute | solution.py:55
  25.5 7.0 %collective-permute-start.7 = (bf16[144,256]{1,0:T(8,128)(2,1)S(1)}, bf16[144,256]{1,0:T(8,128)(2,1)S(1)}, u32[]{:S(2)}, u32[]{:S(2)}) collective-permute-start(bf16[144,256]{1,0:T(8,128)(2,1)S(1)} %get-tuple-element.51.refs_0_), channel_id=1, source_target_pairs={{0,1},{1,0},{2,3},{3,2},{4,5},{5,4},{6,7},{7,6},{8,9},{9,8},{10,11... | collective-permute-start | bytes 221192 | tf_op jit(solution)/shard_map/ppermute | solution.py:55
  26.8 6.3 %collective-permute-start.13 = (bf16[128,256]{1,0:T(8,128)(2,1)S(1)}, bf16[128,256]{1,0:T(8,128)(2,1)S(1)}, u32[]{:S(2)}, u32[]{:S(2)}) collective-permute-start(bf16[128,256]{1,0:T(8,128)(2,1)S(1)} %shard_map.117.refs_0_), channel_id=1, source_target_pairs={{0,24},{4,28},{8,16},{12,20},{16,8},{20,12},{24,0},{28,4},{1,25},{... | collective-permute-start | bytes 196616 | tf_op jit(solution)/shard_map/ppermute | solution.py:51
  28.3 4.8 %collective-permute-start.12 = (bf16[128,256]{1,0:T(8,128)(2,1)S(1)}, bf16[128,256]{1,0:T(8,128)(2,1)S(1)}, u32[]{:S(2)}, u32[]{:S(2)}) collective-permute-start(bf16[128,256]{1,0:T(8,128)(2,1)S(1)} %shard_map.117.refs_0_), channel_id=1, source_target_pairs={{0,16},{4,20},{8,24},{12,28},{16,0},{20,4},{24,8},{28,12},{1,17},{... | collective-permute-start | bytes 196616 | tf_op jit(solution)/shard_map/ppermute | solution.py:51
  29.1 4.3 %collective-permute-start.11 = (bf16[128,256]{1,0:T(8,128)(2,1)S(1)}, bf16[128,256]{1,0:T(8,128)(2,1)S(1)}, u32[]{:S(2)}, u32[]{:S(2)}) collective-permute-start(bf16[128,256]{1,0:T(8,128)(2,1)S(1)} %shard_map.117.refs_0_), channel_id=1, source_target_pairs={{0,8},{4,12},{8,0},{12,4},{16,24},{20,28},{24,16},{28,20},{1,9},{5... | collective-permute-start | bytes 196616 | tf_op jit(solution)/shard_map/ppermute | solution.py:51
  33.5 5.6 %collective-permute-start.14 = (bf16[528,256]{1,0:T(8,128)(2,1)S(1)}, bf16[528,256]{1,0:T(8,128)(2,1)S(1)}, u32[]{:S(2)}, u32[]{:S(2)}) collective-permute-start(bf16[528,256]{1,0:T(8,128)(2,1)S(1)} %get-tuple-element.57), channel_id=1, source_target_pairs={{0,4},{4,0},{8,12},{12,8},{16,20},{20,16},{24,28},{28,24},{1,5},{5... | collective-permute-start | bytes 811016 | tf_op jit(solution)/shard_map/ppermute | solution.py:41
  33.6 7.4 %collective-permute-start.20 = (bf16[128,256]{1,0:T(8,128)(2,1)S(1)}, bf16[128,256]{1,0:T(8,128)(2,1)S(1)}, u32[]{:S(2)}, u32[]{:S(2)}) collective-permute-start(bf16[128,256]{1,0:T(8,128)(2,1)S(1)} %shard_map.118.refs_0_), channel_id=1, source_target_pairs={{0,1},{1,0},{2,3},{3,2},{4,5},{5,4},{6,7},{7,6},{8,9},{9,8},{10,11... | collective-permute-start | bytes 196616 | tf_op jit(solution)/shard_map/ppermute | solution.py:55
  36.2 7.2 %collective-permute-start.19 = (bf16[128,256]{1,0:T(8,128)(2,1)S(1)}, bf16[128,256]{1,0:T(8,128)(2,1)S(1)}, u32[]{:S(2)}, u32[]{:S(2)}) collective-permute-start(bf16[128,256]{1,0:T(8,128)(2,1)S(1)} %shard_map.118.refs_0_), channel_id=1, source_target_pairs={{0,3},{1,2},{2,1},{3,0},{4,7},{5,6},{6,5},{7,4},{8,11},{9,10},{10,... | collective-permute-start | bytes 196616 | tf_op jit(solution)/shard_map/ppermute | solution.py:55
  39.1 6.6 %collective-permute-start.18 = (bf16[128,256]{1,0:T(8,128)(2,1)S(1)}, bf16[128,256]{1,0:T(8,128)(2,1)S(1)}, u32[]{:S(2)}, u32[]{:S(2)}) collective-permute-start(bf16[128,256]{1,0:T(8,128)(2,1)S(1)} %shard_map.118.refs_0_), channel_id=1, source_target_pairs={{0,2},{1,3},{2,0},{3,1},{4,6},{5,7},{6,4},{7,5},{8,10},{9,11},{10,... | collective-permute-start | bytes 196616 | tf_op jit(solution)/shard_map/ppermute | solution.py:55
  39.2 6.7 %collective-permute-start.15 = (bf16[144,256]{1,0:T(8,128)(2,1)S(1)}, bf16[144,256]{1,0:T(8,128)(2,1)S(1)}, u32[]{:S(2)}, u32[]{:S(2)}) collective-permute-start(bf16[144,256]{1,0:T(8,128)(2,1)S(1)} %get-tuple-element.60), channel_id=1, source_target_pairs={{0,24},{4,28},{8,16},{12,20},{16,8},{20,12},{24,0},{28,4},{1,25},{... | collective-permute-start | bytes 221192 | tf_op jit(solution)/shard_map/ppermute | solution.py:51
  40.7 5.2 %collective-permute-start.16 = (bf16[144,256]{1,0:T(8,128)(2,1)S(1)}, bf16[144,256]{1,0:T(8,128)(2,1)S(1)}, u32[]{:S(2)}, u32[]{:S(2)}) collective-permute-start(bf16[144,256]{1,0:T(8,128)(2,1)S(1)} %get-tuple-element.61), channel_id=1, source_target_pairs={{0,16},{4,20},{8,24},{12,28},{16,0},{20,4},{24,8},{28,12},{1,17},{... | collective-permute-start | bytes 221192 | tf_op jit(solution)/shard_map/ppermute | solution.py:51
  41.0 4.9 %collective-permute-start.17 = (bf16[144,256]{1,0:T(8,128)(2,1)S(1)}, bf16[144,256]{1,0:T(8,128)(2,1)S(1)}, u32[]{:S(2)}, u32[]{:S(2)}) collective-permute-start(bf16[144,256]{1,0:T(8,128)(2,1)S(1)} %get-tuple-element.62), channel_id=1, source_target_pairs={{0,8},{4,12},{8,0},{12,4},{16,24},{20,28},{24,16},{28,20},{1,9},{5... | collective-permute-start | bytes 221192 | tf_op jit(solution)/shard_map/ppermute | solution.py:51
  45.8 1.4 %collective-permute-start.21 = (f32[128,256]{1,0:T(8,128)S(1)}, f32[128,256]{1,0:T(8,128)S(1)}, u32[]{:S(2)}, u32[]{:S(2)}) collective-permute-start(f32[128,256]{1,0:T(8,128)S(1)} %shard_map.121.mine_ref), channel_id=1, source_target_pairs={{0,4},{4,0},{8,12},{12,8},{16,20},{20,16},{24,28},{28,24},{1,5},{5... | collective-permute-start | bytes 393224 | tf_op jit(solution)/shard_map/ppermute | solution.py:41
